TPU v7x, 32 devices: a whole 2x2x4 slice. The times are simulated.
32 devices in a mesh: dp: 8 (over z, y), rep: 4 (over x, core).
Axes of the slice: x: 2, y: 2, z: 4, core: 2. Of those that a mesh axis runs over, the one named last changes fastest.
Arguments:
- tokens: bfloat16 [8, 704, 1024], P('dp', 'rep'), may hold values from -6 to 6
- offsets: int32 [8, 8], P('dp'), may hold values from 0 to 703, as said below
- w_proj: bfloat16 [1024, 3072], replicated, may hold values from -0.1875 to 0.1875
- forget_weight: float32 [1024], replicated, may hold values from -1 to 1
- reset_weight: float32 [1024], replicated, may hold values from -1 to 1
- forget_bias: float32 [1024], replicated, may hold values from 0 to 10
- reset_bias: float32 [1024], replicated, may hold values from -1 to 1
- layer_norm_gain: float32 [1024], replicated, may hold values from 0.5 to 1.5
- layer_norm_bias: float32 [1024], replicated, may hold values from -6 to 6
- cotangent: bfloat16 [8, 704, 1024], P('dp', 'rep'), may hold values from -6 to 6
Outputs:
- output: bfloat16 [8, 704, 1024], P('dp', 'rep')
- input_grad: bfloat16 [8, 704, 1024], P('dp', 'rep')
- proj_grad: float32 [1024, 3072], replicated
- forget_weight_grad: float32 [1024], replicated
- reset_weight_grad: float32 [1024], replicated
- forget_bias_grad: float32 [1024], replicated
- reset_bias_grad: float32 [1024], replicated
- gain_grad: float32 [1024], replicated
- bias_grad: float32 [1024], replicated
Inputs may be any that keep to these rules, and one draw needn't show every extreme that they name: offsets[r] lists start positions of row r's documents in ascending order; the first is 0; a position may repeat.
All inputs are finite; a program needn't handle non-finite values.
Results may differ from a plain program's by a relative error of at most 0.0059.
Values sent between devices are 32-bit elements; how exact they have to be, the bound alone decides.
No kernel may reach another device: no remote copies, remote signals or barrier semaphores. Data moves between devices by JAX's collectives and lax.ppermute only.
A program may use at most 128 MiB of HBM per device.

v0:
```python
import functools

import jax
import jax.numpy as jnp
from jax import lax
from jax.experimental import pallas as pl
from jax.experimental.pallas import tpu as pltpu
from jax.sharding import Mesh
from jax.sharding import PartitionSpec as P

EPS = 1e-05
SWAP = [(0, 1), (1, 0)]
VMEM_BYTES = 56 * 2**20
F32 = jnp.float32
BF16 = jnp.bfloat16


def swap(block, axis):
    return lax.ppermute(block, axis, SWAP)


def xor_permute(block, axis, distance):
    size = lax.axis_size(axis)
    return lax.ppermute(block, axis, [(i, i ^ distance) for i in range(size)])


def whole(ref_shape):
    return pl.BlockSpec(ref_shape, lambda i, s: (0,) * len(ref_shape))


def any_spec():
    return pl.BlockSpec(memory_space=pl.ANY)


def vmem():
    return pl.BlockSpec(memory_space=pltpu.VMEM)


def smem():
    return pl.BlockSpec(memory_space=pltpu.SMEM)


def shaped(shape, dtype=F32):
    return jax.ShapeDtypeStruct(shape, dtype)


def params(mib):
    return pltpu.CompilerParams(vmem_limit_bytes=mib * 2**20)


def widen_kernel(tokens_ref, tokens_out):
    tokens_out[...] = tokens_ref[...].astype(F32)


def widen(tokens):
    return pl.pallas_call(
        widen_kernel,
        out_shape=shaped(tokens.shape),
        in_specs=[vmem()],
        out_specs=vmem(),
        name="widen",
    )(tokens)


def widen_cot_kernel(sel, cot_ref, cot_out):
    cols = cot_ref.shape[1] // 4
    for k in range(2):
        at = pl.multiple_of((2 * k + sel[0]) * cols, cols)
        cot_out[:, k * cols : (k + 1) * cols] = cot_ref[:, pl.ds(at, cols)].astype(F32)


def widen_cot(sel, cot):
    return pl.pallas_call(
        widen_cot_kernel,
        out_shape=shaped((cot.shape[0], cot.shape[1] // 2)),
        in_specs=[smem(), vmem()],
        out_specs=vmem(),
        name="widen_cot",
    )(sel, cot)


def pack_cot_kernel(sel, cot_ref, sibling_ref, cot_out):
    block, cols = cot_ref.shape[0], cot_ref.shape[1] // 4
    mine = pl.multiple_of(sel[0] * cols, cols)
    cot_out[0:block, :] = cot_ref[:, pl.ds(mine, cols)].astype(F32)
    sibling = pl.multiple_of(sel[1] * cols, cols)
    cot_out[block:, :] = sibling_ref[:, pl.ds(sibling, cols)]


def pack_cot(sel, cot, sibling):
    return pl.pallas_call(
        pack_cot_kernel,
        out_shape=shaped((2 * cot.shape[0], cot.shape[1] // 4)),
        in_specs=[smem(), vmem(), vmem()],
        out_specs=vmem(),
        name="pack_cot",
    )(sel, cot, sibling)


def standardized(x):
    mean = jnp.mean(x, axis=-1, keepdims=True)
    centred = x - mean
    rdev = lax.rsqrt(jnp.mean(centred * centred, axis=-1, keepdims=True) + EPS)
    return centred * rdev, rdev


def norm_and_project(toks, norm_ref, weights, gates_ref, normed, cand, zf, zr, base):
    gain, bias = norm_ref[0:1, :], norm_ref[1:2, :]
    fb, rb = gates_ref[2:3, :], gates_ref[3:4, :]
    block = toks[0].shape[0]
    step = 16
    for at, tok in enumerate(toks):

        def body(i, carry, tok=tok, at=at):
            here = pl.ds(pl.multiple_of(i * step, step), step)
            there = pl.ds(pl.multiple_of(at * block + i * step, step), step)
            xhat, _ = standardized(tok[here, :])
            normed[there, :] = (xhat * gain + bias).astype(BF16)
            return carry

        lax.fori_loop(0, block // step, body, 0, unroll=True)
    rows = normed[...]
    here = slice(base, base + 2 * block)
    cand[here, :] = jnp.dot(rows, weights[0][...], preferred_element_type=F32)
    zf[here, :] = 0.5 * (jnp.dot(rows, weights[1][...], preferred_element_type=F32) + fb)
    zr[here, :] = 0.5 * (jnp.dot(rows, weights[2][...], preferred_element_type=F32) + rb)


def near_kernel(sel, tok0, tok1, w0, w1, w2, gates_ref, norm_ref, normed, cand, zf, zr):
    norm_and_project((tok0, tok1), norm_ref, (w0, w1, w2), gates_ref, normed, cand, zf, zr, 0)


def weight_specs(width, cols):
    return [
        pl.BlockSpec((width, cols), lambda i, s, k=k: (0, s[0] + k * (width // cols)))
        for k in range(3)
    ]


def run_near(sel, toks, w_proj, gates, norm):
    block, width = toks[0].shape
    cols = width // 4
    return pl.pallas_call(
        near_kernel,
        out_shape=(shaped((2 * block, width), BF16),) + (shaped((2 * block, cols)),) * 3,
        grid_spec=pltpu.PrefetchScalarGridSpec(
            num_scalar_prefetch=1,
            grid=(1,),
            in_specs=[whole((block, width))] * 2
            + weight_specs(width, cols)
            + [pl.BlockSpec((8, cols), lambda i, s: (0, s[0])), whole((8, width))],
            out_specs=(whole((2 * block, width)),) + (whole((2 * block, cols)),) * 3,
        ),
        compiler_params=params(24),
        name="near_blocks",
    )(sel, *toks, w_proj, w_proj, w_proj, gates, norm)


def forward_kernel(
    sel,
    tok0,
    tok1,
    cand_near,
    zf_near,
    zr_near,
    keep_ref,
    w0,
    w1,
    w2,
    gates_ref,
    norm_ref,
    normed,
    cand,
    zf,
    zr,
    state,
    half_prev,
    fwk,
    kh,
):
    length, cols = cand.shape
    block = length // 4
    near = slice(0, 2 * block)
    cand[near, :], zf[near, :], zr[near, :] = cand_near[...], zf_near[...], zr_near[...]
    half_fw = 0.5 * gates_ref[0:1, :]
    step = 16

    def keep_body(i, carry):
        here = pl.ds(pl.multiple_of(i * step, step), step)
        keep = jnp.broadcast_to(keep_ref[here, :], (step, cols))
        kh[here, :] = 0.5 * keep
        fwk[here, :] = keep * half_fw
        return carry

    lax.fori_loop(0, length // step, keep_body, 0, unroll=4)
    norm_and_project(
        (tok0, tok1), norm_ref, (w0, w1, w2), gates_ref, normed, cand, zf, zr, 2 * block
    )
    c = jnp.zeros((1, cols), F32)
    for k in range(4):
        base = sel[1 + k] * block

        def body(i, c, base=base):
            row = pl.ds(base + i, 1)
            th = jnp.tanh(zf[row, :] + fwk[row, :] * c)
            hp = kh[row, :] * c
            hc = 0.5 * cand[row, :]
            c = (hp + hc) + (hp - hc) * th
            state[row, :] = c
            half_prev[row, :] = hp
            return c

        c = lax.fori_loop(0, block, body, c, unroll=16)


def run_forward(sel, toks, near, keep, w_proj, gates, norm):
    block, width = toks[0].shape
    cols = width // 4
    length = 4 * block
    return pl.pallas_call(
        forward_kernel,
        out_shape=(shaped((2 * block, width), BF16),) + (shaped((length, cols)),) * 5,
        grid_spec=pltpu.PrefetchScalarGridSpec(
            num_scalar_prefetch=1,
            grid=(1,),
            in_specs=[whole((block, width))] * 2
            + [whole((2 * block, cols))] * 3
            + [whole((length, 1))]
            + weight_specs(width, cols)
            + [pl.BlockSpec((8, cols), lambda i, s: (0, s[0])), whole((8, width))],
            out_specs=(whole((2 * block, width)),) + (whole((length, cols)),) * 5,
            scratch_shapes=[pltpu.VMEM((length, cols), F32)] * 2,
        ),
        compiler_params=params(30),
        name="forward_scan",
    )(sel, *toks, *near, keep, w_proj, w_proj, w_proj, gates, norm)


def backward_kernel(
    sel,
    x0,
    x1,
    x2,
    x3,
    g0,
    g1,
    g23,
    cand_ref,
    zf_ref,
    zr_ref,
    state,
    half_prev,
    keep_ref,
    gates_ref,
    near_ref,
    far_ref,
    dproj_ref,
    out_ref,
    dxh_ref,
    small_ref,
    *rest,
    pieces,
):
    outs = rest[:pieces]
    coef, add_b, add_e, gz, omf = rest[pieces:]
    length, cols = cand_ref.shape
    block = length // 4
    width = near_ref.shape[1]
    part = outs[0].shape[0]
    fw, rw = gates_ref[0:1, :], gates_ref[1:2, :]
    half_fw, half_rw = 0.5 * fw, 0.5 * rw
    step = 16
    zero = jnp.zeros((step, cols), F32)
    sums = (zero, zero)
    sources = ((x0, g0, 0), (x1, g1, 0), (x2, g23, 0), (x3, g23, block))
    for b, (x_ref, g_ref, g_at) in enumerate(sources):

        def gate_body(i, carry, b=b, x_ref=x_ref, g_ref=g_ref, g_at=g_at):
            at = pl.multiple_of(i * step, step)
            here = pl.ds(pl.multiple_of(b * block + at, step), step)
            x = x_ref[pl.ds(at, step), :]
            g = g_ref[pl.ds(pl.multiple_of(g_at + at, step), step), :].astype(F32)
            keep = keep_ref[here, :]
            prev = 2.0 * half_prev[here, :]
            c, cd = state[here, :], cand_ref[here, :]
            forget = 0.5 + 0.5 * jnp.tanh(zf_ref[here, :] + half_fw * prev)
            reset = 0.5 + 0.5 * jnp.tanh(zr_ref[here, :] + half_rw * prev)
            not_forget, not_reset = 1.0 - forget, 1.0 - reset
            out_ref[here, :] = reset * c + not_reset * x
            dxh_ref[here, :] = g * not_reset
            dzr = g * (c - x) * reset * not_reset
            slope = (prev - cd) * forget * not_forget
            coef[here, :] = keep * (forget + slope * fw)
            add_b[here, :] = keep * (dzr * rw)
            add_e[here, :] = g * reset
            gz[here, :] = slope
            omf[here, :] = not_forget
            dproj_ref[here, 2 * cols : 3 * cols] = dzr.astype(BF16)
            return (carry[0] + dzr * prev, carry[1] + dzr)

        sums = lax.fori_loop(0, block // step, gate_body, sums, unroll=True)
    rw_sum, rb_sum = sums

    s = jnp.zeros((1, cols), F32)
    for k in range(3, -1, -1):
        last = sel[1 + k] * block + block - 1

        def backward_body(i, s, last=last):
            row = pl.ds(last - i, 1)
            total = s + add_e[row, :]
            add_e[row, :] = total
            return coef[row, :] * total + add_b[row, :]

        s = lax.fori_loop(0, block, backward_body, s, unroll=16)

    def grad_body(i, carry):
        here = pl.ds(pl.multiple_of(i * step, step), step)
        total = add_e[here, :]
        prev = 2.0 * half_prev[here, :]
        dzf = total * gz[here, :]
        dproj_ref[here, 0:cols] = (total * omf[here, :]).astype(BF16)
        dproj_ref[here, cols : 2 * cols] = dzf.astype(BF16)
        return (carry[0] + dzf * prev, carry[1] + dzf)

    fw_sum, fb_sum = lax.fori_loop(0, length // step, grad_body, (zero, zero), unroll=4)
    small_ref[...] = jnp.concatenate(
        [jnp.sum(v, axis=0, keepdims=True) for v in (fw_sum, rw_sum, fb_sum, rb_sum)]
        + [jnp.zeros((4, cols), F32)],
        axis=0,
    )
    outer_products(sel, 5, near_ref, far_ref, dproj_ref, outs)


def outer_products(sel, first, near_ref, far_ref, dproj_ref, outs):
    part = outs[0].shape[0]
    half = near_ref.shape[0]
    for i, out in enumerate(outs):
        at = pl.ds(pl.multiple_of(sel[first + i] * part, part), part)
        dims = (((0,), (0,)), ((), ()))
        out[...] = lax.dot_general(
            near_ref[:, at], dproj_ref[0:half, :], dims, preferred_element_type=F32
        ) + lax.dot_general(
            far_ref[:, at], dproj_ref[half:, :], dims, preferred_element_type=F32
        )


def run_backward(sel, toks, cots, scanned, keep, gates, normed, pieces):
    cot_own, cot_sibling, cot_far = cots
    block, width = toks[0].shape
    cols = width // 4
    length = 4 * block
    strip = pl.BlockSpec((block, cols), lambda i, s: (0, s[0]))
    return pl.pallas_call(
        functools.partial(backward_kernel, pieces=pieces),
        out_shape=(
            shaped((length, 3 * cols), BF16),
            shaped((length, cols)),
            shaped((length, cols)),
            shaped((8, cols)),
        )
        + (shaped((width // 8, 3 * cols)),) * pieces,
        grid_spec=pltpu.PrefetchScalarGridSpec(
            num_scalar_prefetch=1,
            grid=(1,),
            in_specs=[strip] * 4
            + [strip, pl.BlockSpec((block, cols), lambda i, s: (0, s[5 + pieces]))]
            + [whole((2 * block, cols))]
            + [whole((length, cols))] * 5
            + [whole((length, 1)), pl.BlockSpec((8, cols), lambda i, s: (0, s[0]))]
            + [whole((2 * block, width))] * 2,
            out_specs=(
                whole((length, 3 * cols)),
                whole((length, cols)),
                whole((length, cols)),
                whole((8, cols)),
            )
            + (whole((width // 8, 3 * cols)),) * pieces,
            scratch_shapes=[pltpu.VMEM((length, cols), F32)] * 5,
        ),
        compiler_params=params(30),
        name="backward_scan",
    )(sel, *toks, cot_own, cot_sibling, cot_far, *scanned, keep, gates, *normed)


def products_kernel(sel, near_ref, far_ref, dproj_ref, *outs):
    outer_products(sel, 0, near_ref, far_ref, dproj_ref, outs)


def run_products(sel, normed, dproj, pieces):
    width = normed[0].shape[1]
    return pl.pallas_call(
        products_kernel,
        out_shape=(shaped((width // 8, dproj.shape[1])),) * pieces,
        in_specs=[smem()] + [vmem()] * 3,
        out_specs=(vmem(),) * pieces,
        compiler_params=params(24),
        name="own_products",
    )(sel, *normed, dproj)


def input_kernel(
    sel,
    tok0,
    tok1,
    tok2,
    tok3,
    dproj_ref,
    dxh_ref,
    out_ref,
    gate_small_ref,
    w0,
    w1,
    w2,
    norm_ref,
    mine_ref,
    send_ref,
    dnormed,
):
    cols = dxh_ref.shape[1]
    block, width = tok0.shape
    gain, bias = norm_ref[0:1, :], norm_ref[1:2, :]
    mine = pl.multiple_of(sel[0] * cols, cols)
    step = 8
    sums = (jnp.zeros((step, width), F32), jnp.zeros((step, width), F32))
    for b, tok in enumerate((tok0, tok1, tok2, tok3)):
        rows = slice(b * block, (b + 1) * block)
        total = None
        for k, w in enumerate((w0, w1, w2)):
            term = lax.dot_general(
                dproj_ref[rows, k * cols : (k + 1) * cols],
                w[...],
                (((1,), (1,)), ((), ())),
                preferred_element_type=F32,
            )
            total = term if total is None else total + term
        dnormed[...] = total
        where = send_ref if b % 2 else mine_ref
        base = (b // 2) * block

        def body(i, carry, tok=tok, base=base, where=where):
            here = pl.ds(pl.multiple_of(i * step, step), step)
            there = pl.ds(pl.multiple_of(base + i * step, step), step)
            xhat, rdev = standardized(tok[here, :])
            dn = dnormed[here, :]
            dxhat = dn * gain
            mean1 = jnp.mean(dxhat, axis=-1, keepdims=True)
            mean2 = jnp.mean(dxhat * xhat, axis=-1, keepdims=True)
            where[there, 0:width] = rdev * (dxhat - mean1 - xhat * mean2)
            return (carry[0] + dn * xhat, carry[1] + dn)

        sums = lax.fori_loop(0, block // step, body, sums, unroll=11)
        to = pl.ds(base, block)
        where[to, pl.ds(mine, cols)] += dxh_ref[rows, :]
        where[to, width : width + cols] = out_ref[rows, :]
    tail = slice(2 * block, 2 * block + 8)
    for ref in (mine_ref, send_ref):
        ref[tail, :] = jnp.zeros((8, width + cols), F32)
    where = mine_ref
    where[2 * block : 2 * block + 4, pl.ds(mine, cols)] = gate_small_ref[0:4, :]
    for i, v in enumerate(sums):
        where[2 * block + 4 + i : 2 * block + 5 + i, 0:width] = jnp.sum(v, axis=0, keepdims=True)
    send_ref[tail, :] = mine_ref[tail, :]


def run_input(sel, toks, dproj, dxh, out, gate_small, w_proj, norm):
    block, width = toks[0].shape
    length, cols = dxh.shape
    shape = (2 * block + 8, width + cols)
    return pl.pallas_call(
        input_kernel,
        out_shape=(shaped(shape), shaped(shape)),
        grid_spec=pltpu.PrefetchScalarGridSpec(
            num_scalar_prefetch=1,
            grid=(1,),
            in_specs=[whole((block, width))] * 4
            + [whole((length, 3 * cols)), whole((length, cols)), whole((length, cols))]
            + [whole((8, cols))]
            + weight_specs(width, cols)
            + [whole((8, width))],
            out_specs=(whole(shape), whole(shape)),
            scratch_shapes=[pltpu.VMEM((block, width), F32)],
        ),
        compiler_params=params(30),
        name="input_side",
    )(sel, *toks, dproj, dxh, out, gate_small, w_proj, w_proj, w_proj, norm)


def combine_kernel(sel, mine_ref, got_ref, keep_ref, send_ref):
    rows = mine_ref.shape[0]
    block = (rows - 8) // 2
    width = mine_ref.shape[1] * 4 // 5
    cols = width // 4
    low = pl.multiple_of(width + sel[0] * cols, cols)
    high = pl.multiple_of(width + (1 - sel[0]) * cols, cols)
    for ref, first, count in ((keep_ref, 0, block), (send_ref, block, block + 8)):
        here = slice(first, first + count)
        ref[:, 0:width] = mine_ref[here, 0:width] + got_ref[here, 0:width]
        ref[:, pl.ds(low, cols)] = mine_ref[here, width:]
        ref[:, pl.ds(high, cols)] = got_ref[here, width:]


def combine(sel, mine, got):
    rows, both = mine.shape
    block, width = (rows - 8) // 2, both * 4 // 5
    return pl.pallas_call(
        combine_kernel,
        out_shape=(shaped((block, width * 3 // 2)), shaped((block + 8, width * 3 // 2))),
        in_specs=[smem(), vmem(), vmem()],
        out_specs=(vmem(), vmem()),
        compiler_params=params(16),
        name="combine",
    )(sel, mine, got)


def join_kernel(sel, mine_ref, sent_ref, got_ref, out_ref, grad_ref, small_ref):
    block, width = out_ref.shape
    half = width // 2
    at = pl.multiple_of(sel[0] * half, half)
    other = pl.multiple_of((1 - sel[0]) * half, half)
    out_ref[:, pl.ds(at, half)] = mine_ref[:, width:].astype(BF16)
    out_ref[:, pl.ds(other, half)] = got_ref[0:block, width:].astype(BF16)
    grad_ref[...] = (mine_ref[:, 0:width] + got_ref[0:block, 0:width]).astype(BF16)
    small_ref[...] = sent_ref[block:, 0:width] + got_ref[block:, 0:width]


def join(sel, mine, sent, got):
    block, width = mine.shape[0], mine.shape[1] * 2 // 3
    return pl.pallas_call(
        join_kernel,
        out_shape=(shaped((block, width), BF16), shaped((block, width), BF16), shaped((8, width))),
        in_specs=[smem(), vmem(), vmem(), vmem()],
        out_specs=(vmem(),) * 3,
        compiler_params=params(16),
        name="join",
    )(sel, mine, sent, got)


def place_kernel(sel, *refs, count, first):
    pieces, target, sem = refs[:count], refs[-2], refs[-1]
    rows, cols = pieces[0].shape[0], pieces[0].shape[1] // 3
    width = target.shape[1] // 3
    copies = []
    for i, piece in enumerate(pieces):
        row = pl.multiple_of(sel[2 * (first + i)] * rows, rows)
        col = sel[2 * (first + i) + 1] * cols
        for k in range(3):
            to = pl.multiple_of(col + k * width, cols)
            copies.append(
                pltpu.make_async_copy(
                    piece.at[:, pl.ds(k * cols, cols)],
                    target.at[pl.ds(row, rows), pl.ds(to, cols)],
                    sem.at[3 * i + k],
                )
            )
    for c in copies:
        c.start()
    for c in copies:
        c.wait()


def place(sel, pieces, first, target, shape):
    count = len(pieces)
    extra = [] if target is None else [target]
    return pl.pallas_call(
        functools.partial(place_kernel, count=count, first=first),
        out_shape=shaped(shape),
        in_specs=[smem()] + [vmem()] * count + [any_spec()] * len(extra),
        out_specs=any_spec(),
        scratch_shapes=[pltpu.SemaphoreType.DMA((3 * count,))],
        input_output_aliases={1 + count: 0} if extra else {},
        compiler_params=params(16),
        name="place",
    )(sel, *pieces, *extra)


def on_device(
    tokens,
    offsets,
    w_proj,
    forget_weight,
    reset_weight,
    forget_bias,
    reset_bias,
    layer_norm_gain,
    layer_norm_bias,
    cotangent,
):
    _, block, width = tokens.shape
    z, y, x, c = (lax.axis_index(a) for a in ("z", "y", "x", "c"))
    tuned = lax.axis_size("z") == 4
    mine = 2 * x + c
    int32 = lambda values: jnp.stack([jnp.asarray(v, jnp.int32) for v in values])

    cot = cotangent[0]
    own = widen(tokens[0])
    tok_x = swap(own, "x")
    tok_c = swap(own, "c")
    cot_sibling = swap(widen_cot(int32([1 - c]), cot), "c")
    cot_far = swap(pack_cot(int32([2 * (1 - x) + c, 1 - x]), cot, cot_sibling), "x")
    tok_xc = swap(tok_x, "c")

    at = jnp.stack([2 * x + c, 2 * x + 1 - c, 2 * (1 - x) + c, 2 * (1 - x) + 1 - c])
    positions = (at[:, None] * block + jnp.arange(block)[None, :]).reshape(-1)
    hits = jnp.any(positions[:, None] == offsets[0][None, :], axis=1)
    keep = jnp.where(hits, 0.0, 1.0).astype(F32)[:, None]
    pad = jnp.zeros((4, width), F32)
    gates = jnp.concatenate([jnp.stack([forget_weight, reset_weight, forget_bias, reset_bias]), pad])
    norm = jnp.concatenate([jnp.stack([layer_norm_gain, layer_norm_bias]), pad, pad[:2]])

    stored = [2 * ((k // 2) ^ x) + ((k % 2) ^ c) for k in range(4)]
    order = (2, 3, 1, 0)
    send_rows = [2 * (z ^ d) + 1 - y for d in order] if tuned else list(range(4))
    keep_rows = [2 * (z ^ d) + y for d in order] if tuned else list(range(4, 8))
    sel = int32([mine, *stored, *send_rows, x])
    near = run_near(sel, (own, tok_c), w_proj, gates, norm)
    far = run_forward(sel, (tok_x, tok_xc), near[1:], keep, w_proj, gates, norm)
    normed = (near[0], far[0])
    toks = (own, tok_c, tok_x, tok_xc)
    dproj, out, dxh, gate_small, *sends = run_backward(
        sel, toks, (cot, cot_sibling, cot_far), far[1:], keep, gates, normed, 4
    )
    keeps = run_products(int32(keep_rows), normed, dproj, 4)

    grad_mine, grad_send = run_input(sel, toks, dproj, dxh, out, gate_small, w_proj, norm)
    kept, sent = combine(int32([c]), grad_mine, swap(grad_send, "c"))
    output, input_grad, small = join(int32([x]), kept, sent, swap(sent, "x"))

    if tuned:
        q2, q3, q1, q0 = (keep + swap(send, "y") for keep, send in zip(keeps, sends))
        h3 = q3 + xor_permute(q2, "z", 1)
        total = q0 + xor_permute(q1, "z", 1) + xor_permute(h3, "z", 3)
        small = small + swap(small, "y")
        small = small + xor_permute(small, "z", 1)
        small = small + xor_permute(small, "z", 2)
        z1, z3 = xor_permute(total, "z", 1), xor_permute(total, "z", 3)
        column = ((0, total), (1, z1), (3, z3), (2, xor_permute(z3, "z", 1)))
        held = []
        for d, piece in column:
            px, py = swap(piece, "x"), swap(piece, "y")
            corner = swap(px, "y") if d in (0, 3) else swap(py, "x")
            row, row_y = 2 * (z ^ d) + y, 2 * (z ^ d) + 1 - y
            held.append(((piece, row, x), (px, row, 1 - x), (py, row_y, x), (corner, row_y, 1 - x)))
    else:
        small = lax.psum(small, ("z", "y"))
        pieces = lax.psum(jnp.stack(sends + list(keeps)), ("z", "y"))
        across = swap(pieces, "x")
        held = [
            tuple((part[r], r, at) for r in range(8)) for part, at in ((pieces, x), (across, 1 - x))
        ]
    where, first = [], 0
    for group in held:
        for _, row, x_at in group:
            where += [row, 2 * x_at + c, row, 2 * x_at + 1 - c]
    where = int32(where)
    proj_grad = None
    for group in held:
        arrays = []
        for piece, _, _ in group:
            arrays += [piece, swap(piece, "c")]
        proj_grad = place(where, arrays, first, proj_grad, (width, 3 * width))
        first += len(arrays)
    return (output[None], input_grad[None], proj_grad, *(small[i] for i in range(6)))


def solution(mesh):
    dp, rep = mesh.shape["dp"], mesh.shape["rep"]
    fine = Mesh(mesh.devices.reshape(dp // 2, 2, rep // 2, 2), ("z", "y", "x", "c"))
    row, seq = ("z", "y"), ("x", "c")
    in_specs = (P(row, seq, None), P(row, None)) + (P(),) * 7 + (P(row, seq, None),)
    out_specs = (P(row, seq, None), P(row, seq, None)) + (P(),) * 7
    return jax.shard_map(
        on_device, mesh=fine, in_specs=in_specs, out_specs=out_specs, check_vma=False
    )
```

profile of v0, /device:TPU:0, one launch (start us, length us, event | category | flops | bytes accessed | tf_op | source)
XLA Modules:
  0.0 217.8 jit_solution(10229406733232588455)
XLA Ops:
  0.7 1.9 widen.1.tok0.x0
  2.6 2.9 %collective-permute-start.1 = (f32[176,1024]{1,0:T(8,128)}, f32[176,1024]{1,0:T(8,128)S(1)}, u32[]{:S(2)}, u32[]{:S(2)}) collective-permute-start(f32[176,1024]{1,0:T(8,128)} %widen.1.tok0.x0), channel_id=1, source_target_pairs={{0,2},{2,0},{1,3},{3,1},{4,6},{6,4},{5,7},{7,5},{8,10},{10,8},{9,1... | collective-permute-start | bytes 2162696 | tf_op jit(solution)/shard_map/ppermute | solution.py:19
  5.6 1.7 widen_cot.1
  7.9 14.1 %collective-permute-done.1.tok0.x2.tok2 = f32[176,1024]{1,0:T(8,128)S(1)} collective-permute-done((f32[176,1024]{1,0:T(8,128)}, f32[176,1024]{1,0:T(8,128)S(1)}, u32[]{:S(2)}, u32[]{:S(2)}) %collective-permute-start.1) | collective-permute-done | bytes 720928 | tf_op jit(solution)/shard_map/ppermute | solution.py:19
  23.7 1.9 pack_cot.1
  25.5 1.7 collective-permute-start.4
  27.7 2.8 %copy-done = bf16[1024,3072]{1,0:T(8,128)(2,1)S(1)} copy-done((bf16[1024,3072]{1,0:T(8,128)(2,1)S(1)}, bf16[1024,3072]{1,0:T(8,128)(2,1)}, u32[]{:S(2)}) %copy-start) | copy-done | bytes 6291480
  33.5 9.8 %forward_scan.1 = (bf16[352,1024]{1,0:T(8,128)(2,1)S(1)}, f32[704,256]{1,0:T(8,128)S(1)}, f32[704,256]{1,0:T(8,128)S(1)}, f32[704,256]{1,0:T(8,128)S(1)}, f32[70...) custom-call(s32[10]{0:T(128)S(1)} %stack.70.sel, f32[176,1024]{1,0:T(8,128)S(1)} %collective-permute-done.1.tok0.x2.tok2, ...), custom_call_target="tpu_custom_call" | custom-call | tf_op jit(solution)/shard_map/forward_scan/pallas_call | solution.py:220
  43.4 7.1 %backward_scan.1 = (bf16[704,768]{1,0:T(8,128)(2,1)S(1)}, f32[704,256]{1,0:T(8,128)S(1)}, f32[704,256]{1,0:T(8,128)S(1)}, f32[8,256]{1,0:T(8,128)S(1)}, f32[128,...) custom-call(s32[10]{0:T(128)S(1)} %stack.70.sel, ...), custom_call_target="tpu_custom_call" | custom-call | tf_op jit(solution)/shard_map/backward_scan/pallas_call | solution.py:353
  63.6 3.6 %collective-permute-done.11 = f32[128,768]{1,0:T(8,128)} collective-permute-done((f32[128,768]{1,0:T(8,128)}, f32[128,768]{1,0:T(8,128)}, u32[]{:S(2)}, u32[]{:S(2)}) %collective-permute-start.11) | collective-permute-done | bytes 393248 | tf_op jit(solution)/shard_map/ppermute | solution.py:19
  69.9 2.8 %copy-done.2 = bf16[1024,3072]{1,0:T(8,128)(2,1)S(1)} copy-done((bf16[1024,3072]{1,0:T(8,128)(2,1)S(1)}, bf16[1024,3072]{1,0:T(8,128)(2,1)}, u32[]{:S(2)}) %copy-start.2) | copy-done | bytes 6291480
  72.6 6.1 %input_side.1 = (f32[360,1280]{1,0:T(8,128)S(1)}, f32[360,1280]{1,0:T(8,128)S(1)}) custom-call(s32[10]{0:T(128)S(1)} %stack.70.sel, f32[176,1024]{1,0:T(8,128)S(1)} %copy-done.3, f32[176,1024]{1,0:T(8,128)S(1)} %collective-permute-done.tok1.x1, f32[176,1024]{1,0:T(8,128)S(1)} %collective-permute-done.1.tok0.x2.tok2, ...), custom_call_target="tpu_custom_call" | custom-call | tf_op jit(solution)/shard_map/input_side/pallas_call | solution.py:469
  81.0 2.9 %collective-permute-done.10 = f32[128,768]{1,0:T(8,128)S(1)} collective-permute-done((f32[128,768]{1,0:T(8,128)}, f32[128,768]{1,0:T(8,128)S(1)}, u32[]{:S(2)}, u32[]{:S(2)}) %collective-permute-start.10) | collective-permute-done | bytes 393248 | tf_op jit(solution)/shard_map/ppermute | solution.py:19
  84.0 3.7 %collective-permute-start.13 = (f32[128,768]{1,0:T(8,128)S(1)}, f32[128,768]{1,0:T(8,128)S(1)}, u32[]{:S(2)}, u32[]{:S(2)}) collective-permute-start(f32[128,768]{1,0:T(8,128)S(1)} %add_add_fusion), channel_id=1, source_target_pairs={{0,24},{8,16},{16,8},{24,0},{1,25},{9,17},{17,9},{25,1},{2,26},{10... | collective-permute-start | bytes 1179656 | tf_op jit(solution)/shard_map/ppermute | solution.py:24
  87.7 4.0 %collective-permute-done.7 = f32[128,768]{1,0:T(8,128)S(1)} collective-permute-done((f32[128,768]{1,0:T(8,128)S(1)}, f32[128,768]{1,0:T(8,128)S(1)}, u32[]{:S(2)}, u32[]{:S(2)}) %collective-permute-start.7) | collective-permute-done | bytes 393248 | tf_op jit(solution)/shard_map/ppermute | solution.py:19
  91.8 10.5 %collective-permute-done.13 = f32[128,768]{1,0:T(8,128)S(1)} collective-permute-done((f32[128,768]{1,0:T(8,128)S(1)}, f32[128,768]{1,0:T(8,128)S(1)}, u32[]{:S(2)}, u32[]{:S(2)}) %collective-permute-start.13) | collective-permute-done | bytes 393248 | tf_op jit(solution)/shard_map/ppermute | solution.py:24
  103.5 2.5 %collective-permute-start.30 = (f32[128,768]{1,0:T(8,128)S(1)}, f32[128,768]{1,0:T(8,128)S(1)}, u32[]{:S(2)}, u32[]{:S(2)}) collective-permute-start(f32[128,768]{1,0:T(8,128)S(1)} %add_add_fusion.1.refs_0_), channel_id=1, source_target_pairs={{0,8},{8,0},{16,24},{24,16},{1,9},{9,1},{17,25},{25,17},{2,10},{10... | collective-permute-start | bytes 1179656 | tf_op jit(solution)/shard_map/ppermute | solution.py:24
  106.0 6.7 %collective-permute-done.39.refs_2_ = f32[128,768]{1,0:T(8,128)S(1)} collective-permute-done((f32[128,768]{1,0:T(8,128)S(1)}, f32[128,768]{1,0:T(8,128)S(1)}, u32[]{:S(2)}, u32[]{:S(2)}) %collective-permute-start.39) | collective-permute-done | bytes 393248 | tf_op jit(solution)/shard_map/ppermute | solution.py:19
  113.6 2.2 %collective-permute-done.30.refs_0_ = f32[128,768]{1,0:T(8,128)S(1)} collective-permute-done((f32[128,768]{1,0:T(8,128)S(1)}, f32[128,768]{1,0:T(8,128)S(1)}, u32[]{:S(2)}, u32[]{:S(2)}) %collective-permute-start.30) | collective-permute-done | bytes 393248 | tf_op jit(solution)/shard_map/ppermute | solution.py:24
  115.8 10.7 %collective-permute-done.14.refs_0_ = f32[128,768]{1,0:T(8,128)S(1)} collective-permute-done((f32[128,768]{1,0:T(8,128)S(1)}, f32[128,768]{1,0:T(8,128)S(1)}, u32[]{:S(2)}, u32[]{:S(2)}) %collective-permute-start.14) | collective-permute-done | bytes 393248 | tf_op jit(solution)/shard_map/ppermute | solution.py:24
  130.9 7.7 %collective-permute-done.34.refs_4_ = f32[128,768]{1,0:T(8,128)S(1)} collective-permute-done((f32[128,768]{1,0:T(8,128)S(1)}, f32[128,768]{1,0:T(8,128)S(1)}, u32[]{:S(2)}, u32[]{:S(2)}) %collective-permute-start.34) | collective-permute-done | bytes 393248 | tf_op jit(solution)/shard_map/ppermute | solution.py:19
  140.1 2.5 %collective-permute-start.15 = (f32[128,768]{1,0:T(8,128)S(1)}, f32[128,768]{1,0:T(8,128)}, u32[]{:S(2)}, u32[]{:S(2)}) collective-permute-start(f32[128,768]{1,0:T(8,128)S(1)} %collective-permute-done.14.refs_0_), channel_id=1, source_target_pairs={{0,8},{8,0},{16,24},{24,16},{1,9},{9,1},{17,25},{25,17},{2,10},{10... | collective-permute-start | bytes 1179656 | tf_op jit(solution)/shard_map/ppermute | solution.py:24
  142.6 4.9 %collective-permute-done.24.refs_2_ = f32[128,768]{1,0:T(8,128)S(1)} collective-permute-done((f32[128,768]{1,0:T(8,128)S(1)}, f32[128,768]{1,0:T(8,128)S(1)}, u32[]{:S(2)}, u32[]{:S(2)}) %collective-permute-start.24) | collective-permute-done | bytes 393248 | tf_op jit(solution)/shard_map/ppermute | solution.py:19
  149.3 3.1 %collective-permute-done.15.refs_0_ = f32[128,768]{1,0:T(8,128)} collective-permute-done((f32[128,768]{1,0:T(8,128)S(1)}, f32[128,768]{1,0:T(8,128)}, u32[]{:S(2)}, u32[]{:S(2)}) %collective-permute-start.15) | collective-permute-done | bytes 393248 | tf_op jit(solution)/shard_map/ppermute | solution.py:24
  153.0 25.5 %collective-permute-done.36.refs_6_ = f32[128,768]{1,0:T(8,128)S(1)} collective-permute-done((f32[128,768]{1,0:T(8,128)S(1)}, f32[128,768]{1,0:T(8,128)S(1)}, u32[]{:S(2)}, u32[]{:S(2)}) %collective-permute-start.36) | collective-permute-done | bytes 393248 | tf_op jit(solution)/shard_map/ppermute | solution.py:19
  183.6 4.7 %collective-permute-done.19.refs_4_ = f32[128,768]{1,0:T(8,128)} collective-permute-done((f32[128,768]{1,0:T(8,128)}, f32[128,768]{1,0:T(8,128)}, u32[]{:S(2)}, u32[]{:S(2)}) %collective-permute-start.19) | collective-permute-done | bytes 393248 | tf_op jit(solution)/shard_map/ppermute | solution.py:19
  193.1 2.4 %collective-permute-done.45 = f32[8,1024]{1,0:T(8,128)S(1)} collective-permute-done((f32[8,1024]{1,0:T(8,128)S(1)}, f32[8,1024]{1,0:T(8,128)S(1)}, u32[]{:S(2)}, u32[]{:S(2)}) %collective-permute-start.45) | collective-permute-done | bytes 32800 | tf_op jit(solution)/shard_map/ppermute | solution.py:19
  197.7 4.2 %collective-permute-done.21.refs_6_ = f32[128,768]{1,0:T(8,128)} collective-permute-done((f32[128,768]{1,0:T(8,128)}, f32[128,768]{1,0:T(8,128)}, u32[]{:S(2)}, u32[]{:S(2)}) %collective-permute-start.21) | collective-permute-done | bytes 393248 | tf_op jit(solution)/shard_map/ppermute | solution.py:19
  205.1 2.4 %place.4.refs_8_ = f32[1024,3072]{1,0:T(8,128)} custom-call(s32[64]{0:T(128)S(1)} %stack.88.sel, f32[128,768]{1,0:T(8,128)S(1)} %add_add_fusion.1.refs_0_, f32[128,768]{1,0:T(8,128)S(1)} %collective-permute-done.38.refs_1_, f32[128,768]{1,0:T(8,128)S(1)} %collective-permute-done.39.refs_2_, f32[128,768]{1,0:T(8,128)S(1)} %collective-permute-done.40.refs_3_, ...), custom_call_target="tpu_custom_call" | custom-call | tf_op jit(solution)/shard_map/place/pallas_call | solution.py:564
  207.6 2.4 %place.5.refs_8_ = f32[1024,3072]{1,0:T(8,128)} custom-call(s32[64]{0:T(128)S(1)} %stack.88.sel, f32[128,768]{1,0:T(8,128)S(1)} %copy-done.19, f32[128,768]{1,0:T(8,128)S(1)} %copy-done.27, f32[128,768]{1,0:T(8,128)S(1)} %copy-done.23, f32[128,768]{1,0:T(8,128)S(1)} %copy-done.35, f32[128,768]{1,0:T(8,128)S(1)} %copy-done.21, ...), custom_call_target="tpu_custom_call", output_to_operand_aliasing={{}: (9, {})} | custom-call | tf_op jit(solution)/shard_map/place/pallas_call | solution.py:564
  210.1 2.4 %place.6.refs_8_ = f32[1024,3072]{1,0:T(8,128)} custom-call(s32[64]{0:T(128)S(1)} %stack.88.sel, f32[128,768]{1,0:T(8,128)S(1)} %collective-permute-done.14.refs_0_, f32[128,768]{1,0:T(8,128)S(1)} %copy-done.31, f32[128,768]{1,0:T(8,128)S(1)} %copy-done.25, f32[128,768]{1,0:T(8,128)S(1)} %copy-done.41, ...), custom_call_target="tpu_custom_call", output_to_operand_aliasing={{}: (9, {})} | custom-call | tf_op jit(solution)/shard_map/place/pallas_call | solution.py:564
  214.0 3.7 %place.7 = f32[1024,3072]{1,0:T(8,128)} custom-call(s32[64]{0:T(128)S(1)} %stack.88.sel, f32[128,768]{1,0:T(8,128)} %collective-permute-done.15.refs_0_, f32[128,768]{1,0:T(8,128)} %collective-permute-done.16.refs_1_, f32[128,768]{1,0:T(8,128)} %collective-permute-done.17.refs_2_, ...), custom_call_target="tpu_custom_call", output_to_operand_aliasing={{}: (9, {})} | custom-call | tf_op jit(solution)/shard_map/place/pallas_call | solution.py:564
  (219 shorter events, 50.6 us)
Async XLA Ops:
  2.6 19.4 %collective-permute-start.1 = (f32[176,1024]{1,0:T(8,128)}, f32[176,1024]{1,0:T(8,128)S(1)}, u32[]{:S(2)}, u32[]{:S(2)}) collective-permute-start(f32[176,1024]{1,0:T(8,128)} %widen.1.tok0.x0), channel_id=1, source_target_pairs={{0,2},{2,0},{1,3},{3,1},{4,6},{6,4},{5,7},{7,5},{8,10},{10,8},{9,1... | collective-permute-start | bytes 2162696 | tf_op jit(solution)/shard_map/ppermute | solution.py:19
  5.6 22.1 %collective-permute-start = (f32[176,1024]{1,0:T(8,128)}, f32[176,1024]{1,0:T(8,128)S(1)}, u32[]{:S(2)}, u32[]{:S(2)}) collective-permute-start(f32[176,1024]{1,0:T(8,128)} %widen.1.tok0.x0), channel_id=1, source_target_pairs={{0,1},{1,0},{2,3},{3,2},{4,5},{5,4},{6,7},{7,6},{8,9},{9,8},{10,11... | collective-permute-start | bytes 2162696 | tf_op jit(solution)/shard_map/ppermute | solution.py:19
  7.3 15.6 %collective-permute-start.3 = (f32[176,512]{1,0:T(8,128)}, f32[176,512]{1,0:T(8,128)S(1)}, u32[]{:S(2)}, u32[]{:S(2)}) collective-permute-start(f32[176,512]{1,0:T(8,128)} %widen_cot.1), channel_id=1, source_target_pairs={{0,1},{1,0},{2,3},{3,2},{4,5},{5,4},{6,7},{7,6},{8,9},{9,8},{10,11... | collective-permute-start | bytes 1081352 | tf_op jit(solution)/shard_map/ppermute | solution.py:19
  25.5 17.9 %collective-permute-start.4 = (f32[352,256]{1,0:T(8,128)}, f32[352,256]{1,0:T(8,128)}, u32[]{:S(2)}, u32[]{:S(2)}) collective-permute-start(f32[352,256]{1,0:T(8,128)} %pack_cot.1), channel_id=1, source_target_pairs={{0,2},{2,0},{1,3},{3,1},{4,6},{6,4},{5,7},{7,5},{8,10},{10,8},{9,1... | collective-permute-start | bytes 1081352 | tf_op jit(solution)/shard_map/ppermute | solution.py:19
  54.9 12.3 %collective-permute-start.11 = (f32[128,768]{1,0:T(8,128)}, f32[128,768]{1,0:T(8,128)}, u32[]{:S(2)}, u32[]{:S(2)}) collective-permute-start(f32[128,768]{1,0:T(8,128)} %get-tuple-element.65), channel_id=1, source_target_pairs={{0,4},{4,0},{1,5},{5,1},{2,6},{6,2},{3,7},{7,3},{8,12},{12,8},{9,1... | collective-permute-start | bytes 1179656 | tf_op jit(solution)/shard_map/ppermute | solution.py:19
  56.5 24.0 %collective-permute-start.8 = (f32[128,768]{1,0:T(8,128)}, f32[128,768]{1,0:T(8,128)S(1)}, u32[]{:S(2)}, u32[]{:S(2)}) collective-permute-start(f32[128,768]{1,0:T(8,128)} %copy-done.51), channel_id=1, source_target_pairs={{0,4},{4,0},{1,5},{5,1},{2,6},{6,2},{3,7},{7,3},{8,12},{12,8},{9,1... | collective-permute-start | bytes 1179656 | tf_op jit(solution)/shard_map/ppermute | solution.py:19
  57.0 26.9 %collective-permute-start.10 = (f32[128,768]{1,0:T(8,128)}, f32[128,768]{1,0:T(8,128)S(1)}, u32[]{:S(2)}, u32[]{:S(2)}) collective-permute-start(f32[128,768]{1,0:T(8,128)} %copy-done.50), channel_id=1, source_target_pairs={{0,4},{4,0},{1,5},{5,1},{2,6},{6,2},{3,7},{7,3},{8,12},{12,8},{9,1... | collective-permute-start | bytes 1179656 | tf_op jit(solution)/shard_map/ppermute | solution.py:19
  68.2 15.7 %collective-permute-start.12 = (f32[128,768]{1,0:T(8,128)S(1)}, f32[128,768]{1,0:T(8,128)S(1)}, u32[]{:S(2)}, u32[]{:S(2)}) collective-permute-start(f32[128,768]{1,0:T(8,128)S(1)} %add.161), channel_id=1, source_target_pairs={{0,8},{8,0},{16,24},{24,16},{1,9},{9,1},{17,25},{25,17},{2,10},{10... | collective-permute-start | bytes 1179656 | tf_op jit(solution)/shard_map/ppermute | solution.py:24
  78.8 48.2 %collective-permute-start.5 = (f32[360,1280]{1,0:T(8,128)S(1)}, f32[360,1280]{1,0:T(8,128)S(1)}, u32[]{:S(2)}, u32[]{:S(2)}) collective-permute-start(f32[360,1280]{1,0:T(8,128)S(1)} %get-tuple-element.53), channel_id=1, source_target_pairs={{0,1},{1,0},{2,3},{3,2},{4,5},{5,4},{6,7},{7,6},{8,9},{9,8},{10,11... | collective-permute-start | bytes 5529608 | tf_op jit(solution)/shard_map/ppermute | solution.py:19
  78.9 12.8 %collective-permute-start.7 = (f32[128,768]{1,0:T(8,128)S(1)}, f32[128,768]{1,0:T(8,128)S(1)}, u32[]{:S(2)}, u32[]{:S(2)}) collective-permute-start(f32[128,768]{1,0:T(8,128)S(1)} %copy-done.49), channel_id=1, source_target_pairs={{0,4},{4,0},{1,5},{5,1},{2,6},{6,2},{3,7},{7,3},{8,12},{12,8},{9,1... | collective-permute-start | bytes 1179656 | tf_op jit(solution)/shard_map/ppermute | solution.py:19
  84.0 18.3 %collective-permute-start.13 = (f32[128,768]{1,0:T(8,128)S(1)}, f32[128,768]{1,0:T(8,128)S(1)}, u32[]{:S(2)}, u32[]{:S(2)}) collective-permute-start(f32[128,768]{1,0:T(8,128)S(1)} %add_add_fusion), channel_id=1, source_target_pairs={{0,24},{8,16},{16,8},{24,0},{1,25},{9,17},{17,9},{25,1},{2,26},{10... | collective-permute-start | bytes 1179656 | tf_op jit(solution)/shard_map/ppermute | solution.py:24
  103.5 12.3 %collective-permute-start.30 = (f32[128,768]{1,0:T(8,128)S(1)}, f32[128,768]{1,0:T(8,128)S(1)}, u32[]{:S(2)}, u32[]{:S(2)}) collective-permute-start(f32[128,768]{1,0:T(8,128)S(1)} %add_add_fusion.1.refs_0_), channel_id=1, source_target_pairs={{0,8},{8,0},{16,24},{24,16},{1,9},{9,1},{17,25},{25,17},{2,10},{10... | collective-permute-start | bytes 1179656 | tf_op jit(solution)/shard_map/ppermute | solution.py:24
  112.8 13.8 %collective-permute-start.14 = (f32[128,768]{1,0:T(8,128)S(1)}, f32[128,768]{1,0:T(8,128)S(1)}, u32[]{:S(2)}, u32[]{:S(2)}) collective-permute-start(f32[128,768]{1,0:T(8,128)S(1)} %add_add_fusion.1.refs_0_), channel_id=1, source_target_pairs={{0,24},{8,16},{16,8},{24,0},{1,25},{9,17},{17,9},{25,1},{2,26},{10... | collective-permute-start | bytes 1179656 | tf_op jit(solution)/shard_map/ppermute | solution.py:24
  113.0 15.5 %collective-permute-start.43 = (f32[128,768]{1,0:T(8,128)S(1)}, f32[128,768]{1,0:T(8,128)S(1)}, u32[]{:S(2)}, u32[]{:S(2)}) collective-permute-start(f32[128,768]{1,0:T(8,128)S(1)} %collective-permute-done.39.refs_2_), channel_id=1, source_target_pairs={{0,4},{4,0},{1,5},{5,1},{2,6},{6,2},{3,7},{7,3},{8,12},{12,8},{9,1... | collective-permute-start | bytes 1179656 | tf_op jit(solution)/shard_map/ppermute | solution.py:19
  113.6 15.0 %collective-permute-start.40 = (f32[128,768]{1,0:T(8,128)S(1)}, f32[128,768]{1,0:T(8,128)S(1)}, u32[]{:S(2)}, u32[]{:S(2)}) collective-permute-start(f32[128,768]{1,0:T(8,128)S(1)} %collective-permute-done.39.refs_2_), channel_id=1, source_target_pairs={{0,1},{1,0},{2,3},{3,2},{4,5},{5,4},{6,7},{7,6},{8,9},{9,8},{10,11... | collective-permute-start | bytes 1179656 | tf_op jit(solution)/shard_map/ppermute | solution.py:19
  115.8 13.3 %collective-permute-start.42 = (f32[128,768]{1,0:T(8,128)S(1)}, f32[128,768]{1,0:T(8,128)S(1)}, u32[]{:S(2)}, u32[]{:S(2)}) collective-permute-start(f32[128,768]{1,0:T(8,128)S(1)} %collective-permute-done.41.refs_4_), channel_id=1, source_target_pairs={{0,1},{1,0},{2,3},{3,2},{4,5},{5,4},{6,7},{7,6},{8,9},{9,8},{10,11... | collective-permute-start | bytes 1179656 | tf_op jit(solution)/shard_map/ppermute | solution.py:19
  126.5 12.0 %collective-permute-start.34 = (f32[128,768]{1,0:T(8,128)S(1)}, f32[128,768]{1,0:T(8,128)S(1)}, u32[]{:S(2)}, u32[]{:S(2)}) collective-permute-start(f32[128,768]{1,0:T(8,128)S(1)} %collective-permute-done.30.refs_0_), channel_id=1, source_target_pairs={{0,4},{4,0},{1,5},{5,1},{2,6},{6,2},{3,7},{7,3},{8,12},{12,8},{9,1... | collective-permute-start | bytes 1179656 | tf_op jit(solution)/shard_map/ppermute | solution.py:19
  127.0 13.0 %collective-permute-start.32 = (f32[128,768]{1,0:T(8,128)S(1)}, f32[128,768]{1,0:T(8,128)S(1)}, u32[]{:S(2)}, u32[]{:S(2)}) collective-permute-start(f32[128,768]{1,0:T(8,128)S(1)} %collective-permute-done.30.refs_0_), channel_id=1, source_target_pairs={{0,2},{2,0},{1,3},{3,1},{4,6},{6,4},{5,7},{7,5},{8,10},{10,8},{9,1... | collective-permute-start | bytes 1179656 | tf_op jit(solution)/shard_map/ppermute | solution.py:19
  128.6 18.9 %collective-permute-start.24 = (f32[128,768]{1,0:T(8,128)S(1)}, f32[128,768]{1,0:T(8,128)S(1)}, u32[]{:S(2)}, u32[]{:S(2)}) collective-permute-start(f32[128,768]{1,0:T(8,128)S(1)} %collective-permute-done.14.refs_0_), channel_id=1, source_target_pairs={{0,2},{2,0},{1,3},{3,1},{4,6},{6,4},{5,7},{7,5},{8,10},{10,8},{9,1... | collective-permute-start | bytes 1179656 | tf_op jit(solution)/shard_map/ppermute | solution.py:19
  129.1 18.4 %collective-permute-start.26 = (f32[128,768]{1,0:T(8,128)S(1)}, f32[128,768]{1,0:T(8,128)S(1)}, u32[]{:S(2)}, u32[]{:S(2)}) collective-permute-start(f32[128,768]{1,0:T(8,128)S(1)} %collective-permute-done.14.refs_0_), channel_id=1, source_target_pairs={{0,4},{4,0},{1,5},{5,1},{2,6},{6,2},{3,7},{7,3},{8,12},{12,8},{9,1... | collective-permute-start | bytes 1179656 | tf_op jit(solution)/shard_map/ppermute | solution.py:19
  138.6 49.8 %collective-permute-start.6 = (f32[184,1536]{1,0:T(8,128)S(1)}, f32[184,1536]{1,0:T(8,128)S(1)}, u32[]{:S(2)}, u32[]{:S(2)}) collective-permute-start(f32[184,1536]{1,0:T(8,128)S(1)} %get-tuple-element.55.sent_ref), channel_id=1, source_target_pairs={{0,2},{2,0},{1,3},{3,1},{4,6},{6,4},{5,7},{7,5},{8,10},{10,8},{9,1... | collective-permute-start | bytes 3391496 | tf_op jit(solution)/shard_map/ppermute | solution.py:19
  140.1 12.3 %collective-permute-start.15 = (f32[128,768]{1,0:T(8,128)S(1)}, f32[128,768]{1,0:T(8,128)}, u32[]{:S(2)}, u32[]{:S(2)}) collective-permute-start(f32[128,768]{1,0:T(8,128)S(1)} %collective-permute-done.14.refs_0_), channel_id=1, source_target_pairs={{0,8},{8,0},{16,24},{24,16},{1,9},{9,1},{17,25},{25,17},{2,10},{10... | collective-permute-start | bytes 1179656 | tf_op jit(solution)/shard_map/ppermute | solution.py:24
  147.5 31.0 %collective-permute-start.36 = (f32[128,768]{1,0:T(8,128)S(1)}, f32[128,768]{1,0:T(8,128)S(1)}, u32[]{:S(2)}, u32[]{:S(2)}) collective-permute-start(f32[128,768]{1,0:T(8,128)S(1)} %collective-permute-done.34.refs_4_), channel_id=1, source_target_pairs={{0,2},{2,0},{1,3},{3,1},{4,6},{6,4},{5,7},{7,5},{8,10},{10,8},{9,1... | collective-permute-start | bytes 1179656 | tf_op jit(solution)/shard_map/ppermute | solution.py:19
  149.1 30.9 %collective-permute-start.33 = (f32[128,768]{1,0:T(8,128)S(1)}, f32[128,768]{1,0:T(8,128)S(1)}, u32[]{:S(2)}, u32[]{:S(2)}) collective-permute-start(f32[128,768]{1,0:T(8,128)S(1)} %collective-permute-done.32.refs_2_), channel_id=1, source_target_pairs={{0,1},{1,0},{2,3},{3,2},{4,5},{5,4},{6,7},{7,6},{8,9},{9,8},{10,11... | collective-permute-start | bytes 1179656 | tf_op jit(solution)/shard_map/ppermute | solution.py:19
  152.4 28.4 %collective-permute-start.35 = (f32[128,768]{1,0:T(8,128)S(1)}, f32[128,768]{1,0:T(8,128)S(1)}, u32[]{:S(2)}, u32[]{:S(2)}) collective-permute-start(f32[128,768]{1,0:T(8,128)S(1)} %collective-permute-done.34.refs_4_), channel_id=1, source_target_pairs={{0,1},{1,0},{2,3},{3,2},{4,5},{5,4},{6,7},{7,6},{8,9},{9,8},{10,11... | collective-permute-start | bytes 1179656 | tf_op jit(solution)/shard_map/ppermute | solution.py:19
  152.4 29.7 %collective-permute-start.28 = (f32[128,768]{1,0:T(8,128)S(1)}, f32[128,768]{1,0:T(8,128)S(1)}, u32[]{:S(2)}, u32[]{:S(2)}) collective-permute-start(f32[128,768]{1,0:T(8,128)S(1)} %collective-permute-done.24.refs_2_), channel_id=1, source_target_pairs={{0,4},{4,0},{1,5},{5,1},{2,6},{6,2},{3,7},{7,3},{8,12},{12,8},{9,1... | collective-permute-start | bytes 1179656 | tf_op jit(solution)/shard_map/ppermute | solution.py:19
  181.6 14.0 %collective-permute-start.27 = (f32[128,768]{1,0:T(8,128)S(1)}, f32[128,768]{1,0:T(8,128)S(1)}, u32[]{:S(2)}, u32[]{:S(2)}) collective-permute-start(f32[128,768]{1,0:T(8,128)S(1)} %collective-permute-done.26.refs_4_), channel_id=1, source_target_pairs={{0,1},{1,0},{2,3},{3,2},{4,5},{5,4},{6,7},{7,6},{8,9},{9,8},{10,11... | collective-permute-start | bytes 1179656 | tf_op jit(solution)/shard_map/ppermute | solution.py:19
  182.1 14.3 %collective-permute-start.17 = (f32[128,768]{1,0:T(8,128)}, f32[128,768]{1,0:T(8,128)}, u32[]{:S(2)}, u32[]{:S(2)}) collective-permute-start(f32[128,768]{1,0:T(8,128)} %collective-permute-done.15.refs_0_), channel_id=1, source_target_pairs={{0,2},{2,0},{1,3},{3,1},{4,6},{6,4},{5,7},{7,5},{8,10},{10,8},{9,1... | collective-permute-start | bytes 1179656 | tf_op jit(solution)/shard_map/ppermute | solution.py:19
  188.3 13.6 %collective-permute-start.21 = (f32[128,768]{1,0:T(8,128)}, f32[128,768]{1,0:T(8,128)}, u32[]{:S(2)}, u32[]{:S(2)}) collective-permute-start(f32[128,768]{1,0:T(8,128)} %collective-permute-done.19.refs_4_), channel_id=1, source_target_pairs={{0,2},{2,0},{1,3},{3,1},{4,6},{6,4},{5,7},{7,5},{8,10},{10,8},{9,1... | collective-permute-start | bytes 1179656 | tf_op jit(solution)/shard_map/ppermute | solution.py:19
  196.4 17.6 %collective-permute-start.16 = (f32[128,768]{1,0:T(8,128)}, f32[128,768]{1,0:T(8,128)}, u32[]{:S(2)}, u32[]{:S(2)}) collective-permute-start(f32[128,768]{1,0:T(8,128)} %collective-permute-done.15.refs_0_), channel_id=1, source_target_pairs={{0,1},{1,0},{2,3},{3,2},{4,5},{5,4},{6,7},{7,6},{8,9},{9,8},{10,11... | collective-permute-start | bytes 1179656 | tf_op jit(solution)/shard_map/ppermute | solution.py:19
  197.7 16.2 %collective-permute-start.20 = (f32[128,768]{1,0:T(8,128)}, f32[128,768]{1,0:T(8,128)}, u32[]{:S(2)}, u32[]{:S(2)}) collective-permute-start(f32[128,768]{1,0:T(8,128)} %collective-permute-done.19.refs_4_), channel_id=1, source_target_pairs={{0,1},{1,0},{2,3},{3,2},{4,5},{5,4},{6,7},{7,6},{8,9},{9,8},{10,11... | collective-permute-start | bytes 1179656 | tf_op jit(solution)/shard_map/ppermute | solution.py:19
  201.9 12.0 %collective-permute-start.22 = (f32[128,768]{1,0:T(8,128)}, f32[128,768]{1,0:T(8,128)}, u32[]{:S(2)}, u32[]{:S(2)}) collective-permute-start(f32[128,768]{1,0:T(8,128)} %collective-permute-done.21.refs_6_), channel_id=1, source_target_pairs={{0,1},{1,0},{2,3},{3,2},{4,5},{5,4},{6,7},{7,6},{8,9},{9,8},{10,11... | collective-permute-start | bytes 1179656 | tf_op jit(solution)/shard_map/ppermute | solution.py:19
  (75 other events, 821.8 us)
where the time goes:
time: 218 us
  waiting for transfers between devices  108 us (50%)
  Pallas kernels  43.8 us (20%)
  starting transfers between devices  39.6 us (18%)
  local copies, waits for them, and re-layouts  21.6 us (10%)
  other arithmetic  3.68 us (2%)
    ppermute x40, waiting for transfers between devices, swap(): return lax.ppermute(block, axis, SWAP)  80.9 us
    ppermute x40, starting transfers between devices, swap(): return lax.ppermute(block, axis, SWAP)  27.6 us
    ppermute x8, waiting for transfers between devices, xor_permute(): return lax.ppermute(block, axis, [(i, i ^ distance) for i in range(size)])  26.7 us
    unnamed x118, local copies, waits for them, and re-layouts  20.3 us
    ppermute x8, starting transfers between devices, xor_permute(): return lax.ppermute(block, axis, [(i, i ^ distance) for i in range(size)])  12 us
    pallas_call x4, Pallas kernels, place(): pl.pallas_call(functools.partial(place_kernel, count=count, first=first),...  10.9 us
    pallas_call x1, Pallas kernels, run_forward(): pl.pallas_call(forward_kernel, out_shape=(shaped((2 * block, width), BF16...  9.82 us
    pallas_call x1, Pallas kernels, run_backward(): pl.pallas_call(functools.partial(backward_kernel, pieces=pieces), out_sha...  7.11 us
  transfers between devices with their start and end apart: 48, of which 17 were waited for; matrix products, arithmetic and copies ran while one was open for 2% of the time, Pallas kernels for 14%

commit v1 on v0

v1 whole, which is shorter than its diff:
```python
import functools

import jax
import jax.numpy as jnp
from jax import lax
from jax.experimental import pallas as pl
from jax.experimental.pallas import tpu as pltpu
from jax.sharding import Mesh
from jax.sharding import PartitionSpec as P

EPS = 1e-05
SWAP = [(0, 1), (1, 0)]
VMEM_BYTES = 56 * 2**20
F32 = jnp.float32
BF16 = jnp.bfloat16


def swap(block, axis):
    return lax.ppermute(block, axis, SWAP)


def xor_permute(block, axis, distance):
    size = lax.axis_size(axis)
    return lax.ppermute(block, axis, [(i, i ^ distance) for i in range(size)])


def any_spec():
    return pl.BlockSpec(memory_space=pl.ANY)


def hbm():
    return pl.BlockSpec(memory_space=pltpu.HBM)


def vmem():
    return pl.BlockSpec(memory_space=pltpu.VMEM)


def smem():
    return pl.BlockSpec(memory_space=pltpu.SMEM)


def shaped(shape, dtype=F32):
    return jax.ShapeDtypeStruct(shape, dtype)


def params(mib):
    return pltpu.CompilerParams(vmem_limit_bytes=mib * 2**20)


def cost(us):
    return pl.CostEstimate(
        flops=int(us * 1.1e9), bytes_accessed=int(us * 3.6e6), transcendentals=0
    )


def own_columns(sel, cols):
    return pl.ds(pl.multiple_of((2 * sel[0] + sel[1]) * cols, cols), cols)


def stored_at(sel, k):
    return 2 * ((k // 2) ^ sel[0]) + ((k % 2) ^ sel[1])


def row_part(sel, row):
    return row if isinstance(row, int) else 2 * (sel[3] ^ row[0]) + (sel[2] ^ row[1])


def tick_kernel(*refs):
    refs[-1][...] = jnp.zeros(refs[-1].shape, F32)


def tick(*values):
    return pl.pallas_call(
        tick_kernel,
        out_shape=shaped((8, 128)),
        in_specs=[any_spec()] * len(values),
        out_specs=vmem(),
        compiler_params=params(1),
        cost_estimate=cost(20),
        name="tick",
    )(*values)


def hold_kernel(*refs):
    del refs


def hold(values, *waits):
    count = len(values)
    return pl.pallas_call(
        hold_kernel,
        out_shape=tuple(shaped(v.shape, v.dtype) for v in values),
        in_specs=[any_spec()] * (count + len(waits)),
        out_specs=(any_spec(),) * count,
        input_output_aliases={i: i for i in range(count)},
        compiler_params=params(1),
        cost_estimate=cost(0.05),
        name="hold",
    )(*values, *waits)


def add_kernel(a_ref, b_ref, *refs):
    refs[-1][...] = a_ref[...] + b_ref[...]


def add(a, b, *waits):
    return pl.pallas_call(
        add_kernel,
        out_shape=shaped(a.shape),
        in_specs=[vmem()] * 2 + [any_spec()] * len(waits),
        out_specs=vmem(),
        compiler_params=params(4),
        cost_estimate=cost(0.05),
        name="add",
    )(a, b, *waits)


def take_weights_kernel(sel, w_ref, mine_ref, sem):
    width, cols = mine_ref.shape[0], mine_ref.shape[1] // 3
    copies = []
    for k in range(3):
        at = pl.multiple_of((2 * sel[0] + sel[1]) * cols + k * width, cols)
        copies.append(
            pltpu.make_async_copy(
                w_ref.at[:, pl.ds(at, cols)], mine_ref.at[:, k * cols : (k + 1) * cols], sem.at[k]
            )
        )
    for c in copies:
        c.start()
    for c in copies:
        c.wait()


def take_weights(sel, w_proj):
    width = w_proj.shape[0]
    return pl.pallas_call(
        take_weights_kernel,
        out_shape=shaped((width, 3 * width // 4), BF16),
        in_specs=[smem(), hbm()],
        out_specs=vmem(),
        scratch_shapes=[pltpu.SemaphoreType.DMA((3,))],
        compiler_params=params(4),
        cost_estimate=cost(3),
        name="take_weights",
    )(sel, w_proj)


def widen_cot_kernel(sel, cot_ref, cot_out):
    cols = cot_ref.shape[1] // 4
    for k in range(2):
        at = pl.multiple_of((2 * k + 1 - sel[1]) * cols, cols)
        cot_out[:, k * cols : (k + 1) * cols] = cot_ref[:, pl.ds(at, cols)].astype(F32)


def widen_cot(sel, cot):
    return pl.pallas_call(
        widen_cot_kernel,
        out_shape=shaped((cot.shape[0], cot.shape[1] // 2)),
        in_specs=[smem(), vmem()],
        out_specs=vmem(),
        compiler_params=params(4),
        cost_estimate=cost(2),
        name="widen_cot",
    )(sel, cot)


def pack_cot_kernel(sel, cot_ref, sibling_ref, cot_out):
    block, cols = cot_ref.shape[0], cot_ref.shape[1] // 4
    mine = pl.multiple_of((2 * (1 - sel[0]) + sel[1]) * cols, cols)
    cot_out[0:block, :] = cot_ref[:, pl.ds(mine, cols)].astype(F32)
    sibling = pl.multiple_of((1 - sel[0]) * cols, cols)
    cot_out[block:, :] = sibling_ref[:, pl.ds(sibling, cols)]


def pack_cot(sel, cot, sibling):
    return pl.pallas_call(
        pack_cot_kernel,
        out_shape=shaped((2 * cot.shape[0], cot.shape[1] // 4)),
        in_specs=[smem(), vmem(), vmem()],
        out_specs=vmem(),
        compiler_params=params(4),
        cost_estimate=cost(2),
        name="pack_cot",
    )(sel, cot, sibling)


def standardized(x):
    mean = jnp.mean(x, axis=-1, keepdims=True)
    centred = x - mean
    rdev = lax.rsqrt(jnp.mean(centred * centred, axis=-1, keepdims=True) + EPS)
    return centred * rdev, rdev


def norm_and_project(sel, toks, norm, w_ref, gates, normed, cand, zf, zr, base):
    cols = cand.shape[1]
    mine = own_columns(sel, cols)
    gain, bias = norm[0][...], norm[1][...]
    fb, rb = gates[2][:, mine], gates[3][:, mine]
    block = toks[0].shape[0]
    step = 16
    for at, tok in enumerate(toks):

        def body(i, carry, tok=tok, at=at):
            here = pl.ds(pl.multiple_of(i * step, step), step)
            there = pl.ds(pl.multiple_of(at * block + i * step, step), step)
            xhat, _ = standardized(tok[here, :])
            normed[there, :] = (xhat * gain + bias).astype(BF16)
            return carry

        lax.fori_loop(0, block // step, body, 0, unroll=True)
    rows = normed[...]
    here = slice(base, base + 2 * block)
    part = lambda k: jnp.dot(
        rows, w_ref[:, k * cols : (k + 1) * cols], preferred_element_type=F32
    )
    cand[here, :] = part(0)
    zf[here, :] = 0.5 * (part(1) + fb)
    zr[here, :] = 0.5 * (part(2) + rb)


def near_kernel(sel, offsets, tok0, tok1, w_ref, *refs):
    gates, norm, (normed, cand, zf, zr, half_keep) = refs[:4], refs[4:6], refs[6:]
    length, cols = half_keep.shape
    block = length // 4
    step = 16
    for b in range(4):
        base = stored_at(sel, b) * block

        def body(i, carry, b=b, base=base):
            at = pl.multiple_of(i * step, step)
            token = base + at + lax.broadcasted_iota(jnp.int32, (step, cols), 0)
            starts = token == offsets[0, 0]
            for k in range(1, offsets.shape[1]):
                starts = starts | (token == offsets[0, k])
            here = pl.ds(pl.multiple_of(b * block + at, step), step)
            half_keep[here, :] = jnp.where(starts, 0.0, 0.5)
            return carry

        lax.fori_loop(0, block // step, body, 0)
    norm_and_project(sel, (tok0, tok1), norm, w_ref, gates, normed, cand, zf, zr, 0)


def run_near(sel, offsets, toks, w_mine, vectors):
    block, width = toks[0].shape
    cols = width // 4
    return pl.pallas_call(
        near_kernel,
        out_shape=(shaped((2 * block, width), BF16),)
        + (shaped((2 * block, cols)),) * 3
        + (shaped((4 * block, cols)),),
        in_specs=[smem()] * 2 + [vmem()] * 9,
        out_specs=(vmem(),) * 5,
        compiler_params=params(16),
        cost_estimate=cost(10),
        name="near_blocks",
    )(sel, offsets, *toks, w_mine, *vectors)


def forward_kernel(sel, tok0, tok1, cand_near, zf_near, zr_near, half_keep, w_ref, *refs):
    gates, norm, (normed, cand, zf, zr, state, half_prev) = refs[:4], refs[4:6], refs[6:]
    length, cols = cand.shape
    block = length // 4
    near = slice(0, 2 * block)
    cand[near, :], zf[near, :], zr[near, :] = cand_near[...], zf_near[...], zr_near[...]
    fw = gates[0][:, own_columns(sel, cols)]
    norm_and_project(sel, (tok0, tok1), norm, w_ref, gates, normed, cand, zf, zr, 2 * block)
    c = jnp.zeros((1, cols), F32)
    for k in range(4):
        base = stored_at(sel, k) * block

        def body(i, c, base=base):
            row = pl.ds(base + i, 1)
            half = half_keep[row, :]
            th = jnp.tanh(zf[row, :] + (half * fw) * c)
            hp = half * c
            hc = 0.5 * cand[row, :]
            c = (hp + hc) + (hp - hc) * th
            state[row, :] = c
            half_prev[row, :] = hp
            return c

        c = lax.fori_loop(0, block, body, c, unroll=16)


def run_forward(sel, toks, near, w_mine, vectors):
    block, width = toks[0].shape
    cols = width // 4
    length = 4 * block
    return pl.pallas_call(
        forward_kernel,
        out_shape=(shaped((2 * block, width), BF16),) + (shaped((length, cols)),) * 5,
        in_specs=[smem()] + [vmem()] * 13,
        out_specs=(vmem(),) * 6,
        compiler_params=params(20),
        cost_estimate=cost(20),
        name="forward_scan",
    )(sel, *toks, *near, w_mine, *vectors)


def backward_kernel(
    sel,
    x0,
    x1,
    x2,
    x3,
    g0,
    g1,
    g23,
    cand_ref,
    zf_ref,
    zr_ref,
    state,
    half_prev,
    half_keep,
    fw_ref,
    rw_ref,
    near_ref,
    far_ref,
    dproj_ref,
    out_ref,
    dxh_ref,
    small_ref,
    *refs,
    rows,
):
    products, (coef, add_b, add_e, gz, omf) = refs[: len(rows)], refs[len(rows) :]
    length, cols = cand_ref.shape
    block = length // 4
    mine = own_columns(sel, cols)
    half = pl.ds(pl.multiple_of(sel[0] * cols, cols), cols)
    fw, rw = fw_ref[:, mine], rw_ref[:, mine]
    half_fw, half_rw = 0.5 * fw, 0.5 * rw
    step = 16
    zero = jnp.zeros((step, cols), F32)
    sums = (zero, zero)
    everything = slice(0, cols)
    sources = (
        (x0, g0, 0, mine),
        (x1, g1, 0, half),
        (x2, g23, 0, everything),
        (x3, g23, block, everything),
    )
    for b, (x_ref, g_ref, g_at, g_cols) in enumerate(sources):

        def gate_body(i, carry, b=b, x_ref=x_ref, g_ref=g_ref, g_at=g_at, g_cols=g_cols):
            at = pl.multiple_of(i * step, step)
            here = pl.ds(pl.multiple_of(b * block + at, step), step)
            x = x_ref[pl.ds(at, step), mine]
            g = g_ref[pl.ds(pl.multiple_of(g_at + at, step), step), g_cols].astype(F32)
            keep = 2.0 * half_keep[here, :]
            prev = 2.0 * half_prev[here, :]
            c, cd = state[here, :], cand_ref[here, :]
            forget = 0.5 + 0.5 * jnp.tanh(zf_ref[here, :] + half_fw * prev)
            reset = 0.5 + 0.5 * jnp.tanh(zr_ref[here, :] + half_rw * prev)
            not_forget, not_reset = 1.0 - forget, 1.0 - reset
            out_ref[here, :] = reset * c + not_reset * x
            dxh_ref[here, :] = g * not_reset
            dzr = g * (c - x) * reset * not_reset
            slope = (prev - cd) * forget * not_forget
            coef[here, :] = keep * (forget + slope * fw)
            add_b[here, :] = keep * (dzr * rw)
            add_e[here, :] = g * reset
            gz[here, :] = slope
            omf[here, :] = not_forget
            dproj_ref[here, 2 * cols : 3 * cols] = dzr.astype(BF16)
            return (carry[0] + dzr * prev, carry[1] + dzr)

        sums = lax.fori_loop(0, block // step, gate_body, sums, unroll=True)
    rw_sum, rb_sum = sums

    s = jnp.zeros((1, cols), F32)
    for k in range(3, -1, -1):
        last = stored_at(sel, k) * block + block - 1

        def backward_body(i, s, last=last):
            row = pl.ds(last - i, 1)
            total = s + add_e[row, :]
            add_e[row, :] = total
            return coef[row, :] * total + add_b[row, :]

        s = lax.fori_loop(0, block, backward_body, s, unroll=16)

    def grad_body(i, carry):
        here = pl.ds(pl.multiple_of(i * step, step), step)
        total = add_e[here, :]
        prev = 2.0 * half_prev[here, :]
        dzf = total * gz[here, :]
        dproj_ref[here, 0:cols] = (total * omf[here, :]).astype(BF16)
        dproj_ref[here, cols : 2 * cols] = dzf.astype(BF16)
        return (carry[0] + dzf * prev, carry[1] + dzf)

    fw_sum, fb_sum = lax.fori_loop(0, length // step, grad_body, (zero, zero), unroll=4)
    small_ref[...] = jnp.concatenate(
        [jnp.sum(v, axis=0, keepdims=True) for v in (fw_sum, rw_sum, fb_sum, rb_sum)]
        + [jnp.zeros((4, cols), F32)],
        axis=0,
    )
    outer_products(sel, rows, near_ref, far_ref, dproj_ref, products)


def outer_products(sel, rows, near_ref, far_ref, dproj_ref, outs):
    half, width = near_ref.shape
    part = width // 8
    dims = (((0,), (0,)), ((), ()))
    for out, places in zip(outs, rows):
        for k, place_of in enumerate(places):
            at = pl.ds(pl.multiple_of(row_part(sel, place_of) * part, part), part)
            out[k * part : (k + 1) * part, :] = lax.dot_general(
                near_ref[:, at], dproj_ref[0:half, :], dims, preferred_element_type=F32
            ) + lax.dot_general(
                far_ref[:, at], dproj_ref[half:, :], dims, preferred_element_type=F32
            )


def product_shapes(width, rows):
    return tuple(shaped((len(places) * width // 8, 3 * width // 4)) for places in rows)


def run_backward(sel, toks, cots, scanned, half_keep, gates, normed, rows):
    block, width = toks[0].shape
    cols = width // 4
    length = 4 * block
    return pl.pallas_call(
        functools.partial(backward_kernel, rows=rows),
        out_shape=(
            shaped((length, 3 * cols), BF16),
            shaped((length, cols)),
            shaped((length, cols)),
            shaped((8, cols)),
        )
        + product_shapes(width, rows),
        in_specs=[smem()] + [vmem()] * 17,
        out_specs=(vmem(),) * (4 + len(rows)),
        scratch_shapes=[pltpu.VMEM((length, cols), F32)] * 5,
        compiler_params=params(24),
        cost_estimate=cost(20),
        name="backward_scan",
    )(sel, *toks, *cots, *scanned, half_keep, *gates[:2], *normed)


def products_kernel(sel, near_ref, far_ref, dproj_ref, *outs, rows):
    outer_products(sel, rows, near_ref, far_ref, dproj_ref, outs)


def run_products(sel, normed, dproj, rows):
    return pl.pallas_call(
        functools.partial(products_kernel, rows=rows),
        out_shape=product_shapes(normed[0].shape[1], rows),
        in_specs=[smem()] + [vmem()] * 3,
        out_specs=(vmem(),) * len(rows),
        compiler_params=params(12),
        cost_estimate=cost(0.05),
        name="products",
    )(sel, *normed, dproj)


def input_kernel(
    sel,
    tok0,
    tok1,
    tok2,
    tok3,
    dproj_ref,
    dxh_ref,
    out_ref,
    gate_small_ref,
    w_ref,
    gain_ref,
    *refs,
):
    mine_ref, send_ref, dnormed = refs[-3:]
    cols = dxh_ref.shape[1]
    block, width = tok0.shape
    gain = gain_ref[...]
    mine = own_columns(sel, cols)
    step = 8
    sums = (jnp.zeros((step, width), F32), jnp.zeros((step, width), F32))
    for b, tok in enumerate((tok0, tok1, tok2, tok3)):
        rows = slice(b * block, (b + 1) * block)
        dnormed[...] = lax.dot_general(
            dproj_ref[rows, :], w_ref[...], (((1,), (1,)), ((), ())), preferred_element_type=F32
        )
        where = send_ref if b % 2 else mine_ref
        base = (b // 2) * block

        def body(i, carry, tok=tok, base=base, where=where):
            here = pl.ds(pl.multiple_of(i * step, step), step)
            there = pl.ds(pl.multiple_of(base + i * step, step), step)
            xhat, rdev = standardized(tok[here, :])
            dn = dnormed[here, :]
            dxhat = dn * gain
            mean1 = jnp.mean(dxhat, axis=-1, keepdims=True)
            mean2 = jnp.mean(dxhat * xhat, axis=-1, keepdims=True)
            where[there, 0:width] = rdev * (dxhat - mean1 - xhat * mean2)
            return (carry[0] + dn * xhat, carry[1] + dn)

        sums = lax.fori_loop(0, block // step, body, sums, unroll=11)
        to = pl.ds(base, block)
        where[to, mine] += dxh_ref[rows, :]
        where[to, width : width + cols] = out_ref[rows, :]
    tail = slice(2 * block, 2 * block + 8)
    mine_ref[tail, :] = jnp.zeros((8, width + cols), F32)
    mine_ref[2 * block : 2 * block + 4, mine] = gate_small_ref[0:4, :]
    for i, v in enumerate(sums):
        row = 2 * block + 4 + i
        mine_ref[row : row + 1, 0:width] = jnp.sum(v, axis=0, keepdims=True)
    send_ref[tail, :] = mine_ref[tail, :]


def run_input(sel, toks, dproj, dxh, out, gate_small, w_mine, gain, *waits):
    block, width = toks[0].shape
    shape = (2 * block + 8, width + width // 4)
    return pl.pallas_call(
        input_kernel,
        out_shape=(shaped(shape), shaped(shape)),
        in_specs=[smem()] + [vmem()] * 10 + [any_spec()] * len(waits),
        out_specs=(vmem(),) * 2,
        scratch_shapes=[pltpu.VMEM((block, width), F32)],
        compiler_params=params(20),
        cost_estimate=cost(0.05),
        name="input_side",
    )(sel, *toks, dproj, dxh, out, gate_small, w_mine, gain, *waits)


def combine_kernel(sel, mine_ref, got_ref, *refs):
    keep_ref, send_ref, small_ref = refs[-3:]
    block, width = keep_ref.shape[0], small_ref.shape[1]
    cols = width // 4
    low = pl.ds(pl.multiple_of(width + sel[1] * cols, cols), cols)
    high = pl.ds(pl.multiple_of(width + (1 - sel[1]) * cols, cols), cols)
    for ref, first in ((keep_ref, 0), (send_ref, block)):
        here = slice(first, first + block)
        ref[:, 0:width] = mine_ref[here, 0:width] + got_ref[here, 0:width]
        ref[:, low] = mine_ref[here, width:]
        ref[:, high] = got_ref[here, width:]
    small_ref[...] = mine_ref[2 * block :, 0:width] + got_ref[2 * block :, 0:width]


def combine(sel, mine, got, *waits):
    block, width = (mine.shape[0] - 8) // 2, mine.shape[1] * 4 // 5
    return pl.pallas_call(
        combine_kernel,
        out_shape=(shaped((block, width * 3 // 2)),) * 2 + (shaped((8, width)),),
        in_specs=[smem(), vmem(), vmem()] + [any_spec()] * len(waits),
        out_specs=(vmem(),) * 3,
        compiler_params=params(16),
        cost_estimate=cost(0.05),
        name="combine",
    )(sel, mine, got, *waits)


def join_kernel(sel, mine_ref, got_ref, out_ref, grad_ref):
    width = out_ref.shape[1]
    half = width // 2
    at = pl.multiple_of(sel[0] * half, half)
    other = pl.multiple_of((1 - sel[0]) * half, half)
    out_ref[:, pl.ds(at, half)] = mine_ref[:, width:].astype(BF16)
    out_ref[:, pl.ds(other, half)] = got_ref[:, width:].astype(BF16)
    grad_ref[...] = (mine_ref[:, 0:width] + got_ref[:, 0:width]).astype(BF16)


def join(sel, mine, got):
    block, width = mine.shape[0], mine.shape[1] * 2 // 3
    return pl.pallas_call(
        join_kernel,
        out_shape=(shaped((block, width), BF16),) * 2,
        in_specs=[smem()] + [vmem()] * 2,
        out_specs=(vmem(),) * 2,
        compiler_params=params(16),
        cost_estimate=cost(0.05),
        name="join",
    )(sel, mine, got)


def fold_small(small):
    rows, cols = 6, small.shape[1] // 4
    tails = [small[i : i + 1, 3 * cols :] for i in range(rows)]
    last = [jnp.concatenate(tails[:3], axis=1), jnp.concatenate(tails[3:], axis=1)]
    return jnp.concatenate([small[0:rows, : 3 * cols]] + last, axis=0)


def finish_kernel(keep_ref, got_ref, a1_ref, a3_ref, small_mine, small_got, total_ref):
    part = keep_ref.shape[0]
    total_ref[0:part, :] = keep_ref[...] + got_ref[...] + a1_ref[...] + a3_ref[...]
    total_ref[part:, :] = fold_small(small_mine[...] + small_got[...])


def finish(keep, got, a1, a3, small_mine, small_got):
    part, cols3 = keep.shape
    return pl.pallas_call(
        finish_kernel,
        out_shape=shaped((part + 8, cols3)),
        in_specs=[vmem()] * 6,
        out_specs=vmem(),
        compiler_params=params(8),
        cost_estimate=cost(0.05),
        name="finish",
    )(keep, got, a1, a3, small_mine, small_got)


def first_kernel(a_ref, first_ref):
    first_ref[...] = a_ref[0 : first_ref.shape[0], :]


def first_half(a):
    return pl.pallas_call(
        first_kernel,
        out_shape=shaped((a.shape[0] // 2, a.shape[1])),
        in_specs=[vmem()],
        out_specs=vmem(),
        compiler_params=params(6),
        cost_estimate=cost(0.05),
        name="first_half",
    )(a)


def pair_kernel(a_ref, b_ref, pair_ref):
    rows = a_ref.shape[0]
    pair_ref[0:rows, :] = a_ref[...]
    pair_ref[rows:, :] = b_ref[...]


def pair(a, b):
    rows, cols3 = a.shape
    return pl.pallas_call(
        pair_kernel,
        out_shape=shaped((2 * rows, cols3)),
        in_specs=[vmem()] * 2,
        out_specs=vmem(),
        compiler_params=params(6),
        cost_estimate=cost(0.05),
        name="pair",
    )(a, b)


def small_kernel(*refs, where):
    pieces, outs = refs[:-6], refs[-6:]
    sums = [pieces[i][at : at + 8, :] for i, at in where]
    while len(sums) > 1:
        sums = [a + b for a, b in zip(sums[::2], sums[1::2])]
    total = sums[0]
    cols = total.shape[1] // 3
    for i, out in enumerate(outs):
        out[:, 0 : 3 * cols] = total[i : i + 1, :]
        out[:, 3 * cols :] = total[6 + i // 3 : 7 + i // 3, (i % 3) * cols : (i % 3 + 1) * cols]


def small_sums(pieces, where):
    width = pieces[0].shape[1] // 3 * 4
    return pl.pallas_call(
        functools.partial(small_kernel, where=where),
        out_shape=(shaped((1, width)),) * 6,
        in_specs=[vmem()] * len(pieces),
        out_specs=(vmem(),) * 6,
        compiler_params=params(8),
        cost_estimate=cost(0.05),
        name="small_sums",
    )(*pieces)


def place_kernel(sel, *refs, where, give):
    target, sem = refs[-2 - bool(give)], refs[-1]
    cols = refs[0].shape[1] // 3
    width = target.shape[1] // 3
    part = width // 8
    copies = []

    def copy(src, dst):
        copies.append(pltpu.make_async_copy(src, dst, sem.at[len(copies)]))
        copies[-1].start()

    for at, (array, first, row, x_off, c_off) in enumerate(where):
        piece = refs[array].at[pl.ds(first, part)]
        to_row = pl.multiple_of(row_part(sel, row) * part, part)
        col = (2 * (sel[0] ^ x_off) + (sel[1] ^ c_off)) * cols
        for k in range(3):
            to = pl.multiple_of(col + k * width, cols)
            copy(piece.at[:, pl.ds(k * cols, cols)], target.at[pl.ds(to_row, part), pl.ds(to, cols)])
        if at < give:
            copy(piece, refs[-2].at[pl.ds(at * part, part)])
    for c in copies:
        c.wait()


def place(sel, arrays, where, target, width, give, *waits):
    count = len(arrays)
    extra = [] if target is None else [target]
    cols3 = 3 * width // 4
    return pl.pallas_call(
        functools.partial(place_kernel, where=where, give=give),
        out_shape=(shaped((width, 3 * width)),)
        + ((shaped((give * width // 8, cols3)),) if give else ()),
        in_specs=[smem()]
        + [vmem()] * count
        + [hbm()] * len(extra)
        + [any_spec()] * len(waits),
        out_specs=(hbm(), vmem()) if give else (hbm(),),
        scratch_shapes=[pltpu.SemaphoreType.DMA((3 * len(where) + give,))],
        input_output_aliases={1 + count: 0} if extra else {},
        compiler_params=params(8),
        cost_estimate=cost(0.05),
        name="place",
    )(sel, *arrays, *extra, *waits)


def given(array, where, part):
    return [(array, i * part, row, x_off, 1) for i, (_, _, row, x_off, _) in enumerate(where)]


def on_device(
    tokens,
    offsets,
    w_proj,
    forget_weight,
    reset_weight,
    forget_bias,
    reset_bias,
    layer_norm_gain,
    layer_norm_bias,
    cotangent,
):
    _, block, width = tokens.shape
    z, y, x, c = (lax.axis_index(a) for a in ("z", "y", "x", "c"))
    tuned = lax.axis_size("z") == 4
    sel = jnp.stack([x, c, y, z]).astype(jnp.int32)
    part = width // 8

    cot = cotangent[0]
    own = lax.optimization_barrier(tokens[0].astype(F32))
    tok_x = swap(own, "x")
    tok_c = swap(own, "c")
    cot_sibling = swap(widen_cot(sel, cot), "c")
    cot_packed = pack_cot(sel, cot, cot_sibling)
    cot_far = swap(cot_packed, "x")

    gates = [
        v.reshape(1, width) for v in (forget_weight, reset_weight, forget_bias, reset_bias)
    ]
    gain = layer_norm_gain.reshape(1, width)
    vectors = (*gates, gain, layer_norm_bias.reshape(1, width))
    w_mine = take_weights(sel, w_proj)
    near = run_near(sel, offsets, (own, tok_c), w_mine, vectors)
    (tok_x,) = hold((tok_x,), near[4], cot_packed)
    tok_xc = swap(tok_x, "c")
    far = run_forward(sel, (tok_x, tok_xc), near[1:], w_mine, vectors)
    normed = (near[0], far[0])
    toks = (own, tok_c, tok_x, tok_xc)
    if tuned:
        rows = [[[(d, 1)] for d in (2, 3, 1, 0)], [[(d, 0)] for d in (2, 3, 1, 0)]]
    else:
        rows = [[[0], [1], [2], [3]], [[4], [5], [6], [7]]]
    dproj, out, dxh, gate_small, s2 = run_backward(
        sel, toks, (cot, cot_sibling, cot_far), far[1:], near[4], gates, normed, rows[0][:1]
    )
    s3, s1, s0 = run_products(sel, normed, dproj, rows[0][1:])
    k2, k3, k1, k0 = run_products(sel, normed, dproj, rows[1])
    input_side = lambda *waits: run_input(
        sel, toks, dproj, dxh, out, gate_small, w_mine, gain, *waits
    )

    if tuned:
        r2, r3, r1, r0 = (swap(piece, "y") for piece in (s2, s3, s1, s0))
        q2 = add(k2, r2, s0)
        a2 = xor_permute(q2, "z", 1)
        grad_mine, grad_send = input_side(q2)
        h3 = add(add(k3, r3), a2)
        a3 = xor_permute(h3, "z", 3)
        kept, sent, small = combine(
            sel, grad_mine, swap(grad_send, "c"), h3, tick(grad_send)
        )
        small_got = swap(small, "x")
        (sent,) = hold((sent,), small_got)
        got = swap(sent, "x")
        a1 = xor_permute(add(k1, r1, sent), "z", 1)
        total = finish(k0, r0, a1, a3, small, small_got)
        output, input_grad = join(sel, kept, got)

        z3, px0, py0 = xor_permute(total, "z", 3), swap(total, "x"), swap(total, "y")
        z1 = xor_permute(total, "z", 1)
        (px0,) = hold((px0,), input_grad)
        corner0 = swap(px0, "y")
        z3, z1, corner0, py0 = hold((z3, z1, corner0, py0))
        z13 = pair(z1, z3)
        z2, px13, py13 = xor_permute(z3, "z", 1), swap(z13, "x"), swap(z13, "y")
        corner3 = xor_permute(corner0, "z", 3)
        own = [(0, 0, (0, 0), 0, 0), (1, 0, (0, 0), 1, 0), (2, 0, (0, 1), 0, 0), (3, 0, (0, 1), 1, 0)]
        proj_grad, give = place(sel, (total, px0, py0, corner0), own, None, width, 4)
        z2, px13, py13, corner3 = hold((z2, px13, py13, corner3), give)
        px2, py2 = swap(z2, "x"), swap(z2, "y")
        corner12 = xor_permute(pair(corner0, corner3), "z", 1)
        other = given(3, own, part)
        own = [
            (array, (part + 8) * i, (d, y_off), x_off, 0)
            for array, y_off, x_off in ((0, 0, 0), (1, 0, 1), (2, 1, 0))
            for i, d in ((0, 1), (1, 3))
        ]
        proj_grad, give = place(
            sel,
            (z13, px13, py13, swap(give, "c")),
            own + other,
            proj_grad,
            width,
            6,
            tick(give),
        )
        other = given(2, own, part)
        own = [(0, 0, (2, 0), 0, 0), (1, 0, (3, 1), 1, 0)]
        proj_grad, give = place(
            sel, (z2, corner3, swap(give, "c")), own + other, proj_grad, width, 2, tick(give)
        )
        px2, py2, corner12 = hold((px2, py2, corner12), give)
        other = given(0, own, part)
        arrays, places = [swap(give, "c")], []
        last = (
            (px2, (((2, 0), 1),)),
            (py2, (((2, 1), 0),)),
            (corner12, (((1, 1), 1), ((2, 1), 1))),
        )
        for piece, parts in last:
            for held, c_off in ((piece, 0), (swap(piece, "c"), 1)):
                for i, (row, x_off) in enumerate(parts):
                    places.append((len(arrays), (part + 8) * i, row, x_off, c_off))
                arrays.append(held)
        (proj_grad,) = place(sel, arrays, other + places, proj_grad, width, 0, tick(give))
        tail = part + 8 + part
        where = [(0, part), (1, part), (2, part), (3, part), (4, part), (5, part), (2, tail), (3, tail)]
        small = small_sums((total, py0, z13, py13, z2, py2), where)
    else:
        grad_mine, grad_send = input_side()
        kept, sent, small = combine(sel, grad_mine, swap(grad_send, "c"))
        got = swap(sent, "x")
        small = lax.psum(small + swap(small, "x"), ("z", "y"))
        pieces = jnp.stack([s2, s3, s1, s0, k2, k3, k1, k0])
        pieces = lax.psum(pieces, ("z", "y"))
        proj_grad = None
        for x_off, held in ((0, pieces), (1, swap(pieces, "x"))):
            own = [(r, 0, r, x_off, 0) for r in range(8)]
            proj_grad, give = place(sel, list(held), own, proj_grad, width, 8)
            other = given(0, own, part)
            (proj_grad,) = place(sel, [swap(give, "c")], other, proj_grad, width, 0)
        output, input_grad = join(sel, kept, got)
    small = [small[i].reshape(width) for i in range(6)]
    return (output[None], input_grad[None], proj_grad, *small)


def solution(mesh):
    dp, rep = mesh.shape["dp"], mesh.shape["rep"]
    fine = Mesh(mesh.devices.reshape(dp // 2, 2, rep // 2, 2), ("z", "y", "x", "c"))
    row, seq = ("z", "y"), ("x", "c")
    in_specs = (P(row, seq, None), P(row, None)) + (P(),) * 7 + (P(row, seq, None),)
    out_specs = (P(row, seq, None), P(row, seq, None)) + (P(),) * 7
    return jax.shard_map(
        on_device, mesh=fine, in_specs=in_specs, out_specs=out_specs, check_vma=False
    )
```

time: 218 us -> 167 us (0.77)
  local copies, waits for them, and re-layouts: 21.6 us -> 2.09 us
  waiting for transfers between devices: 108 us -> 89 us
  starting transfers between devices: 39.6 us -> 33.1 us
  Pallas kernels: 43.8 us -> 40.5 us
  other arithmetic: 3.68 us -> 1.12 us
    ppermute x40 -> x25, waiting for transfers between devices: 80.9 us -> 46 us  [swap(): return lax.ppermute(block, axis, SWAP)]
    unnamed x118 -> x22, local copies, waits for them, and re-layouts: 20.3 us -> 2.09 us
    ppermute x8, waiting for transfers between devices: 26.7 us -> 43 us  [xor_permute(): return lax.ppermute(block, axis, [(i, i ^ distance) for i in range(size)])]
    ppermute x40 -> x25, starting transfers between devices: 27.6 us -> 20.5 us  [swap(): return lax.ppermute(block, axis, SWAP)]
    add x8 -> x0, other arithmetic: 2.69 us -> none  [the longest x2 1.08 us: on_device(): keep + swap(send, 'y')]
    pallas_call x9 -> x28, Pallas kernels: 28.6 us -> 27.6 us  [the longest x4 10.5 us: place(): pl.pallas_call(functools.partial(place_kernel, where=where, give=give), o...]
  transfers between devices with their start and end apart: 48 -> 33, of which waited for: 17 -> 24; matrix products, arithmetic and copies ran while one was open for 2% -> 0% of each run, Pallas kernels for 14% -> 18%
where the time goes in v1:
time: 167 us
  waiting for transfers between devices  89 us (53%)
  Pallas kernels  40.5 us (24%)
  starting transfers between devices  33.1 us (20%)
  local copies, waits for them, and re-layouts  2.09 us (1%)
    ppermute x25, waiting for transfers between devices, swap(): return lax.ppermute(block, axis, SWAP)  46 us
    ppermute x8, waiting for transfers between devices, xor_permute(): return lax.ppermute(block, axis, [(i, i ^ distance) for i in range(size)])  43 us
    ppermute x25, starting transfers between devices, swap(): return lax.ppermute(block, axis, SWAP)  20.5 us
    ppermute x8, starting transfers between devices, xor_permute(): return lax.ppermute(block, axis, [(i, i ^ distance) for i in range(size)])  12.6 us
    pallas_call x4, Pallas kernels, place(): pl.pallas_call(functools.partial(place_kernel, where=where, give=give), o...  10.5 us
    pallas_call x1, Pallas kernels, run_forward(): pl.pallas_call(forward_kernel, out_shape=(shaped((2 * block, width), BF16...  8.78 us
    pallas_call x1, Pallas kernels, run_input(): pl.pallas_call(input_kernel, out_shape=(shaped(shape), shaped(shape)), in...  5.95 us
    pallas_call x1, Pallas kernels, run_backward(): pl.pallas_call(functools.partial(backward_kernel, rows=rows), out_shape=(...  4.94 us
  transfers between devices with their start and end apart: 33, of which 24 were waited for; matrix products, arithmetic and copies ran while one was open for 0% of the time, Pallas kernels for 18%

profile of v1, /device:TPU:0, one launch (start us, length us, event | category | flops | bytes accessed | tf_op | source)
XLA Modules:
  0.0 166.8 jit_solution(4720095833557845364)
XLA Ops:
  4.0 2.9 %collective-permute-start.1 = (f32[176,1024]{1,0:T(8,128)S(1)}, f32[176,1024]{1,0:T(8,128)S(1)}, u32[]{:S(2)}, u32[]{:S(2)}) collective-permute-start(f32[176,1024]{1,0:T(8,128)S(1)} %bitcast_convert_fusion.tok0.x0), channel_id=1, source_target_pairs={{0,2},{2,0},{1,3},{3,1},{4,6},{6,4},{5,7},{7,5},{8,10},{10,8},{9,1... | collective-permute-start | bytes 2162696 | tf_op jit(solution)/shard_map/ppermute | solution.py:19
  8.5 2.2 %near_blocks.1 = (bf16[352,1024]{1,0:T(8,128)(2,1)S(1)}, f32[352,256]{1,0:T(8,128)S(1)}, f32[352,256]{1,0:T(8,128)S(1)}, f32[352,256]{1,0:T(8,128)S(1)}, f32[704,256]{1,0:T(8,128)S(1)}) custom-call(s32[4]{0:T(128)S(1)} %pad_add_fusion.sel, s32[1,8]{1,0:T(1,128)S(1)} %copy-done.10, f32[176,1024]{1,0:T(8,128)S(1)} %bitcast_convert_fusion.tok0.x0, ...), custom_call_target="tpu_custom_call" | custom-call | flops 11000000512 | bytes 36000000 | tf_op jit(solution)/shard_map/near_blocks/pallas_call | solution.py:247
  10.7 12.6 %collective-permute-done.1.refs_0_ = f32[176,1024]{1,0:T(8,128)S(1)} collective-permute-done((f32[176,1024]{1,0:T(8,128)S(1)}, f32[176,1024]{1,0:T(8,128)S(1)}, u32[]{:S(2)}, u32[]{:S(2)}) %collective-permute-start.1) | collective-permute-done | bytes 720928 | tf_op jit(solution)/shard_map/ppermute | solution.py:19
  23.3 1.7 %collective-permute-start.4 = (f32[352,256]{1,0:T(8,128)S(1)}, f32[352,256]{1,0:T(8,128)S(1)}, u32[]{:S(2)}, u32[]{:S(2)}) collective-permute-start(f32[352,256]{1,0:T(8,128)S(1)} %pack_cot.1.refs_2_), channel_id=1, source_target_pairs={{0,2},{2,0},{1,3},{3,1},{4,6},{6,4},{5,7},{7,5},{8,10},{10,8},{9,1... | collective-permute-start | bytes 1081352 | tf_op jit(solution)/shard_map/ppermute | solution.py:19
  25.5 8.8 %forward_scan.1 = (bf16[352,1024]{1,0:T(8,128)(2,1)S(1)}, f32[704,256]{1,0:T(8,128)S(1)}, f32[704,256]{1,0:T(8,128)S(1)}, f32[704,256]{1,0:T(8,128)S(1)}, f32[70...) custom-call(s32[4]{0:T(128)S(1)} %pad_add_fusion.sel, f32[176,1024]{1,0:T(8,128)S(1)} %hold.6.tok0.x2.tok2, ...), custom_call_target="tpu_custom_call" | custom-call | flops 22000001024 | bytes 72000000 | tf_op jit(solution)/shard_map/forward_scan/pallas_call | solution.py:290
  34.3 4.9 %backward_scan.1 = (bf16[704,768]{1,0:T(8,128)(2,1)S(1)}, f32[704,256]{1,0:T(8,128)S(1)}, f32[704,256]{1,0:T(8,128)S(1)}, f32[8,256]{1,0:T(8,128)S(1)}, f32[128,768]{1,0:T(8,128)S(1)}) custom-call(s32[4]{0:T(128)S(1)} %pad_add_fusion.sel, f32[176,1024]{1,0:T(8,128)S(1)} %bitcast_convert_fusion.tok0.x0, f32[176,1024]{1,0:T(8,128)S(1)} %collective-permute-done.tok1.x1, ...), custom_call_target="tpu_custom_call" | custom-call | flops 22000001024 | bytes 72000000 | tf_op jit(solution)/shard_map/backward_scan/pallas_call | solution.py:424
  39.3 1.8 %collective-permute-start.5 = (f32[128,768]{1,0:T(8,128)S(1)}, f32[128,768]{1,0:T(8,128)S(1)}, u32[]{:S(2)}, u32[]{:S(2)}) collective-permute-start(f32[128,768]{1,0:T(8,128)S(1)} %get-tuple-element.78), channel_id=1, source_target_pairs={{0,4},{4,0},{1,5},{5,1},{2,6},{6,2},{3,7},{7,3},{8,12},{12,8},{9,1... | collective-permute-start | bytes 1179656 | tf_op jit(solution)/shard_map/ppermute | solution.py:19
  42.8 1.8 %collective-permute-start.12 = (f32[128,768]{1,0:T(8,128)S(1)}, f32[128,768]{1,0:T(8,128)S(1)}, u32[]{:S(2)}, u32[]{:S(2)}) collective-permute-start(f32[128,768]{1,0:T(8,128)S(1)} %get-tuple-element.91), channel_id=1, source_target_pairs={{0,4},{4,0},{1,5},{5,1},{2,6},{6,2},{3,7},{7,3},{8,12},{12,8},{9,1... | collective-permute-start | bytes 1179656 | tf_op jit(solution)/shard_map/ppermute | solution.py:19
  46.1 5.2 %collective-permute-done.5.b_ref = f32[128,768]{1,0:T(8,128)S(1)} collective-permute-done((f32[128,768]{1,0:T(8,128)S(1)}, f32[128,768]{1,0:T(8,128)S(1)}, u32[]{:S(2)}, u32[]{:S(2)}) %collective-permute-start.5) | collective-permute-done | bytes 393248 | tf_op jit(solution)/shard_map/ppermute | solution.py:19
  51.3 1.9 %collective-permute-start.8 = (f32[128,768]{1,0:T(8,128)S(1)}, f32[128,768]{1,0:T(8,128)S(1)}, u32[]{:S(2)}, u32[]{:S(2)}) collective-permute-start(f32[128,768]{1,0:T(8,128)S(1)} %add.10.refs_0_), channel_id=1, source_target_pairs={{0,8},{8,0},{16,24},{24,16},{1,9},{9,1},{17,25},{25,17},{2,10},{10... | collective-permute-start | bytes 1179656 | tf_op jit(solution)/shard_map/ppermute | solution.py:24
  53.2 5.9 %input_side.1 = (f32[360,1280]{1,0:T(8,128)S(1)}, f32[360,1280]{1,0:T(8,128)S(1)}) custom-call(s32[4]{0:T(128)S(1)} %pad_add_fusion.sel, f32[176,1024]{1,0:T(8,128)S(1)} %bitcast_convert_fusion.tok0.x0, f32[176,1024]{1,0:T(8,128)S(1)} %collective-permute-done.tok1.x1, f32[176,1024]{1,0:T(8,128)S(1)} %hold.6.tok0.x2.tok2, ...), custom_call_target="tpu_custom_call" | custom-call | flops 55000000 | bytes 180000 | tf_op jit(solution)/shard_map/input_side/pallas_call | solution.py:514
  61.0 2.0 %collective-permute-done.6.got_ref = f32[360,1280]{1,0:T(8,128)S(1)} collective-permute-done((f32[360,1280]{1,0:T(8,128)S(1)}, f32[360,1280]{1,0:T(8,128)S(1)}, u32[]{:S(2)}, u32[]{:S(2)}) %collective-permute-start.6) | collective-permute-done | bytes 1843232 | tf_op jit(solution)/shard_map/ppermute | solution.py:19
  65.4 2.4 %collective-permute-done.9.refs_1_.small_got = f32[8,1024]{1,0:T(8,128)S(1)} collective-permute-done((f32[8,1024]{1,0:T(8,128)S(1)}, f32[8,1024]{1,0:T(8,128)S(1)}, u32[]{:S(2)}, u32[]{:S(2)}) %collective-permute-start.9) | collective-permute-done | bytes 32800 | tf_op jit(solution)/shard_map/ppermute | solution.py:19
  70.8 2.5 %collective-permute-start.14 = (f32[128,768]{1,0:T(8,128)S(1)}, f32[128,768]{1,0:T(8,128)S(1)}, u32[]{:S(2)}, u32[]{:S(2)}) collective-permute-start(f32[128,768]{1,0:T(8,128)S(1)} %add.12.refs_0_), channel_id=1, source_target_pairs={{0,24},{8,16},{16,8},{24,0},{1,25},{9,17},{17,9},{25,1},{2,26},{10... | collective-permute-start | bytes 1179656 | tf_op jit(solution)/shard_map/ppermute | solution.py:24
  74.1 5.2 %collective-permute-done.11.got_ref = f32[128,768]{1,0:T(8,128)S(1)} collective-permute-done((f32[128,768]{1,0:T(8,128)S(1)}, f32[128,768]{1,0:T(8,128)S(1)}, u32[]{:S(2)}, u32[]{:S(2)}) %collective-permute-start.11) | collective-permute-done | bytes 393248 | tf_op jit(solution)/shard_map/ppermute | solution.py:19
  79.3 5.4 %collective-permute-done.14.a3_ref = f32[128,768]{1,0:T(8,128)S(1)} collective-permute-done((f32[128,768]{1,0:T(8,128)S(1)}, f32[128,768]{1,0:T(8,128)S(1)}, u32[]{:S(2)}, u32[]{:S(2)}) %collective-permute-start.14) | collective-permute-done | bytes 393248 | tf_op jit(solution)/shard_map/ppermute | solution.py:24
  84.7 6.2 %collective-permute-done.13.a1_ref = f32[128,768]{1,0:T(8,128)S(1)} collective-permute-done((f32[128,768]{1,0:T(8,128)S(1)}, f32[128,768]{1,0:T(8,128)S(1)}, u32[]{:S(2)}, u32[]{:S(2)}) %collective-permute-start.13) | collective-permute-done | bytes 393248 | tf_op jit(solution)/shard_map/ppermute | solution.py:24
  91.6 1.8 %collective-permute-start.15 = (f32[136,768]{1,0:T(8,128)S(1)}, f32[136,768]{1,0:T(8,128)S(1)}, u32[]{:S(2)}, u32[]{:S(2)}) collective-permute-start(f32[136,768]{1,0:T(8,128)S(1)} %finish.1.refs_0_), channel_id=1, source_target_pairs={{0,24},{8,16},{16,8},{24,0},{1,25},{9,17},{17,9},{25,1},{2,26},{10... | collective-permute-start | bytes 1253384 | tf_op jit(solution)/shard_map/ppermute | solution.py:24
  95.4 7.2 %collective-permute-done.17.refs_0_ = f32[136,768]{1,0:T(8,128)S(1)} collective-permute-done((f32[136,768]{1,0:T(8,128)S(1)}, f32[136,768]{1,0:T(8,128)S(1)}, u32[]{:S(2)}, u32[]{:S(2)}) %collective-permute-start.17) | collective-permute-done | bytes 417824 | tf_op jit(solution)/shard_map/ppermute | solution.py:19
  104.3 1.6 collective-permute-done.15.refs_0_
  106.0 6.6 %collective-permute-done.16.refs_1_ = f32[136,768]{1,0:T(8,128)S(1)} collective-permute-done((f32[136,768]{1,0:T(8,128)S(1)}, f32[136,768]{1,0:T(8,128)S(1)}, u32[]{:S(2)}, u32[]{:S(2)}) %collective-permute-start.16) | collective-permute-done | bytes 417824 | tf_op jit(solution)/shard_map/ppermute | solution.py:24
  112.6 1.7 %collective-permute-done.18.refs_2_ = f32[136,768]{1,0:T(8,128)S(1)} collective-permute-done((f32[136,768]{1,0:T(8,128)S(1)}, f32[136,768]{1,0:T(8,128)S(1)}, u32[]{:S(2)}, u32[]{:S(2)}) %collective-permute-start.18) | collective-permute-done | bytes 417824 | tf_op jit(solution)/shard_map/ppermute | solution.py:19
  116.5 3.4 %collective-permute-start.23 = (f32[136,768]{1,0:T(8,128)S(1)}, f32[136,768]{1,0:T(8,128)S(1)}, u32[]{:S(2)}, u32[]{:S(2)}) collective-permute-start(f32[136,768]{1,0:T(8,128)S(1)} %get-tuple-element.94.refs_3_.a_ref), channel_id=1, source_target_pairs={{0,24},{8,16},{16,8},{24,0},{1,25},{9,17},{17,9},{25,1},{2,26},{10... | collective-permute-start | bytes 1253384 | tf_op jit(solution)/shard_map/ppermute | solution.py:24
  119.9 2.0 %place.4 = (f32[1024,3072]{1,0:T(8,128)}, f32[512,768]{1,0:T(8,128)S(1)}) custom-call(s32[4]{0:T(128)S(1)} %pad_add_fusion.sel, f32[136,768]{1,0:T(8,128)S(1)} %finish.1.refs_0_, f32[136,768]{1,0:T(8,128)S(1)} %hold.8.refs_1_, f32[136,768]{1,0:T(8,128)S(1)} %get-tuple-element.95.refs_2_.refs_1_, f32[136,768]{1,0:T(8,128)S(1)} %get-tuple-element.94.refs_3_.a_ref), custom_call_target="tpu_custom_call" | custom-call | flops 55000000 | bytes 180000 | tf_op jit(solution)/shard_map/place/pallas_call | solution.py:690
  122.0 4.6 %collective-permute-done.20.refs_0_ = f32[136,768]{1,0:T(8,128)S(1)} collective-permute-done((f32[136,768]{1,0:T(8,128)S(1)}, f32[136,768]{1,0:T(8,128)S(1)}, u32[]{:S(2)}, u32[]{:S(2)}) %collective-permute-start.20) | collective-permute-done | bytes 417824 | tf_op jit(solution)/shard_map/ppermute | solution.py:24
  126.6 7.1 %collective-permute-done.23.refs_3_ = f32[136,768]{1,0:T(8,128)S(1)} collective-permute-done((f32[136,768]{1,0:T(8,128)S(1)}, f32[136,768]{1,0:T(8,128)S(1)}, u32[]{:S(2)}, u32[]{:S(2)}) %collective-permute-start.23) | collective-permute-done | bytes 417824 | tf_op jit(solution)/shard_map/ppermute | solution.py:24
  134.5 3.2 %place.5 = (f32[1024,3072]{1,0:T(8,128)}, f32[768,768]{1,0:T(8,128)S(1)}) custom-call(s32[4]{0:T(128)S(1)} %pad_add_fusion.sel, f32[272,768]{1,0:T(8,128)S(1)} %pair.2.refs_0_.refs_2_, f32[272,768]{1,0:T(8,128)S(1)} %get-tuple-element.99.refs_1_, f32[272,768]{1,0:T(8,128)S(1)} %get-tuple-element.100.refs_2_.refs_3_, ...), custom_call_target="tpu_custom_call", output_to_operand_aliasing={{0}: (5, {})} | custom-call | flops 55000000 | bytes 180000 | tf_op jit(solution)/shard_map/place/pallas_call | solution.py:690
  139.5 2.4 %collective-permute-start.29 = (f32[272,768]{1,0:T(8,128)S(1)}, f32[272,768]{1,0:T(8,128)S(1)}, u32[]{:S(2)}, u32[]{:S(2)}) collective-permute-start(f32[272,768]{1,0:T(8,128)S(1)} %pair.3), channel_id=1, source_target_pairs={{0,8},{8,0},{16,24},{24,16},{1,9},{9,1},{17,25},{25,17},{2,10},{10... | collective-permute-start | bytes 2506760 | tf_op jit(solution)/shard_map/ppermute | solution.py:24
  142.2 2.6 %place.6 = (f32[1024,3072]{1,0:T(8,128)}, f32[256,768]{1,0:T(8,128)S(1)}) custom-call(s32[4]{0:T(128)S(1)} %pad_add_fusion.sel, f32[136,768]{1,0:T(8,128)S(1)} %get-tuple-element.97.refs_0_.refs_4_, f32[136,768]{1,0:T(8,128)S(1)} %get-tuple-element.98.refs_1_.b_ref, f32[768,768]{1,0:T(8,128)S(1)} %collective-permute-done.25.refs_2_, ...), custom_call_target="tpu_custom_call", output_to_operand_aliasing={{0}: (4, {})} | custom-call | flops 55000000 | bytes 180000 | tf_op jit(solution)/shard_map/place/pallas_call | solution.py:690
  145.0 4.8 %collective-permute-done.27.refs_0_ = f32[136,768]{1,0:T(8,128)S(1)} collective-permute-done((f32[136,768]{1,0:T(8,128)S(1)}, f32[136,768]{1,0:T(8,128)S(1)}, u32[]{:S(2)}, u32[]{:S(2)}) %collective-permute-start.27) | collective-permute-done | bytes 417824 | tf_op jit(solution)/shard_map/ppermute | solution.py:19
  150.3 10.3 %collective-permute-done.29.refs_2_ = f32[272,768]{1,0:T(8,128)S(1)} collective-permute-done((f32[272,768]{1,0:T(8,128)S(1)}, f32[272,768]{1,0:T(8,128)S(1)}, u32[]{:S(2)}, u32[]{:S(2)}) %collective-permute-start.29) | collective-permute-done | bytes 835616 | tf_op jit(solution)/shard_map/ppermute | solution.py:24
  164.1 2.7 %place.7 = f32[1024,3072]{1,0:T(8,128)} custom-call(s32[4]{0:T(128)S(1)} %pad_add_fusion.sel, f32[256,768]{1,0:T(8,128)S(1)} %collective-permute-done.26.refs_0_, f32[136,768]{1,0:T(8,128)S(1)} %get-tuple-element.105.refs_1_, f32[136,768]{1,0:T(8,128)S(1)} %collective-permute-done.30.refs_2_, ...), custom_call_target="tpu_custom_call", output_to_operand_aliasing={{}: (8, {})} | custom-call | flops 55000000 | bytes 180000 | tf_op jit(solution)/shard_map/place/pallas_call | solution.py:690
  (91 shorter events, 30.4 us)
Async XLA Ops:
  1.7 6.7 %collective-permute-start = (f32[176,1024]{1,0:T(8,128)S(1)}, f32[176,1024]{1,0:T(8,128)S(1)}, u32[]{:S(2)}, u32[]{:S(2)}) collective-permute-start(f32[176,1024]{1,0:T(8,128)S(1)} %bitcast_convert_fusion.tok0.x0), channel_id=1, source_target_pairs={{0,1},{1,0},{2,3},{3,2},{4,5},{5,4},{6,7},{7,6},{8,9},{9,8},{10,11... | collective-permute-start | bytes 2162696 | tf_op jit(solution)/shard_map/ppermute | solution.py:19
  3.9 3.9 %collective-permute-start.2 = (f32[176,512]{1,0:T(8,128)S(1)}, f32[176,512]{1,0:T(8,128)S(1)}, u32[]{:S(2)}, u32[]{:S(2)}) collective-permute-start(f32[176,512]{1,0:T(8,128)S(1)} %widen_cot.1), channel_id=1, source_target_pairs={{0,1},{1,0},{2,3},{3,2},{4,5},{5,4},{6,7},{7,6},{8,9},{9,8},{10,11... | collective-permute-start | bytes 1081352 | tf_op jit(solution)/shard_map/ppermute | solution.py:19
  4.0 19.3 %collective-permute-start.1 = (f32[176,1024]{1,0:T(8,128)S(1)}, f32[176,1024]{1,0:T(8,128)S(1)}, u32[]{:S(2)}, u32[]{:S(2)}) collective-permute-start(f32[176,1024]{1,0:T(8,128)S(1)} %bitcast_convert_fusion.tok0.x0), channel_id=1, source_target_pairs={{0,2},{2,0},{1,3},{3,1},{4,6},{6,4},{5,7},{7,5},{8,10},{10,8},{9,1... | collective-permute-start | bytes 2162696 | tf_op jit(solution)/shard_map/ppermute | solution.py:19
  23.3 2.2 %collective-permute-start.3 = (f32[176,1024]{1,0:T(8,128)S(1)}, f32[176,1024]{1,0:T(8,128)S(1)}, u32[]{:S(2)}, u32[]{:S(2)}) collective-permute-start(f32[176,1024]{1,0:T(8,128)S(1)} %hold.6.tok0.x2.tok2), channel_id=1, source_target_pairs={{0,1},{1,0},{2,3},{3,2},{4,5},{5,4},{6,7},{7,6},{8,9},{9,8},{10,11... | collective-permute-start | bytes 2162696 | tf_op jit(solution)/shard_map/ppermute | solution.py:19
  23.3 11.0 %collective-permute-start.4 = (f32[352,256]{1,0:T(8,128)S(1)}, f32[352,256]{1,0:T(8,128)S(1)}, u32[]{:S(2)}, u32[]{:S(2)}) collective-permute-start(f32[352,256]{1,0:T(8,128)S(1)} %pack_cot.1.refs_2_), channel_id=1, source_target_pairs={{0,2},{2,0},{1,3},{3,1},{4,6},{6,4},{5,7},{7,5},{8,10},{10,8},{9,1... | collective-permute-start | bytes 1081352 | tf_op jit(solution)/shard_map/ppermute | solution.py:19
  39.3 12.0 %collective-permute-start.5 = (f32[128,768]{1,0:T(8,128)S(1)}, f32[128,768]{1,0:T(8,128)S(1)}, u32[]{:S(2)}, u32[]{:S(2)}) collective-permute-start(f32[128,768]{1,0:T(8,128)S(1)} %get-tuple-element.78), channel_id=1, source_target_pairs={{0,4},{4,0},{1,5},{5,1},{2,6},{6,2},{3,7},{7,3},{8,12},{12,8},{9,1... | collective-permute-start | bytes 1179656 | tf_op jit(solution)/shard_map/ppermute | solution.py:19
  42.5 17.2 %collective-permute-start.7 = (f32[128,768]{1,0:T(8,128)S(1)}, f32[128,768]{1,0:T(8,128)S(1)}, u32[]{:S(2)}, u32[]{:S(2)}) collective-permute-start(f32[128,768]{1,0:T(8,128)S(1)} %get-tuple-element.83), channel_id=1, source_target_pairs={{0,4},{4,0},{1,5},{5,1},{2,6},{6,2},{3,7},{7,3},{8,12},{12,8},{9,1... | collective-permute-start | bytes 1179656 | tf_op jit(solution)/shard_map/ppermute | solution.py:19
  42.8 30.5 %collective-permute-start.12 = (f32[128,768]{1,0:T(8,128)S(1)}, f32[128,768]{1,0:T(8,128)S(1)}, u32[]{:S(2)}, u32[]{:S(2)}) collective-permute-start(f32[128,768]{1,0:T(8,128)S(1)} %get-tuple-element.91), channel_id=1, source_target_pairs={{0,4},{4,0},{1,5},{5,1},{2,6},{6,2},{3,7},{7,3},{8,12},{12,8},{9,1... | collective-permute-start | bytes 1179656 | tf_op jit(solution)/shard_map/ppermute | solution.py:19
  51.3 9.6 %collective-permute-start.8 = (f32[128,768]{1,0:T(8,128)S(1)}, f32[128,768]{1,0:T(8,128)S(1)}, u32[]{:S(2)}, u32[]{:S(2)}) collective-permute-start(f32[128,768]{1,0:T(8,128)S(1)} %add.10.refs_0_), channel_id=1, source_target_pairs={{0,8},{8,0},{16,24},{24,16},{1,9},{9,1},{17,25},{25,17},{2,10},{10... | collective-permute-start | bytes 1179656 | tf_op jit(solution)/shard_map/ppermute | solution.py:24
  59.2 3.9 %collective-permute-start.6 = (f32[360,1280]{1,0:T(8,128)S(1)}, f32[360,1280]{1,0:T(8,128)S(1)}, u32[]{:S(2)}, u32[]{:S(2)}) collective-permute-start(f32[360,1280]{1,0:T(8,128)S(1)} %get-tuple-element.81.refs_0_), channel_id=1, source_target_pairs={{0,1},{1,0},{2,3},{3,2},{4,5},{5,4},{6,7},{7,6},{8,9},{9,8},{10,11... | collective-permute-start | bytes 5529608 | tf_op jit(solution)/shard_map/ppermute | solution.py:19
  63.9 4.0 %collective-permute-start.9 = (f32[8,1024]{1,0:T(8,128)S(1)}, f32[8,1024]{1,0:T(8,128)S(1)}, u32[]{:S(2)}, u32[]{:S(2)}) collective-permute-start(f32[8,1024]{1,0:T(8,128)S(1)} %get-tuple-element.86.small_mine), channel_id=1, source_target_pairs={{0,2},{2,0},{1,3},{3,1},{4,6},{6,4},{5,7},{7,5},{8,10},{10,8},{9,1... | collective-permute-start | bytes 98312 | tf_op jit(solution)/shard_map/ppermute | solution.py:19
  67.8 26.0 %collective-permute-start.10 = (f32[176,1536]{1,0:T(8,128)S(1)}, f32[176,1536]{1,0:T(8,128)S(1)}, u32[]{:S(2)}, u32[]{:S(2)}) collective-permute-start(f32[176,1536]{1,0:T(8,128)S(1)} %hold.7.refs_0_), channel_id=1, source_target_pairs={{0,2},{2,0},{1,3},{3,1},{4,6},{6,4},{5,7},{7,5},{8,10},{10,8},{9,1... | collective-permute-start | bytes 3244040 | tf_op jit(solution)/shard_map/ppermute | solution.py:19
  69.3 10.0 %collective-permute-start.11 = (f32[128,768]{1,0:T(8,128)S(1)}, f32[128,768]{1,0:T(8,128)S(1)}, u32[]{:S(2)}, u32[]{:S(2)}) collective-permute-start(f32[128,768]{1,0:T(8,128)S(1)} %get-tuple-element.79.refs_0_), channel_id=1, source_target_pairs={{0,4},{4,0},{1,5},{5,1},{2,6},{6,2},{3,7},{7,3},{8,12},{12,8},{9,1... | collective-permute-start | bytes 1179656 | tf_op jit(solution)/shard_map/ppermute | solution.py:19
  70.8 13.9 %collective-permute-start.14 = (f32[128,768]{1,0:T(8,128)S(1)}, f32[128,768]{1,0:T(8,128)S(1)}, u32[]{:S(2)}, u32[]{:S(2)}) collective-permute-start(f32[128,768]{1,0:T(8,128)S(1)} %add.12.refs_0_), channel_id=1, source_target_pairs={{0,24},{8,16},{16,8},{24,0},{1,25},{9,17},{17,9},{25,1},{2,26},{10... | collective-permute-start | bytes 1179656 | tf_op jit(solution)/shard_map/ppermute | solution.py:24
  73.4 17.5 %collective-permute-start.13 = (f32[128,768]{1,0:T(8,128)S(1)}, f32[128,768]{1,0:T(8,128)S(1)}, u32[]{:S(2)}, u32[]{:S(2)}) collective-permute-start(f32[128,768]{1,0:T(8,128)S(1)} %add.13), channel_id=1, source_target_pairs={{0,8},{8,0},{16,24},{24,16},{1,9},{9,1},{17,25},{25,17},{2,10},{10... | collective-permute-start | bytes 1179656 | tf_op jit(solution)/shard_map/ppermute | solution.py:24
  91.0 11.6 %collective-permute-start.17 = (f32[136,768]{1,0:T(8,128)S(1)}, f32[136,768]{1,0:T(8,128)S(1)}, u32[]{:S(2)}, u32[]{:S(2)}) collective-permute-start(f32[136,768]{1,0:T(8,128)S(1)} %finish.1.refs_0_), channel_id=1, source_target_pairs={{0,2},{2,0},{1,3},{3,1},{4,6},{6,4},{5,7},{7,5},{8,10},{10,8},{9,1... | collective-permute-start | bytes 1253384 | tf_op jit(solution)/shard_map/ppermute | solution.py:19
  91.6 14.3 %collective-permute-start.15 = (f32[136,768]{1,0:T(8,128)S(1)}, f32[136,768]{1,0:T(8,128)S(1)}, u32[]{:S(2)}, u32[]{:S(2)}) collective-permute-start(f32[136,768]{1,0:T(8,128)S(1)} %finish.1.refs_0_), channel_id=1, source_target_pairs={{0,24},{8,16},{16,8},{24,0},{1,25},{9,17},{17,9},{25,1},{2,26},{10... | collective-permute-start | bytes 1253384 | tf_op jit(solution)/shard_map/ppermute | solution.py:24
  93.4 19.2 %collective-permute-start.16 = (f32[136,768]{1,0:T(8,128)S(1)}, f32[136,768]{1,0:T(8,128)S(1)}, u32[]{:S(2)}, u32[]{:S(2)}) collective-permute-start(f32[136,768]{1,0:T(8,128)S(1)} %finish.1.refs_0_), channel_id=1, source_target_pairs={{0,8},{8,0},{16,24},{24,16},{1,9},{9,1},{17,25},{25,17},{2,10},{10... | collective-permute-start | bytes 1253384 | tf_op jit(solution)/shard_map/ppermute | solution.py:24
  93.4 19.2 %collective-permute-start.19 = (f32[136,768]{1,0:T(8,128)S(1)}, f32[136,768]{1,0:T(8,128)S(1)}, u32[]{:S(2)}, u32[]{:S(2)}) collective-permute-start(f32[136,768]{1,0:T(8,128)S(1)} %finish.1.refs_0_), channel_id=1, source_target_pairs={{0,4},{4,0},{1,5},{5,1},{2,6},{6,2},{3,7},{7,3},{8,12},{12,8},{9,1... | collective-permute-start | bytes 1253384 | tf_op jit(solution)/shard_map/ppermute | solution.py:19
  103.6 10.7 %collective-permute-start.18 = (f32[136,768]{1,0:T(8,128)S(1)}, f32[136,768]{1,0:T(8,128)S(1)}, u32[]{:S(2)}, u32[]{:S(2)}) collective-permute-start(f32[136,768]{1,0:T(8,128)S(1)} %hold.8.refs_1_), channel_id=1, source_target_pairs={{0,4},{4,0},{1,5},{5,1},{2,6},{6,2},{3,7},{7,3},{8,12},{12,8},{9,1... | collective-permute-start | bytes 1253384 | tf_op jit(solution)/shard_map/ppermute | solution.py:19
  114.3 12.3 %collective-permute-start.20 = (f32[136,768]{1,0:T(8,128)S(1)}, f32[136,768]{1,0:T(8,128)S(1)}, u32[]{:S(2)}, u32[]{:S(2)}) collective-permute-start(f32[136,768]{1,0:T(8,128)S(1)} %get-tuple-element.92.b_ref), channel_id=1, source_target_pairs={{0,8},{8,0},{16,24},{24,16},{1,9},{9,1},{17,25},{25,17},{2,10},{10... | collective-permute-start | bytes 1253384 | tf_op jit(solution)/shard_map/ppermute | solution.py:24
  114.4 19.3 %collective-permute-start.21 = (f32[272,768]{1,0:T(8,128)S(1)}, f32[272,768]{1,0:T(8,128)S(1)}, u32[]{:S(2)}, u32[]{:S(2)}) collective-permute-start(f32[272,768]{1,0:T(8,128)S(1)} %pair.2.refs_0_.refs_2_), channel_id=1, source_target_pairs={{0,2},{2,0},{1,3},{3,1},{4,6},{6,4},{5,7},{7,5},{8,10},{10,8},{9,1... | collective-permute-start | bytes 2506760 | tf_op jit(solution)/shard_map/ppermute | solution.py:19
  115.9 18.5 %collective-permute-start.22 = (f32[272,768]{1,0:T(8,128)S(1)}, f32[272,768]{1,0:T(8,128)S(1)}, u32[]{:S(2)}, u32[]{:S(2)}) collective-permute-start(f32[272,768]{1,0:T(8,128)S(1)} %pair.2.refs_0_.refs_2_), channel_id=1, source_target_pairs={{0,4},{4,0},{1,5},{5,1},{2,6},{6,2},{3,7},{7,3},{8,12},{12,8},{9,1... | collective-permute-start | bytes 2506760 | tf_op jit(solution)/shard_map/ppermute | solution.py:19
  116.5 17.2 %collective-permute-start.23 = (f32[136,768]{1,0:T(8,128)S(1)}, f32[136,768]{1,0:T(8,128)S(1)}, u32[]{:S(2)}, u32[]{:S(2)}) collective-permute-start(f32[136,768]{1,0:T(8,128)S(1)} %get-tuple-element.94.refs_3_.a_ref), channel_id=1, source_target_pairs={{0,24},{8,16},{16,8},{24,0},{1,25},{9,17},{17,9},{25,1},{2,26},{10... | collective-permute-start | bytes 1253384 | tf_op jit(solution)/shard_map/ppermute | solution.py:24
  121.9 12.5 %collective-permute-start.24 = (f32[512,768]{1,0:T(8,128)S(1)}, f32[512,768]{1,0:T(8,128)S(1)}, u32[]{:S(2)}, u32[]{:S(2)}) collective-permute-start(f32[512,768]{1,0:T(8,128)S(1)} %get-tuple-element.96.refs_4_.refs_0_), channel_id=1, source_target_pairs={{0,1},{1,0},{2,3},{3,2},{4,5},{5,4},{6,7},{7,6},{8,9},{9,8},{10,11... | collective-permute-start | bytes 4718600 | tf_op jit(solution)/shard_map/ppermute | solution.py:19
  137.6 4.6 %collective-permute-start.25 = (f32[768,768]{1,0:T(8,128)S(1)}, f32[768,768]{1,0:T(8,128)S(1)}, u32[]{:S(2)}, u32[]{:S(2)}) collective-permute-start(f32[768,768]{1,0:T(8,128)S(1)} %get-tuple-element.102.refs_0_), channel_id=1, source_target_pairs={{0,1},{1,0},{2,3},{3,2},{4,5},{5,4},{6,7},{7,6},{8,9},{9,8},{10,11... | collective-permute-start | bytes 7077896 | tf_op jit(solution)/shard_map/ppermute | solution.py:19
  137.7 12.1 %collective-permute-start.27 = (f32[136,768]{1,0:T(8,128)S(1)}, f32[136,768]{1,0:T(8,128)S(1)}, u32[]{:S(2)}, u32[]{:S(2)}) collective-permute-start(f32[136,768]{1,0:T(8,128)S(1)} %get-tuple-element.97.refs_0_.refs_4_), channel_id=1, source_target_pairs={{0,2},{2,0},{1,3},{3,1},{4,6},{6,4},{5,7},{7,5},{8,10},{10,8},{9,1... | collective-permute-start | bytes 1253384 | tf_op jit(solution)/shard_map/ppermute | solution.py:19
  138.5 11.7 %collective-permute-start.28 = (f32[136,768]{1,0:T(8,128)S(1)}, f32[136,768]{1,0:T(8,128)S(1)}, u32[]{:S(2)}, u32[]{:S(2)}) collective-permute-start(f32[136,768]{1,0:T(8,128)S(1)} %get-tuple-element.97.refs_0_.refs_4_), channel_id=1, source_target_pairs={{0,4},{4,0},{1,5},{5,1},{2,6},{6,2},{3,7},{7,3},{8,12},{12,8},{9,1... | collective-permute-start | bytes 1253384 | tf_op jit(solution)/shard_map/ppermute | solution.py:19
  139.5 21.0 %collective-permute-start.29 = (f32[272,768]{1,0:T(8,128)S(1)}, f32[272,768]{1,0:T(8,128)S(1)}, u32[]{:S(2)}, u32[]{:S(2)}) collective-permute-start(f32[272,768]{1,0:T(8,128)S(1)} %pair.3), channel_id=1, source_target_pairs={{0,8},{8,0},{16,24},{24,16},{1,9},{9,1},{17,25},{25,17},{2,10},{10... | collective-permute-start | bytes 2506760 | tf_op jit(solution)/shard_map/ppermute | solution.py:24
  144.8 18.1 %collective-permute-start.26 = (f32[256,768]{1,0:T(8,128)S(1)}, f32[256,768]{1,0:T(8,128)S(1)}, u32[]{:S(2)}, u32[]{:S(2)}) collective-permute-start(f32[256,768]{1,0:T(8,128)S(1)} %get-tuple-element.104.refs_3_.refs_0_), channel_id=1, source_target_pairs={{0,1},{1,0},{2,3},{3,2},{4,5},{5,4},{6,7},{7,6},{8,9},{9,8},{10,11... | collective-permute-start | bytes 2359304 | tf_op jit(solution)/shard_map/ppermute | solution.py:19
  160.6 2.4 %collective-permute-start.31 = (f32[136,768]{1,0:T(8,128)S(1)}, f32[136,768]{1,0:T(8,128)S(1)}, u32[]{:S(2)}, u32[]{:S(2)}) collective-permute-start(f32[136,768]{1,0:T(8,128)S(1)} %get-tuple-element.106.refs_3_.refs_5_), channel_id=1, source_target_pairs={{0,1},{1,0},{2,3},{3,2},{4,5},{5,4},{6,7},{7,6},{8,9},{9,8},{10,11... | collective-permute-start | bytes 1253384 | tf_op jit(solution)/shard_map/ppermute | solution.py:19
  161.1 3.0 %collective-permute-start.32 = (f32[272,768]{1,0:T(8,128)S(1)}, f32[272,768]{1,0:T(8,128)S(1)}, u32[]{:S(2)}, u32[]{:S(2)}) collective-permute-start(f32[272,768]{1,0:T(8,128)S(1)} %get-tuple-element.107.refs_5_), channel_id=1, source_target_pairs={{0,1},{1,0},{2,3},{3,2},{4,5},{5,4},{6,7},{7,6},{8,9},{9,8},{10,11... | collective-permute-start | bytes 2506760 | tf_op jit(solution)/shard_map/ppermute | solution.py:19
  (12 other events, 21.1 us)

commit v2 on v1

--- a/solution.py
+++ b/solution.py
@@ -141,7 +141,7 @@
         out_specs=vmem(),
         scratch_shapes=[pltpu.SemaphoreType.DMA((3,))],
         compiler_params=params(4),
-        cost_estimate=cost(3),
+        cost_estimate=cost(0.05),
         name="take_weights",
     )(sel, w_proj)
 
@@ -160,7 +160,7 @@
         in_specs=[smem(), vmem()],
         out_specs=vmem(),
         compiler_params=params(4),
-        cost_estimate=cost(2),
+        cost_estimate=cost(0.05),
         name="widen_cot",
     )(sel, cot)
 
@@ -180,7 +180,7 @@
         in_specs=[smem(), vmem(), vmem()],
         out_specs=vmem(),
         compiler_params=params(4),
-        cost_estimate=cost(2),
+        cost_estimate=cost(0.05),
         name="pack_cot",
     )(sel, cot, sibling)
 
@@ -252,7 +252,7 @@
         in_specs=[smem()] * 2 + [vmem()] * 9,
         out_specs=(vmem(),) * 5,
         compiler_params=params(16),
-        cost_estimate=cost(10),
+        cost_estimate=cost(0.05),
         name="near_blocks",
     )(sel, offsets, *toks, w_mine, *vectors)
 
@@ -293,7 +293,7 @@
         in_specs=[smem()] + [vmem()] * 13,
         out_specs=(vmem(),) * 6,
         compiler_params=params(20),
-        cost_estimate=cost(20),
+        cost_estimate=cost(0.05),
         name="forward_scan",
     )(sel, *toks, *near, w_mine, *vectors)
 
@@ -434,7 +434,7 @@
         out_specs=(vmem(),) * (4 + len(rows)),
         scratch_shapes=[pltpu.VMEM((length, cols), F32)] * 5,
         compiler_params=params(24),
-        cost_estimate=cost(20),
+        cost_estimate=cost(0.05),
         name="backward_scan",
     )(sel, *toks, *cots, *scanned, half_keep, *gates[:2], *normed)
 
@@ -580,58 +580,43 @@
     return jnp.concatenate([small[0:rows, : 3 * cols]] + last, axis=0)
 
 
-def finish_kernel(keep_ref, got_ref, a1_ref, a3_ref, small_mine, small_got, total_ref):
+def finish_kernel(keep_ref, got_ref, a1_ref, a3_ref, small_ref, total_ref):
     part = keep_ref.shape[0]
     total_ref[0:part, :] = keep_ref[...] + got_ref[...] + a1_ref[...] + a3_ref[...]
-    total_ref[part:, :] = fold_small(small_mine[...] + small_got[...])
-
-
-def finish(keep, got, a1, a3, small_mine, small_got):
+    total_ref[part:, :] = fold_small(small_ref[...])
+
+
+def finish(keep, got, a1, a3, small):
     part, cols3 = keep.shape
     return pl.pallas_call(
         finish_kernel,
         out_shape=shaped((part + 8, cols3)),
-        in_specs=[vmem()] * 6,
+        in_specs=[vmem()] * 5,
         out_specs=vmem(),
         compiler_params=params(8),
         cost_estimate=cost(0.05),
         name="finish",
-    )(keep, got, a1, a3, small_mine, small_got)
-
-
-def first_kernel(a_ref, first_ref):
-    first_ref[...] = a_ref[0 : first_ref.shape[0], :]
-
-
-def first_half(a):
-    return pl.pallas_call(
-        first_kernel,
-        out_shape=shaped((a.shape[0] // 2, a.shape[1])),
-        in_specs=[vmem()],
+    )(keep, got, a1, a3, small)
+
+
+def stack_kernel(*refs, rows):
+    at = 0
+    for ref, (first, count) in zip(refs, rows):
+        refs[-1][at : at + count, :] = ref[first : first + count, :]
+        at += count
+
+
+def stack(*parts):
+    rows = tuple((first, count) for _, first, count in parts)
+    return pl.pallas_call(
+        functools.partial(stack_kernel, rows=rows),
+        out_shape=shaped((sum(count for _, count in rows), parts[0][0].shape[1])),
+        in_specs=[vmem()] * len(parts),
         out_specs=vmem(),
         compiler_params=params(6),
         cost_estimate=cost(0.05),
-        name="first_half",
-    )(a)
-
-
-def pair_kernel(a_ref, b_ref, pair_ref):
-    rows = a_ref.shape[0]
-    pair_ref[0:rows, :] = a_ref[...]
-    pair_ref[rows:, :] = b_ref[...]
-
-
-def pair(a, b):
-    rows, cols3 = a.shape
-    return pl.pallas_call(
-        pair_kernel,
-        out_shape=shaped((2 * rows, cols3)),
-        in_specs=[vmem()] * 2,
-        out_specs=vmem(),
-        compiler_params=params(6),
-        cost_estimate=cost(0.05),
-        name="pair",
-    )(a, b)
+        name="stack",
+    )(*(array for array, _, _ in parts))
 
 
 def small_kernel(*refs, where):
@@ -670,13 +655,13 @@
         copies.append(pltpu.make_async_copy(src, dst, sem.at[len(copies)]))
         copies[-1].start()
 
-    for at, (array, first, row, x_off, c_off) in enumerate(where):
-        piece = refs[array].at[pl.ds(first, part)]
-        to_row = pl.multiple_of(row_part(sel, row) * part, part)
+    for at, (array, first, rows, row, row_off, x_off, c_off) in enumerate(where):
+        piece = refs[array].at[pl.ds(first, rows)]
+        to_row = pl.multiple_of(row_part(sel, row) * part + row_off, 8)
         col = (2 * (sel[0] ^ x_off) + (sel[1] ^ c_off)) * cols
         for k in range(3):
             to = pl.multiple_of(col + k * width, cols)
-            copy(piece.at[:, pl.ds(k * cols, cols)], target.at[pl.ds(to_row, part), pl.ds(to, cols)])
+            copy(piece.at[:, pl.ds(k * cols, cols)], target.at[pl.ds(to_row, rows), pl.ds(to, cols)])
         if at < give:
             copy(piece, refs[-2].at[pl.ds(at * part, part)])
     for c in copies:
@@ -704,8 +689,11 @@
     )(sel, *arrays, *extra, *waits)
 
 
-def given(array, where, part):
-    return [(array, i * part, row, x_off, 1) for i, (_, _, row, x_off, _) in enumerate(where)]
+def given(array, where):
+    return [
+        (array, i * rows, rows, row, row_off, x_off, 1)
+        for i, (_, _, rows, row, row_off, x_off, _) in enumerate(where)
+    ]
 
 
 def on_device(
@@ -761,19 +749,17 @@
 
     if tuned:
         r2, r3, r1, r0 = (swap(piece, "y") for piece in (s2, s3, s1, s0))
-        q2 = add(k2, r2, s0)
+        grad_mine, grad_send = input_side()
+        q2 = add(k2, r2, s0, grad_send)
         a2 = xor_permute(q2, "z", 1)
-        grad_mine, grad_send = input_side(q2)
         h3 = add(add(k3, r3), a2)
         a3 = xor_permute(h3, "z", 3)
         kept, sent, small = combine(
-            sel, grad_mine, swap(grad_send, "c"), h3, tick(grad_send)
+            sel, grad_mine, swap(grad_send, "c"), q2, tick(grad_send)
         )
-        small_got = swap(small, "x")
-        (sent,) = hold((sent,), small_got)
         got = swap(sent, "x")
         a1 = xor_permute(add(k1, r1, sent), "z", 1)
-        total = finish(k0, r0, a1, a3, small, small_got)
+        total = finish(k0, r0, a1, a3, small)
         output, input_grad = join(sel, kept, got)
 
         z3, px0, py0 = xor_permute(total, "z", 3), swap(total, "x"), swap(total, "y")
@@ -781,17 +767,26 @@
         (px0,) = hold((px0,), input_grad)
         corner0 = swap(px0, "y")
         z3, z1, corner0, py0 = hold((z3, z1, corner0, py0))
-        z13 = pair(z1, z3)
+        full = part + 8
+        z13 = stack((z1, 0, full), (z3, 0, full))
         z2, px13, py13 = xor_permute(z3, "z", 1), swap(z13, "x"), swap(z13, "y")
         corner3 = xor_permute(corner0, "z", 3)
-        own = [(0, 0, (0, 0), 0, 0), (1, 0, (0, 0), 1, 0), (2, 0, (0, 1), 0, 0), (3, 0, (0, 1), 1, 0)]
+        own = [
+            (0, 0, part, (0, 0), 0, 0, 0),
+            (1, 0, part, (0, 0), 0, 1, 0),
+            (2, 0, part, (0, 1), 0, 0, 0),
+            (3, 0, part, (0, 1), 0, 1, 0),
+        ]
         proj_grad, give = place(sel, (total, px0, py0, corner0), own, None, width, 4)
         z2, px13, py13, corner3 = hold((z2, px13, py13, corner3), give)
-        px2, py2 = swap(z2, "x"), swap(z2, "y")
-        corner12 = xor_permute(pair(corner0, corner3), "z", 1)
-        other = given(3, own, part)
+        third = 3 * part // 8
+        rest = full - 2 * third
+        px2 = swap(stack((z2, 0, full), (py13, 0, third)), "x")
+        py2 = swap(stack((z2, 0, full), (px13, third, third)), "y")
+        corner12 = xor_permute(stack((corner3, 0, full), (corner0, 2 * third, rest)), "z", 1)
+        other = given(3, own)
         own = [
-            (array, (part + 8) * i, (d, y_off), x_off, 0)
+            (array, full * i, part, (d, y_off), 0, x_off, 0)
             for array, y_off, x_off in ((0, 0, 0), (1, 0, 1), (2, 1, 0))
             for i, d in ((0, 1), (1, 3))
         ]
@@ -804,28 +799,31 @@
             6,
             tick(give),
         )
-        other = given(2, own, part)
-        own = [(0, 0, (2, 0), 0, 0), (1, 0, (3, 1), 1, 0)]
-        proj_grad, give = place(
-            sel, (z2, corner3, swap(give, "c")), own + other, proj_grad, width, 2, tick(give)
-        )
+        other = given(3, own)
+        first_give, wait = swap(give, "c"), tick(give)
+        own = [(0, 0, part, (2, 0), 0, 0, 0), (1, 0, part, (3, 1), 0, 1, 0)]
+        proj_grad, give = place(sel, (z2, corner3), own, proj_grad, width, 2)
+        other += given(4, own)
         px2, py2, corner12 = hold((px2, py2, corner12), give)
-        other = given(0, own, part)
-        arrays, places = [swap(give, "c")], []
-        last = (
-            (px2, (((2, 0), 1),)),
-            (py2, (((2, 1), 0),)),
-            (corner12, (((1, 1), 1), ((2, 1), 1))),
-        )
-        for piece, parts in last:
-            for held, c_off in ((piece, 0), (swap(piece, "c"), 1)):
-                for i, (row, x_off) in enumerate(parts):
-                    places.append((len(arrays), (part + 8) * i, row, x_off, c_off))
-                arrays.append(held)
-        (proj_grad,) = place(sel, arrays, other + places, proj_grad, width, 0, tick(give))
-        tail = part + 8 + part
-        where = [(0, part), (1, part), (2, part), (3, part), (4, part), (5, part), (2, tail), (3, tail)]
-        small = small_sums((total, py0, z13, py13, z2, py2), where)
+        own = [
+            (0, 0, part, (2, 0), 0, 1, 0),
+            (0, full, third, (1, 1), 0, 1, 0),
+            (1, 0, part, (2, 1), 0, 0, 0),
+            (1, full, third, (1, 1), third, 1, 0),
+            (2, 0, part, (2, 1), 0, 1, 0),
+            (2, full, rest - 8, (1, 1), 2 * third, 1, 0),
+        ]
+        arrays = (px2, py2, corner12, first_give, swap(give, "c"))
+        (proj_grad,) = place(sel, arrays, own + other, proj_grad, width, 0, wait, tick(give))
+        own = [(*place_of[:-1], 1) for place_of in own]
+        arrays = [swap(a, "c") for a in (px2, py2, corner12)]
+        (proj_grad,) = place(sel, arrays, own, proj_grad, width, 0)
+        where = [(0, part), (1, part), (2, part), (3, part)]
+        where += [(4, part), (5, part), (6, part), (9, full + rest - 8)]
+        where += [(8, part), (7, part), (10, part), (9, part)]
+        where += [(array, full + part) for array in (4, 5, 6)] + [(11, part)]
+        arrays = (total, px0, py0, corner0, z13, px13, py13, px2, z2, corner12, py2, corner3)
+        small = small_sums(arrays, where)
     else:
         grad_mine, grad_send = input_side()
         kept, sent, small = combine(sel, grad_mine, swap(grad_send, "c"))
@@ -835,9 +833,9 @@
         pieces = lax.psum(pieces, ("z", "y"))
         proj_grad = None
         for x_off, held in ((0, pieces), (1, swap(pieces, "x"))):
-            own = [(r, 0, r, x_off, 0) for r in range(8)]
+            own = [(r, 0, part, r, 0, x_off, 0) for r in range(8)]
             proj_grad, give = place(sel, list(held), own, proj_grad, width, 8)
-            other = given(0, own, part)
+            other = given(0, own)
             (proj_grad,) = place(sel, [swap(give, "c")], other, proj_grad, width, 0)
         output, input_grad = join(sel, kept, got)
     small = [small[i].reshape(width) for i in range(6)]

time: 167 us -> 148 us (0.89)
  waiting for transfers between devices: 89 us -> 66.1 us
  local copies, waits for them, and re-layouts: 2.09 us -> 4.79 us
    ppermute x25 -> x24, waiting for transfers between devices: 46 us -> 26.4 us  [swap(): return lax.ppermute(block, axis, SWAP)]
    ppermute x8, waiting for transfers between devices: 43 us -> 39.7 us  [xor_permute(): return lax.ppermute(block, axis, [(i, i ^ distance) for i in range(size)])]
    unnamed x22, local copies, waits for them, and re-layouts: 2.09 us -> 4.79 us
    ppermute x8, starting transfers between devices: 12.6 us -> 15 us  [xor_permute(): return lax.ppermute(block, axis, [(i, i ^ distance) for i in range(size)])]
    ppermute x25 -> x24, starting transfers between devices: 20.5 us -> 18.2 us  [swap(): return lax.ppermute(block, axis, SWAP)]
    pallas_call x4 -> x5, Pallas kernels: 10.5 us -> 11.7 us  [place(): pl.pallas_call(functools.partial(place_kernel, where=where, give=give), o...]
  transfers between devices with their start and end apart: 33 -> 32, of which waited for: 24 -> 18; matrix products, arithmetic and copies ran while one was open for 0% -> 0% of each run, Pallas kernels for 18% -> 24%
where the time goes in v2:
time: 148 us
  waiting for transfers between devices  66.1 us (45%)
  Pallas kernels  41.8 us (28%)
  starting transfers between devices  33.2 us (22%)
  local copies, waits for them, and re-layouts  4.79 us (3%)
    ppermute x8, waiting for transfers between devices, xor_permute(): return lax.ppermute(block, axis, [(i, i ^ distance) for i in range(size)])  39.7 us
    ppermute x24, waiting for transfers between devices, swap(): return lax.ppermute(block, axis, SWAP)  26.4 us
    ppermute x24, starting transfers between devices, swap(): return lax.ppermute(block, axis, SWAP)  18.2 us
    ppermute x8, starting transfers between devices, xor_permute(): return lax.ppermute(block, axis, [(i, i ^ distance) for i in range(size)])  15 us
    pallas_call x5, Pallas kernels, place(): pl.pallas_call(functools.partial(place_kernel, where=where, give=give), o...  11.7 us
    pallas_call x1, Pallas kernels, run_forward(): pl.pallas_call(forward_kernel, out_shape=(shaped((2 * block, width), BF16...  8.79 us
    pallas_call x1, Pallas kernels, run_input(): pl.pallas_call(input_kernel, out_shape=(shaped(shape), shaped(shape)), in...  5.94 us
    pallas_call x1, Pallas kernels, run_backward(): pl.pallas_call(functools.partial(backward_kernel, rows=rows), out_shape=(...  4.93 us
  transfers between devices with their start and end apart: 32, of which 18 were waited for; matrix products, arithmetic and copies ran while one was open for 0% of the time, Pallas kernels for 24%

profile of v2, /device:TPU:0, one launch (start us, length us, event | category | flops | bytes accessed | tf_op | source)
XLA Modules:
  0.0 148.1 jit_solution(2945999837390026965)
XLA Ops:
  2.2 2.6 %collective-permute-start.1 = (f32[176,1024]{1,0:T(8,128)S(1)}, f32[176,1024]{1,0:T(8,128)S(1)}, u32[]{:S(2)}, u32[]{:S(2)}) collective-permute-start(f32[176,1024]{1,0:T(8,128)S(1)} %bitcast_convert_fusion.tok0.x0), channel_id=1, source_target_pairs={{0,2},{2,0},{1,3},{3,1},{4,6},{6,4},{5,7},{7,5},{8,10},{10,8},{9,1... | collective-permute-start | bytes 2162696 | tf_op jit(solution)/shard_map/ppermute | solution.py:19
  6.7 2.8 %copy-done = bf16[1024,3072]{1,0:T(8,128)(2,1)S(1)} copy-done((bf16[1024,3072]{1,0:T(8,128)(2,1)S(1)}, bf16[1024,3072]{1,0:T(8,128)(2,1)}, u32[]{:S(2)}) %copy-start) | copy-done | bytes 6291480
  11.0 2.2 %near_blocks.1 = (bf16[352,1024]{1,0:T(8,128)(2,1)S(1)}, f32[352,256]{1,0:T(8,128)S(1)}, f32[352,256]{1,0:T(8,128)S(1)}, f32[352,256]{1,0:T(8,128)S(1)}, f32[704,256]{1,0:T(8,128)S(1)}) custom-call(s32[4]{0:T(128)S(1)} %pad_add_fusion.sel, s32[1,8]{1,0:T(1,128)S(1)} %copy-done.10, f32[176,1024]{1,0:T(8,128)S(1)} %bitcast_convert_fusion.tok0.x0, ...), custom_call_target="tpu_custom_call" | custom-call | flops 55000000 | bytes 180000 | tf_op jit(solution)/shard_map/near_blocks/pallas_call | solution.py:247
  13.2 8.4 %collective-permute-done.1.refs_0_ = f32[176,1024]{1,0:T(8,128)S(1)} collective-permute-done((f32[176,1024]{1,0:T(8,128)S(1)}, f32[176,1024]{1,0:T(8,128)S(1)}, u32[]{:S(2)}, u32[]{:S(2)}) %collective-permute-start.1) | collective-permute-done | bytes 720928 | tf_op jit(solution)/shard_map/ppermute | solution.py:19
  21.5 1.8 %collective-permute-start.4 = (f32[352,256]{1,0:T(8,128)S(1)}, f32[352,256]{1,0:T(8,128)S(1)}, u32[]{:S(2)}, u32[]{:S(2)}) collective-permute-start(f32[352,256]{1,0:T(8,128)S(1)} %pack_cot.1.refs_2_), channel_id=1, source_target_pairs={{0,2},{2,0},{1,3},{3,1},{4,6},{6,4},{5,7},{7,5},{8,10},{10,8},{9,1... | collective-permute-start | bytes 1081352 | tf_op jit(solution)/shard_map/ppermute | solution.py:19
  23.7 8.8 %forward_scan.1 = (bf16[352,1024]{1,0:T(8,128)(2,1)S(1)}, f32[704,256]{1,0:T(8,128)S(1)}, f32[704,256]{1,0:T(8,128)S(1)}, f32[704,256]{1,0:T(8,128)S(1)}, f32[70...) custom-call(s32[4]{0:T(128)S(1)} %pad_add_fusion.sel, f32[176,1024]{1,0:T(8,128)S(1)} %hold.5.tok0.x2.tok2, ...), custom_call_target="tpu_custom_call" | custom-call | flops 55000000 | bytes 180000 | tf_op jit(solution)/shard_map/forward_scan/pallas_call | solution.py:290
  32.5 4.9 %backward_scan.1 = (bf16[704,768]{1,0:T(8,128)(2,1)S(1)}, f32[704,256]{1,0:T(8,128)S(1)}, f32[704,256]{1,0:T(8,128)S(1)}, f32[8,256]{1,0:T(8,128)S(1)}, f32[128,768]{1,0:T(8,128)S(1)}) custom-call(s32[4]{0:T(128)S(1)} %pad_add_fusion.sel, f32[176,1024]{1,0:T(8,128)S(1)} %bitcast_convert_fusion.tok0.x0, f32[176,1024]{1,0:T(8,128)S(1)} %collective-permute-done.tok1.x1, ...), custom_call_target="tpu_custom_call" | custom-call | flops 55000000 | bytes 180000 | tf_op jit(solution)/shard_map/backward_scan/pallas_call | solution.py:424
  37.5 1.8 %collective-permute-start.6 = (f32[128,768]{1,0:T(8,128)S(1)}, f32[128,768]{1,0:T(8,128)S(1)}, u32[]{:S(2)}, u32[]{:S(2)}) collective-permute-start(f32[128,768]{1,0:T(8,128)S(1)} %get-tuple-element.80), channel_id=1, source_target_pairs={{0,4},{4,0},{1,5},{5,1},{2,6},{6,2},{3,7},{7,3},{8,12},{12,8},{9,1... | collective-permute-start | bytes 1179656 | tf_op jit(solution)/shard_map/ppermute | solution.py:19
  41.0 5.9 %input_side.1 = (f32[360,1280]{1,0:T(8,128)S(1)}, f32[360,1280]{1,0:T(8,128)S(1)}) custom-call(s32[4]{0:T(128)S(1)} %pad_add_fusion.sel, f32[176,1024]{1,0:T(8,128)S(1)} %bitcast_convert_fusion.tok0.x0, f32[176,1024]{1,0:T(8,128)S(1)} %collective-permute-done.tok1.x1, f32[176,1024]{1,0:T(8,128)S(1)} %hold.5.tok0.x2.tok2, ...), custom_call_target="tpu_custom_call" | custom-call | flops 55000000 | bytes 180000 | tf_op jit(solution)/shard_map/input_side/pallas_call | solution.py:514
  47.0 1.9 %collective-permute-start.9 = (f32[128,768]{1,0:T(8,128)S(1)}, f32[128,768]{1,0:T(8,128)S(1)}, u32[]{:S(2)}, u32[]{:S(2)}) collective-permute-start(f32[128,768]{1,0:T(8,128)S(1)} %get-tuple-element.88), channel_id=1, source_target_pairs={{0,4},{4,0},{1,5},{5,1},{2,6},{6,2},{3,7},{7,3},{8,12},{12,8},{9,1... | collective-permute-start | bytes 1179656 | tf_op jit(solution)/shard_map/ppermute | solution.py:19
  50.5 1.7 %collective-permute-start.12 = (f32[128,768]{1,0:T(8,128)S(1)}, f32[128,768]{1,0:T(8,128)S(1)}, u32[]{:S(2)}, u32[]{:S(2)}) collective-permute-start(f32[128,768]{1,0:T(8,128)S(1)} %add.10.refs_0_), channel_id=1, source_target_pairs={{0,8},{8,0},{16,24},{24,16},{1,9},{9,1},{17,25},{25,17},{2,10},{10... | collective-permute-start | bytes 1179656 | tf_op jit(solution)/shard_map/ppermute | solution.py:24
  55.4 2.6 %collective-permute-done.11.b_ref = f32[128,768]{1,0:T(8,128)S(1)} collective-permute-done((f32[128,768]{1,0:T(8,128)S(1)}, f32[128,768]{1,0:T(8,128)S(1)}, u32[]{:S(2)}, u32[]{:S(2)}) %collective-permute-start.11) | collective-permute-done | bytes 393248 | tf_op jit(solution)/shard_map/ppermute | solution.py:19
  58.0 3.8 %collective-permute-done.12.b_ref = f32[128,768]{1,0:T(8,128)S(1)} collective-permute-done((f32[128,768]{1,0:T(8,128)S(1)}, f32[128,768]{1,0:T(8,128)S(1)}, u32[]{:S(2)}, u32[]{:S(2)}) %collective-permute-start.12) | collective-permute-done | bytes 393248 | tf_op jit(solution)/shard_map/ppermute | solution.py:24
  61.8 3.7 %collective-permute-start.13 = (f32[128,768]{1,0:T(8,128)S(1)}, f32[128,768]{1,0:T(8,128)S(1)}, u32[]{:S(2)}, u32[]{:S(2)}) collective-permute-start(f32[128,768]{1,0:T(8,128)S(1)} %add.13), channel_id=1, source_target_pairs={{0,24},{8,16},{16,8},{24,0},{1,25},{9,17},{17,9},{25,1},{2,26},{10... | collective-permute-start | bytes 1179656 | tf_op jit(solution)/shard_map/ppermute | solution.py:24
  66.4 1.9 %collective-permute-start.10 = (f32[128,768]{1,0:T(8,128)S(1)}, f32[128,768]{1,0:T(8,128)S(1)}, u32[]{:S(2)}, u32[]{:S(2)}) collective-permute-start(f32[128,768]{1,0:T(8,128)S(1)} %add.11), channel_id=1, source_target_pairs={{0,8},{8,0},{16,24},{24,16},{1,9},{9,1},{17,25},{25,17},{2,10},{10... | collective-permute-start | bytes 1179656 | tf_op jit(solution)/shard_map/ppermute | solution.py:24
  68.3 5.7 %collective-permute-done.8.got_ref = f32[128,768]{1,0:T(8,128)S(1)} collective-permute-done((f32[128,768]{1,0:T(8,128)S(1)}, f32[128,768]{1,0:T(8,128)S(1)}, u32[]{:S(2)}, u32[]{:S(2)}) %collective-permute-start.8) | collective-permute-done | bytes 393248 | tf_op jit(solution)/shard_map/ppermute | solution.py:19
  74.0 1.8 %collective-permute-done.13.a3_ref = f32[128,768]{1,0:T(8,128)S(1)} collective-permute-done((f32[128,768]{1,0:T(8,128)S(1)}, f32[128,768]{1,0:T(8,128)S(1)}, u32[]{:S(2)}, u32[]{:S(2)}) %collective-permute-start.13) | collective-permute-done | bytes 393248 | tf_op jit(solution)/shard_map/ppermute | solution.py:24
  75.8 6.8 %collective-permute-done.10.a1_ref = f32[128,768]{1,0:T(8,128)S(1)} collective-permute-done((f32[128,768]{1,0:T(8,128)S(1)}, f32[128,768]{1,0:T(8,128)S(1)}, u32[]{:S(2)}, u32[]{:S(2)}) %collective-permute-start.10) | collective-permute-done | bytes 393248 | tf_op jit(solution)/shard_map/ppermute | solution.py:24
  84.3 3.5 %collective-permute-start.14 = (f32[136,768]{1,0:T(8,128)S(1)}, f32[136,768]{1,0:T(8,128)S(1)}, u32[]{:S(2)}, u32[]{:S(2)}) collective-permute-start(f32[136,768]{1,0:T(8,128)S(1)} %finish.1.refs_0_), channel_id=1, source_target_pairs={{0,24},{8,16},{16,8},{24,0},{1,25},{9,17},{17,9},{25,1},{2,26},{10... | collective-permute-start | bytes 1253384 | tf_op jit(solution)/shard_map/ppermute | solution.py:24
  89.5 4.9 %collective-permute-done.16.refs_0_ = f32[136,768]{1,0:T(8,128)S(1)} collective-permute-done((f32[136,768]{1,0:T(8,128)S(1)}, f32[136,768]{1,0:T(8,128)S(1)}, u32[]{:S(2)}, u32[]{:S(2)}) %collective-permute-start.16) | collective-permute-done | bytes 417824 | tf_op jit(solution)/shard_map/ppermute | solution.py:19
  95.5 3.2 %collective-permute-done.14.refs_0_ = f32[136,768]{1,0:T(8,128)S(1)} collective-permute-done((f32[136,768]{1,0:T(8,128)S(1)}, f32[136,768]{1,0:T(8,128)S(1)}, u32[]{:S(2)}, u32[]{:S(2)}) %collective-permute-start.14) | collective-permute-done | bytes 417824 | tf_op jit(solution)/shard_map/ppermute | solution.py:24
  98.7 7.7 %collective-permute-done.15.refs_1_ = f32[136,768]{1,0:T(8,128)S(1)} collective-permute-done((f32[136,768]{1,0:T(8,128)S(1)}, f32[136,768]{1,0:T(8,128)S(1)}, u32[]{:S(2)}, u32[]{:S(2)}) %collective-permute-start.15) | collective-permute-done | bytes 417824 | tf_op jit(solution)/shard_map/ppermute | solution.py:24
  108.7 1.7 %collective-permute-start.19 = (f32[136,768]{1,0:T(8,128)S(1)}, f32[136,768]{1,0:T(8,128)S(1)}, u32[]{:S(2)}, u32[]{:S(2)}) collective-permute-start(f32[136,768]{1,0:T(8,128)S(1)} %get-tuple-element.92.refs_1_), channel_id=1, source_target_pairs={{0,8},{8,0},{16,24},{24,16},{1,9},{9,1},{17,25},{25,17},{2,10},{10... | collective-permute-start | bytes 1253384 | tf_op jit(solution)/shard_map/ppermute | solution.py:24
  111.5 2.0 %place.5 = (f32[1024,3072]{1,0:T(8,128)}, f32[512,768]{1,0:T(8,128)S(1)}) custom-call(s32[4]{0:T(128)S(1)} %pad_add_fusion.sel, f32[136,768]{1,0:T(8,128)S(1)} %finish.1.refs_0_, f32[136,768]{1,0:T(8,128)S(1)} %hold.6.refs_1_, f32[136,768]{1,0:T(8,128)S(1)} %get-tuple-element.95.refs_2_, f32[136,768]{1,0:T(8,128)S(1)} %get-tuple-element.94.refs_3_.refs_1_), custom_call_target="tpu_custom_call" | custom-call | flops 55000000 | bytes 180000 | tf_op jit(solution)/shard_map/place/pallas_call | solution.py:675
  113.6 7.9 %collective-permute-done.19.refs_0_ = f32[136,768]{1,0:T(8,128)S(1)} collective-permute-done((f32[136,768]{1,0:T(8,128)S(1)}, f32[136,768]{1,0:T(8,128)S(1)}, u32[]{:S(2)}, u32[]{:S(2)}) %collective-permute-start.19) | collective-permute-done | bytes 417824 | tf_op jit(solution)/shard_map/ppermute | solution.py:24
  121.5 6.7 %collective-permute-done.22.refs_3_ = f32[136,768]{1,0:T(8,128)S(1)} collective-permute-done((f32[136,768]{1,0:T(8,128)S(1)}, f32[136,768]{1,0:T(8,128)S(1)}, u32[]{:S(2)}, u32[]{:S(2)}) %collective-permute-start.22) | collective-permute-done | bytes 417824 | tf_op jit(solution)/shard_map/ppermute | solution.py:24
  129.7 1.7 %collective-permute-start.24 = (f32[184,768]{1,0:T(8,128)S(1)}, f32[184,768]{1,0:T(8,128)S(1)}, u32[]{:S(2)}, u32[]{:S(2)}) collective-permute-start(f32[184,768]{1,0:T(8,128)S(1)} %stack.26), channel_id=1, source_target_pairs={{0,4},{4,0},{1,5},{5,1},{2,6},{6,2},{3,7},{7,3},{8,12},{12,8},{9,1... | collective-permute-start | bytes 1695752 | tf_op jit(solution)/shard_map/ppermute | solution.py:19
  132.6 3.2 %place.6 = (f32[1024,3072]{1,0:T(8,128)}, f32[768,768]{1,0:T(8,128)S(1)}) custom-call(s32[4]{0:T(128)S(1)} %pad_add_fusion.sel, f32[272,768]{1,0:T(8,128)S(1)} %stack.24.refs_0_.refs_4_, f32[272,768]{1,0:T(8,128)S(1)} %get-tuple-element.99.refs_1_.refs_5_, f32[272,768]{1,0:T(8,128)S(1)} %get-tuple-element.98.refs_1_.refs_2_.refs_6_, ...), custom_call_target="tpu_custom_call", output_to_operand_aliasing={{0}: (5, {})} | custom-call | flops 55000000 | bytes 180000 | tf_op jit(solution)/shard_map/place/pallas_call | solution.py:675
  135.8 1.6 %place.7 = (f32[1024,3072]{1,0:T(8,128)}, f32[256,768]{1,0:T(8,128)S(1)}) custom-call(s32[4]{0:T(128)S(1)} %pad_add_fusion.sel, f32[136,768]{1,0:T(8,128)S(1)} %get-tuple-element.97.refs_0_.refs_8_, f32[136,768]{1,0:T(8,128)S(1)} %get-tuple-element.100.refs_0_.refs_1_.refs_11_, f32[1024,3072]{1,0:T(8,128)} %get-tuple-element.102.refs_2_), custom_call_target="tpu_custom_call", output_to_operand_aliasing={{0}: (3, {})} | custom-call | flops 55000000 | bytes 180000 | tf_op jit(solution)/shard_map/place/pallas_call | solution.py:675
  138.0 1.8 %collective-permute-done.25.refs_2_ = f32[176,768]{1,0:T(8,128)S(1)} collective-permute-done((f32[176,768]{1,0:T(8,128)S(1)}, f32[176,768]{1,0:T(8,128)S(1)}, u32[]{:S(2)}, u32[]{:S(2)}) %collective-permute-start.25) | collective-permute-done | bytes 540704 | tf_op jit(solution)/shard_map/ppermute | solution.py:24
  143.1 3.1 %place.8.refs_3_ = f32[1024,3072]{1,0:T(8,128)} custom-call(s32[4]{0:T(128)S(1)} %pad_add_fusion.sel, f32[184,768]{1,0:T(8,128)S(1)} %get-tuple-element.104.refs_0_.refs_7_, f32[184,768]{1,0:T(8,128)S(1)} %get-tuple-element.105.refs_1_.refs_10_, f32[176,768]{1,0:T(8,128)S(1)} %get-tuple-element.106.refs_2_.refs_9_, ...), custom_call_target="tpu_custom_call", output_to_operand_aliasing={{}: (6, {})} | custom-call | flops 55000000 | bytes 180000 | tf_op jit(solution)/shard_map/place/pallas_call | solution.py:675
  146.2 1.8 %place.9 = f32[1024,3072]{1,0:T(8,128)} custom-call(s32[4]{0:T(128)S(1)} %pad_add_fusion.sel, f32[184,768]{1,0:T(8,128)S(1)} %collective-permute-done.27.refs_0_, f32[184,768]{1,0:T(8,128)S(1)} %collective-permute-done.28.refs_1_, f32[176,768]{1,0:T(8,128)S(1)} %collective-permute-done.29.refs_2_, ...), custom_call_target="tpu_custom_call", output_to_operand_aliasing={{}: (4, {})} | custom-call | flops 55000000 | bytes 180000 | tf_op jit(solution)/shard_map/place/pallas_call | solution.py:675
  (91 shorter events, 27.3 us)
Async XLA Ops:
  1.7 9.2 %collective-permute-start = (f32[176,1024]{1,0:T(8,128)S(1)}, f32[176,1024]{1,0:T(8,128)S(1)}, u32[]{:S(2)}, u32[]{:S(2)}) collective-permute-start(f32[176,1024]{1,0:T(8,128)S(1)} %bitcast_convert_fusion.tok0.x0), channel_id=1, source_target_pairs={{0,1},{1,0},{2,3},{3,2},{4,5},{5,4},{6,7},{7,6},{8,9},{9,8},{10,11... | collective-permute-start | bytes 2162696 | tf_op jit(solution)/shard_map/ppermute | solution.py:19
  2.2 19.3 %collective-permute-start.1 = (f32[176,1024]{1,0:T(8,128)S(1)}, f32[176,1024]{1,0:T(8,128)S(1)}, u32[]{:S(2)}, u32[]{:S(2)}) collective-permute-start(f32[176,1024]{1,0:T(8,128)S(1)} %bitcast_convert_fusion.tok0.x0), channel_id=1, source_target_pairs={{0,2},{2,0},{1,3},{3,1},{4,6},{6,4},{5,7},{7,5},{8,10},{10,8},{9,1... | collective-permute-start | bytes 2162696 | tf_op jit(solution)/shard_map/ppermute | solution.py:19
  6.4 3.9 %collective-permute-start.2 = (f32[176,512]{1,0:T(8,128)S(1)}, f32[176,512]{1,0:T(8,128)S(1)}, u32[]{:S(2)}, u32[]{:S(2)}) collective-permute-start(f32[176,512]{1,0:T(8,128)S(1)} %widen_cot.1), channel_id=1, source_target_pairs={{0,1},{1,0},{2,3},{3,2},{4,5},{5,4},{6,7},{7,6},{8,9},{9,8},{10,11... | collective-permute-start | bytes 1081352 | tf_op jit(solution)/shard_map/ppermute | solution.py:19
  21.5 2.2 %collective-permute-start.3 = (f32[176,1024]{1,0:T(8,128)S(1)}, f32[176,1024]{1,0:T(8,128)S(1)}, u32[]{:S(2)}, u32[]{:S(2)}) collective-permute-start(f32[176,1024]{1,0:T(8,128)S(1)} %hold.5.tok0.x2.tok2), channel_id=1, source_target_pairs={{0,1},{1,0},{2,3},{3,2},{4,5},{5,4},{6,7},{7,6},{8,9},{9,8},{10,11... | collective-permute-start | bytes 2162696 | tf_op jit(solution)/shard_map/ppermute | solution.py:19
  21.5 11.0 %collective-permute-start.4 = (f32[352,256]{1,0:T(8,128)S(1)}, f32[352,256]{1,0:T(8,128)S(1)}, u32[]{:S(2)}, u32[]{:S(2)}) collective-permute-start(f32[352,256]{1,0:T(8,128)S(1)} %pack_cot.1.refs_2_), channel_id=1, source_target_pairs={{0,2},{2,0},{1,3},{3,1},{4,6},{6,4},{5,7},{7,5},{8,10},{10,8},{9,1... | collective-permute-start | bytes 1081352 | tf_op jit(solution)/shard_map/ppermute | solution.py:19
  37.5 13.0 %collective-permute-start.6 = (f32[128,768]{1,0:T(8,128)S(1)}, f32[128,768]{1,0:T(8,128)S(1)}, u32[]{:S(2)}, u32[]{:S(2)}) collective-permute-start(f32[128,768]{1,0:T(8,128)S(1)} %get-tuple-element.80), channel_id=1, source_target_pairs={{0,4},{4,0},{1,5},{5,1},{2,6},{6,2},{3,7},{7,3},{8,12},{12,8},{9,1... | collective-permute-start | bytes 1179656 | tf_op jit(solution)/shard_map/ppermute | solution.py:19
  40.7 17.2 %collective-permute-start.11 = (f32[128,768]{1,0:T(8,128)S(1)}, f32[128,768]{1,0:T(8,128)S(1)}, u32[]{:S(2)}, u32[]{:S(2)}) collective-permute-start(f32[128,768]{1,0:T(8,128)S(1)} %get-tuple-element.90), channel_id=1, source_target_pairs={{0,4},{4,0},{1,5},{5,1},{2,6},{6,2},{3,7},{7,3},{8,12},{12,8},{9,1... | collective-permute-start | bytes 1179656 | tf_op jit(solution)/shard_map/ppermute | solution.py:19
  46.9 5.2 %collective-permute-start.5 = (f32[360,1280]{1,0:T(8,128)S(1)}, f32[360,1280]{1,0:T(8,128)S(1)}, u32[]{:S(2)}, u32[]{:S(2)}) collective-permute-start(f32[360,1280]{1,0:T(8,128)S(1)} %get-tuple-element.78.refs_1_.refs_0_), channel_id=1, source_target_pairs={{0,1},{1,0},{2,3},{3,2},{4,5},{5,4},{6,7},{7,6},{8,9},{9,8},{10,11... | collective-permute-start | bytes 5529608 | tf_op jit(solution)/shard_map/ppermute | solution.py:19
  47.0 19.3 %collective-permute-start.9 = (f32[128,768]{1,0:T(8,128)S(1)}, f32[128,768]{1,0:T(8,128)S(1)}, u32[]{:S(2)}, u32[]{:S(2)}) collective-permute-start(f32[128,768]{1,0:T(8,128)S(1)} %get-tuple-element.88), channel_id=1, source_target_pairs={{0,4},{4,0},{1,5},{5,1},{2,6},{6,2},{3,7},{7,3},{8,12},{12,8},{9,1... | collective-permute-start | bytes 1179656 | tf_op jit(solution)/shard_map/ppermute | solution.py:19
  50.5 11.3 %collective-permute-start.12 = (f32[128,768]{1,0:T(8,128)S(1)}, f32[128,768]{1,0:T(8,128)S(1)}, u32[]{:S(2)}, u32[]{:S(2)}) collective-permute-start(f32[128,768]{1,0:T(8,128)S(1)} %add.10.refs_0_), channel_id=1, source_target_pairs={{0,8},{8,0},{16,24},{24,16},{1,9},{9,1},{17,25},{25,17},{2,10},{10... | collective-permute-start | bytes 1179656 | tf_op jit(solution)/shard_map/ppermute | solution.py:24
  53.0 35.0 %collective-permute-start.7 = (f32[176,1536]{1,0:T(8,128)S(1)}, f32[176,1536]{1,0:T(8,128)S(1)}, u32[]{:S(2)}, u32[]{:S(2)}) collective-permute-start(f32[176,1536]{1,0:T(8,128)S(1)} %get-tuple-element.83.refs_0_), channel_id=1, source_target_pairs={{0,2},{2,0},{1,3},{3,1},{4,6},{6,4},{5,7},{7,5},{8,10},{10,8},{9,1... | collective-permute-start | bytes 3244040 | tf_op jit(solution)/shard_map/ppermute | solution.py:19
  54.6 19.4 %collective-permute-start.8 = (f32[128,768]{1,0:T(8,128)S(1)}, f32[128,768]{1,0:T(8,128)S(1)}, u32[]{:S(2)}, u32[]{:S(2)}) collective-permute-start(f32[128,768]{1,0:T(8,128)S(1)} %get-tuple-element.81.refs_0_), channel_id=1, source_target_pairs={{0,4},{4,0},{1,5},{5,1},{2,6},{6,2},{3,7},{7,3},{8,12},{12,8},{9,1... | collective-permute-start | bytes 1179656 | tf_op jit(solution)/shard_map/ppermute | solution.py:19
  61.8 14.0 %collective-permute-start.13 = (f32[128,768]{1,0:T(8,128)S(1)}, f32[128,768]{1,0:T(8,128)S(1)}, u32[]{:S(2)}, u32[]{:S(2)}) collective-permute-start(f32[128,768]{1,0:T(8,128)S(1)} %add.13), channel_id=1, source_target_pairs={{0,24},{8,16},{16,8},{24,0},{1,25},{9,17},{17,9},{25,1},{2,26},{10... | collective-permute-start | bytes 1179656 | tf_op jit(solution)/shard_map/ppermute | solution.py:24
  66.4 16.2 %collective-permute-start.10 = (f32[128,768]{1,0:T(8,128)S(1)}, f32[128,768]{1,0:T(8,128)S(1)}, u32[]{:S(2)}, u32[]{:S(2)}) collective-permute-start(f32[128,768]{1,0:T(8,128)S(1)} %add.11), channel_id=1, source_target_pairs={{0,8},{8,0},{16,24},{24,16},{1,9},{9,1},{17,25},{25,17},{2,10},{10... | collective-permute-start | bytes 1179656 | tf_op jit(solution)/shard_map/ppermute | solution.py:24
  82.7 11.6 %collective-permute-start.16 = (f32[136,768]{1,0:T(8,128)S(1)}, f32[136,768]{1,0:T(8,128)S(1)}, u32[]{:S(2)}, u32[]{:S(2)}) collective-permute-start(f32[136,768]{1,0:T(8,128)S(1)} %finish.1.refs_0_), channel_id=1, source_target_pairs={{0,2},{2,0},{1,3},{3,1},{4,6},{6,4},{5,7},{7,5},{8,10},{10,8},{9,1... | collective-permute-start | bytes 1253384 | tf_op jit(solution)/shard_map/ppermute | solution.py:19
  84.3 14.4 %collective-permute-start.14 = (f32[136,768]{1,0:T(8,128)S(1)}, f32[136,768]{1,0:T(8,128)S(1)}, u32[]{:S(2)}, u32[]{:S(2)}) collective-permute-start(f32[136,768]{1,0:T(8,128)S(1)} %finish.1.refs_0_), channel_id=1, source_target_pairs={{0,24},{8,16},{16,8},{24,0},{1,25},{9,17},{17,9},{25,1},{2,26},{10... | collective-permute-start | bytes 1253384 | tf_op jit(solution)/shard_map/ppermute | solution.py:24
  87.8 18.6 %collective-permute-start.15 = (f32[136,768]{1,0:T(8,128)S(1)}, f32[136,768]{1,0:T(8,128)S(1)}, u32[]{:S(2)}, u32[]{:S(2)}) collective-permute-start(f32[136,768]{1,0:T(8,128)S(1)} %finish.1.refs_0_), channel_id=1, source_target_pairs={{0,8},{8,0},{16,24},{24,16},{1,9},{9,1},{17,25},{25,17},{2,10},{10... | collective-permute-start | bytes 1253384 | tf_op jit(solution)/shard_map/ppermute | solution.py:24
  87.8 18.6 %collective-permute-start.18 = (f32[136,768]{1,0:T(8,128)S(1)}, f32[136,768]{1,0:T(8,128)S(1)}, u32[]{:S(2)}, u32[]{:S(2)}) collective-permute-start(f32[136,768]{1,0:T(8,128)S(1)} %finish.1.refs_0_), channel_id=1, source_target_pairs={{0,4},{4,0},{1,5},{5,1},{2,6},{6,2},{3,7},{7,3},{8,12},{12,8},{9,1... | collective-permute-start | bytes 1253384 | tf_op jit(solution)/shard_map/ppermute | solution.py:19
  95.4 12.4 %collective-permute-start.17 = (f32[136,768]{1,0:T(8,128)S(1)}, f32[136,768]{1,0:T(8,128)S(1)}, u32[]{:S(2)}, u32[]{:S(2)}) collective-permute-start(f32[136,768]{1,0:T(8,128)S(1)} %hold.6.refs_1_), channel_id=1, source_target_pairs={{0,4},{4,0},{1,5},{5,1},{2,6},{6,2},{3,7},{7,3},{8,12},{12,8},{9,1... | collective-permute-start | bytes 1253384 | tf_op jit(solution)/shard_map/ppermute | solution.py:19
  107.8 20.4 %collective-permute-start.20 = (f32[272,768]{1,0:T(8,128)S(1)}, f32[272,768]{1,0:T(8,128)S(1)}, u32[]{:S(2)}, u32[]{:S(2)}) collective-permute-start(f32[272,768]{1,0:T(8,128)S(1)} %stack.24.refs_0_.refs_4_), channel_id=1, source_target_pairs={{0,2},{2,0},{1,3},{3,1},{4,6},{6,4},{5,7},{7,5},{8,10},{10,8},{9,1... | collective-permute-start | bytes 2506760 | tf_op jit(solution)/shard_map/ppermute | solution.py:19
  108.5 19.8 %collective-permute-start.21 = (f32[272,768]{1,0:T(8,128)S(1)}, f32[272,768]{1,0:T(8,128)S(1)}, u32[]{:S(2)}, u32[]{:S(2)}) collective-permute-start(f32[272,768]{1,0:T(8,128)S(1)} %stack.24.refs_0_.refs_4_), channel_id=1, source_target_pairs={{0,4},{4,0},{1,5},{5,1},{2,6},{6,2},{3,7},{7,3},{8,12},{12,8},{9,1... | collective-permute-start | bytes 2506760 | tf_op jit(solution)/shard_map/ppermute | solution.py:19
  108.7 12.8 %collective-permute-start.19 = (f32[136,768]{1,0:T(8,128)S(1)}, f32[136,768]{1,0:T(8,128)S(1)}, u32[]{:S(2)}, u32[]{:S(2)}) collective-permute-start(f32[136,768]{1,0:T(8,128)S(1)} %get-tuple-element.92.refs_1_), channel_id=1, source_target_pairs={{0,8},{8,0},{16,24},{24,16},{1,9},{9,1},{17,25},{25,17},{2,10},{10... | collective-permute-start | bytes 1253384 | tf_op jit(solution)/shard_map/ppermute | solution.py:24
  110.5 17.7 %collective-permute-start.22 = (f32[136,768]{1,0:T(8,128)S(1)}, f32[136,768]{1,0:T(8,128)S(1)}, u32[]{:S(2)}, u32[]{:S(2)}) collective-permute-start(f32[136,768]{1,0:T(8,128)S(1)} %get-tuple-element.94.refs_3_.refs_1_), channel_id=1, source_target_pairs={{0,24},{8,16},{16,8},{24,0},{1,25},{9,17},{17,9},{25,1},{2,26},{10... | collective-permute-start | bytes 1253384 | tf_op jit(solution)/shard_map/ppermute | solution.py:24
  113.5 19.1 %collective-permute-start.26 = (f32[512,768]{1,0:T(8,128)S(1)}, f32[512,768]{1,0:T(8,128)S(1)}, u32[]{:S(2)}, u32[]{:S(2)}) collective-permute-start(f32[512,768]{1,0:T(8,128)S(1)} %get-tuple-element.96.refs_4_.refs_0_), channel_id=1, source_target_pairs={{0,1},{1,0},{2,3},{3,2},{4,5},{5,4},{6,7},{7,6},{8,9},{9,8},{10,11... | collective-permute-start | bytes 4718600 | tf_op jit(solution)/shard_map/ppermute | solution.py:19
  128.2 11.6 %collective-permute-start.25 = (f32[176,768]{1,0:T(8,128)S(1)}, f32[176,768]{1,0:T(8,128)S(1)}, u32[]{:S(2)}, u32[]{:S(2)}) collective-permute-start(f32[176,768]{1,0:T(8,128)S(1)} %stack.27), channel_id=1, source_target_pairs={{0,8},{8,0},{16,24},{24,16},{1,9},{9,1},{17,25},{25,17},{2,10},{10... | collective-permute-start | bytes 1622024 | tf_op jit(solution)/shard_map/ppermute | solution.py:24
  129.7 10.7 %collective-permute-start.24 = (f32[184,768]{1,0:T(8,128)S(1)}, f32[184,768]{1,0:T(8,128)S(1)}, u32[]{:S(2)}, u32[]{:S(2)}) collective-permute-start(f32[184,768]{1,0:T(8,128)S(1)} %stack.26), channel_id=1, source_target_pairs={{0,4},{4,0},{1,5},{5,1},{2,6},{6,2},{3,7},{7,3},{8,12},{12,8},{9,1... | collective-permute-start | bytes 1695752 | tf_op jit(solution)/shard_map/ppermute | solution.py:19
  131.4 10.1 %collective-permute-start.23 = (f32[184,768]{1,0:T(8,128)S(1)}, f32[184,768]{1,0:T(8,128)S(1)}, u32[]{:S(2)}, u32[]{:S(2)}) collective-permute-start(f32[184,768]{1,0:T(8,128)S(1)} %stack.25), channel_id=1, source_target_pairs={{0,2},{2,0},{1,3},{3,1},{4,6},{6,4},{5,7},{7,5},{8,10},{10,8},{9,1... | collective-permute-start | bytes 1695752 | tf_op jit(solution)/shard_map/ppermute | solution.py:19
  137.4 5.3 %collective-permute-start.31 = (f32[256,768]{1,0:T(8,128)S(1)}, f32[256,768]{1,0:T(8,128)S(1)}, u32[]{:S(2)}, u32[]{:S(2)}) collective-permute-start(f32[256,768]{1,0:T(8,128)S(1)} %get-tuple-element.103.refs_3_.refs_0_), channel_id=1, source_target_pairs={{0,1},{1,0},{2,3},{3,2},{4,5},{5,4},{6,7},{7,6},{8,9},{9,8},{10,11... | collective-permute-start | bytes 2359304 | tf_op jit(solution)/shard_map/ppermute | solution.py:19
  137.5 5.6 %collective-permute-start.30 = (f32[768,768]{1,0:T(8,128)S(1)}, f32[768,768]{1,0:T(8,128)S(1)}, u32[]{:S(2)}, u32[]{:S(2)}) collective-permute-start(f32[768,768]{1,0:T(8,128)S(1)} %get-tuple-element.107.refs_0_), channel_id=1, source_target_pairs={{0,1},{1,0},{2,3},{3,2},{4,5},{5,4},{6,7},{7,6},{8,9},{9,8},{10,11... | collective-permute-start | bytes 7077896 | tf_op jit(solution)/shard_map/ppermute | solution.py:19
  141.6 4.7 %collective-permute-start.27 = (f32[184,768]{1,0:T(8,128)S(1)}, f32[184,768]{1,0:T(8,128)S(1)}, u32[]{:S(2)}, u32[]{:S(2)}) collective-permute-start(f32[184,768]{1,0:T(8,128)S(1)} %get-tuple-element.104.refs_0_.refs_7_), channel_id=1, source_target_pairs={{0,1},{1,0},{2,3},{3,2},{4,5},{5,4},{6,7},{7,6},{8,9},{9,8},{10,11... | collective-permute-start | bytes 1695752 | tf_op jit(solution)/shard_map/ppermute | solution.py:19
  141.6 4.7 %collective-permute-start.28 = (f32[184,768]{1,0:T(8,128)S(1)}, f32[184,768]{1,0:T(8,128)S(1)}, u32[]{:S(2)}, u32[]{:S(2)}) collective-permute-start(f32[184,768]{1,0:T(8,128)S(1)} %get-tuple-element.105.refs_1_.refs_10_), channel_id=1, source_target_pairs={{0,1},{1,0},{2,3},{3,2},{4,5},{5,4},{6,7},{7,6},{8,9},{9,8},{10,11... | collective-permute-start | bytes 1695752 | tf_op jit(solution)/shard_map/ppermute | solution.py:19
  142.1 4.1 %collective-permute-start.29 = (f32[176,768]{1,0:T(8,128)S(1)}, f32[176,768]{1,0:T(8,128)S(1)}, u32[]{:S(2)}, u32[]{:S(2)}) collective-permute-start(f32[176,768]{1,0:T(8,128)S(1)} %get-tuple-element.106.refs_2_.refs_9_), channel_id=1, source_target_pairs={{0,1},{1,0},{2,3},{3,2},{4,5},{5,4},{6,7},{7,6},{8,9},{9,8},{10,11... | collective-permute-start | bytes 1622024 | tf_op jit(solution)/shard_map/ppermute | solution.py:19
  (11 other events, 23.8 us)

commit v3 on v2

--- a/solution.py
+++ b/solution.py
@@ -9,6 +9,7 @@
 from jax.sharding import PartitionSpec as P
 
 EPS = 1e-05
+LANES = 128
 SWAP = [(0, 1), (1, 0)]
 VMEM_BYTES = 56 * 2**20
 F32 = jnp.float32
@@ -60,6 +61,26 @@
 
 def stored_at(sel, k):
     return 2 * ((k // 2) ^ sel[0]) + ((k % 2) ^ sel[1])
+
+
+def chunks(block):
+    unit = block // 88 * 16
+    sizes = (unit, 2 * unit, block - 3 * unit)
+    return tuple((sum(sizes[:i]), size) for i, size in enumerate(sizes))
+
+
+def segments(block):
+    far = [(b, first, rows) for first, rows in chunks(block) for b in (2, 3)]
+    return ((0, 0, block), (1, 0, block), *far)
+
+
+def stretches(sel, block, k):
+    held = stored_at(sel, k)
+    near = held < 2
+    return tuple(
+        (jnp.where(near, held * block + first, 2 * (block + first) + (held - 2) * rows), rows)
+        for first, rows in chunks(block)
+    )
 
 
 def row_part(sel, row):
@@ -189,28 +210,31 @@
     mean = jnp.mean(x, axis=-1, keepdims=True)
     centred = x - mean
     rdev = lax.rsqrt(jnp.mean(centred * centred, axis=-1, keepdims=True) + EPS)
-    return centred * rdev, rdev
-
-
-def norm_and_project(sel, toks, norm, w_ref, gates, normed, cand, zf, zr, base):
+    return centred * rdev, mean, rdev
+
+
+def norm_and_project(sel, toks, norm, w_ref, gates, normed, stats, cand, zf, zr, first, base):
     cols = cand.shape[1]
     mine = own_columns(sel, cols)
     gain, bias = norm[0][...], norm[1][...]
     fb, rb = gates[2][:, mine], gates[3][:, mine]
-    block = toks[0].shape[0]
     step = 16
-    for at, tok in enumerate(toks):
+    at = first
+    for tok in toks:
 
         def body(i, carry, tok=tok, at=at):
             here = pl.ds(pl.multiple_of(i * step, step), step)
-            there = pl.ds(pl.multiple_of(at * block + i * step, step), step)
-            xhat, _ = standardized(tok[here, :])
+            there = pl.ds(pl.multiple_of(at + i * step, step), step)
+            xhat, mean, rdev = standardized(tok[here, :])
             normed[there, :] = (xhat * gain + bias).astype(BF16)
+            stats[there, 0:LANES] = jnp.broadcast_to(mean, (step, LANES))
+            stats[there, LANES:] = jnp.broadcast_to(rdev, (step, LANES))
             return carry
 
-        lax.fori_loop(0, block // step, body, 0, unroll=True)
-    rows = normed[...]
-    here = slice(base, base + 2 * block)
+        lax.fori_loop(0, tok.shape[0] // step, body, 0, unroll=True)
+        at += tok.shape[0]
+    rows = normed[first:at, :]
+    here = slice(base, base + at - first)
     part = lambda k: jnp.dot(
         rows, w_ref[:, k * cols : (k + 1) * cols], preferred_element_type=F32
     )
@@ -220,25 +244,26 @@
 
 
 def near_kernel(sel, offsets, tok0, tok1, w_ref, *refs):
-    gates, norm, (normed, cand, zf, zr, half_keep) = refs[:4], refs[4:6], refs[6:]
+    gates, norm, (normed, stats, cand, zf, zr, half_keep) = refs[:4], refs[4:6], refs[6:]
     length, cols = half_keep.shape
     block = length // 4
     step = 16
-    for b in range(4):
-        base = stored_at(sel, b) * block
-
-        def body(i, carry, b=b, base=base):
+    row = 0
+    for b, first, rows in segments(block):
+        base = stored_at(sel, b) * block + first
+
+        def body(i, carry, row=row, base=base):
             at = pl.multiple_of(i * step, step)
             token = base + at + lax.broadcasted_iota(jnp.int32, (step, cols), 0)
             starts = token == offsets[0, 0]
             for k in range(1, offsets.shape[1]):
                 starts = starts | (token == offsets[0, k])
-            here = pl.ds(pl.multiple_of(b * block + at, step), step)
-            half_keep[here, :] = jnp.where(starts, 0.0, 0.5)
+            half_keep[pl.ds(pl.multiple_of(row + at, step), step), :] = jnp.where(starts, 0.0, 0.5)
             return carry
 
-        lax.fori_loop(0, block // step, body, 0)
-    norm_and_project(sel, (tok0, tok1), norm, w_ref, gates, normed, cand, zf, zr, 0)
+        lax.fori_loop(0, rows // step, body, 0)
+        row += rows
+    norm_and_project(sel, (tok0, tok1), norm, w_ref, gates, normed, stats, cand, zf, zr, 0, 0)
 
 
 def run_near(sel, offsets, toks, w_mine, vectors):
@@ -246,85 +271,112 @@
     cols = width // 4
     return pl.pallas_call(
         near_kernel,
-        out_shape=(shaped((2 * block, width), BF16),)
+        out_shape=(shaped((2 * block, width), BF16), shaped((2 * block, 2 * LANES)))
         + (shaped((2 * block, cols)),) * 3
         + (shaped((4 * block, cols)),),
         in_specs=[smem()] * 2 + [vmem()] * 9,
-        out_specs=(vmem(),) * 5,
+        out_specs=(vmem(),) * 6,
         compiler_params=params(16),
         cost_estimate=cost(0.05),
         name="near_blocks",
     )(sel, offsets, *toks, w_mine, *vectors)
 
 
-def forward_kernel(sel, tok0, tok1, cand_near, zf_near, zr_near, half_keep, w_ref, *refs):
-    gates, norm, (normed, cand, zf, zr, state, half_prev) = refs[:4], refs[4:6], refs[6:]
+def early_kernel(sel, *refs, count):
+    toks, w_ref, refs = refs[:count], refs[count], refs[count + 1 :]
+    gates, norm, (normed, stats, cand, zf, zr) = refs[:4], refs[4:6], refs[-5:]
+    norm_and_project(sel, toks, norm, w_ref, gates, normed, stats, cand, zf, zr, 0, 0)
+
+
+def run_early(sel, toks, w_mine, vectors):
+    rows, width = sum(tok.shape[0] for tok in toks), toks[0].shape[1]
+    cols = width // 4
+    return pl.pallas_call(
+        functools.partial(early_kernel, count=len(toks)),
+        out_shape=(shaped((rows, width), BF16), shaped((rows, 2 * LANES)))
+        + (shaped((rows, cols)),) * 3,
+        in_specs=[smem()] + [vmem()] * (7 + len(toks)),
+        out_specs=(vmem(),) * 5,
+        compiler_params=params(12),
+        cost_estimate=cost(0.05),
+        name="early_blocks",
+    )(sel, *toks, w_mine, *vectors)
+
+
+def forward_kernel(
+    sel,
+    tok0,
+    tok1,
+    cand_near,
+    zf_near,
+    zr_near,
+    half_keep,
+    normed_early,
+    stats_early,
+    cand_early,
+    zf_early,
+    zr_early,
+    w_ref,
+    *refs,
+):
+    gates, norm, (normed, stats, cand, zf, zr, state, half_prev) = refs[:4], refs[4:6], refs[6:]
     length, cols = cand.shape
     block = length // 4
-    near = slice(0, 2 * block)
+    early = normed_early.shape[0]
+    normed[0:early, :] = normed_early[...]
+    stats[0:early, :] = stats_early[...]
+    first = 2 * block
+    near, mid = slice(0, first), slice(first, first + early)
     cand[near, :], zf[near, :], zr[near, :] = cand_near[...], zf_near[...], zr_near[...]
+    cand[mid, :], zf[mid, :], zr[mid, :] = cand_early[...], zf_early[...], zr_early[...]
     fw = gates[0][:, own_columns(sel, cols)]
-    norm_and_project(sel, (tok0, tok1), norm, w_ref, gates, normed, cand, zf, zr, 2 * block)
-    c = jnp.zeros((1, cols), F32)
+    norm_and_project(
+        sel, (tok0, tok1), norm, w_ref, gates, normed, stats, cand, zf, zr, early, first + early
+    )
+    zero = jnp.zeros((1, cols), F32)
+    carry = (zero, zero, zero)
     for k in range(4):
-        base = stored_at(sel, k) * block
-
-        def body(i, c, base=base):
-            row = pl.ds(base + i, 1)
-            half = half_keep[row, :]
-            th = jnp.tanh(zf[row, :] + (half * fw) * c)
-            hp = half * c
-            hc = 0.5 * cand[row, :]
-            c = (hp + hc) + (hp - hc) * th
-            state[row, :] = c
-            half_prev[row, :] = hp
-            return c
-
-        c = lax.fori_loop(0, block, body, c, unroll=16)
-
-
-def run_forward(sel, toks, near, w_mine, vectors):
-    block, width = toks[0].shape
+        for base, rows in stretches(sel, block, k):
+
+            def body(i, carry, base=base):
+                middle, spread, th = carry
+                row = pl.ds(base + i, 1)
+                half = half_keep[row, :]
+                weight = half * fw
+                last = middle + spread * th
+                th = jnp.tanh((zf[row, :] + weight * middle) + (weight * spread) * th)
+                hp = half * last
+                hc = 0.5 * cand[row, :]
+                middle, spread = hp + hc, hp - hc
+                state[row, :] = middle + spread * th
+                half_prev[row, :] = hp
+                return (middle, spread, th)
+
+            carry = lax.fori_loop(0, rows, body, carry, unroll=16)
+
+
+def run_forward(sel, toks, near, early, w_mine, vectors):
+    late, width = toks[0].shape
     cols = width // 4
-    length = 4 * block
+    length = near[-1].shape[0]
     return pl.pallas_call(
         forward_kernel,
-        out_shape=(shaped((2 * block, width), BF16),) + (shaped((length, cols)),) * 5,
-        in_specs=[smem()] + [vmem()] * 13,
-        out_specs=(vmem(),) * 6,
+        out_shape=(shaped((length // 2, width), BF16), shaped((length // 2, 2 * LANES)))
+        + (shaped((length, cols)),) * 5,
+        in_specs=[smem()] + [vmem()] * 18,
+        out_specs=(vmem(),) * 7,
         compiler_params=params(20),
         cost_estimate=cost(0.05),
         name="forward_scan",
-    )(sel, *toks, *near, w_mine, *vectors)
-
-
-def backward_kernel(
-    sel,
-    x0,
-    x1,
-    x2,
-    x3,
-    g0,
-    g1,
-    g23,
-    cand_ref,
-    zf_ref,
-    zr_ref,
-    state,
-    half_prev,
-    half_keep,
-    fw_ref,
-    rw_ref,
-    near_ref,
-    far_ref,
-    dproj_ref,
-    out_ref,
-    dxh_ref,
-    small_ref,
-    *refs,
-    rows,
-):
-    products, (coef, add_b, add_e, gz, omf) = refs[: len(rows)], refs[len(rows) :]
+    )(sel, *toks, *near, *early, w_mine, *vectors)
+
+
+def backward_kernel(sel, *refs, rows, count):
+    toks, refs = refs[:count], refs[count:]
+    (g0, g1, g23, cand_ref, zf_ref, zr_ref, state, half_prev), refs = refs[:8], refs[8:]
+    (half_keep, fw_ref, rw_ref, near_ref, far_ref), refs = refs[:5], refs[5:]
+    (dproj_ref, out_ref, dxh_ref, small_ref), refs = refs[:4], refs[4:]
+    products, (coef, add, add_e, gz, omf, states) = refs[: len(rows)], refs[len(rows) :]
     length, cols = cand_ref.shape
     block = length // 4
     mine = own_columns(sel, cols)
@@ -335,17 +387,16 @@
     zero = jnp.zeros((step, cols), F32)
     sums = (zero, zero)
     everything = slice(0, cols)
-    sources = (
-        (x0, g0, 0, mine),
-        (x1, g1, 0, half),
-        (x2, g23, 0, everything),
-        (x3, g23, block, everything),
-    )
-    for b, (x_ref, g_ref, g_at, g_cols) in enumerate(sources):
-
-        def gate_body(i, carry, b=b, x_ref=x_ref, g_ref=g_ref, g_at=g_at, g_cols=g_cols):
+    grads = ((g0, 0, mine), (g1, 0, half), (g23, 0, everything), (g23, block, everything))
+    row = 0
+    for x_ref, (b, first, count) in zip(toks, segments(block)):
+        g_ref, g_at, g_cols = grads[b]
+
+        def gate_body(
+            i, carry, row=row, x_ref=x_ref, g_ref=g_ref, g_at=g_at + first, g_cols=g_cols
+        ):
             at = pl.multiple_of(i * step, step)
-            here = pl.ds(pl.multiple_of(b * block + at, step), step)
+            here = pl.ds(pl.multiple_of(row + at, step), step)
             x = x_ref[pl.ds(at, step), mine]
             g = g_ref[pl.ds(pl.multiple_of(g_at + at, step), step), g_cols].astype(F32)
             keep = 2.0 * half_keep[here, :]
@@ -358,32 +409,37 @@
             dxh_ref[here, :] = g * not_reset
             dzr = g * (c - x) * reset * not_reset
             slope = (prev - cd) * forget * not_forget
-            coef[here, :] = keep * (forget + slope * fw)
-            add_b[here, :] = keep * (dzr * rw)
-            add_e[here, :] = g * reset
+            back, extra = keep * (forget + slope * fw), g * reset
+            coef[here, :] = back
+            add[here, :] = back * extra + keep * (dzr * rw)
+            add_e[here, :] = extra
             gz[here, :] = slope
             omf[here, :] = not_forget
             dproj_ref[here, 2 * cols : 3 * cols] = dzr.astype(BF16)
             return (carry[0] + dzr * prev, carry[1] + dzr)
 
-        sums = lax.fori_loop(0, block // step, gate_body, sums, unroll=True)
+        sums = lax.fori_loop(0, count // step, gate_body, sums, unroll=True)
+        row += count
     rw_sum, rb_sum = sums
 
-    s = jnp.zeros((1, cols), F32)
+    dc = jnp.zeros((1, cols), F32)
+    group = 8
     for k in range(3, -1, -1):
-        last = stored_at(sel, k) * block + block - 1
-
-        def backward_body(i, s, last=last):
-            row = pl.ds(last - i, 1)
-            total = s + add_e[row, :]
-            add_e[row, :] = total
-            return coef[row, :] * total + add_b[row, :]
-
-        s = lax.fori_loop(0, block, backward_body, s, unroll=16)
+        for first, count in reversed(stretches(sel, block, k)):
+
+            def backward_body(i, dc, end=first + count):
+                base = pl.multiple_of(end - (i + 1) * group, group)
+                for r in range(group - 1, -1, -1):
+                    row = pl.ds(base + r, 1)
+                    states[row, :] = dc
+                    dc = coef[row, :] * dc + add[row, :]
+                return dc
+
+            dc = lax.fori_loop(0, count // group, backward_body, dc, unroll=2)
 
     def grad_body(i, carry):
         here = pl.ds(pl.multiple_of(i * step, step), step)
-        total = add_e[here, :]
+        total = states[here, :] + add_e[here, :]
         prev = 2.0 * half_prev[here, :]
         dzf = total * gz[here, :]
         dproj_ref[here, 0:cols] = (total * omf[here, :]).astype(BF16)
@@ -418,11 +474,10 @@
 
 
 def run_backward(sel, toks, cots, scanned, half_keep, gates, normed, rows):
-    block, width = toks[0].shape
-    cols = width // 4
-    length = 4 * block
-    return pl.pallas_call(
-        functools.partial(backward_kernel, rows=rows),
+    length, cols = half_keep.shape
+    width = 4 * cols
+    return pl.pallas_call(
+        functools.partial(backward_kernel, rows=rows, count=len(toks)),
         out_shape=(
             shaped((length, 3 * cols), BF16),
             shaped((length, cols)),
@@ -430,9 +485,9 @@
             shaped((8, cols)),
         )
         + product_shapes(width, rows),
-        in_specs=[smem()] + [vmem()] * 17,
+        in_specs=[smem()] + [vmem()] * (13 + len(toks)),
         out_specs=(vmem(),) * (4 + len(rows)),
-        scratch_shapes=[pltpu.VMEM((length, cols), F32)] * 5,
+        scratch_shapes=[pltpu.VMEM((length, cols), F32)] * 6,
         compiler_params=params(24),
         cost_estimate=cost(0.05),
         name="backward_scan",
@@ -440,65 +495,66 @@
 
 
 def products_kernel(sel, near_ref, far_ref, dproj_ref, *outs, rows):
-    outer_products(sel, rows, near_ref, far_ref, dproj_ref, outs)
-
-
-def run_products(sel, normed, dproj, rows):
+    outer_products(sel, rows, near_ref, far_ref, dproj_ref, outs[-len(rows) :])
+
+
+def run_products(sel, normed, dproj, rows, *waits):
     return pl.pallas_call(
         functools.partial(products_kernel, rows=rows),
         out_shape=product_shapes(normed[0].shape[1], rows),
-        in_specs=[smem()] + [vmem()] * 3,
+        in_specs=[smem()] + [vmem()] * 3 + [any_spec()] * len(waits),
         out_specs=(vmem(),) * len(rows),
         compiler_params=params(12),
         cost_estimate=cost(0.05),
         name="products",
-    )(sel, *normed, dproj)
-
-
-def input_kernel(
-    sel,
-    tok0,
-    tok1,
-    tok2,
-    tok3,
-    dproj_ref,
-    dxh_ref,
-    out_ref,
-    gate_small_ref,
-    w_ref,
-    gain_ref,
-    *refs,
-):
-    mine_ref, send_ref, dnormed = refs[-3:]
+    )(sel, *normed, dproj, *waits)
+
+
+def input_kernel(sel, *refs, count):
+    toks, (mine_ref, send_ref, dnormed) = refs[:count], refs[-3:]
+    (stats_near, stats_far, dproj_ref, dxh_ref, out_ref), refs = refs[count : count + 5], refs[count + 5 :]
+    gate_small_ref, w_ref, gain_ref = refs[:3]
     cols = dxh_ref.shape[1]
-    block, width = tok0.shape
+    block, width = toks[0].shape
     gain = gain_ref[...]
     mine = own_columns(sel, cols)
     step = 8
     sums = (jnp.zeros((step, width), F32), jnp.zeros((step, width), F32))
-    for b, tok in enumerate((tok0, tok1, tok2, tok3)):
-        rows = slice(b * block, (b + 1) * block)
-        dnormed[...] = lax.dot_general(
-            dproj_ref[rows, :], w_ref[...], (((1,), (1,)), ((), ())), preferred_element_type=F32
-        )
+    row = 0
+    for tok, (b, first, count) in zip(toks, segments(block)):
+        if row % (2 * block) == 0:
+            dnormed[...] = lax.dot_general(
+                dproj_ref[row : row + 2 * block, :],
+                w_ref[...],
+                (((1,), (1,)), ((), ())),
+                preferred_element_type=F32,
+            )
+        rows = slice(row, row + count)
         where = send_ref if b % 2 else mine_ref
-        base = (b // 2) * block
-
-        def body(i, carry, tok=tok, base=base, where=where):
+        base = (b // 2) * block + first
+        stats, at = (stats_near, row) if b < 2 else (stats_far, row - 2 * block)
+
+        def body(i, carry, tok=tok, base=base, where=where, stats=stats, at=at):
             here = pl.ds(pl.multiple_of(i * step, step), step)
             there = pl.ds(pl.multiple_of(base + i * step, step), step)
-            xhat, rdev = standardized(tok[here, :])
-            dn = dnormed[here, :]
+            kept = pl.ds(pl.multiple_of(at + i * step, step), step)
+            mean, rdev = (
+                jnp.concatenate([stats[kept, k : k + LANES]] * (width // LANES), axis=1)
+                for k in (0, LANES)
+            )
+            xhat = (tok[here, :] - mean) * rdev
+            dn = dnormed[kept, :]
             dxhat = dn * gain
             mean1 = jnp.mean(dxhat, axis=-1, keepdims=True)
             mean2 = jnp.mean(dxhat * xhat, axis=-1, keepdims=True)
             where[there, 0:width] = rdev * (dxhat - mean1 - xhat * mean2)
             return (carry[0] + dn * xhat, carry[1] + dn)
 
-        sums = lax.fori_loop(0, block // step, body, sums, unroll=11)
-        to = pl.ds(base, block)
+        sums = lax.fori_loop(0, count // step, body, sums, unroll=11 if count == block else 4)
+        to = pl.ds(base, count)
         where[to, mine] += dxh_ref[rows, :]
         where[to, width : width + cols] = out_ref[rows, :]
+        row += count
     tail = slice(2 * block, 2 * block + 8)
     mine_ref[tail, :] = jnp.zeros((8, width + cols), F32)
     mine_ref[2 * block : 2 * block + 4, mine] = gate_small_ref[0:4, :]
@@ -508,19 +564,19 @@
     send_ref[tail, :] = mine_ref[tail, :]
 
 
-def run_input(sel, toks, dproj, dxh, out, gate_small, w_mine, gain, *waits):
+def run_input(sel, toks, stats, dproj, dxh, out, gate_small, w_mine, gain, *waits):
     block, width = toks[0].shape
     shape = (2 * block + 8, width + width // 4)
     return pl.pallas_call(
-        input_kernel,
+        functools.partial(input_kernel, count=len(toks)),
         out_shape=(shaped(shape), shaped(shape)),
-        in_specs=[smem()] + [vmem()] * 10 + [any_spec()] * len(waits),
+        in_specs=[smem()] + [vmem()] * (8 + len(toks)) + [any_spec()] * len(waits),
         out_specs=(vmem(),) * 2,
-        scratch_shapes=[pltpu.VMEM((block, width), F32)],
+        scratch_shapes=[pltpu.VMEM((2 * block, width), F32)],
         compiler_params=params(20),
         cost_estimate=cost(0.05),
         name="input_side",
-    )(sel, *toks, dproj, dxh, out, gate_small, w_mine, gain, *waits)
+    )(sel, *toks, *stats, dproj, dxh, out, gate_small, w_mine, gain, *waits)
 
 
 def combine_kernel(sel, mine_ref, got_ref, *refs):
@@ -550,7 +606,8 @@
     )(sel, mine, got, *waits)
 
 
-def join_kernel(sel, mine_ref, got_ref, out_ref, grad_ref):
+def join_kernel(sel, mine_ref, got_ref, out_ref, grad_ref, done_ref):
+    done_ref[...] = jnp.zeros(done_ref.shape, F32)
     width = out_ref.shape[1]
     half = width // 2
     at = pl.multiple_of(sel[0] * half, half)
@@ -564,9 +621,9 @@
     block, width = mine.shape[0], mine.shape[1] * 2 // 3
     return pl.pallas_call(
         join_kernel,
-        out_shape=(shaped((block, width), BF16),) * 2,
+        out_shape=(shaped((block, width), BF16),) * 2 + (shaped((8, LANES)),),
         in_specs=[smem()] + [vmem()] * 2,
-        out_specs=(vmem(),) * 2,
+        out_specs=(vmem(),) * 3,
         compiler_params=params(16),
         cost_estimate=cost(0.05),
         name="join",
@@ -580,10 +637,10 @@
     return jnp.concatenate([small[0:rows, : 3 * cols]] + last, axis=0)
 
 
-def finish_kernel(keep_ref, got_ref, a1_ref, a3_ref, small_ref, total_ref):
+def finish_kernel(keep_ref, got_ref, a1_ref, a3_ref, small_ref, both_ref):
     part = keep_ref.shape[0]
-    total_ref[0:part, :] = keep_ref[...] + got_ref[...] + a1_ref[...] + a3_ref[...]
-    total_ref[part:, :] = fold_small(small_ref[...])
+    both_ref[0:part, :] = keep_ref[...] + got_ref[...] + a1_ref[...] + a3_ref[...]
+    both_ref[part:, :] = fold_small(small_ref[...])
 
 
 def finish(keep, got, a1, a3, small):
@@ -597,6 +654,29 @@
         cost_estimate=cost(0.05),
         name="finish",
     )(keep, got, a1, a3, small)
+
+
+def second_kernel(both_ref, px0_ref, py0_ref, corner_ref, z1_ref, z3_ref, z13_ref, zs_ref, cs_ref):
+    part = z1_ref.shape[0] - 8
+    z13_ref[0:part, :] = z1_ref[0:part, :]
+    z13_ref[part:, :] = z3_ref[0:part, :]
+    small = (both_ref[part:, :] + px0_ref[part:, :]) + (py0_ref[part:, :] + corner_ref[part:, :])
+    for ref, out in ((z3_ref, zs_ref), (corner_ref, cs_ref)):
+        out[0:part, :] = ref[0:part, :]
+        out[part:, :] = small
+
+
+def second(*pieces):
+    part, cols3 = pieces[-1].shape[0] - 8, pieces[-1].shape[1]
+    return pl.pallas_call(
+        second_kernel,
+        out_shape=(shaped((2 * part, cols3)),) + (shaped((part + 8, cols3)),) * 2,
+        in_specs=[vmem()] * 6,
+        out_specs=(vmem(),) * 3,
+        compiler_params=params(10),
+        cost_estimate=cost(0.05),
+        name="second",
+    )(*pieces)
 
 
 def stack_kernel(*refs, rows):
@@ -715,12 +795,14 @@
     part = width // 8
 
     cot = cotangent[0]
-    own = lax.optimization_barrier(tokens[0].astype(F32))
-    tok_x = swap(own, "x")
+    own = tokens[0].astype(F32)
+    own, *parts = lax.optimization_barrier(
+        (own, *(own[first : first + rows] for first, rows in chunks(block)))
+    )
+    x_a, x_b, x_c = (swap(piece, "x") for piece in parts)
     tok_c = swap(own, "c")
     cot_sibling = swap(widen_cot(sel, cot), "c")
-    cot_packed = pack_cot(sel, cot, cot_sibling)
-    cot_far = swap(cot_packed, "x")
+    cot_far = swap(pack_cot(sel, cot, cot_sibling), "x")
 
     gates = [
         v.reshape(1, width) for v in (forget_weight, reset_weight, forget_bias, reset_bias)
@@ -729,28 +811,33 @@
     vectors = (*gates, gain, layer_norm_bias.reshape(1, width))
     w_mine = take_weights(sel, w_proj)
     near = run_near(sel, offsets, (own, tok_c), w_mine, vectors)
-    (tok_x,) = hold((tok_x,), near[4], cot_packed)
-    tok_xc = swap(tok_x, "c")
-    far = run_forward(sel, (tok_x, tok_xc), near[1:], w_mine, vectors)
+    (x_a,) = hold((x_a,), near[5])
+    xc_a = swap(x_a, "c")
+    (x_b,) = hold((x_b,), xc_a)
+    xc_b = swap(x_b, "c")
+    early = run_early(sel, (x_a, xc_a, x_b, xc_b), w_mine, vectors)
+    (x_c,) = hold((x_c,), early[0])
+    xc_c = swap(x_c, "c")
+    far = run_forward(sel, (x_c, xc_c), near[2:], early, w_mine, vectors)
     normed = (near[0], far[0])
-    toks = (own, tok_c, tok_x, tok_xc)
+    toks = (own, tok_c, x_a, xc_a, x_b, xc_b, x_c, xc_c)
     if tuned:
         rows = [[[(d, 1)] for d in (2, 3, 1, 0)], [[(d, 0)] for d in (2, 3, 1, 0)]]
     else:
         rows = [[[0], [1], [2], [3]], [[4], [5], [6], [7]]]
     dproj, out, dxh, gate_small, s2 = run_backward(
-        sel, toks, (cot, cot_sibling, cot_far), far[1:], near[4], gates, normed, rows[0][:1]
+        sel, toks, (cot, cot_sibling, cot_far), far[2:], near[5], gates, normed, rows[0][:1]
     )
-    s3, s1, s0 = run_products(sel, normed, dproj, rows[0][1:])
-    k2, k3, k1, k0 = run_products(sel, normed, dproj, rows[1])
-    input_side = lambda *waits: run_input(
-        sel, toks, dproj, dxh, out, gate_small, w_mine, gain, *waits
+    s3, k2 = run_products(sel, normed, dproj, (rows[0][1], rows[1][0]))
+    grad_mine, grad_send = run_input(
+        sel, toks, (near[1], far[1]), dproj, dxh, out, gate_small, w_mine, gain
     )
+    late = (*rows[0][2:], *rows[1][1:])
 
     if tuned:
-        r2, r3, r1, r0 = (swap(piece, "y") for piece in (s2, s3, s1, s0))
-        grad_mine, grad_send = input_side()
-        q2 = add(k2, r2, s0, grad_send)
+        s1, s0, k3, k1, k0 = run_products(sel, normed, dproj, late)
+        q2 = add(k2, swap(s2, "y"), s3, s0, grad_send)
+        r3, r1, r0 = (swap(piece, "y") for piece in (s3, s1, s0))
         a2 = xor_permute(q2, "z", 1)
         h3 = add(add(k3, r3), a2)
         a3 = xor_permute(h3, "z", 3)
@@ -759,34 +846,40 @@
         )
         got = swap(sent, "x")
         a1 = xor_permute(add(k1, r1, sent), "z", 1)
-        total = finish(k0, r0, a1, a3, small)
-        output, input_grad = join(sel, kept, got)
-
-        z3, px0, py0 = xor_permute(total, "z", 3), swap(total, "x"), swap(total, "y")
-        z1 = xor_permute(total, "z", 1)
-        (px0,) = hold((px0,), input_grad)
+        both = finish(k0, r0, a1, a3, small)
+        output, input_grad, joined = join(sel, kept, got)
+
+        px0, z3, z1, py0 = (
+            swap(both, "x"),
+            xor_permute(both, "z", 3),
+            xor_permute(both, "z", 1),
+            swap(both, "y"),
+        )
+        (px0,) = hold((px0,), joined)
         corner0 = swap(px0, "y")
         z3, z1, corner0, py0 = hold((z3, z1, corner0, py0))
         full = part + 8
-        z13 = stack((z1, 0, full), (z3, 0, full))
-        z2, px13, py13 = xor_permute(z3, "z", 1), swap(z13, "x"), swap(z13, "y")
-        corner3 = xor_permute(corner0, "z", 3)
+        z13, zs, cs = second(both, px0, py0, corner0, z1, z3)
+        z2, px13, py13 = xor_permute(zs, "z", 1), swap(z13, "x"), swap(z13, "y")
+        corner3 = xor_permute(cs, "z", 3)
         own = [
             (0, 0, part, (0, 0), 0, 0, 0),
             (1, 0, part, (0, 0), 0, 1, 0),
             (2, 0, part, (0, 1), 0, 0, 0),
             (3, 0, part, (0, 1), 0, 1, 0),
         ]
-        proj_grad, give = place(sel, (total, px0, py0, corner0), own, None, width, 4)
+        proj_grad, give = place(sel, (both, px0, py0, corner0), own, None, width, 4)
         z2, px13, py13, corner3 = hold((z2, px13, py13, corner3), give)
         third = 3 * part // 8
-        rest = full - 2 * third
-        px2 = swap(stack((z2, 0, full), (py13, 0, third)), "x")
-        py2 = swap(stack((z2, 0, full), (px13, third, third)), "y")
-        corner12 = xor_permute(stack((corner3, 0, full), (corner0, 2 * third, rest)), "z", 1)
+        rest = part - 2 * third
+        px2 = swap(stack((z2, 0, part), (py13, 0, third)), "x")
+        py2 = swap(stack((z2, 0, part), (px13, third, third)), "y")
+        corner12 = xor_permute(
+            stack((corner3, 0, part), (corner0, 2 * third, rest), (corner3, part, 8)), "z", 1
+        )
         other = given(3, own)
         own = [
-            (array, full * i, part, (d, y_off), 0, x_off, 0)
+            (array, part * i, part, (d, y_off), 0, x_off, 0)
             for array, y_off, x_off in ((0, 0, 0), (1, 0, 1), (2, 1, 0))
             for i, d in ((0, 1), (1, 3))
         ]
@@ -797,35 +890,33 @@
             proj_grad,
             width,
             6,
-            tick(give),
+            tick(give, corner3),
         )
         other = given(3, own)
-        first_give, wait = swap(give, "c"), tick(give)
+        first_give, marked = swap(give, "c"), give
         own = [(0, 0, part, (2, 0), 0, 0, 0), (1, 0, part, (3, 1), 0, 1, 0)]
         proj_grad, give = place(sel, (z2, corner3), own, proj_grad, width, 2)
         other += given(4, own)
         px2, py2, corner12 = hold((px2, py2, corner12), give)
         own = [
             (0, 0, part, (2, 0), 0, 1, 0),
-            (0, full, third, (1, 1), 0, 1, 0),
+            (0, part, third, (1, 1), 0, 1, 0),
             (1, 0, part, (2, 1), 0, 0, 0),
-            (1, full, third, (1, 1), third, 1, 0),
+            (1, part, third, (1, 1), third, 1, 0),
             (2, 0, part, (2, 1), 0, 1, 0),
-            (2, full, rest - 8, (1, 1), 2 * third, 1, 0),
+            (2, part, rest, (1, 1), 2 * third, 1, 0),
         ]
         arrays = (px2, py2, corner12, first_give, swap(give, "c"))
-        (proj_grad,) = place(sel, arrays, own + other, proj_grad, width, 0, wait, tick(give))
+        (proj_grad,) = place(
+            sel, arrays, own + other, proj_grad, width, 0, tick(marked, give, px2)
+        )
         own = [(*place_of[:-1], 1) for place_of in own]
         arrays = [swap(a, "c") for a in (px2, py2, corner12)]
         (proj_grad,) = place(sel, arrays, own, proj_grad, width, 0)
-        where = [(0, part), (1, part), (2, part), (3, part)]
-        where += [(4, part), (5, part), (6, part), (9, full + rest - 8)]
-        where += [(8, part), (7, part), (10, part), (9, part)]
-        where += [(array, full + part) for array in (4, 5, 6)] + [(11, part)]
-        arrays = (total, px0, py0, corner0, z13, px13, py13, px2, z2, corner12, py2, corner3)
-        small = small_sums(arrays, where)
+        where = [(0, part), (1, part), (2, part + rest), (3, part)]
+        small = small_sums((zs, z2, corner12, corner3), where)
     else:
-        grad_mine, grad_send = input_side()
+        s1, s0, k3, k1, k0 = run_products(sel, normed, dproj, late)
         kept, sent, small = combine(sel, grad_mine, swap(grad_send, "c"))
         got = swap(sent, "x")
         small = lax.psum(small + swap(small, "x"), ("z", "y"))
@@ -837,7 +928,7 @@
             proj_grad, give = place(sel, list(held), own, proj_grad, width, 8)
             other = given(0, own)
             (proj_grad,) = place(sel, [swap(give, "c")], other, proj_grad, width, 0)
-        output, input_grad = join(sel, kept, got)
+        output, input_grad, _ = join(sel, kept, got)
     small = [small[i].reshape(width) for i in range(6)]
     return (output[None], input_grad[None], proj_grad, *small)
 

time: 148 us -> 144 us (0.973)
  waiting for transfers between devices: 66.1 us -> 61.9 us
  starting transfers between devices: 33.2 us -> 37.1 us
  Pallas kernels: 41.8 us -> 39.3 us
  local copies, waits for them, and re-layouts: 4.79 us -> 2.88 us
    ppermute x8, waiting for transfers between devices: 39.7 us -> 36.3 us  [xor_permute(): return lax.ppermute(block, axis, [(i, i ^ distance) for i in range(size)])]
    ppermute x24 -> x28, starting transfers between devices: 18.2 us -> 21 us  [swap(): return lax.ppermute(block, axis, SWAP)]
    pallas_call x4 -> x6, Pallas kernels: 21.9 us -> 19.4 us  [the longest x1 7.21 us: run_forward(): pl.pallas_call(forward_kernel, out_shape=(shaped((length // 2, width), BF...]
    unnamed x22 -> x18, local copies, waits for them, and re-layouts: 4.79 us -> 2.83 us
    ppermute x24 -> x28, waiting for transfers between devices: 26.4 us -> 25.5 us  [swap(): return lax.ppermute(block, axis, SWAP)]
  transfers between devices with their start and end apart: 32 -> 36, of which waited for: 18 -> 19; matrix products, arithmetic and copies ran while one was open for 0% -> 0% of each run, Pallas kernels for 24% -> 23%
where the time goes in v3:
time: 144 us; the launch traced here: 143 us
  waiting for transfers between devices  61.9 us (43%)
  Pallas kernels  39.3 us (27%)
  starting transfers between devices  37.1 us (26%)
  local copies, waits for them, and re-layouts  2.88 us (2%)
    ppermute x8, waiting for transfers between devices, xor_permute(): return lax.ppermute(block, axis, [(i, i ^ distance) for i in range(size)])  36.3 us
    ppermute x28, waiting for transfers between devices, swap(): return lax.ppermute(block, axis, SWAP)  25.5 us
    ppermute x28, starting transfers between devices, swap(): return lax.ppermute(block, axis, SWAP)  21 us
    ppermute x8, starting transfers between devices, xor_permute(): return lax.ppermute(block, axis, [(i, i ^ distance) for i in range(size)])  16.1 us
    pallas_call x5, Pallas kernels, place(): pl.pallas_call(functools.partial(place_kernel, where=where, give=give), o...  11.7 us
    pallas_call x1, Pallas kernels, run_forward(): pl.pallas_call(forward_kernel, out_shape=(shaped((length // 2, width), BF...  7.21 us
    pallas_call x1, Pallas kernels, run_input(): pl.pallas_call(functools.partial(input_kernel, count=len(toks)), out_shap...  4.5 us
    pallas_call x1, Pallas kernels, run_backward(): pl.pallas_call(functools.partial(backward_kernel, rows=rows, count=len(to...  4.12 us
  transfers between devices with their start and end apart: 36, of which 19 were waited for; matrix products, arithmetic and copies ran while one was open for 0% of the time, Pallas kernels for 23%

profile of v3, /device:TPU:0, one launch (start us, length us, event | category | flops | bytes accessed | tf_op | source)
XLA Modules:
  0.0 143.4 jit_solution(771702950352920997)
XLA Ops:
  2.4 2.6 %collective-permute-start.1 = (f32[32,1024]{1,0:T(8,128)S(1)}, f32[32,1024]{1,0:T(8,128)S(1)}, u32[]{:S(2)}, u32[]{:S(2)}) collective-permute-start(f32[32,1024]{1,0:T(8,128)S(1)} %slice_bitcast_fusion.2), channel_id=1, source_target_pairs={{0,2},{2,0},{1,3},{3,1},{4,6},{6,4},{5,7},{7,5},{8,10},{10,8},{9,1... | collective-permute-start | bytes 393224 | tf_op jit(solution)/shard_map/ppermute | solution.py:20
  5.1 2.8 %copy-done = bf16[1024,3072]{1,0:T(8,128)(2,1)S(1)} copy-done((bf16[1024,3072]{1,0:T(8,128)(2,1)S(1)}, bf16[1024,3072]{1,0:T(8,128)(2,1)}, u32[]{:S(2)}) %copy-start) | copy-done | bytes 6291480
  8.8 2.2 %near_blocks.1 = (bf16[352,1024]{1,0:T(8,128)(2,1)S(1)}, f32[352,256]{1,0:T(8,128)S(1)}, f32[352,256]{1,0:T(8,128)S(1)}, f32[352,256]{1,0:T(8,128)S(1)}, f32[352,256]{1,0:T(8,128)S(1)}, /*index=5*/f32[704,256]{1,0:T(8,128)S(1)}) custom-call(s32[4]{0:T(128)S(1)} %pad_add_fusion.sel, s32[1,8]{1,0:T(1,128)S(1)} %copy-done.8, ...), custom_call_target="tpu_custom_call" | custom-call | flops 55000000 | bytes 180000 | tf_op jit(solution)/shard_map/near_blocks/pallas_call | solution.py:272
  12.3 1.9 %collective-permute-start.5 = (f32[80,1024]{1,0:T(8,128)S(1)}, f32[80,1024]{1,0:T(8,128)S(1)}, u32[]{:S(2)}, u32[]{:S(2)}) collective-permute-start(f32[80,1024]{1,0:T(8,128)S(1)} %slice_bitcast_fusion), channel_id=1, source_target_pairs={{0,2},{2,0},{1,3},{3,1},{4,6},{6,4},{5,7},{7,5},{8,10},{10,8},{9,1... | collective-permute-start | bytes 983048 | tf_op jit(solution)/shard_map/ppermute | solution.py:20
  15.3 1.8 %collective-permute-start.8 = (f32[352,256]{1,0:T(8,128)S(1)}, f32[352,256]{1,0:T(8,128)S(1)}, u32[]{:S(2)}, u32[]{:S(2)}) collective-permute-start(f32[352,256]{1,0:T(8,128)S(1)} %pack_cot.1), channel_id=1, source_target_pairs={{0,2},{2,0},{1,3},{3,1},{4,6},{6,4},{5,7},{7,5},{8,10},{10,8},{9,1... | collective-permute-start | bytes 1081352 | tf_op jit(solution)/shard_map/ppermute | solution.py:20
  18.3 4.5 %collective-permute-done.5.refs_0_ = f32[80,1024]{1,0:T(8,128)S(1)} collective-permute-done((f32[80,1024]{1,0:T(8,128)S(1)}, f32[80,1024]{1,0:T(8,128)S(1)}, u32[]{:S(2)}, u32[]{:S(2)}) %collective-permute-start.5) | collective-permute-done | bytes 327712 | tf_op jit(solution)/shard_map/ppermute | solution.py:20
  24.5 7.2 %forward_scan.1 = (bf16[352,1024]{1,0:T(8,128)(2,1)S(1)}, f32[352,256]{1,0:T(8,128)S(1)}, f32[704,256]{1,0:T(8,128)S(1)}, f32[704,256]{1,0:T(8,128)S(1)}, f32[70...) custom-call(s32[4]{0:T(128)S(1)} %pad_add_fusion.sel, f32[80,1024]{1,0:T(8,128)S(1)} %hold.9.tok0.refs_6_, ...), custom_call_target="tpu_custom_call" | custom-call | flops 55000000 | bytes 180000 | tf_op jit(solution)/shard_map/forward_scan/pallas_call | solution.py:362
  31.7 4.1 %backward_scan.1 = (bf16[704,768]{1,0:T(8,128)(2,1)S(1)}, f32[704,256]{1,0:T(8,128)S(1)}, f32[704,256]{1,0:T(8,128)S(1)}, f32[8,256]{1,0:T(8,128)S(1)}, f32[128,768]{1,0:T(8,128)S(1)}) custom-call(s32[4]{0:T(128)S(1)} %pad_add_fusion.sel, f32[176,1024]{1,0:T(8,128)S(1)} %get-tuple-element.77.tok0.refs_0_, f32[176,1024]{1,0:T(8,128)S(1)} %collective-permute-done.tok1.refs_1_, ...), custom_call_target="tpu_custom_call" | custom-call | flops 55000000 | bytes 180000 | tf_op jit(solution)/shard_map/backward_scan/pallas_call | solution.py:479
  35.8 2.0 %collective-permute-start.10 = (f32[128,768]{1,0:T(8,128)S(1)}, f32[128,768]{1,0:T(8,128)S(1)}, u32[]{:S(2)}, u32[]{:S(2)}) collective-permute-start(f32[128,768]{1,0:T(8,128)S(1)} %get-tuple-element.106), channel_id=1, source_target_pairs={{0,4},{4,0},{1,5},{5,1},{2,6},{6,2},{3,7},{7,3},{8,12},{12,8},{9,1... | collective-permute-start | bytes 1179656 | tf_op jit(solution)/shard_map/ppermute | solution.py:20
  39.1 4.5 %input_side.1 = (f32[360,1280]{1,0:T(8,128)S(1)}, f32[360,1280]{1,0:T(8,128)S(1)}) custom-call(s32[4]{0:T(128)S(1)} %pad_add_fusion.sel, f32[176,1024]{1,0:T(8,128)S(1)} %get-tuple-element.77.tok0.refs_0_, f32[176,1024]{1,0:T(8,128)S(1)} %collective-permute-done.tok1.refs_1_, f32[32,1024]{1,0:T(8,128)S(1)} %hold.7.refs_0_.refs_2_, ...), custom_call_target="tpu_custom_call" | custom-call | flops 55000000 | bytes 180000 | tf_op jit(solution)/shard_map/input_side/pallas_call | solution.py:570
  43.7 1.8 %products.3 = (f32[128,768]{1,0:T(8,128)S(1)}, f32[128,768]{1,0:T(8,128)S(1)}, f32[128,768]{1,0:T(8,128)S(1)}, f32[128,768]{1,0:T(8,128)S(1)}, f32[128,768]{1,0:T(8,128)S(1)}) custom-call(s32[4]{0:T(128)S(1)} %pad_add_fusion.sel, bf16[352,1024]{1,0:T(8,128)(2,1)S(1)} %get-tuple-element.97.refs_19_.near_ref, ...), custom_call_target="tpu_custom_call" | custom-call | flops 55000000 | bytes 180000 | tf_op jit(solution)/shard_map/products/pallas_call | solution.py:502
  45.5 2.0 %collective-permute-start.13 = (f32[128,768]{1,0:T(8,128)S(1)}, f32[128,768]{1,0:T(8,128)S(1)}, u32[]{:S(2)}, u32[]{:S(2)}) collective-permute-start(f32[128,768]{1,0:T(8,128)S(1)} %get-tuple-element.115), channel_id=1, source_target_pairs={{0,4},{4,0},{1,5},{5,1},{2,6},{6,2},{3,7},{7,3},{8,12},{12,8},{9,1... | collective-permute-start | bytes 1179656 | tf_op jit(solution)/shard_map/ppermute | solution.py:20
  47.9 2.1 %collective-permute-start.16 = (f32[128,768]{1,0:T(8,128)S(1)}, f32[128,768]{1,0:T(8,128)S(1)}, u32[]{:S(2)}, u32[]{:S(2)}) collective-permute-start(f32[128,768]{1,0:T(8,128)S(1)} %add.10.refs_0_), channel_id=1, source_target_pairs={{0,8},{8,0},{16,24},{24,16},{1,9},{9,1},{17,25},{25,17},{2,10},{10... | collective-permute-start | bytes 1179656 | tf_op jit(solution)/shard_map/ppermute | solution.py:25
  53.9 2.4 %collective-permute-done.15.b_ref = f32[128,768]{1,0:T(8,128)S(1)} collective-permute-done((f32[128,768]{1,0:T(8,128)S(1)}, f32[128,768]{1,0:T(8,128)S(1)}, u32[]{:S(2)}, u32[]{:S(2)}) %collective-permute-start.15) | collective-permute-done | bytes 393248 | tf_op jit(solution)/shard_map/ppermute | solution.py:20
  56.3 2.6 %collective-permute-done.16.b_ref = f32[128,768]{1,0:T(8,128)S(1)} collective-permute-done((f32[128,768]{1,0:T(8,128)S(1)}, f32[128,768]{1,0:T(8,128)S(1)}, u32[]{:S(2)}, u32[]{:S(2)}) %collective-permute-start.16) | collective-permute-done | bytes 393248 | tf_op jit(solution)/shard_map/ppermute | solution.py:25
  59.0 3.7 %collective-permute-start.17 = (f32[128,768]{1,0:T(8,128)S(1)}, f32[128,768]{1,0:T(8,128)S(1)}, u32[]{:S(2)}, u32[]{:S(2)}) collective-permute-start(f32[128,768]{1,0:T(8,128)S(1)} %add.13), channel_id=1, source_target_pairs={{0,24},{8,16},{16,8},{24,0},{1,25},{9,17},{17,9},{25,1},{2,26},{10... | collective-permute-start | bytes 1179656 | tf_op jit(solution)/shard_map/ppermute | solution.py:25
  62.6 2.0 %collective-permute-done.13.b_ref = f32[128,768]{1,0:T(8,128)S(1)} collective-permute-done((f32[128,768]{1,0:T(8,128)S(1)}, f32[128,768]{1,0:T(8,128)S(1)}, u32[]{:S(2)}, u32[]{:S(2)}) %collective-permute-start.13) | collective-permute-done | bytes 393248 | tf_op jit(solution)/shard_map/ppermute | solution.py:20
  64.7 2.1 %collective-permute-start.14 = (f32[128,768]{1,0:T(8,128)S(1)}, f32[128,768]{1,0:T(8,128)S(1)}, u32[]{:S(2)}, u32[]{:S(2)}) collective-permute-start(f32[128,768]{1,0:T(8,128)S(1)} %add.11), channel_id=1, source_target_pairs={{0,8},{8,0},{16,24},{24,16},{1,9},{9,1},{17,25},{25,17},{2,10},{10... | collective-permute-start | bytes 1179656 | tf_op jit(solution)/shard_map/ppermute | solution.py:25
  66.9 5.7 %collective-permute-done.12.got_ref = f32[128,768]{1,0:T(8,128)S(1)} collective-permute-done((f32[128,768]{1,0:T(8,128)S(1)}, f32[128,768]{1,0:T(8,128)S(1)}, u32[]{:S(2)}, u32[]{:S(2)}) %collective-permute-start.12) | collective-permute-done | bytes 393248 | tf_op jit(solution)/shard_map/ppermute | solution.py:20
  72.9 6.5 %collective-permute-done.14.a1_ref = f32[128,768]{1,0:T(8,128)S(1)} collective-permute-done((f32[128,768]{1,0:T(8,128)S(1)}, f32[128,768]{1,0:T(8,128)S(1)}, u32[]{:S(2)}, u32[]{:S(2)}) %collective-permute-start.14) | collective-permute-done | bytes 393248 | tf_op jit(solution)/shard_map/ppermute | solution.py:25
  80.6 3.5 %collective-permute-start.19 = (f32[136,768]{1,0:T(8,128)S(1)}, f32[136,768]{1,0:T(8,128)S(1)}, u32[]{:S(2)}, u32[]{:S(2)}) collective-permute-start(f32[136,768]{1,0:T(8,128)S(1)} %finish.1.both_ref.refs_0_), channel_id=1, source_target_pairs={{0,24},{8,16},{16,8},{24,0},{1,25},{9,17},{17,9},{25,1},{2,26},{10... | collective-permute-start | bytes 1253384 | tf_op jit(solution)/shard_map/ppermute | solution.py:25
  85.7 5.4 %collective-permute-done.18.refs_0_ = f32[136,768]{1,0:T(8,128)S(1)} collective-permute-done((f32[136,768]{1,0:T(8,128)S(1)}, f32[136,768]{1,0:T(8,128)S(1)}, u32[]{:S(2)}, u32[]{:S(2)}) %collective-permute-start.18) | collective-permute-done | bytes 417824 | tf_op jit(solution)/shard_map/ppermute | solution.py:20
  91.1 3.9 %collective-permute-done.19.refs_0_ = f32[136,768]{1,0:T(8,128)S(1)} collective-permute-done((f32[136,768]{1,0:T(8,128)S(1)}, f32[136,768]{1,0:T(8,128)S(1)}, u32[]{:S(2)}, u32[]{:S(2)}) %collective-permute-start.19) | collective-permute-done | bytes 417824 | tf_op jit(solution)/shard_map/ppermute | solution.py:25
  95.0 7.7 %collective-permute-done.20.refs_1_ = f32[136,768]{1,0:T(8,128)S(1)} collective-permute-done((f32[136,768]{1,0:T(8,128)S(1)}, f32[136,768]{1,0:T(8,128)S(1)}, u32[]{:S(2)}, u32[]{:S(2)}) %collective-permute-start.20) | collective-permute-done | bytes 417824 | tf_op jit(solution)/shard_map/ppermute | solution.py:25
  107.6 2.0 %place.5 = (f32[1024,3072]{1,0:T(8,128)}, f32[512,768]{1,0:T(8,128)S(1)}) custom-call(s32[4]{0:T(128)S(1)} %pad_add_fusion.sel, f32[136,768]{1,0:T(8,128)S(1)} %finish.1.both_ref.refs_0_, f32[136,768]{1,0:T(8,128)S(1)} %hold.10.px0_ref.refs_1_, f32[136,768]{1,0:T(8,128)S(1)} %get-tuple-element.119.py0_ref.refs_2_, ...), custom_call_target="tpu_custom_call" | custom-call | flops 55000000 | bytes 180000 | tf_op jit(solution)/shard_map/place/pallas_call | solution.py:755
  109.7 8.8 %collective-permute-done.23.refs_0_ = f32[136,768]{1,0:T(8,128)S(1)} collective-permute-done((f32[136,768]{1,0:T(8,128)S(1)}, f32[136,768]{1,0:T(8,128)S(1)}, u32[]{:S(2)}, u32[]{:S(2)}) %collective-permute-start.23) | collective-permute-done | bytes 417824 | tf_op jit(solution)/shard_map/ppermute | solution.py:25
  118.5 5.7 %collective-permute-done.26.refs_3_ = f32[136,768]{1,0:T(8,128)S(1)} collective-permute-done((f32[136,768]{1,0:T(8,128)S(1)}, f32[136,768]{1,0:T(8,128)S(1)}, u32[]{:S(2)}, u32[]{:S(2)}) %collective-permute-start.26) | collective-permute-done | bytes 417824 | tf_op jit(solution)/shard_map/ppermute | solution.py:25
  124.2 1.8 %collective-permute-start.29 = (f32[168,768]{1,0:T(8,128)S(1)}, f32[168,768]{1,0:T(8,128)S(1)}, u32[]{:S(2)}, u32[]{:S(2)}) collective-permute-start(f32[168,768]{1,0:T(8,128)S(1)} %stack.25), channel_id=1, source_target_pairs={{0,8},{8,0},{16,24},{24,16},{1,9},{9,1},{17,25},{25,17},{2,10},{10... | collective-permute-start | bytes 1548296 | tf_op jit(solution)/shard_map/ppermute | solution.py:25
  126.1 1.8 %collective-permute-start.28 = (f32[176,768]{1,0:T(8,128)S(1)}, f32[176,768]{1,0:T(8,128)S(1)}, u32[]{:S(2)}, u32[]{:S(2)}) collective-permute-start(f32[176,768]{1,0:T(8,128)S(1)} %stack.24), channel_id=1, source_target_pairs={{0,4},{4,0},{1,5},{5,1},{2,6},{6,2},{3,7},{7,3},{8,12},{12,8},{9,1... | collective-permute-start | bytes 1622024 | tf_op jit(solution)/shard_map/ppermute | solution.py:20
  129.0 3.2 %place.6 = (f32[1024,3072]{1,0:T(8,128)}, f32[768,768]{1,0:T(8,128)S(1)}) custom-call(s32[4]{0:T(128)S(1)} %pad_add_fusion.sel, f32[256,768]{1,0:T(8,128)S(1)} %get-tuple-element.124.refs_0_, f32[256,768]{1,0:T(8,128)S(1)} %get-tuple-element.129.refs_1_, f32[256,768]{1,0:T(8,128)S(1)} %get-tuple-element.128.refs_1_.refs_2_, ...), custom_call_target="tpu_custom_call", output_to_operand_aliasing={{0}: (5, {})} | custom-call | flops 55000000 | bytes 180000 | tf_op jit(solution)/shard_map/place/pallas_call | solution.py:755
  138.5 3.1 %place.8.refs_3_ = f32[1024,3072]{1,0:T(8,128)} custom-call(s32[4]{0:T(128)S(1)} %pad_add_fusion.sel, f32[176,768]{1,0:T(8,128)S(1)} %get-tuple-element.134.refs_2_.refs_0_, f32[176,768]{1,0:T(8,128)S(1)} %get-tuple-element.135.refs_1_, f32[168,768]{1,0:T(8,128)S(1)} %get-tuple-element.136.refs_2_, ...), custom_call_target="tpu_custom_call", output_to_operand_aliasing={{}: (6, {})} | custom-call | flops 55000000 | bytes 180000 | tf_op jit(solution)/shard_map/place/pallas_call | solution.py:755
  141.6 1.8 %place.9 = f32[1024,3072]{1,0:T(8,128)} custom-call(s32[4]{0:T(128)S(1)} %pad_add_fusion.sel, f32[176,768]{1,0:T(8,128)S(1)} %collective-permute-done.31.refs_0_, f32[176,768]{1,0:T(8,128)S(1)} %collective-permute-done.32.refs_1_, f32[168,768]{1,0:T(8,128)S(1)} %collective-permute-done.33.refs_2_, ...), custom_call_target="tpu_custom_call", output_to_operand_aliasing={{}: (4, {})} | custom-call | flops 55000000 | bytes 180000 | tf_op jit(solution)/shard_map/place/pallas_call | solution.py:755
  (100 shorter events, 28.9 us)
Async XLA Ops:
  1.9 6.9 %collective-permute-start = (f32[176,1024]{1,0:T(8,128)S(1)}, f32[176,1024]{1,0:T(8,128)S(1)}, u32[]{:S(2)}, u32[]{:S(2)}) collective-permute-start(f32[176,1024]{1,0:T(8,128)S(1)} %get-tuple-element.77.tok0.refs_0_), channel_id=1, source_target_pairs={{0,1},{1,0},{2,3},{3,2},{4,5},{5,4},{6,7},{7,6},{8,9},{9,8},{10,11... | collective-permute-start | bytes 2162696 | tf_op jit(solution)/shard_map/ppermute | solution.py:20
  2.4 8.7 %collective-permute-start.1 = (f32[32,1024]{1,0:T(8,128)S(1)}, f32[32,1024]{1,0:T(8,128)S(1)}, u32[]{:S(2)}, u32[]{:S(2)}) collective-permute-start(f32[32,1024]{1,0:T(8,128)S(1)} %slice_bitcast_fusion.2), channel_id=1, source_target_pairs={{0,2},{2,0},{1,3},{3,1},{4,6},{6,4},{5,7},{7,5},{8,10},{10,8},{9,1... | collective-permute-start | bytes 393224 | tf_op jit(solution)/shard_map/ppermute | solution.py:20
  5.0 9.7 %collective-permute-start.3 = (f32[64,1024]{1,0:T(8,128)S(1)}, f32[64,1024]{1,0:T(8,128)S(1)}, u32[]{:S(2)}, u32[]{:S(2)}) collective-permute-start(f32[64,1024]{1,0:T(8,128)S(1)} %slice_bitcast_fusion.1), channel_id=1, source_target_pairs={{0,2},{2,0},{1,3},{3,1},{4,6},{6,4},{5,7},{7,5},{8,10},{10,8},{9,1... | collective-permute-start | bytes 786440 | tf_op jit(solution)/shard_map/ppermute | solution.py:20
  12.3 10.5 %collective-permute-start.5 = (f32[80,1024]{1,0:T(8,128)S(1)}, f32[80,1024]{1,0:T(8,128)S(1)}, u32[]{:S(2)}, u32[]{:S(2)}) collective-permute-start(f32[80,1024]{1,0:T(8,128)S(1)} %slice_bitcast_fusion), channel_id=1, source_target_pairs={{0,2},{2,0},{1,3},{3,1},{4,6},{6,4},{5,7},{7,5},{8,10},{10,8},{9,1... | collective-permute-start | bytes 983048 | tf_op jit(solution)/shard_map/ppermute | solution.py:20
  15.3 16.5 %collective-permute-start.8 = (f32[352,256]{1,0:T(8,128)S(1)}, f32[352,256]{1,0:T(8,128)S(1)}, u32[]{:S(2)}, u32[]{:S(2)}) collective-permute-start(f32[352,256]{1,0:T(8,128)S(1)} %pack_cot.1), channel_id=1, source_target_pairs={{0,2},{2,0},{1,3},{3,1},{4,6},{6,4},{5,7},{7,5},{8,10},{10,8},{9,1... | collective-permute-start | bytes 1081352 | tf_op jit(solution)/shard_map/ppermute | solution.py:20
  35.8 12.0 %collective-permute-start.10 = (f32[128,768]{1,0:T(8,128)S(1)}, f32[128,768]{1,0:T(8,128)S(1)}, u32[]{:S(2)}, u32[]{:S(2)}) collective-permute-start(f32[128,768]{1,0:T(8,128)S(1)} %get-tuple-element.106), channel_id=1, source_target_pairs={{0,4},{4,0},{1,5},{5,1},{2,6},{6,2},{3,7},{7,3},{8,12},{12,8},{9,1... | collective-permute-start | bytes 1179656 | tf_op jit(solution)/shard_map/ppermute | solution.py:20
  39.0 17.2 %collective-permute-start.15 = (f32[128,768]{1,0:T(8,128)S(1)}, f32[128,768]{1,0:T(8,128)S(1)}, u32[]{:S(2)}, u32[]{:S(2)}) collective-permute-start(f32[128,768]{1,0:T(8,128)S(1)} %get-tuple-element.107.refs_0_), channel_id=1, source_target_pairs={{0,4},{4,0},{1,5},{5,1},{2,6},{6,2},{3,7},{7,3},{8,12},{12,8},{9,1... | collective-permute-start | bytes 1179656 | tf_op jit(solution)/shard_map/ppermute | solution.py:20
  43.6 6.4 %collective-permute-start.9 = (f32[360,1280]{1,0:T(8,128)S(1)}, f32[360,1280]{1,0:T(8,128)S(1)}, u32[]{:S(2)}, u32[]{:S(2)}) collective-permute-start(f32[360,1280]{1,0:T(8,128)S(1)} %get-tuple-element.104.refs_2_.refs_0_), channel_id=1, source_target_pairs={{0,1},{1,0},{2,3},{3,2},{4,5},{5,4},{6,7},{7,6},{8,9},{9,8},{10,11... | collective-permute-start | bytes 5529608 | tf_op jit(solution)/shard_map/ppermute | solution.py:20
  45.5 19.2 %collective-permute-start.13 = (f32[128,768]{1,0:T(8,128)S(1)}, f32[128,768]{1,0:T(8,128)S(1)}, u32[]{:S(2)}, u32[]{:S(2)}) collective-permute-start(f32[128,768]{1,0:T(8,128)S(1)} %get-tuple-element.115), channel_id=1, source_target_pairs={{0,4},{4,0},{1,5},{5,1},{2,6},{6,2},{3,7},{7,3},{8,12},{12,8},{9,1... | collective-permute-start | bytes 1179656 | tf_op jit(solution)/shard_map/ppermute | solution.py:20
  47.9 11.0 %collective-permute-start.16 = (f32[128,768]{1,0:T(8,128)S(1)}, f32[128,768]{1,0:T(8,128)S(1)}, u32[]{:S(2)}, u32[]{:S(2)}) collective-permute-start(f32[128,768]{1,0:T(8,128)S(1)} %add.10.refs_0_), channel_id=1, source_target_pairs={{0,8},{8,0},{16,24},{24,16},{1,9},{9,1},{17,25},{25,17},{2,10},{10... | collective-permute-start | bytes 1179656 | tf_op jit(solution)/shard_map/ppermute | solution.py:25
  50.8 33.4 %collective-permute-start.11 = (f32[176,1536]{1,0:T(8,128)S(1)}, f32[176,1536]{1,0:T(8,128)S(1)}, u32[]{:S(2)}, u32[]{:S(2)}) collective-permute-start(f32[176,1536]{1,0:T(8,128)S(1)} %get-tuple-element.110.refs_0_), channel_id=1, source_target_pairs={{0,2},{2,0},{1,3},{3,1},{4,6},{6,4},{5,7},{7,5},{8,10},{10,8},{9,1... | collective-permute-start | bytes 3244040 | tf_op jit(solution)/shard_map/ppermute | solution.py:20
  52.4 20.2 %collective-permute-start.12 = (f32[128,768]{1,0:T(8,128)S(1)}, f32[128,768]{1,0:T(8,128)S(1)}, u32[]{:S(2)}, u32[]{:S(2)}) collective-permute-start(f32[128,768]{1,0:T(8,128)S(1)} %get-tuple-element.108.refs_1_), channel_id=1, source_target_pairs={{0,4},{4,0},{1,5},{5,1},{2,6},{6,2},{3,7},{7,3},{8,12},{12,8},{9,1... | collective-permute-start | bytes 1179656 | tf_op jit(solution)/shard_map/ppermute | solution.py:20
  59.0 13.9 %collective-permute-start.17 = (f32[128,768]{1,0:T(8,128)S(1)}, f32[128,768]{1,0:T(8,128)S(1)}, u32[]{:S(2)}, u32[]{:S(2)}) collective-permute-start(f32[128,768]{1,0:T(8,128)S(1)} %add.13), channel_id=1, source_target_pairs={{0,24},{8,16},{16,8},{24,0},{1,25},{9,17},{17,9},{25,1},{2,26},{10... | collective-permute-start | bytes 1179656 | tf_op jit(solution)/shard_map/ppermute | solution.py:25
  64.7 14.7 %collective-permute-start.14 = (f32[128,768]{1,0:T(8,128)S(1)}, f32[128,768]{1,0:T(8,128)S(1)}, u32[]{:S(2)}, u32[]{:S(2)}) collective-permute-start(f32[128,768]{1,0:T(8,128)S(1)} %add.11), channel_id=1, source_target_pairs={{0,8},{8,0},{16,24},{24,16},{1,9},{9,1},{17,25},{25,17},{2,10},{10... | collective-permute-start | bytes 1179656 | tf_op jit(solution)/shard_map/ppermute | solution.py:25
  79.5 11.6 %collective-permute-start.18 = (f32[136,768]{1,0:T(8,128)S(1)}, f32[136,768]{1,0:T(8,128)S(1)}, u32[]{:S(2)}, u32[]{:S(2)}) collective-permute-start(f32[136,768]{1,0:T(8,128)S(1)} %finish.1.both_ref.refs_0_), channel_id=1, source_target_pairs={{0,2},{2,0},{1,3},{3,1},{4,6},{6,4},{5,7},{7,5},{8,10},{10,8},{9,1... | collective-permute-start | bytes 1253384 | tf_op jit(solution)/shard_map/ppermute | solution.py:20
  80.6 14.4 %collective-permute-start.19 = (f32[136,768]{1,0:T(8,128)S(1)}, f32[136,768]{1,0:T(8,128)S(1)}, u32[]{:S(2)}, u32[]{:S(2)}) collective-permute-start(f32[136,768]{1,0:T(8,128)S(1)} %finish.1.both_ref.refs_0_), channel_id=1, source_target_pairs={{0,24},{8,16},{16,8},{24,0},{1,25},{9,17},{17,9},{25,1},{2,26},{10... | collective-permute-start | bytes 1253384 | tf_op jit(solution)/shard_map/ppermute | solution.py:25
  84.2 18.6 %collective-permute-start.20 = (f32[136,768]{1,0:T(8,128)S(1)}, f32[136,768]{1,0:T(8,128)S(1)}, u32[]{:S(2)}, u32[]{:S(2)}) collective-permute-start(f32[136,768]{1,0:T(8,128)S(1)} %finish.1.both_ref.refs_0_), channel_id=1, source_target_pairs={{0,8},{8,0},{16,24},{24,16},{1,9},{9,1},{17,25},{25,17},{2,10},{10... | collective-permute-start | bytes 1253384 | tf_op jit(solution)/shard_map/ppermute | solution.py:25
  84.2 18.6 %collective-permute-start.22 = (f32[136,768]{1,0:T(8,128)S(1)}, f32[136,768]{1,0:T(8,128)S(1)}, u32[]{:S(2)}, u32[]{:S(2)}) collective-permute-start(f32[136,768]{1,0:T(8,128)S(1)} %finish.1.both_ref.refs_0_), channel_id=1, source_target_pairs={{0,4},{4,0},{1,5},{5,1},{2,6},{6,2},{3,7},{7,3},{8,12},{12,8},{9,1... | collective-permute-start | bytes 1253384 | tf_op jit(solution)/shard_map/ppermute | solution.py:20
  91.1 12.7 %collective-permute-start.21 = (f32[136,768]{1,0:T(8,128)S(1)}, f32[136,768]{1,0:T(8,128)S(1)}, u32[]{:S(2)}, u32[]{:S(2)}) collective-permute-start(f32[136,768]{1,0:T(8,128)S(1)} %hold.10.px0_ref.refs_1_), channel_id=1, source_target_pairs={{0,4},{4,0},{1,5},{5,1},{2,6},{6,2},{3,7},{7,3},{8,12},{12,8},{9,1... | collective-permute-start | bytes 1253384 | tf_op jit(solution)/shard_map/ppermute | solution.py:20
  103.9 20.3 %collective-permute-start.24 = (f32[256,768]{1,0:T(8,128)S(1)}, f32[256,768]{1,0:T(8,128)S(1)}, u32[]{:S(2)}, u32[]{:S(2)}) collective-permute-start(f32[256,768]{1,0:T(8,128)S(1)} %get-tuple-element.124.refs_0_), channel_id=1, source_target_pairs={{0,2},{2,0},{1,3},{3,1},{4,6},{6,4},{5,7},{7,5},{8,10},{10,8},{9,1... | collective-permute-start | bytes 2359304 | tf_op jit(solution)/shard_map/ppermute | solution.py:20
  104.5 19.7 %collective-permute-start.25 = (f32[256,768]{1,0:T(8,128)S(1)}, f32[256,768]{1,0:T(8,128)S(1)}, u32[]{:S(2)}, u32[]{:S(2)}) collective-permute-start(f32[256,768]{1,0:T(8,128)S(1)} %get-tuple-element.124.refs_0_), channel_id=1, source_target_pairs={{0,4},{4,0},{1,5},{5,1},{2,6},{6,2},{3,7},{7,3},{8,12},{12,8},{9,1... | collective-permute-start | bytes 2359304 | tf_op jit(solution)/shard_map/ppermute | solution.py:20
  104.8 13.7 %collective-permute-start.23 = (f32[136,768]{1,0:T(8,128)S(1)}, f32[136,768]{1,0:T(8,128)S(1)}, u32[]{:S(2)}, u32[]{:S(2)}) collective-permute-start(f32[136,768]{1,0:T(8,128)S(1)} %get-tuple-element.123.refs_0_), channel_id=1, source_target_pairs={{0,8},{8,0},{16,24},{24,16},{1,9},{9,1},{17,25},{25,17},{2,10},{10... | collective-permute-start | bytes 1253384 | tf_op jit(solution)/shard_map/ppermute | solution.py:25
  106.5 17.6 %collective-permute-start.26 = (f32[136,768]{1,0:T(8,128)S(1)}, f32[136,768]{1,0:T(8,128)S(1)}, u32[]{:S(2)}, u32[]{:S(2)}) collective-permute-start(f32[136,768]{1,0:T(8,128)S(1)} %get-tuple-element.125), channel_id=1, source_target_pairs={{0,24},{8,16},{16,8},{24,0},{1,25},{9,17},{17,9},{25,1},{2,26},{10... | collective-permute-start | bytes 1253384 | tf_op jit(solution)/shard_map/ppermute | solution.py:25
  109.6 19.4 %collective-permute-start.30 = (f32[512,768]{1,0:T(8,128)S(1)}, f32[512,768]{1,0:T(8,128)S(1)}, u32[]{:S(2)}, u32[]{:S(2)}) collective-permute-start(f32[512,768]{1,0:T(8,128)S(1)} %get-tuple-element.126.refs_4_.refs_0_), channel_id=1, source_target_pairs={{0,1},{1,0},{2,3},{3,2},{4,5},{5,4},{6,7},{7,6},{8,9},{9,8},{10,11... | collective-permute-start | bytes 4718600 | tf_op jit(solution)/shard_map/ppermute | solution.py:20
  124.2 11.0 %collective-permute-start.29 = (f32[168,768]{1,0:T(8,128)S(1)}, f32[168,768]{1,0:T(8,128)S(1)}, u32[]{:S(2)}, u32[]{:S(2)}) collective-permute-start(f32[168,768]{1,0:T(8,128)S(1)} %stack.25), channel_id=1, source_target_pairs={{0,8},{8,0},{16,24},{24,16},{1,9},{9,1},{17,25},{25,17},{2,10},{10... | collective-permute-start | bytes 1548296 | tf_op jit(solution)/shard_map/ppermute | solution.py:25
  126.1 9.7 %collective-permute-start.28 = (f32[176,768]{1,0:T(8,128)S(1)}, f32[176,768]{1,0:T(8,128)S(1)}, u32[]{:S(2)}, u32[]{:S(2)}) collective-permute-start(f32[176,768]{1,0:T(8,128)S(1)} %stack.24), channel_id=1, source_target_pairs={{0,4},{4,0},{1,5},{5,1},{2,6},{6,2},{3,7},{7,3},{8,12},{12,8},{9,1... | collective-permute-start | bytes 1622024 | tf_op jit(solution)/shard_map/ppermute | solution.py:20
  127.9 9.4 %collective-permute-start.27 = (f32[176,768]{1,0:T(8,128)S(1)}, f32[176,768]{1,0:T(8,128)S(1)}, u32[]{:S(2)}, u32[]{:S(2)}) collective-permute-start(f32[176,768]{1,0:T(8,128)S(1)} %stack.23), channel_id=1, source_target_pairs={{0,2},{2,0},{1,3},{3,1},{4,6},{6,4},{5,7},{7,5},{8,10},{10,8},{9,1... | collective-permute-start | bytes 1622024 | tf_op jit(solution)/shard_map/ppermute | solution.py:20
  132.2 6.3 %collective-permute-start.34 = (f32[768,768]{1,0:T(8,128)S(1)}, f32[768,768]{1,0:T(8,128)S(1)}, u32[]{:S(2)}, u32[]{:S(2)}) collective-permute-start(f32[768,768]{1,0:T(8,128)S(1)} %get-tuple-element.137.refs_0_), channel_id=1, source_target_pairs={{0,1},{1,0},{2,3},{3,2},{4,5},{5,4},{6,7},{7,6},{8,9},{9,8},{10,11... | collective-permute-start | bytes 7077896 | tf_op jit(solution)/shard_map/ppermute | solution.py:20
  133.9 4.6 %collective-permute-start.35 = (f32[256,768]{1,0:T(8,128)S(1)}, f32[256,768]{1,0:T(8,128)S(1)}, u32[]{:S(2)}, u32[]{:S(2)}) collective-permute-start(f32[256,768]{1,0:T(8,128)S(1)} %get-tuple-element.133.refs_3_.refs_1_), channel_id=1, source_target_pairs={{0,1},{1,0},{2,3},{3,2},{4,5},{5,4},{6,7},{7,6},{8,9},{9,8},{10,11... | collective-permute-start | bytes 2359304 | tf_op jit(solution)/shard_map/ppermute | solution.py:20
  137.3 4.2 %collective-permute-start.31 = (f32[176,768]{1,0:T(8,128)S(1)}, f32[176,768]{1,0:T(8,128)S(1)}, u32[]{:S(2)}, u32[]{:S(2)}) collective-permute-start(f32[176,768]{1,0:T(8,128)S(1)} %get-tuple-element.134.refs_2_.refs_0_), channel_id=1, source_target_pairs={{0,1},{1,0},{2,3},{3,2},{4,5},{5,4},{6,7},{7,6},{8,9},{9,8},{10,11... | collective-permute-start | bytes 1622024 | tf_op jit(solution)/shard_map/ppermute | solution.py:20
  137.3 4.2 %collective-permute-start.32 = (f32[176,768]{1,0:T(8,128)S(1)}, f32[176,768]{1,0:T(8,128)S(1)}, u32[]{:S(2)}, u32[]{:S(2)}) collective-permute-start(f32[176,768]{1,0:T(8,128)S(1)} %get-tuple-element.135.refs_1_), channel_id=1, source_target_pairs={{0,1},{1,0},{2,3},{3,2},{4,5},{5,4},{6,7},{7,6},{8,9},{9,8},{10,11... | collective-permute-start | bytes 1622024 | tf_op jit(solution)/shard_map/ppermute | solution.py:20
  137.8 3.7 %collective-permute-start.33 = (f32[168,768]{1,0:T(8,128)S(1)}, f32[168,768]{1,0:T(8,128)S(1)}, u32[]{:S(2)}, u32[]{:S(2)}) collective-permute-start(f32[168,768]{1,0:T(8,128)S(1)} %get-tuple-element.136.refs_2_), channel_id=1, source_target_pairs={{0,1},{1,0},{2,3},{3,2},{4,5},{5,4},{6,7},{7,6},{8,9},{9,8},{10,11... | collective-permute-start | bytes 1548296 | tf_op jit(solution)/shard_map/ppermute | solution.py:20
  (13 other events, 21.8 us)

commit v4 on v3

--- a/solution.py
+++ b/solution.py
@@ -580,16 +580,16 @@
 
 
 def combine_kernel(sel, mine_ref, got_ref, *refs):
-    keep_ref, send_ref, small_ref = refs[-3:]
-    block, width = keep_ref.shape[0], small_ref.shape[1]
+    keep_grad, keep_out, send_grad, send_out, small_ref = refs[-5:]
+    block, width = keep_grad.shape
     cols = width // 4
-    low = pl.ds(pl.multiple_of(width + sel[1] * cols, cols), cols)
-    high = pl.ds(pl.multiple_of(width + (1 - sel[1]) * cols, cols), cols)
-    for ref, first in ((keep_ref, 0), (send_ref, block)):
+    low = pl.ds(pl.multiple_of(sel[1] * cols, cols), cols)
+    high = pl.ds(pl.multiple_of((1 - sel[1]) * cols, cols), cols)
+    for grad, out, first in ((keep_grad, keep_out, 0), (send_grad, send_out, block)):
         here = slice(first, first + block)
-        ref[:, 0:width] = mine_ref[here, 0:width] + got_ref[here, 0:width]
-        ref[:, low] = mine_ref[here, width:]
-        ref[:, high] = got_ref[here, width:]
+        grad[...] = mine_ref[here, 0:width] + got_ref[here, 0:width]
+        out[:, low] = mine_ref[here, width:]
+        out[:, high] = got_ref[here, width:]
     small_ref[...] = mine_ref[2 * block :, 0:width] + got_ref[2 * block :, 0:width]
 
 
@@ -597,36 +597,50 @@
     block, width = (mine.shape[0] - 8) // 2, mine.shape[1] * 4 // 5
     return pl.pallas_call(
         combine_kernel,
-        out_shape=(shaped((block, width * 3 // 2)),) * 2 + (shaped((8, width)),),
+        out_shape=(shaped((block, width)), shaped((block, width // 2))) * 2 + (shaped((8, width)),),
         in_specs=[smem(), vmem(), vmem()] + [any_spec()] * len(waits),
-        out_specs=(vmem(),) * 3,
+        out_specs=(vmem(),) * 5,
         compiler_params=params(16),
         cost_estimate=cost(0.05),
         name="combine",
     )(sel, mine, got, *waits)
 
 
-def join_kernel(sel, mine_ref, got_ref, out_ref, grad_ref, done_ref):
+def join_grad_kernel(mine_ref, got_ref, grad_ref, done_ref):
     done_ref[...] = jnp.zeros(done_ref.shape, F32)
-    width = out_ref.shape[1]
-    half = width // 2
+    grad_ref[...] = (mine_ref[...] + got_ref[...]).astype(BF16)
+
+
+def join_grad(mine, got):
+    return pl.pallas_call(
+        join_grad_kernel,
+        out_shape=(shaped(mine.shape, BF16), shaped((8, LANES))),
+        in_specs=[vmem()] * 2,
+        out_specs=(vmem(),) * 2,
+        compiler_params=params(8),
+        cost_estimate=cost(0.05),
+        name="join_grad",
+    )(mine, got)
+
+
+def join_out_kernel(sel, mine_ref, got_ref, out_ref):
+    half = mine_ref.shape[1]
     at = pl.multiple_of(sel[0] * half, half)
     other = pl.multiple_of((1 - sel[0]) * half, half)
-    out_ref[:, pl.ds(at, half)] = mine_ref[:, width:].astype(BF16)
-    out_ref[:, pl.ds(other, half)] = got_ref[:, width:].astype(BF16)
-    grad_ref[...] = (mine_ref[:, 0:width] + got_ref[:, 0:width]).astype(BF16)
-
-
-def join(sel, mine, got):
-    block, width = mine.shape[0], mine.shape[1] * 2 // 3
-    return pl.pallas_call(
-        join_kernel,
-        out_shape=(shaped((block, width), BF16),) * 2 + (shaped((8, LANES)),),
+    out_ref[:, pl.ds(at, half)] = mine_ref[...].astype(BF16)
+    out_ref[:, pl.ds(other, half)] = got_ref[...].astype(BF16)
+
+
+def join_out(sel, mine, got):
+    block, half = mine.shape
+    return pl.pallas_call(
+        join_out_kernel,
+        out_shape=shaped((block, 2 * half), BF16),
         in_specs=[smem()] + [vmem()] * 2,
-        out_specs=(vmem(),) * 3,
-        compiler_params=params(16),
-        cost_estimate=cost(0.05),
-        name="join",
+        out_specs=vmem(),
+        compiler_params=params(8),
+        cost_estimate=cost(0.05),
+        name="join_out",
     )(sel, mine, got)
 
 
@@ -828,26 +842,27 @@
     dproj, out, dxh, gate_small, s2 = run_backward(
         sel, toks, (cot, cot_sibling, cot_far), far[2:], near[5], gates, normed, rows[0][:1]
     )
-    s3, k2 = run_products(sel, normed, dproj, (rows[0][1], rows[1][0]))
+    s1, s3, k2 = run_products(sel, normed, dproj, (rows[0][2], rows[0][1], rows[1][0]))
     grad_mine, grad_send = run_input(
         sel, toks, (near[1], far[1]), dproj, dxh, out, gate_small, w_mine, gain
     )
-    late = (*rows[0][2:], *rows[1][1:])
+    late = (rows[0][3], *rows[1][1:])
 
     if tuned:
-        s1, s0, k3, k1, k0 = run_products(sel, normed, dproj, late)
+        s0, k3, k1, k0 = run_products(sel, normed, dproj, late)
         q2 = add(k2, swap(s2, "y"), s3, s0, grad_send)
-        r3, r1, r0 = (swap(piece, "y") for piece in (s3, s1, s0))
+        r3 = swap(s3, "y")
+        r0 = swap(add(s0, xor_permute(s1, "z", 1), q2), "y")
         a2 = xor_permute(q2, "z", 1)
         h3 = add(add(k3, r3), a2)
         a3 = xor_permute(h3, "z", 3)
-        kept, sent, small = combine(
+        kept, kept_out, sent, sent_out, small = combine(
             sel, grad_mine, swap(grad_send, "c"), q2, tick(grad_send)
         )
         got = swap(sent, "x")
-        a1 = xor_permute(add(k1, r1, sent), "z", 1)
+        a1 = xor_permute(k1, "z", 1)
         both = finish(k0, r0, a1, a3, small)
-        output, input_grad, joined = join(sel, kept, got)
+        input_grad, joined = join_grad(kept, got)
 
         px0, z3, z1, py0 = (
             swap(both, "x"),
@@ -857,7 +872,10 @@
         )
         (px0,) = hold((px0,), joined)
         corner0 = swap(px0, "y")
-        z3, z1, corner0, py0 = hold((z3, z1, corner0, py0))
+        (sent_out,) = hold((sent_out,), px0)
+        got_out = swap(sent_out, "x")
+        z3, z1, corner0, py0, got_out = hold((z3, z1, corner0, py0, got_out))
+        output = join_out(sel, kept_out, got_out)
         full = part + 8
         z13, zs, cs = second(both, px0, py0, corner0, z1, z3)
         z2, px13, py13 = xor_permute(zs, "z", 1), swap(z13, "x"), swap(z13, "y")
@@ -870,12 +888,12 @@
         ]
         proj_grad, give = place(sel, (both, px0, py0, corner0), own, None, width, 4)
         z2, px13, py13, corner3 = hold((z2, px13, py13, corner3), give)
-        third = 3 * part // 8
-        rest = part - 2 * third
-        px2 = swap(stack((z2, 0, part), (py13, 0, third)), "x")
-        py2 = swap(stack((z2, 0, part), (px13, third, third)), "y")
+        by_x, by_y = part // 4, 3 * part // 8
+        rest = part - by_x - by_y
+        px2 = swap(stack((z2, 0, part), (py13, 0, by_x)), "x")
+        py2 = swap(stack((z2, 0, part), (px13, by_x, by_y)), "y")
         corner12 = xor_permute(
-            stack((corner3, 0, part), (corner0, 2 * third, rest), (corner3, part, 8)), "z", 1
+            stack((corner3, 0, part), (corner0, by_x + by_y, rest), (corner3, part, 8)), "z", 1
         )
         other = given(3, own)
         own = [
@@ -900,11 +918,11 @@
         px2, py2, corner12 = hold((px2, py2, corner12), give)
         own = [
             (0, 0, part, (2, 0), 0, 1, 0),
-            (0, part, third, (1, 1), 0, 1, 0),
+            (0, part, by_x, (1, 1), 0, 1, 0),
             (1, 0, part, (2, 1), 0, 0, 0),
-            (1, part, third, (1, 1), third, 1, 0),
+            (1, part, by_y, (1, 1), by_x, 1, 0),
             (2, 0, part, (2, 1), 0, 1, 0),
-            (2, part, rest, (1, 1), 2 * third, 1, 0),
+            (2, part, rest, (1, 1), by_x + by_y, 1, 0),
         ]
         arrays = (px2, py2, corner12, first_give, swap(give, "c"))
         (proj_grad,) = place(
@@ -916,9 +934,10 @@
         where = [(0, part), (1, part), (2, part + rest), (3, part)]
         small = small_sums((zs, z2, corner12, corner3), where)
     else:
-        s1, s0, k3, k1, k0 = run_products(sel, normed, dproj, late)
-        kept, sent, small = combine(sel, grad_mine, swap(grad_send, "c"))
-        got = swap(sent, "x")
+        s0, k3, k1, k0 = run_products(sel, normed, dproj, late)
+        kept, kept_out, sent, sent_out, small = combine(sel, grad_mine, swap(grad_send, "c"))
+        input_grad, _ = join_grad(kept, swap(sent, "x"))
+        output = join_out(sel, kept_out, swap(sent_out, "x"))
         small = lax.psum(small + swap(small, "x"), ("z", "y"))
         pieces = jnp.stack([s2, s3, s1, s0, k2, k3, k1, k0])
         pieces = lax.psum(pieces, ("z", "y"))
@@ -928,7 +947,6 @@
             proj_grad, give = place(sel, list(held), own, proj_grad, width, 8)
             other = given(0, own)
             (proj_grad,) = place(sel, [swap(give, "c")], other, proj_grad, width, 0)
-        output, input_grad, _ = join(sel, kept, got)
     small = [small[i].reshape(width) for i in range(6)]
     return (output[None], input_grad[None], proj_grad, *small)
 

time: 144 us -> 141 us (0.979)
  waiting for transfers between devices: 61.9 us -> 55.1 us
  starting transfers between devices: 37.1 us -> 40.1 us
    ppermute x28, waiting for transfers between devices: 25.5 us -> 15.7 us  [swap(): return lax.ppermute(block, axis, SWAP)]
    ppermute x28, starting transfers between devices: 21 us -> 24.6 us  [swap(): return lax.ppermute(block, axis, SWAP)]
    ppermute x8 -> x9, waiting for transfers between devices: 36.3 us -> 39.4 us  [xor_permute(): return lax.ppermute(block, axis, [(i, i ^ distance) for i in range(size)])]
    pallas_call x2 -> x3, Pallas kernels: 2.36 us -> 2.99 us  [the longest x1 1.31 us: join_out(): pl.pallas_call(join_out_kernel, out_shape=shaped((block, 2 * half), BF16)...]
    ppermute x8 -> x9, starting transfers between devices: 16.1 us -> 15.6 us  [xor_permute(): return lax.ppermute(block, axis, [(i, i ^ distance) for i in range(size)])]
  transfers between devices with their start and end apart: 36 -> 37, of which waited for: 19 -> 18; matrix products, arithmetic and copies ran while one was open for 0% -> 0% of each run, Pallas kernels for 23% -> 24%
where the time goes in v4:
time: 141 us; the launch traced here: 140 us
  waiting for transfers between devices  55.1 us (39%)
  starting transfers between devices  40.1 us (28%)
  Pallas kernels  40 us (28%)
  local copies, waits for them, and re-layouts  2.88 us (2%)
    ppermute x9, waiting for transfers between devices, xor_permute(): return lax.ppermute(block, axis, [(i, i ^ distance) for i in range(size)])  39.4 us
    ppermute x28, starting transfers between devices, swap(): return lax.ppermute(block, axis, SWAP)  24.6 us
    ppermute x28, waiting for transfers between devices, swap(): return lax.ppermute(block, axis, SWAP)  15.7 us
    ppermute x9, starting transfers between devices, xor_permute(): return lax.ppermute(block, axis, [(i, i ^ distance) for i in range(size)])  15.6 us
    pallas_call x5, Pallas kernels, place(): pl.pallas_call(functools.partial(place_kernel, where=where, give=give), o...  11.7 us
    pallas_call x1, Pallas kernels, run_forward(): pl.pallas_call(forward_kernel, out_shape=(shaped((length // 2, width), BF...  7.21 us
    pallas_call x1, Pallas kernels, run_input(): pl.pallas_call(functools.partial(input_kernel, count=len(toks)), out_shap...  4.5 us
    pallas_call x1, Pallas kernels, run_backward(): pl.pallas_call(functools.partial(backward_kernel, rows=rows, count=len(to...  4.11 us
  transfers between devices with their start and end apart: 37, of which 18 were waited for; matrix products, arithmetic and copies ran while one was open for 0% of the time, Pallas kernels for 24%

profile of v4, /device:TPU:0, one launch (start us, length us, event | category | flops | bytes accessed | tf_op | source)
XLA Modules:
  0.0 140.4 jit_solution(10478831546058154438)
XLA Ops:
  2.4 2.6 %collective-permute-start.1 = (f32[32,1024]{1,0:T(8,128)S(1)}, f32[32,1024]{1,0:T(8,128)S(1)}, u32[]{:S(2)}, u32[]{:S(2)}) collective-permute-start(f32[32,1024]{1,0:T(8,128)S(1)} %slice_bitcast_fusion.2), channel_id=1, source_target_pairs={{0,2},{2,0},{1,3},{3,1},{4,6},{6,4},{5,7},{7,5},{8,10},{10,8},{9,1... | collective-permute-start | bytes 393224 | tf_op jit(solution)/shard_map/ppermute | solution.py:20
  5.1 2.8 %copy-done = bf16[1024,3072]{1,0:T(8,128)(2,1)S(1)} copy-done((bf16[1024,3072]{1,0:T(8,128)(2,1)S(1)}, bf16[1024,3072]{1,0:T(8,128)(2,1)}, u32[]{:S(2)}) %copy-start) | copy-done | bytes 6291480
  8.8 2.2 %near_blocks.1 = (bf16[352,1024]{1,0:T(8,128)(2,1)S(1)}, f32[352,256]{1,0:T(8,128)S(1)}, f32[352,256]{1,0:T(8,128)S(1)}, f32[352,256]{1,0:T(8,128)S(1)}, f32[352,256]{1,0:T(8,128)S(1)}, /*index=5*/f32[704,256]{1,0:T(8,128)S(1)}) custom-call(s32[4]{0:T(128)S(1)} %pad_add_fusion.sel, s32[1,8]{1,0:T(1,128)S(1)} %copy-done.8, ...), custom_call_target="tpu_custom_call" | custom-call | flops 55000000 | bytes 180000 | tf_op jit(solution)/shard_map/near_blocks/pallas_call | solution.py:272
  12.3 1.9 %collective-permute-start.5 = (f32[80,1024]{1,0:T(8,128)S(1)}, f32[80,1024]{1,0:T(8,128)S(1)}, u32[]{:S(2)}, u32[]{:S(2)}) collective-permute-start(f32[80,1024]{1,0:T(8,128)S(1)} %slice_bitcast_fusion), channel_id=1, source_target_pairs={{0,2},{2,0},{1,3},{3,1},{4,6},{6,4},{5,7},{7,5},{8,10},{10,8},{9,1... | collective-permute-start | bytes 983048 | tf_op jit(solution)/shard_map/ppermute | solution.py:20
  15.3 1.8 %collective-permute-start.8 = (f32[352,256]{1,0:T(8,128)S(1)}, f32[352,256]{1,0:T(8,128)S(1)}, u32[]{:S(2)}, u32[]{:S(2)}) collective-permute-start(f32[352,256]{1,0:T(8,128)S(1)} %pack_cot.1), channel_id=1, source_target_pairs={{0,2},{2,0},{1,3},{3,1},{4,6},{6,4},{5,7},{7,5},{8,10},{10,8},{9,1... | collective-permute-start | bytes 1081352 | tf_op jit(solution)/shard_map/ppermute | solution.py:20
  18.3 4.5 %collective-permute-done.5.refs_0_ = f32[80,1024]{1,0:T(8,128)S(1)} collective-permute-done((f32[80,1024]{1,0:T(8,128)S(1)}, f32[80,1024]{1,0:T(8,128)S(1)}, u32[]{:S(2)}, u32[]{:S(2)}) %collective-permute-start.5) | collective-permute-done | bytes 327712 | tf_op jit(solution)/shard_map/ppermute | solution.py:20
  22.9 1.6 %collective-permute-done.6.tok1.refs_7_ = f32[80,1024]{1,0:T(8,128)S(1)} collective-permute-done((f32[80,1024]{1,0:T(8,128)S(1)}, f32[80,1024]{1,0:T(8,128)S(1)}, u32[]{:S(2)}, u32[]{:S(2)}) %collective-permute-start.6) | collective-permute-done | bytes 327712 | tf_op jit(solution)/shard_map/ppermute | solution.py:20
  24.5 7.2 %forward_scan.1 = (bf16[352,1024]{1,0:T(8,128)(2,1)S(1)}, f32[352,256]{1,0:T(8,128)S(1)}, f32[704,256]{1,0:T(8,128)S(1)}, f32[704,256]{1,0:T(8,128)S(1)}, f32[70...) custom-call(s32[4]{0:T(128)S(1)} %pad_add_fusion.sel, f32[80,1024]{1,0:T(8,128)S(1)} %hold.10.tok0.refs_6_, ...), custom_call_target="tpu_custom_call" | custom-call | flops 55000000 | bytes 180000 | tf_op jit(solution)/shard_map/forward_scan/pallas_call | solution.py:362
  31.7 4.1 %backward_scan.1 = (bf16[704,768]{1,0:T(8,128)(2,1)S(1)}, f32[704,256]{1,0:T(8,128)S(1)}, f32[704,256]{1,0:T(8,128)S(1)}, f32[8,256]{1,0:T(8,128)S(1)}, f32[128,768]{1,0:T(8,128)S(1)}) custom-call(s32[4]{0:T(128)S(1)} %pad_add_fusion.sel, f32[176,1024]{1,0:T(8,128)S(1)} %get-tuple-element.79.tok0.refs_0_, f32[176,1024]{1,0:T(8,128)S(1)} %collective-permute-done.tok1.refs_1_, ...), custom_call_target="tpu_custom_call" | custom-call | flops 55000000 | bytes 180000 | tf_op jit(solution)/shard_map/backward_scan/pallas_call | solution.py:479
  35.8 2.0 %collective-permute-start.10 = (f32[128,768]{1,0:T(8,128)S(1)}, f32[128,768]{1,0:T(8,128)S(1)}, u32[]{:S(2)}, u32[]{:S(2)}) collective-permute-start(f32[128,768]{1,0:T(8,128)S(1)} %get-tuple-element.108), channel_id=1, source_target_pairs={{0,4},{4,0},{1,5},{5,1},{2,6},{6,2},{3,7},{7,3},{8,12},{12,8},{9,1... | collective-permute-start | bytes 1179656 | tf_op jit(solution)/shard_map/ppermute | solution.py:20
  39.4 2.0 %collective-permute-start.11 = (f32[128,768]{1,0:T(8,128)S(1)}, f32[128,768]{1,0:T(8,128)S(1)}, u32[]{:S(2)}, u32[]{:S(2)}) collective-permute-start(f32[128,768]{1,0:T(8,128)S(1)} %get-tuple-element.113), channel_id=1, source_target_pairs={{0,8},{8,0},{16,24},{24,16},{1,9},{9,1},{17,25},{25,17},{2,10},{10... | collective-permute-start | bytes 1179656 | tf_op jit(solution)/shard_map/ppermute | solution.py:25
  41.4 1.6 %products.3 = (f32[128,768]{1,0:T(8,128)S(1)}, f32[128,768]{1,0:T(8,128)S(1)}, f32[128,768]{1,0:T(8,128)S(1)}, f32[128,768]{1,0:T(8,128)S(1)}) custom-call(s32[4]{0:T(128)S(1)} %pad_add_fusion.sel, bf16[352,1024]{1,0:T(8,128)(2,1)S(1)} %get-tuple-element.99.refs_19_.near_ref, bf16[352,1024]{1,0:T(8,128)(2,1)S(1)} %get-tuple-element.100.refs_20_.far_ref, ...), custom_call_target="tpu_custom_call" | custom-call | flops 55000000 | bytes 180000 | tf_op jit(solution)/shard_map/products/pallas_call | solution.py:502
  43.0 4.5 %input_side.1 = (f32[360,1280]{1,0:T(8,128)S(1)}, f32[360,1280]{1,0:T(8,128)S(1)}) custom-call(s32[4]{0:T(128)S(1)} %pad_add_fusion.sel, f32[176,1024]{1,0:T(8,128)S(1)} %get-tuple-element.79.tok0.refs_0_, f32[176,1024]{1,0:T(8,128)S(1)} %collective-permute-done.tok1.refs_1_, f32[32,1024]{1,0:T(8,128)S(1)} %hold.8.refs_0_.refs_2_, ...), custom_call_target="tpu_custom_call" | custom-call | flops 55000000 | bytes 180000 | tf_op jit(solution)/shard_map/input_side/pallas_call | solution.py:570
  47.9 2.1 %collective-permute-start.15 = (f32[128,768]{1,0:T(8,128)S(1)}, f32[128,768]{1,0:T(8,128)S(1)}, u32[]{:S(2)}, u32[]{:S(2)}) collective-permute-start(f32[128,768]{1,0:T(8,128)S(1)} %add.10.refs_0_), channel_id=1, source_target_pairs={{0,8},{8,0},{16,24},{24,16},{1,9},{9,1},{17,25},{25,17},{2,10},{10... | collective-permute-start | bytes 1179656 | tf_op jit(solution)/shard_map/ppermute | solution.py:25
  50.9 1.9 %collective-permute-start.12 = (f32[128,768]{1,0:T(8,128)S(1)}, f32[128,768]{1,0:T(8,128)S(1)}, u32[]{:S(2)}, u32[]{:S(2)}) collective-permute-start(f32[128,768]{1,0:T(8,128)S(1)} %add.11), channel_id=1, source_target_pairs={{0,4},{4,0},{1,5},{5,1},{2,6},{6,2},{3,7},{7,3},{8,12},{12,8},{9,1... | collective-permute-start | bytes 1179656 | tf_op jit(solution)/shard_map/ppermute | solution.py:20
  52.9 3.4 %collective-permute-done.14.b_ref = f32[128,768]{1,0:T(8,128)S(1)} collective-permute-done((f32[128,768]{1,0:T(8,128)S(1)}, f32[128,768]{1,0:T(8,128)S(1)}, u32[]{:S(2)}, u32[]{:S(2)}) %collective-permute-start.14) | collective-permute-done | bytes 393248 | tf_op jit(solution)/shard_map/ppermute | solution.py:20
  56.3 3.8 %collective-permute-done.15.b_ref = f32[128,768]{1,0:T(8,128)S(1)} collective-permute-done((f32[128,768]{1,0:T(8,128)S(1)}, f32[128,768]{1,0:T(8,128)S(1)}, u32[]{:S(2)}, u32[]{:S(2)}) %collective-permute-start.15) | collective-permute-done | bytes 393248 | tf_op jit(solution)/shard_map/ppermute | solution.py:25
  60.1 4.1 %collective-permute-start.16 = (f32[128,768]{1,0:T(8,128)S(1)}, f32[128,768]{1,0:T(8,128)S(1)}, u32[]{:S(2)}, u32[]{:S(2)}) collective-permute-start(f32[128,768]{1,0:T(8,128)S(1)} %add.13), channel_id=1, source_target_pairs={{0,24},{8,16},{16,8},{24,0},{1,25},{9,17},{17,9},{25,1},{2,26},{10... | collective-permute-start | bytes 1179656 | tf_op jit(solution)/shard_map/ppermute | solution.py:25
  68.0 9.8 %collective-permute-done.16.a3_ref = f32[128,768]{1,0:T(8,128)S(1)} collective-permute-done((f32[128,768]{1,0:T(8,128)S(1)}, f32[128,768]{1,0:T(8,128)S(1)}, u32[]{:S(2)}, u32[]{:S(2)}) %collective-permute-start.16) | collective-permute-done | bytes 393248 | tf_op jit(solution)/shard_map/ppermute | solution.py:25
  81.0 2.0 %collective-permute-start.18 = (f32[136,768]{1,0:T(8,128)S(1)}, f32[136,768]{1,0:T(8,128)S(1)}, u32[]{:S(2)}, u32[]{:S(2)}) collective-permute-start(f32[136,768]{1,0:T(8,128)S(1)} %finish.1.both_ref.refs_0_), channel_id=1, source_target_pairs={{0,8},{8,0},{16,24},{24,16},{1,9},{9,1},{17,25},{25,17},{2,10},{10... | collective-permute-start | bytes 1253384 | tf_op jit(solution)/shard_map/ppermute | solution.py:25
  83.0 1.6 %collective-permute-start.22 = (f32[136,768]{1,0:T(8,128)S(1)}, f32[136,768]{1,0:T(8,128)S(1)}, u32[]{:S(2)}, u32[]{:S(2)}) collective-permute-start(f32[136,768]{1,0:T(8,128)S(1)} %finish.1.both_ref.refs_0_), channel_id=1, source_target_pairs={{0,4},{4,0},{1,5},{5,1},{2,6},{6,2},{3,7},{7,3},{8,12},{12,8},{9,1... | collective-permute-start | bytes 1253384 | tf_op jit(solution)/shard_map/ppermute | solution.py:20
  85.4 3.3 %collective-permute-done.19.refs_0_ = f32[136,768]{1,0:T(8,128)S(1)} collective-permute-done((f32[136,768]{1,0:T(8,128)S(1)}, f32[136,768]{1,0:T(8,128)S(1)}, u32[]{:S(2)}, u32[]{:S(2)}) %collective-permute-start.19) | collective-permute-done | bytes 417824 | tf_op jit(solution)/shard_map/ppermute | solution.py:20
  88.7 1.6 %collective-permute-start.21 = (f32[136,768]{1,0:T(8,128)S(1)}, f32[136,768]{1,0:T(8,128)S(1)}, u32[]{:S(2)}, u32[]{:S(2)}) collective-permute-start(f32[136,768]{1,0:T(8,128)S(1)} %hold.11.refs_1_.px0_ref), channel_id=1, source_target_pairs={{0,4},{4,0},{1,5},{5,1},{2,6},{6,2},{3,7},{7,3},{8,12},{12,8},{9,1... | collective-permute-start | bytes 1253384 | tf_op jit(solution)/shard_map/ppermute | solution.py:20
  91.7 2.2 %collective-permute-done.17.refs_0_ = f32[136,768]{1,0:T(8,128)S(1)} collective-permute-done((f32[136,768]{1,0:T(8,128)S(1)}, f32[136,768]{1,0:T(8,128)S(1)}, u32[]{:S(2)}, u32[]{:S(2)}) %collective-permute-start.17) | collective-permute-done | bytes 417824 | tf_op jit(solution)/shard_map/ppermute | solution.py:25
  93.9 5.3 %collective-permute-done.18.refs_1_ = f32[136,768]{1,0:T(8,128)S(1)} collective-permute-done((f32[136,768]{1,0:T(8,128)S(1)}, f32[136,768]{1,0:T(8,128)S(1)}, u32[]{:S(2)}, u32[]{:S(2)}) %collective-permute-start.18) | collective-permute-done | bytes 417824 | tf_op jit(solution)/shard_map/ppermute | solution.py:25
  103.2 2.5 %collective-permute-start.27 = (f32[136,768]{1,0:T(8,128)S(1)}, f32[136,768]{1,0:T(8,128)S(1)}, u32[]{:S(2)}, u32[]{:S(2)}) collective-permute-start(f32[136,768]{1,0:T(8,128)S(1)} %get-tuple-element.129), channel_id=1, source_target_pairs={{0,24},{8,16},{16,8},{24,0},{1,25},{9,17},{17,9},{25,1},{2,26},{10... | collective-permute-start | bytes 1253384 | tf_op jit(solution)/shard_map/ppermute | solution.py:25
  105.7 2.0 %place.5 = (f32[1024,3072]{1,0:T(8,128)}, f32[512,768]{1,0:T(8,128)S(1)}) custom-call(s32[4]{0:T(128)S(1)} %pad_add_fusion.sel, f32[136,768]{1,0:T(8,128)S(1)} %finish.1.both_ref.refs_0_, f32[136,768]{1,0:T(8,128)S(1)} %hold.11.refs_1_.px0_ref, f32[136,768]{1,0:T(8,128)S(1)} %get-tuple-element.123.py0_ref.refs_2_, ...), custom_call_target="tpu_custom_call" | custom-call | flops 55000000 | bytes 180000 | tf_op jit(solution)/shard_map/place/pallas_call | solution.py:769
  107.8 5.9 %collective-permute-done.24.refs_0_ = f32[136,768]{1,0:T(8,128)S(1)} collective-permute-done((f32[136,768]{1,0:T(8,128)S(1)}, f32[136,768]{1,0:T(8,128)S(1)}, u32[]{:S(2)}, u32[]{:S(2)}) %collective-permute-start.24) | collective-permute-done | bytes 417824 | tf_op jit(solution)/shard_map/ppermute | solution.py:25
  113.7 9.2 %collective-permute-done.27.refs_3_ = f32[136,768]{1,0:T(8,128)S(1)} collective-permute-done((f32[136,768]{1,0:T(8,128)S(1)}, f32[136,768]{1,0:T(8,128)S(1)}, u32[]{:S(2)}, u32[]{:S(2)}) %collective-permute-start.27) | collective-permute-done | bytes 417824 | tf_op jit(solution)/shard_map/ppermute | solution.py:25
  125.0 3.2 %place.6 = (f32[1024,3072]{1,0:T(8,128)}, f32[768,768]{1,0:T(8,128)S(1)}) custom-call(s32[4]{0:T(128)S(1)} %pad_add_fusion.sel, f32[256,768]{1,0:T(8,128)S(1)} %get-tuple-element.128.refs_0_, f32[256,768]{1,0:T(8,128)S(1)} %get-tuple-element.133.refs_1_, f32[256,768]{1,0:T(8,128)S(1)} %get-tuple-element.132.refs_1_.refs_2_, ...), custom_call_target="tpu_custom_call", output_to_operand_aliasing={{0}: (5, {})} | custom-call | flops 55000000 | bytes 180000 | tf_op jit(solution)/shard_map/place/pallas_call | solution.py:769
  135.4 3.1 %place.8.refs_3_ = f32[1024,3072]{1,0:T(8,128)} custom-call(s32[4]{0:T(128)S(1)} %pad_add_fusion.sel, f32[160,768]{1,0:T(8,128)S(1)} %get-tuple-element.138.refs_2_.refs_0_, f32[176,768]{1,0:T(8,128)S(1)} %get-tuple-element.139.refs_1_, f32[184,768]{1,0:T(8,128)S(1)} %get-tuple-element.140.refs_2_, ...), custom_call_target="tpu_custom_call", output_to_operand_aliasing={{}: (6, {})} | custom-call | flops 55000000 | bytes 180000 | tf_op jit(solution)/shard_map/place/pallas_call | solution.py:769
  138.5 1.8 %place.9 = f32[1024,3072]{1,0:T(8,128)} custom-call(s32[4]{0:T(128)S(1)} %pad_add_fusion.sel, f32[160,768]{1,0:T(8,128)S(1)} %collective-permute-done.32.refs_0_, f32[176,768]{1,0:T(8,128)S(1)} %collective-permute-done.33.refs_1_, f32[184,768]{1,0:T(8,128)S(1)} %collective-permute-done.34.refs_2_, ...), custom_call_target="tpu_custom_call", output_to_operand_aliasing={{}: (4, {})} | custom-call | flops 55000000 | bytes 180000 | tf_op jit(solution)/shard_map/place/pallas_call | solution.py:769
  (104 shorter events, 31.6 us)
Async XLA Ops:
  1.9 6.9 %collective-permute-start = (f32[176,1024]{1,0:T(8,128)S(1)}, f32[176,1024]{1,0:T(8,128)S(1)}, u32[]{:S(2)}, u32[]{:S(2)}) collective-permute-start(f32[176,1024]{1,0:T(8,128)S(1)} %get-tuple-element.79.tok0.refs_0_), channel_id=1, source_target_pairs={{0,1},{1,0},{2,3},{3,2},{4,5},{5,4},{6,7},{7,6},{8,9},{9,8},{10,11... | collective-permute-start | bytes 2162696 | tf_op jit(solution)/shard_map/ppermute | solution.py:20
  2.4 8.7 %collective-permute-start.1 = (f32[32,1024]{1,0:T(8,128)S(1)}, f32[32,1024]{1,0:T(8,128)S(1)}, u32[]{:S(2)}, u32[]{:S(2)}) collective-permute-start(f32[32,1024]{1,0:T(8,128)S(1)} %slice_bitcast_fusion.2), channel_id=1, source_target_pairs={{0,2},{2,0},{1,3},{3,1},{4,6},{6,4},{5,7},{7,5},{8,10},{10,8},{9,1... | collective-permute-start | bytes 393224 | tf_op jit(solution)/shard_map/ppermute | solution.py:20
  5.0 9.7 %collective-permute-start.3 = (f32[64,1024]{1,0:T(8,128)S(1)}, f32[64,1024]{1,0:T(8,128)S(1)}, u32[]{:S(2)}, u32[]{:S(2)}) collective-permute-start(f32[64,1024]{1,0:T(8,128)S(1)} %slice_bitcast_fusion.1), channel_id=1, source_target_pairs={{0,2},{2,0},{1,3},{3,1},{4,6},{6,4},{5,7},{7,5},{8,10},{10,8},{9,1... | collective-permute-start | bytes 786440 | tf_op jit(solution)/shard_map/ppermute | solution.py:20
  12.3 10.5 %collective-permute-start.5 = (f32[80,1024]{1,0:T(8,128)S(1)}, f32[80,1024]{1,0:T(8,128)S(1)}, u32[]{:S(2)}, u32[]{:S(2)}) collective-permute-start(f32[80,1024]{1,0:T(8,128)S(1)} %slice_bitcast_fusion), channel_id=1, source_target_pairs={{0,2},{2,0},{1,3},{3,1},{4,6},{6,4},{5,7},{7,5},{8,10},{10,8},{9,1... | collective-permute-start | bytes 983048 | tf_op jit(solution)/shard_map/ppermute | solution.py:20
  15.3 16.5 %collective-permute-start.8 = (f32[352,256]{1,0:T(8,128)S(1)}, f32[352,256]{1,0:T(8,128)S(1)}, u32[]{:S(2)}, u32[]{:S(2)}) collective-permute-start(f32[352,256]{1,0:T(8,128)S(1)} %pack_cot.1), channel_id=1, source_target_pairs={{0,2},{2,0},{1,3},{3,1},{4,6},{6,4},{5,7},{7,5},{8,10},{10,8},{9,1... | collective-permute-start | bytes 1081352 | tf_op jit(solution)/shard_map/ppermute | solution.py:20
  35.8 12.0 %collective-permute-start.10 = (f32[128,768]{1,0:T(8,128)S(1)}, f32[128,768]{1,0:T(8,128)S(1)}, u32[]{:S(2)}, u32[]{:S(2)}) collective-permute-start(f32[128,768]{1,0:T(8,128)S(1)} %get-tuple-element.108), channel_id=1, source_target_pairs={{0,4},{4,0},{1,5},{5,1},{2,6},{6,2},{3,7},{7,3},{8,12},{12,8},{9,1... | collective-permute-start | bytes 1179656 | tf_op jit(solution)/shard_map/ppermute | solution.py:20
  39.3 17.0 %collective-permute-start.14 = (f32[128,768]{1,0:T(8,128)S(1)}, f32[128,768]{1,0:T(8,128)S(1)}, u32[]{:S(2)}, u32[]{:S(2)}) collective-permute-start(f32[128,768]{1,0:T(8,128)S(1)} %get-tuple-element.109.refs_0_), channel_id=1, source_target_pairs={{0,4},{4,0},{1,5},{5,1},{2,6},{6,2},{3,7},{7,3},{8,12},{12,8},{9,1... | collective-permute-start | bytes 1179656 | tf_op jit(solution)/shard_map/ppermute | solution.py:20
  39.4 11.5 %collective-permute-start.11 = (f32[128,768]{1,0:T(8,128)S(1)}, f32[128,768]{1,0:T(8,128)S(1)}, u32[]{:S(2)}, u32[]{:S(2)}) collective-permute-start(f32[128,768]{1,0:T(8,128)S(1)} %get-tuple-element.113), channel_id=1, source_target_pairs={{0,8},{8,0},{16,24},{24,16},{1,9},{9,1},{17,25},{25,17},{2,10},{10... | collective-permute-start | bytes 1179656 | tf_op jit(solution)/shard_map/ppermute | solution.py:25
  47.9 12.2 %collective-permute-start.15 = (f32[128,768]{1,0:T(8,128)S(1)}, f32[128,768]{1,0:T(8,128)S(1)}, u32[]{:S(2)}, u32[]{:S(2)}) collective-permute-start(f32[128,768]{1,0:T(8,128)S(1)} %add.10.refs_0_), channel_id=1, source_target_pairs={{0,8},{8,0},{16,24},{24,16},{1,9},{9,1},{17,25},{25,17},{2,10},{10... | collective-permute-start | bytes 1179656 | tf_op jit(solution)/shard_map/ppermute | solution.py:25
  50.0 14.2 %collective-permute-start.9 = (f32[360,1280]{1,0:T(8,128)S(1)}, f32[360,1280]{1,0:T(8,128)S(1)}, u32[]{:S(2)}, u32[]{:S(2)}) collective-permute-start(f32[360,1280]{1,0:T(8,128)S(1)} %get-tuple-element.106.refs_2_.refs_0_), channel_id=1, source_target_pairs={{0,1},{1,0},{2,3},{3,2},{4,5},{5,4},{6,7},{7,6},{8,9},{9,8},{10,11... | collective-permute-start | bytes 5529608 | tf_op jit(solution)/shard_map/ppermute | solution.py:20
  50.0 18.0 %collective-permute-start.13 = (f32[128,768]{1,0:T(8,128)S(1)}, f32[128,768]{1,0:T(8,128)S(1)}, u32[]{:S(2)}, u32[]{:S(2)}) collective-permute-start(f32[128,768]{1,0:T(8,128)S(1)} %get-tuple-element.114), channel_id=1, source_target_pairs={{0,8},{8,0},{16,24},{24,16},{1,9},{9,1},{17,25},{25,17},{2,10},{10... | collective-permute-start | bytes 1179656 | tf_op jit(solution)/shard_map/ppermute | solution.py:25
  50.9 17.1 %collective-permute-start.12 = (f32[128,768]{1,0:T(8,128)S(1)}, f32[128,768]{1,0:T(8,128)S(1)}, u32[]{:S(2)}, u32[]{:S(2)}) collective-permute-start(f32[128,768]{1,0:T(8,128)S(1)} %add.11), channel_id=1, source_target_pairs={{0,4},{4,0},{1,5},{5,1},{2,6},{6,2},{3,7},{7,3},{8,12},{12,8},{9,1... | collective-permute-start | bytes 1179656 | tf_op jit(solution)/shard_map/ppermute | solution.py:20
  60.1 17.7 %collective-permute-start.16 = (f32[128,768]{1,0:T(8,128)S(1)}, f32[128,768]{1,0:T(8,128)S(1)}, u32[]{:S(2)}, u32[]{:S(2)}) collective-permute-start(f32[128,768]{1,0:T(8,128)S(1)} %add.13), channel_id=1, source_target_pairs={{0,24},{8,16},{16,8},{24,0},{1,25},{9,17},{17,9},{25,1},{2,26},{10... | collective-permute-start | bytes 1179656 | tf_op jit(solution)/shard_map/ppermute | solution.py:25
  65.1 19.5 %collective-permute-start.20 = (f32[176,1024]{1,0:T(8,128)S(1)}, f32[176,1024]{1,0:T(8,128)S(1)}, u32[]{:S(2)}, u32[]{:S(2)}) collective-permute-start(f32[176,1024]{1,0:T(8,128)S(1)} %get-tuple-element.118), channel_id=1, source_target_pairs={{0,2},{2,0},{1,3},{3,1},{4,6},{6,4},{5,7},{7,5},{8,10},{10,8},{9,1... | collective-permute-start | bytes 2162696 | tf_op jit(solution)/shard_map/ppermute | solution.py:20
  78.0 10.7 %collective-permute-start.19 = (f32[136,768]{1,0:T(8,128)S(1)}, f32[136,768]{1,0:T(8,128)S(1)}, u32[]{:S(2)}, u32[]{:S(2)}) collective-permute-start(f32[136,768]{1,0:T(8,128)S(1)} %finish.1.both_ref.refs_0_), channel_id=1, source_target_pairs={{0,2},{2,0},{1,3},{3,1},{4,6},{6,4},{5,7},{7,5},{8,10},{10,8},{9,1... | collective-permute-start | bytes 1253384 | tf_op jit(solution)/shard_map/ppermute | solution.py:20
  79.5 14.4 %collective-permute-start.17 = (f32[136,768]{1,0:T(8,128)S(1)}, f32[136,768]{1,0:T(8,128)S(1)}, u32[]{:S(2)}, u32[]{:S(2)}) collective-permute-start(f32[136,768]{1,0:T(8,128)S(1)} %finish.1.both_ref.refs_0_), channel_id=1, source_target_pairs={{0,24},{8,16},{16,8},{24,0},{1,25},{9,17},{17,9},{25,1},{2,26},{10... | collective-permute-start | bytes 1253384 | tf_op jit(solution)/shard_map/ppermute | solution.py:25
  81.0 18.2 %collective-permute-start.18 = (f32[136,768]{1,0:T(8,128)S(1)}, f32[136,768]{1,0:T(8,128)S(1)}, u32[]{:S(2)}, u32[]{:S(2)}) collective-permute-start(f32[136,768]{1,0:T(8,128)S(1)} %finish.1.both_ref.refs_0_), channel_id=1, source_target_pairs={{0,8},{8,0},{16,24},{24,16},{1,9},{9,1},{17,25},{25,17},{2,10},{10... | collective-permute-start | bytes 1253384 | tf_op jit(solution)/shard_map/ppermute | solution.py:25
  83.0 16.3 %collective-permute-start.22 = (f32[136,768]{1,0:T(8,128)S(1)}, f32[136,768]{1,0:T(8,128)S(1)}, u32[]{:S(2)}, u32[]{:S(2)}) collective-permute-start(f32[136,768]{1,0:T(8,128)S(1)} %finish.1.both_ref.refs_0_), channel_id=1, source_target_pairs={{0,4},{4,0},{1,5},{5,1},{2,6},{6,2},{3,7},{7,3},{8,12},{12,8},{9,1... | collective-permute-start | bytes 1253384 | tf_op jit(solution)/shard_map/ppermute | solution.py:20
  88.7 11.3 %collective-permute-start.21 = (f32[136,768]{1,0:T(8,128)S(1)}, f32[136,768]{1,0:T(8,128)S(1)}, u32[]{:S(2)}, u32[]{:S(2)}) collective-permute-start(f32[136,768]{1,0:T(8,128)S(1)} %hold.11.refs_1_.px0_ref), channel_id=1, source_target_pairs={{0,4},{4,0},{1,5},{5,1},{2,6},{6,2},{3,7},{7,3},{8,12},{12,8},{9,1... | collective-permute-start | bytes 1253384 | tf_op jit(solution)/shard_map/ppermute | solution.py:20
  90.2 9.0 %collective-permute-start.23 = (f32[176,512]{1,0:T(8,128)S(1)}, f32[176,512]{1,0:T(8,128)S(1)}, u32[]{:S(2)}, u32[]{:S(2)}) collective-permute-start(f32[176,512]{1,0:T(8,128)S(1)} %hold.12), channel_id=1, source_target_pairs={{0,2},{2,0},{1,3},{3,1},{4,6},{6,4},{5,7},{7,5},{8,10},{10,8},{9,1... | collective-permute-start | bytes 1081352 | tf_op jit(solution)/shard_map/ppermute | solution.py:20
  100.1 22.8 %collective-permute-start.25 = (f32[256,768]{1,0:T(8,128)S(1)}, f32[256,768]{1,0:T(8,128)S(1)}, u32[]{:S(2)}, u32[]{:S(2)}) collective-permute-start(f32[256,768]{1,0:T(8,128)S(1)} %get-tuple-element.128.refs_0_), channel_id=1, source_target_pairs={{0,2},{2,0},{1,3},{3,1},{4,6},{6,4},{5,7},{7,5},{8,10},{10,8},{9,1... | collective-permute-start | bytes 2359304 | tf_op jit(solution)/shard_map/ppermute | solution.py:20
  100.6 22.3 %collective-permute-start.26 = (f32[256,768]{1,0:T(8,128)S(1)}, f32[256,768]{1,0:T(8,128)S(1)}, u32[]{:S(2)}, u32[]{:S(2)}) collective-permute-start(f32[256,768]{1,0:T(8,128)S(1)} %get-tuple-element.128.refs_0_), channel_id=1, source_target_pairs={{0,4},{4,0},{1,5},{5,1},{2,6},{6,2},{3,7},{7,3},{8,12},{12,8},{9,1... | collective-permute-start | bytes 2359304 | tf_op jit(solution)/shard_map/ppermute | solution.py:20
  102.1 11.6 %collective-permute-start.24 = (f32[136,768]{1,0:T(8,128)S(1)}, f32[136,768]{1,0:T(8,128)S(1)}, u32[]{:S(2)}, u32[]{:S(2)}) collective-permute-start(f32[136,768]{1,0:T(8,128)S(1)} %get-tuple-element.127.refs_0_), channel_id=1, source_target_pairs={{0,8},{8,0},{16,24},{24,16},{1,9},{9,1},{17,25},{25,17},{2,10},{10... | collective-permute-start | bytes 1253384 | tf_op jit(solution)/shard_map/ppermute | solution.py:25
  103.2 19.7 %collective-permute-start.27 = (f32[136,768]{1,0:T(8,128)S(1)}, f32[136,768]{1,0:T(8,128)S(1)}, u32[]{:S(2)}, u32[]{:S(2)}) collective-permute-start(f32[136,768]{1,0:T(8,128)S(1)} %get-tuple-element.129), channel_id=1, source_target_pairs={{0,24},{8,16},{16,8},{24,0},{1,25},{9,17},{17,9},{25,1},{2,26},{10... | collective-permute-start | bytes 1253384 | tf_op jit(solution)/shard_map/ppermute | solution.py:25
  107.7 17.3 %collective-permute-start.31 = (f32[512,768]{1,0:T(8,128)S(1)}, f32[512,768]{1,0:T(8,128)S(1)}, u32[]{:S(2)}, u32[]{:S(2)}) collective-permute-start(f32[512,768]{1,0:T(8,128)S(1)} %get-tuple-element.130.refs_4_.refs_0_), channel_id=1, source_target_pairs={{0,1},{1,0},{2,3},{3,2},{4,5},{5,4},{6,7},{7,6},{8,9},{9,8},{10,11... | collective-permute-start | bytes 4718600 | tf_op jit(solution)/shard_map/ppermute | solution.py:20
  122.9 11.3 %collective-permute-start.30 = (f32[184,768]{1,0:T(8,128)S(1)}, f32[184,768]{1,0:T(8,128)S(1)}, u32[]{:S(2)}, u32[]{:S(2)}) collective-permute-start(f32[184,768]{1,0:T(8,128)S(1)} %stack.25), channel_id=1, source_target_pairs={{0,8},{8,0},{16,24},{24,16},{1,9},{9,1},{17,25},{25,17},{2,10},{10... | collective-permute-start | bytes 1695752 | tf_op jit(solution)/shard_map/ppermute | solution.py:25
  123.1 10.1 %collective-permute-start.29 = (f32[176,768]{1,0:T(8,128)S(1)}, f32[176,768]{1,0:T(8,128)S(1)}, u32[]{:S(2)}, u32[]{:S(2)}) collective-permute-start(f32[176,768]{1,0:T(8,128)S(1)} %stack.24), channel_id=1, source_target_pairs={{0,4},{4,0},{1,5},{5,1},{2,6},{6,2},{3,7},{7,3},{8,12},{12,8},{9,1... | collective-permute-start | bytes 1622024 | tf_op jit(solution)/shard_map/ppermute | solution.py:20
  123.5 8.9 %collective-permute-start.28 = (f32[160,768]{1,0:T(8,128)S(1)}, f32[160,768]{1,0:T(8,128)S(1)}, u32[]{:S(2)}, u32[]{:S(2)}) collective-permute-start(f32[160,768]{1,0:T(8,128)S(1)} %stack.23), channel_id=1, source_target_pairs={{0,2},{2,0},{1,3},{3,1},{4,6},{6,4},{5,7},{7,5},{8,10},{10,8},{9,1... | collective-permute-start | bytes 1474568 | tf_op jit(solution)/shard_map/ppermute | solution.py:20
  128.2 7.2 %collective-permute-start.35 = (f32[768,768]{1,0:T(8,128)S(1)}, f32[768,768]{1,0:T(8,128)S(1)}, u32[]{:S(2)}, u32[]{:S(2)}) collective-permute-start(f32[768,768]{1,0:T(8,128)S(1)} %get-tuple-element.141.refs_0_), channel_id=1, source_target_pairs={{0,1},{1,0},{2,3},{3,2},{4,5},{5,4},{6,7},{7,6},{8,9},{9,8},{10,11... | collective-permute-start | bytes 7077896 | tf_op jit(solution)/shard_map/ppermute | solution.py:20
  131.2 4.2 %collective-permute-start.36 = (f32[256,768]{1,0:T(8,128)S(1)}, f32[256,768]{1,0:T(8,128)S(1)}, u32[]{:S(2)}, u32[]{:S(2)}) collective-permute-start(f32[256,768]{1,0:T(8,128)S(1)} %get-tuple-element.137.refs_3_.refs_1_), channel_id=1, source_target_pairs={{0,1},{1,0},{2,3},{3,2},{4,5},{5,4},{6,7},{7,6},{8,9},{9,8},{10,11... | collective-permute-start | bytes 2359304 | tf_op jit(solution)/shard_map/ppermute | solution.py:20
  134.3 4.2 %collective-permute-start.34 = (f32[184,768]{1,0:T(8,128)S(1)}, f32[184,768]{1,0:T(8,128)S(1)}, u32[]{:S(2)}, u32[]{:S(2)}) collective-permute-start(f32[184,768]{1,0:T(8,128)S(1)} %get-tuple-element.140.refs_2_), channel_id=1, source_target_pairs={{0,1},{1,0},{2,3},{3,2},{4,5},{5,4},{6,7},{7,6},{8,9},{9,8},{10,11... | collective-permute-start | bytes 1695752 | tf_op jit(solution)/shard_map/ppermute | solution.py:20
  134.3 4.2 %collective-permute-start.33 = (f32[176,768]{1,0:T(8,128)S(1)}, f32[176,768]{1,0:T(8,128)S(1)}, u32[]{:S(2)}, u32[]{:S(2)}) collective-permute-start(f32[176,768]{1,0:T(8,128)S(1)} %get-tuple-element.139.refs_1_), channel_id=1, source_target_pairs={{0,1},{1,0},{2,3},{3,2},{4,5},{5,4},{6,7},{7,6},{8,9},{9,8},{10,11... | collective-permute-start | bytes 1622024 | tf_op jit(solution)/shard_map/ppermute | solution.py:20
  (14 other events, 25.7 us)

commit v5 on v4

--- a/solution.py
+++ b/solution.py
@@ -518,7 +518,7 @@
     block, width = toks[0].shape
     gain = gain_ref[...]
     mine = own_columns(sel, cols)
-    step = 8
+    step = 16
     sums = (jnp.zeros((step, width), F32), jnp.zeros((step, width), F32))
     row = 0
     for tok, (b, first, count) in zip(toks, segments(block)):
@@ -550,7 +550,7 @@
             where[there, 0:width] = rdev * (dxhat - mean1 - xhat * mean2)
             return (carry[0] + dn * xhat, carry[1] + dn)
 
-        sums = lax.fori_loop(0, count // step, body, sums, unroll=11 if count == block else 4)
+        sums = lax.fori_loop(0, count // step, body, sums, unroll=True if count < block else 11)
         to = pl.ds(base, count)
         where[to, mine] += dxh_ref[rows, :]
         where[to, width : width + cols] = out_ref[rows, :]
@@ -839,10 +839,10 @@
         rows = [[[(d, 1)] for d in (2, 3, 1, 0)], [[(d, 0)] for d in (2, 3, 1, 0)]]
     else:
         rows = [[[0], [1], [2], [3]], [[4], [5], [6], [7]]]
-    dproj, out, dxh, gate_small, s2 = run_backward(
-        sel, toks, (cot, cot_sibling, cot_far), far[2:], near[5], gates, normed, rows[0][:1]
+    dproj, out, dxh, gate_small, s2, s1 = run_backward(
+        sel, toks, (cot, cot_sibling, cot_far), far[2:], near[5], gates, normed, (rows[0][0], rows[0][2])
     )
-    s1, s3, k2 = run_products(sel, normed, dproj, (rows[0][2], rows[0][1], rows[1][0]))
+    s3, k2 = run_products(sel, normed, dproj, (rows[0][1], rows[1][0]))
     grad_mine, grad_send = run_input(
         sel, toks, (near[1], far[1]), dproj, dxh, out, gate_small, w_mine, gain
     )
@@ -885,29 +885,31 @@
             (1, 0, part, (0, 0), 0, 1, 0),
             (2, 0, part, (0, 1), 0, 0, 0),
             (3, 0, part, (0, 1), 0, 1, 0),
+            (4, 0, part, (1, 0), 0, 0, 0),
+            (4, part, part, (3, 0), 0, 0, 0),
         ]
-        proj_grad, give = place(sel, (both, px0, py0, corner0), own, None, width, 4)
+        proj_grad, give = place(sel, (both, px0, py0, corner0, z13), own, None, width, 6)
         z2, px13, py13, corner3 = hold((z2, px13, py13, corner3), give)
-        by_x, by_y = part // 4, 3 * part // 8
+        by_x, by_y = 3 * part // 8, 3 * part // 8
         rest = part - by_x - by_y
         px2 = swap(stack((z2, 0, part), (py13, 0, by_x)), "x")
         py2 = swap(stack((z2, 0, part), (px13, by_x, by_y)), "y")
         corner12 = xor_permute(
             stack((corner3, 0, part), (corner0, by_x + by_y, rest), (corner3, part, 8)), "z", 1
         )
-        other = given(3, own)
+        other = given(2, own)
         own = [
             (array, part * i, part, (d, y_off), 0, x_off, 0)
-            for array, y_off, x_off in ((0, 0, 0), (1, 0, 1), (2, 1, 0))
+            for array, y_off, x_off in ((0, 0, 1), (1, 1, 0))
             for i, d in ((0, 1), (1, 3))
         ]
         proj_grad, give = place(
             sel,
-            (z13, px13, py13, swap(give, "c")),
+            (px13, py13, swap(give, "c")),
             own + other,
             proj_grad,
             width,
-            6,
+            4,
             tick(give, corner3),
         )
         other = given(3, own)

time: 141 us -> 139 us (0.986)
  Pallas kernels: 40 us -> 38.3 us
    pallas_call x1, Pallas kernels: 4.5 us -> 2.86 us  [run_input(): pl.pallas_call(functools.partial(input_kernel, count=len(toks)), out_shap...]
  transfers between devices with their start and end apart: 37 -> 37, of which waited for: 18 -> 16; matrix products, arithmetic and copies ran while one was open for 0% -> 0% of each run, Pallas kernels for 24% -> 23%
where the time goes in v5:
time: 139 us
  waiting for transfers between devices  55 us (40%)
  starting transfers between devices  40.2 us (29%)
  Pallas kernels  38.3 us (28%)
  local copies, waits for them, and re-layouts  2.88 us (2%)
    ppermute x9, waiting for transfers between devices, xor_permute(): return lax.ppermute(block, axis, [(i, i ^ distance) for i in range(size)])  38.3 us
    ppermute x28, starting transfers between devices, swap(): return lax.ppermute(block, axis, SWAP)  24.2 us
    ppermute x28, waiting for transfers between devices, swap(): return lax.ppermute(block, axis, SWAP)  16.7 us
    ppermute x9, starting transfers between devices, xor_permute(): return lax.ppermute(block, axis, [(i, i ^ distance) for i in range(size)])  16 us
    pallas_call x5, Pallas kernels, place(): pl.pallas_call(functools.partial(place_kernel, where=where, give=give), o...  11.7 us
    pallas_call x1, Pallas kernels, run_forward(): pl.pallas_call(forward_kernel, out_shape=(shaped((length // 2, width), BF...  7.21 us
    pallas_call x1, Pallas kernels, run_backward(): pl.pallas_call(functools.partial(backward_kernel, rows=rows, count=len(to...  4.33 us
    pallas_call x1, Pallas kernels, run_input(): pl.pallas_call(functools.partial(input_kernel, count=len(toks)), out_shap...  2.86 us
  transfers between devices with their start and end apart: 37, of which 16 were waited for; matrix products, arithmetic and copies ran while one was open for 0% of the time, Pallas kernels for 23%

profile of v5, /device:TPU:0, one launch (start us, length us, event | category | flops | bytes accessed | tf_op | source)
XLA Modules:
  0.0 138.7 jit_solution(8147220045174926379)
XLA Ops:
  2.4 2.6 %collective-permute-start.1 = (f32[32,1024]{1,0:T(8,128)S(1)}, f32[32,1024]{1,0:T(8,128)S(1)}, u32[]{:S(2)}, u32[]{:S(2)}) collective-permute-start(f32[32,1024]{1,0:T(8,128)S(1)} %slice_bitcast_fusion.2), channel_id=1, source_target_pairs={{0,2},{2,0},{1,3},{3,1},{4,6},{6,4},{5,7},{7,5},{8,10},{10,8},{9,1... | collective-permute-start | bytes 393224 | tf_op jit(solution)/shard_map/ppermute | solution.py:20
  5.1 2.8 %copy-done = bf16[1024,3072]{1,0:T(8,128)(2,1)S(1)} copy-done((bf16[1024,3072]{1,0:T(8,128)(2,1)S(1)}, bf16[1024,3072]{1,0:T(8,128)(2,1)}, u32[]{:S(2)}) %copy-start) | copy-done | bytes 6291480
  8.8 2.2 %near_blocks.1 = (bf16[352,1024]{1,0:T(8,128)(2,1)S(1)}, f32[352,256]{1,0:T(8,128)S(1)}, f32[352,256]{1,0:T(8,128)S(1)}, f32[352,256]{1,0:T(8,128)S(1)}, f32[352,256]{1,0:T(8,128)S(1)}, /*index=5*/f32[704,256]{1,0:T(8,128)S(1)}) custom-call(s32[4]{0:T(128)S(1)} %pad_add_fusion.sel, s32[1,8]{1,0:T(1,128)S(1)} %copy-done.8, ...), custom_call_target="tpu_custom_call" | custom-call | flops 55000000 | bytes 180000 | tf_op jit(solution)/shard_map/near_blocks/pallas_call | solution.py:272
  12.3 1.9 %collective-permute-start.5 = (f32[80,1024]{1,0:T(8,128)S(1)}, f32[80,1024]{1,0:T(8,128)S(1)}, u32[]{:S(2)}, u32[]{:S(2)}) collective-permute-start(f32[80,1024]{1,0:T(8,128)S(1)} %slice_bitcast_fusion), channel_id=1, source_target_pairs={{0,2},{2,0},{1,3},{3,1},{4,6},{6,4},{5,7},{7,5},{8,10},{10,8},{9,1... | collective-permute-start | bytes 983048 | tf_op jit(solution)/shard_map/ppermute | solution.py:20
  15.3 1.8 %collective-permute-start.8 = (f32[352,256]{1,0:T(8,128)S(1)}, f32[352,256]{1,0:T(8,128)S(1)}, u32[]{:S(2)}, u32[]{:S(2)}) collective-permute-start(f32[352,256]{1,0:T(8,128)S(1)} %pack_cot.1), channel_id=1, source_target_pairs={{0,2},{2,0},{1,3},{3,1},{4,6},{6,4},{5,7},{7,5},{8,10},{10,8},{9,1... | collective-permute-start | bytes 1081352 | tf_op jit(solution)/shard_map/ppermute | solution.py:20
  18.3 4.5 %collective-permute-done.5.refs_0_ = f32[80,1024]{1,0:T(8,128)S(1)} collective-permute-done((f32[80,1024]{1,0:T(8,128)S(1)}, f32[80,1024]{1,0:T(8,128)S(1)}, u32[]{:S(2)}, u32[]{:S(2)}) %collective-permute-start.5) | collective-permute-done | bytes 327712 | tf_op jit(solution)/shard_map/ppermute | solution.py:20
  22.9 1.6 %collective-permute-done.6.tok1.refs_7_ = f32[80,1024]{1,0:T(8,128)S(1)} collective-permute-done((f32[80,1024]{1,0:T(8,128)S(1)}, f32[80,1024]{1,0:T(8,128)S(1)}, u32[]{:S(2)}, u32[]{:S(2)}) %collective-permute-start.6) | collective-permute-done | bytes 327712 | tf_op jit(solution)/shard_map/ppermute | solution.py:20
  24.5 7.2 %forward_scan.1 = (bf16[352,1024]{1,0:T(8,128)(2,1)S(1)}, f32[352,256]{1,0:T(8,128)S(1)}, f32[704,256]{1,0:T(8,128)S(1)}, f32[704,256]{1,0:T(8,128)S(1)}, f32[70...) custom-call(s32[4]{0:T(128)S(1)} %pad_add_fusion.sel, f32[80,1024]{1,0:T(8,128)S(1)} %hold.10.tok0.refs_6_, ...), custom_call_target="tpu_custom_call" | custom-call | flops 55000000 | bytes 180000 | tf_op jit(solution)/shard_map/forward_scan/pallas_call | solution.py:362
  31.7 4.3 %backward_scan.1 = (bf16[704,768]{1,0:T(8,128)(2,1)S(1)}, f32[704,256]{1,0:T(8,128)S(1)}, f32[704,256]{1,0:T(8,128)S(1)}, f32[8,256]{1,0:T(8,128)S(1)}, f32[128,768]{1,0:T(8,128)S(1)}, /*index=5*/f32[128,768]{1,0:T(8,128)S(1)}) custom-call(s32[4]{0:T(128)S(1)} %pad_add_fusion.sel, f32[176,1024]{1,0:T(8,128)S(1)} %get-tuple-element.79.tok0.refs_0_, ...), custom_call_target="tpu_custom_call" | custom-call | flops 55000000 | bytes 180000 | tf_op jit(solution)/shard_map/backward_scan/pallas_call | solution.py:479
  36.1 2.0 %collective-permute-start.10 = (f32[128,768]{1,0:T(8,128)S(1)}, f32[128,768]{1,0:T(8,128)S(1)}, u32[]{:S(2)}, u32[]{:S(2)}) collective-permute-start(f32[128,768]{1,0:T(8,128)S(1)} %get-tuple-element.108), channel_id=1, source_target_pairs={{0,4},{4,0},{1,5},{5,1},{2,6},{6,2},{3,7},{7,3},{8,12},{12,8},{9,1... | collective-permute-start | bytes 1179656 | tf_op jit(solution)/shard_map/ppermute | solution.py:20
  39.4 2.0 %collective-permute-start.11 = (f32[128,768]{1,0:T(8,128)S(1)}, f32[128,768]{1,0:T(8,128)S(1)}, u32[]{:S(2)}, u32[]{:S(2)}) collective-permute-start(f32[128,768]{1,0:T(8,128)S(1)} %get-tuple-element.113), channel_id=1, source_target_pairs={{0,8},{8,0},{16,24},{24,16},{1,9},{9,1},{17,25},{25,17},{2,10},{10... | collective-permute-start | bytes 1179656 | tf_op jit(solution)/shard_map/ppermute | solution.py:25
  43.0 2.9 %input_side.1 = (f32[360,1280]{1,0:T(8,128)S(1)}, f32[360,1280]{1,0:T(8,128)S(1)}) custom-call(s32[4]{0:T(128)S(1)} %pad_add_fusion.sel, f32[176,1024]{1,0:T(8,128)S(1)} %get-tuple-element.79.tok0.refs_0_, f32[176,1024]{1,0:T(8,128)S(1)} %collective-permute-done.tok1.refs_1_, f32[32,1024]{1,0:T(8,128)S(1)} %hold.8.refs_0_.refs_2_, ...), custom_call_target="tpu_custom_call" | custom-call | flops 55000000 | bytes 180000 | tf_op jit(solution)/shard_map/input_side/pallas_call | solution.py:570
  45.8 2.2 %collective-permute-done.10.b_ref = f32[128,768]{1,0:T(8,128)S(1)} collective-permute-done((f32[128,768]{1,0:T(8,128)S(1)}, f32[128,768]{1,0:T(8,128)S(1)}, u32[]{:S(2)}, u32[]{:S(2)}) %collective-permute-start.10) | collective-permute-done | bytes 393248 | tf_op jit(solution)/shard_map/ppermute | solution.py:20
  48.1 2.2 %collective-permute-start.15 = (f32[128,768]{1,0:T(8,128)S(1)}, f32[128,768]{1,0:T(8,128)S(1)}, u32[]{:S(2)}, u32[]{:S(2)}) collective-permute-start(f32[128,768]{1,0:T(8,128)S(1)} %add.10.refs_0_), channel_id=1, source_target_pairs={{0,8},{8,0},{16,24},{24,16},{1,9},{9,1},{17,25},{25,17},{2,10},{10... | collective-permute-start | bytes 1179656 | tf_op jit(solution)/shard_map/ppermute | solution.py:25
  50.7 1.9 %collective-permute-start.12 = (f32[128,768]{1,0:T(8,128)S(1)}, f32[128,768]{1,0:T(8,128)S(1)}, u32[]{:S(2)}, u32[]{:S(2)}) collective-permute-start(f32[128,768]{1,0:T(8,128)S(1)} %add.11), channel_id=1, source_target_pairs={{0,4},{4,0},{1,5},{5,1},{2,6},{6,2},{3,7},{7,3},{8,12},{12,8},{9,1... | collective-permute-start | bytes 1179656 | tf_op jit(solution)/shard_map/ppermute | solution.py:20
  52.6 3.8 %collective-permute-done.14.b_ref = f32[128,768]{1,0:T(8,128)S(1)} collective-permute-done((f32[128,768]{1,0:T(8,128)S(1)}, f32[128,768]{1,0:T(8,128)S(1)}, u32[]{:S(2)}, u32[]{:S(2)}) %collective-permute-start.14) | collective-permute-done | bytes 393248 | tf_op jit(solution)/shard_map/ppermute | solution.py:20
  56.5 3.7 %collective-permute-done.15.b_ref = f32[128,768]{1,0:T(8,128)S(1)} collective-permute-done((f32[128,768]{1,0:T(8,128)S(1)}, f32[128,768]{1,0:T(8,128)S(1)}, u32[]{:S(2)}, u32[]{:S(2)}) %collective-permute-start.15) | collective-permute-done | bytes 393248 | tf_op jit(solution)/shard_map/ppermute | solution.py:25
  60.3 4.1 %collective-permute-start.16 = (f32[128,768]{1,0:T(8,128)S(1)}, f32[128,768]{1,0:T(8,128)S(1)}, u32[]{:S(2)}, u32[]{:S(2)}) collective-permute-start(f32[128,768]{1,0:T(8,128)S(1)} %add.13), channel_id=1, source_target_pairs={{0,24},{8,16},{16,8},{24,0},{1,25},{9,17},{17,9},{25,1},{2,26},{10... | collective-permute-start | bytes 1179656 | tf_op jit(solution)/shard_map/ppermute | solution.py:25
  68.2 9.6 %collective-permute-done.16.a3_ref = f32[128,768]{1,0:T(8,128)S(1)} collective-permute-done((f32[128,768]{1,0:T(8,128)S(1)}, f32[128,768]{1,0:T(8,128)S(1)}, u32[]{:S(2)}, u32[]{:S(2)}) %collective-permute-start.16) | collective-permute-done | bytes 393248 | tf_op jit(solution)/shard_map/ppermute | solution.py:25
  81.0 2.5 %collective-permute-start.18 = (f32[136,768]{1,0:T(8,128)S(1)}, f32[136,768]{1,0:T(8,128)S(1)}, u32[]{:S(2)}, u32[]{:S(2)}) collective-permute-start(f32[136,768]{1,0:T(8,128)S(1)} %finish.1.both_ref.refs_0_), channel_id=1, source_target_pairs={{0,8},{8,0},{16,24},{24,16},{1,9},{9,1},{17,25},{25,17},{2,10},{10... | collective-permute-start | bytes 1253384 | tf_op jit(solution)/shard_map/ppermute | solution.py:25
  85.8 2.6 %collective-permute-done.19.refs_0_ = f32[136,768]{1,0:T(8,128)S(1)} collective-permute-done((f32[136,768]{1,0:T(8,128)S(1)}, f32[136,768]{1,0:T(8,128)S(1)}, u32[]{:S(2)}, u32[]{:S(2)}) %collective-permute-start.19) | collective-permute-done | bytes 417824 | tf_op jit(solution)/shard_map/ppermute | solution.py:20
  91.5 2.4 %collective-permute-done.17.refs_0_ = f32[136,768]{1,0:T(8,128)S(1)} collective-permute-done((f32[136,768]{1,0:T(8,128)S(1)}, f32[136,768]{1,0:T(8,128)S(1)}, u32[]{:S(2)}, u32[]{:S(2)}) %collective-permute-start.17) | collective-permute-done | bytes 417824 | tf_op jit(solution)/shard_map/ppermute | solution.py:25
  93.9 5.1 %collective-permute-done.18.refs_1_ = f32[136,768]{1,0:T(8,128)S(1)} collective-permute-done((f32[136,768]{1,0:T(8,128)S(1)}, f32[136,768]{1,0:T(8,128)S(1)}, u32[]{:S(2)}, u32[]{:S(2)}) %collective-permute-start.18) | collective-permute-done | bytes 417824 | tf_op jit(solution)/shard_map/ppermute | solution.py:25
  103.0 2.9 %collective-permute-start.27 = (f32[136,768]{1,0:T(8,128)S(1)}, f32[136,768]{1,0:T(8,128)S(1)}, u32[]{:S(2)}, u32[]{:S(2)}) collective-permute-start(f32[136,768]{1,0:T(8,128)S(1)} %get-tuple-element.129), channel_id=1, source_target_pairs={{0,24},{8,16},{16,8},{24,0},{1,25},{9,17},{17,9},{25,1},{2,26},{10... | collective-permute-start | bytes 1253384 | tf_op jit(solution)/shard_map/ppermute | solution.py:25
  105.9 2.5 %place.5 = (f32[1024,3072]{1,0:T(8,128)}, f32[768,768]{1,0:T(8,128)S(1)}) custom-call(s32[4]{0:T(128)S(1)} %pad_add_fusion.sel, f32[136,768]{1,0:T(8,128)S(1)} %finish.1.both_ref.refs_0_, f32[136,768]{1,0:T(8,128)S(1)} %hold.11.refs_1_.px0_ref, f32[136,768]{1,0:T(8,128)S(1)} %get-tuple-element.123.py0_ref.refs_2_, ...), custom_call_target="tpu_custom_call" | custom-call | flops 55000000 | bytes 180000 | tf_op jit(solution)/shard_map/place/pallas_call | solution.py:769
  109.8 4.4 %collective-permute-done.24.refs_0_ = f32[136,768]{1,0:T(8,128)S(1)} collective-permute-done((f32[136,768]{1,0:T(8,128)S(1)}, f32[136,768]{1,0:T(8,128)S(1)}, u32[]{:S(2)}, u32[]{:S(2)}) %collective-permute-start.24) | collective-permute-done | bytes 417824 | tf_op jit(solution)/shard_map/ppermute | solution.py:25
  114.2 8.5 %collective-permute-done.27.refs_3_ = f32[136,768]{1,0:T(8,128)S(1)} collective-permute-done((f32[136,768]{1,0:T(8,128)S(1)}, f32[136,768]{1,0:T(8,128)S(1)}, u32[]{:S(2)}, u32[]{:S(2)}) %collective-permute-start.27) | collective-permute-done | bytes 417824 | tf_op jit(solution)/shard_map/ppermute | solution.py:25
  123.2 1.6 %collective-permute-start.28 = (f32[176,768]{1,0:T(8,128)S(1)}, f32[176,768]{1,0:T(8,128)S(1)}, u32[]{:S(2)}, u32[]{:S(2)}) collective-permute-start(f32[176,768]{1,0:T(8,128)S(1)} %stack.23), channel_id=1, source_target_pairs={{0,2},{2,0},{1,3},{3,1},{4,6},{6,4},{5,7},{7,5},{8,10},{10,8},{9,1... | collective-permute-start | bytes 1622024 | tf_op jit(solution)/shard_map/ppermute | solution.py:20
  124.8 3.0 %place.6 = (f32[1024,3072]{1,0:T(8,128)}, f32[512,768]{1,0:T(8,128)S(1)}) custom-call(s32[4]{0:T(128)S(1)} %pad_add_fusion.sel, f32[256,768]{1,0:T(8,128)S(1)} %get-tuple-element.133.refs_1_.refs_0_, f32[256,768]{1,0:T(8,128)S(1)} %get-tuple-element.132.refs_1_, f32[768,768]{1,0:T(8,128)S(1)} %collective-permute-done.31.refs_2_, ...), custom_call_target="tpu_custom_call", output_to_operand_aliasing={{0}: (4, {})} | custom-call | flops 55000000 | bytes 180000 | tf_op jit(solution)/shard_map/place/pallas_call | solution.py:769
  130.0 2.8 %collective-permute-done.30.refs_2_ = f32[168,768]{1,0:T(8,128)S(1)} collective-permute-done((f32[168,768]{1,0:T(8,128)S(1)}, f32[168,768]{1,0:T(8,128)S(1)}, u32[]{:S(2)}, u32[]{:S(2)}) %collective-permute-start.30) | collective-permute-done | bytes 516128 | tf_op jit(solution)/shard_map/ppermute | solution.py:25
  134.1 2.8 %place.8.refs_3_ = f32[1024,3072]{1,0:T(8,128)} custom-call(s32[4]{0:T(128)S(1)} %pad_add_fusion.sel, f32[176,768]{1,0:T(8,128)S(1)} %get-tuple-element.138.refs_2_.refs_0_, f32[176,768]{1,0:T(8,128)S(1)} %get-tuple-element.139.refs_1_, f32[168,768]{1,0:T(8,128)S(1)} %get-tuple-element.140.refs_2_, ...), custom_call_target="tpu_custom_call", output_to_operand_aliasing={{}: (6, {})} | custom-call | flops 55000000 | bytes 180000 | tf_op jit(solution)/shard_map/place/pallas_call | solution.py:769
  136.9 1.8 %place.9 = f32[1024,3072]{1,0:T(8,128)} custom-call(s32[4]{0:T(128)S(1)} %pad_add_fusion.sel, f32[176,768]{1,0:T(8,128)S(1)} %collective-permute-done.32.refs_0_, f32[176,768]{1,0:T(8,128)S(1)} %collective-permute-done.33.refs_1_, f32[168,768]{1,0:T(8,128)S(1)} %collective-permute-done.34.refs_2_, ...), custom_call_target="tpu_custom_call", output_to_operand_aliasing={{}: (4, {})} | custom-call | flops 55000000 | bytes 180000 | tf_op jit(solution)/shard_map/place/pallas_call | solution.py:769
  (104 shorter events, 31.2 us)
Async XLA Ops:
  1.9 6.9 %collective-permute-start = (f32[176,1024]{1,0:T(8,128)S(1)}, f32[176,1024]{1,0:T(8,128)S(1)}, u32[]{:S(2)}, u32[]{:S(2)}) collective-permute-start(f32[176,1024]{1,0:T(8,128)S(1)} %get-tuple-element.79.tok0.refs_0_), channel_id=1, source_target_pairs={{0,1},{1,0},{2,3},{3,2},{4,5},{5,4},{6,7},{7,6},{8,9},{9,8},{10,11... | collective-permute-start | bytes 2162696 | tf_op jit(solution)/shard_map/ppermute | solution.py:20
  2.4 8.7 %collective-permute-start.1 = (f32[32,1024]{1,0:T(8,128)S(1)}, f32[32,1024]{1,0:T(8,128)S(1)}, u32[]{:S(2)}, u32[]{:S(2)}) collective-permute-start(f32[32,1024]{1,0:T(8,128)S(1)} %slice_bitcast_fusion.2), channel_id=1, source_target_pairs={{0,2},{2,0},{1,3},{3,1},{4,6},{6,4},{5,7},{7,5},{8,10},{10,8},{9,1... | collective-permute-start | bytes 393224 | tf_op jit(solution)/shard_map/ppermute | solution.py:20
  5.0 9.7 %collective-permute-start.3 = (f32[64,1024]{1,0:T(8,128)S(1)}, f32[64,1024]{1,0:T(8,128)S(1)}, u32[]{:S(2)}, u32[]{:S(2)}) collective-permute-start(f32[64,1024]{1,0:T(8,128)S(1)} %slice_bitcast_fusion.1), channel_id=1, source_target_pairs={{0,2},{2,0},{1,3},{3,1},{4,6},{6,4},{5,7},{7,5},{8,10},{10,8},{9,1... | collective-permute-start | bytes 786440 | tf_op jit(solution)/shard_map/ppermute | solution.py:20
  12.3 10.5 %collective-permute-start.5 = (f32[80,1024]{1,0:T(8,128)S(1)}, f32[80,1024]{1,0:T(8,128)S(1)}, u32[]{:S(2)}, u32[]{:S(2)}) collective-permute-start(f32[80,1024]{1,0:T(8,128)S(1)} %slice_bitcast_fusion), channel_id=1, source_target_pairs={{0,2},{2,0},{1,3},{3,1},{4,6},{6,4},{5,7},{7,5},{8,10},{10,8},{9,1... | collective-permute-start | bytes 983048 | tf_op jit(solution)/shard_map/ppermute | solution.py:20
  15.3 16.5 %collective-permute-start.8 = (f32[352,256]{1,0:T(8,128)S(1)}, f32[352,256]{1,0:T(8,128)S(1)}, u32[]{:S(2)}, u32[]{:S(2)}) collective-permute-start(f32[352,256]{1,0:T(8,128)S(1)} %pack_cot.1), channel_id=1, source_target_pairs={{0,2},{2,0},{1,3},{3,1},{4,6},{6,4},{5,7},{7,5},{8,10},{10,8},{9,1... | collective-permute-start | bytes 1081352 | tf_op jit(solution)/shard_map/ppermute | solution.py:20
  36.1 12.0 %collective-permute-start.10 = (f32[128,768]{1,0:T(8,128)S(1)}, f32[128,768]{1,0:T(8,128)S(1)}, u32[]{:S(2)}, u32[]{:S(2)}) collective-permute-start(f32[128,768]{1,0:T(8,128)S(1)} %get-tuple-element.108), channel_id=1, source_target_pairs={{0,4},{4,0},{1,5},{5,1},{2,6},{6,2},{3,7},{7,3},{8,12},{12,8},{9,1... | collective-permute-start | bytes 1179656 | tf_op jit(solution)/shard_map/ppermute | solution.py:20
  39.2 17.2 %collective-permute-start.14 = (f32[128,768]{1,0:T(8,128)S(1)}, f32[128,768]{1,0:T(8,128)S(1)}, u32[]{:S(2)}, u32[]{:S(2)}) collective-permute-start(f32[128,768]{1,0:T(8,128)S(1)} %get-tuple-element.109.refs_0_), channel_id=1, source_target_pairs={{0,4},{4,0},{1,5},{5,1},{2,6},{6,2},{3,7},{7,3},{8,12},{12,8},{9,1... | collective-permute-start | bytes 1179656 | tf_op jit(solution)/shard_map/ppermute | solution.py:20
  39.4 11.3 %collective-permute-start.11 = (f32[128,768]{1,0:T(8,128)S(1)}, f32[128,768]{1,0:T(8,128)S(1)}, u32[]{:S(2)}, u32[]{:S(2)}) collective-permute-start(f32[128,768]{1,0:T(8,128)S(1)} %get-tuple-element.113), channel_id=1, source_target_pairs={{0,8},{8,0},{16,24},{24,16},{1,9},{9,1},{17,25},{25,17},{2,10},{10... | collective-permute-start | bytes 1179656 | tf_op jit(solution)/shard_map/ppermute | solution.py:25
  48.1 12.2 %collective-permute-start.15 = (f32[128,768]{1,0:T(8,128)S(1)}, f32[128,768]{1,0:T(8,128)S(1)}, u32[]{:S(2)}, u32[]{:S(2)}) collective-permute-start(f32[128,768]{1,0:T(8,128)S(1)} %add.10.refs_0_), channel_id=1, source_target_pairs={{0,8},{8,0},{16,24},{24,16},{1,9},{9,1},{17,25},{25,17},{2,10},{10... | collective-permute-start | bytes 1179656 | tf_op jit(solution)/shard_map/ppermute | solution.py:25
  50.2 14.2 %collective-permute-start.9 = (f32[360,1280]{1,0:T(8,128)S(1)}, f32[360,1280]{1,0:T(8,128)S(1)}, u32[]{:S(2)}, u32[]{:S(2)}) collective-permute-start(f32[360,1280]{1,0:T(8,128)S(1)} %get-tuple-element.106.refs_2_.refs_0_), channel_id=1, source_target_pairs={{0,1},{1,0},{2,3},{3,2},{4,5},{5,4},{6,7},{7,6},{8,9},{9,8},{10,11... | collective-permute-start | bytes 5529608 | tf_op jit(solution)/shard_map/ppermute | solution.py:20
  50.2 18.0 %collective-permute-start.13 = (f32[128,768]{1,0:T(8,128)S(1)}, f32[128,768]{1,0:T(8,128)S(1)}, u32[]{:S(2)}, u32[]{:S(2)}) collective-permute-start(f32[128,768]{1,0:T(8,128)S(1)} %get-tuple-element.114), channel_id=1, source_target_pairs={{0,8},{8,0},{16,24},{24,16},{1,9},{9,1},{17,25},{25,17},{2,10},{10... | collective-permute-start | bytes 1179656 | tf_op jit(solution)/shard_map/ppermute | solution.py:25
  50.7 17.5 %collective-permute-start.12 = (f32[128,768]{1,0:T(8,128)S(1)}, f32[128,768]{1,0:T(8,128)S(1)}, u32[]{:S(2)}, u32[]{:S(2)}) collective-permute-start(f32[128,768]{1,0:T(8,128)S(1)} %add.11), channel_id=1, source_target_pairs={{0,4},{4,0},{1,5},{5,1},{2,6},{6,2},{3,7},{7,3},{8,12},{12,8},{9,1... | collective-permute-start | bytes 1179656 | tf_op jit(solution)/shard_map/ppermute | solution.py:20
  60.3 17.5 %collective-permute-start.16 = (f32[128,768]{1,0:T(8,128)S(1)}, f32[128,768]{1,0:T(8,128)S(1)}, u32[]{:S(2)}, u32[]{:S(2)}) collective-permute-start(f32[128,768]{1,0:T(8,128)S(1)} %add.13), channel_id=1, source_target_pairs={{0,24},{8,16},{16,8},{24,0},{1,25},{9,17},{17,9},{25,1},{2,26},{10... | collective-permute-start | bytes 1179656 | tf_op jit(solution)/shard_map/ppermute | solution.py:25
  65.3 19.7 %collective-permute-start.20 = (f32[176,1024]{1,0:T(8,128)S(1)}, f32[176,1024]{1,0:T(8,128)S(1)}, u32[]{:S(2)}, u32[]{:S(2)}) collective-permute-start(f32[176,1024]{1,0:T(8,128)S(1)} %get-tuple-element.118), channel_id=1, source_target_pairs={{0,2},{2,0},{1,3},{3,1},{4,6},{6,4},{5,7},{7,5},{8,10},{10,8},{9,1... | collective-permute-start | bytes 2162696 | tf_op jit(solution)/shard_map/ppermute | solution.py:20
  77.9 10.5 %collective-permute-start.19 = (f32[136,768]{1,0:T(8,128)S(1)}, f32[136,768]{1,0:T(8,128)S(1)}, u32[]{:S(2)}, u32[]{:S(2)}) collective-permute-start(f32[136,768]{1,0:T(8,128)S(1)} %finish.1.both_ref.refs_0_), channel_id=1, source_target_pairs={{0,2},{2,0},{1,3},{3,1},{4,6},{6,4},{5,7},{7,5},{8,10},{10,8},{9,1... | collective-permute-start | bytes 1253384 | tf_op jit(solution)/shard_map/ppermute | solution.py:20
  79.5 14.4 %collective-permute-start.17 = (f32[136,768]{1,0:T(8,128)S(1)}, f32[136,768]{1,0:T(8,128)S(1)}, u32[]{:S(2)}, u32[]{:S(2)}) collective-permute-start(f32[136,768]{1,0:T(8,128)S(1)} %finish.1.both_ref.refs_0_), channel_id=1, source_target_pairs={{0,24},{8,16},{16,8},{24,0},{1,25},{9,17},{17,9},{25,1},{2,26},{10... | collective-permute-start | bytes 1253384 | tf_op jit(solution)/shard_map/ppermute | solution.py:25
  81.0 18.0 %collective-permute-start.18 = (f32[136,768]{1,0:T(8,128)S(1)}, f32[136,768]{1,0:T(8,128)S(1)}, u32[]{:S(2)}, u32[]{:S(2)}) collective-permute-start(f32[136,768]{1,0:T(8,128)S(1)} %finish.1.both_ref.refs_0_), channel_id=1, source_target_pairs={{0,8},{8,0},{16,24},{24,16},{1,9},{9,1},{17,25},{25,17},{2,10},{10... | collective-permute-start | bytes 1253384 | tf_op jit(solution)/shard_map/ppermute | solution.py:25
  83.5 15.5 %collective-permute-start.22 = (f32[136,768]{1,0:T(8,128)S(1)}, f32[136,768]{1,0:T(8,128)S(1)}, u32[]{:S(2)}, u32[]{:S(2)}) collective-permute-start(f32[136,768]{1,0:T(8,128)S(1)} %finish.1.both_ref.refs_0_), channel_id=1, source_target_pairs={{0,4},{4,0},{1,5},{5,1},{2,6},{6,2},{3,7},{7,3},{8,12},{12,8},{9,1... | collective-permute-start | bytes 1253384 | tf_op jit(solution)/shard_map/ppermute | solution.py:20
  88.4 12.0 %collective-permute-start.21 = (f32[136,768]{1,0:T(8,128)S(1)}, f32[136,768]{1,0:T(8,128)S(1)}, u32[]{:S(2)}, u32[]{:S(2)}) collective-permute-start(f32[136,768]{1,0:T(8,128)S(1)} %hold.11.refs_1_.px0_ref), channel_id=1, source_target_pairs={{0,4},{4,0},{1,5},{5,1},{2,6},{6,2},{3,7},{7,3},{8,12},{12,8},{9,1... | collective-permute-start | bytes 1253384 | tf_op jit(solution)/shard_map/ppermute | solution.py:20
  90.0 9.0 %collective-permute-start.23 = (f32[176,512]{1,0:T(8,128)S(1)}, f32[176,512]{1,0:T(8,128)S(1)}, u32[]{:S(2)}, u32[]{:S(2)}) collective-permute-start(f32[176,512]{1,0:T(8,128)S(1)} %hold.12), channel_id=1, source_target_pairs={{0,2},{2,0},{1,3},{3,1},{4,6},{6,4},{5,7},{7,5},{8,10},{10,8},{9,1... | collective-permute-start | bytes 1081352 | tf_op jit(solution)/shard_map/ppermute | solution.py:20
  100.6 22.1 %collective-permute-start.25 = (f32[256,768]{1,0:T(8,128)S(1)}, f32[256,768]{1,0:T(8,128)S(1)}, u32[]{:S(2)}, u32[]{:S(2)}) collective-permute-start(f32[256,768]{1,0:T(8,128)S(1)} %get-tuple-element.128.refs_4_), channel_id=1, source_target_pairs={{0,2},{2,0},{1,3},{3,1},{4,6},{6,4},{5,7},{7,5},{8,10},{10,8},{9,1... | collective-permute-start | bytes 2359304 | tf_op jit(solution)/shard_map/ppermute | solution.py:20
  100.9 21.8 %collective-permute-start.26 = (f32[256,768]{1,0:T(8,128)S(1)}, f32[256,768]{1,0:T(8,128)S(1)}, u32[]{:S(2)}, u32[]{:S(2)}) collective-permute-start(f32[256,768]{1,0:T(8,128)S(1)} %get-tuple-element.128.refs_4_), channel_id=1, source_target_pairs={{0,4},{4,0},{1,5},{5,1},{2,6},{6,2},{3,7},{7,3},{8,12},{12,8},{9,1... | collective-permute-start | bytes 2359304 | tf_op jit(solution)/shard_map/ppermute | solution.py:20
  102.3 11.8 %collective-permute-start.24 = (f32[136,768]{1,0:T(8,128)S(1)}, f32[136,768]{1,0:T(8,128)S(1)}, u32[]{:S(2)}, u32[]{:S(2)}) collective-permute-start(f32[136,768]{1,0:T(8,128)S(1)} %get-tuple-element.127.refs_0_), channel_id=1, source_target_pairs={{0,8},{8,0},{16,24},{24,16},{1,9},{9,1},{17,25},{25,17},{2,10},{10... | collective-permute-start | bytes 1253384 | tf_op jit(solution)/shard_map/ppermute | solution.py:25
  103.0 19.7 %collective-permute-start.27 = (f32[136,768]{1,0:T(8,128)S(1)}, f32[136,768]{1,0:T(8,128)S(1)}, u32[]{:S(2)}, u32[]{:S(2)}) collective-permute-start(f32[136,768]{1,0:T(8,128)S(1)} %get-tuple-element.129), channel_id=1, source_target_pairs={{0,24},{8,16},{16,8},{24,0},{1,25},{9,17},{17,9},{25,1},{2,26},{10... | collective-permute-start | bytes 1253384 | tf_op jit(solution)/shard_map/ppermute | solution.py:25
  108.4 16.4 %collective-permute-start.31 = (f32[768,768]{1,0:T(8,128)S(1)}, f32[768,768]{1,0:T(8,128)S(1)}, u32[]{:S(2)}, u32[]{:S(2)}) collective-permute-start(f32[768,768]{1,0:T(8,128)S(1)} %get-tuple-element.130.refs_4_.refs_0_), channel_id=1, source_target_pairs={{0,1},{1,0},{2,3},{3,2},{4,5},{5,4},{6,7},{7,6},{8,9},{9,8},{10,11... | collective-permute-start | bytes 7077896 | tf_op jit(solution)/shard_map/ppermute | solution.py:20
  122.7 10.1 %collective-permute-start.30 = (f32[168,768]{1,0:T(8,128)S(1)}, f32[168,768]{1,0:T(8,128)S(1)}, u32[]{:S(2)}, u32[]{:S(2)}) collective-permute-start(f32[168,768]{1,0:T(8,128)S(1)} %stack.25), channel_id=1, source_target_pairs={{0,8},{8,0},{16,24},{24,16},{1,9},{9,1},{17,25},{25,17},{2,10},{10... | collective-permute-start | bytes 1548296 | tf_op jit(solution)/shard_map/ppermute | solution.py:25
  122.9 10.0 %collective-permute-start.29 = (f32[176,768]{1,0:T(8,128)S(1)}, f32[176,768]{1,0:T(8,128)S(1)}, u32[]{:S(2)}, u32[]{:S(2)}) collective-permute-start(f32[176,768]{1,0:T(8,128)S(1)} %stack.24), channel_id=1, source_target_pairs={{0,4},{4,0},{1,5},{5,1},{2,6},{6,2},{3,7},{7,3},{8,12},{12,8},{9,1... | collective-permute-start | bytes 1622024 | tf_op jit(solution)/shard_map/ppermute | solution.py:20
  123.2 9.6 %collective-permute-start.28 = (f32[176,768]{1,0:T(8,128)S(1)}, f32[176,768]{1,0:T(8,128)S(1)}, u32[]{:S(2)}, u32[]{:S(2)}) collective-permute-start(f32[176,768]{1,0:T(8,128)S(1)} %stack.23), channel_id=1, source_target_pairs={{0,2},{2,0},{1,3},{3,1},{4,6},{6,4},{5,7},{7,5},{8,10},{10,8},{9,1... | collective-permute-start | bytes 1622024 | tf_op jit(solution)/shard_map/ppermute | solution.py:20
  129.4 4.7 %collective-permute-start.36 = (f32[256,768]{1,0:T(8,128)S(1)}, f32[256,768]{1,0:T(8,128)S(1)}, u32[]{:S(2)}, u32[]{:S(2)}) collective-permute-start(f32[256,768]{1,0:T(8,128)S(1)} %get-tuple-element.137.refs_3_.refs_1_), channel_id=1, source_target_pairs={{0,1},{1,0},{2,3},{3,2},{4,5},{5,4},{6,7},{7,6},{8,9},{9,8},{10,11... | collective-permute-start | bytes 2359304 | tf_op jit(solution)/shard_map/ppermute | solution.py:20
  129.5 4.6 %collective-permute-start.35 = (f32[512,768]{1,0:T(8,128)S(1)}, f32[512,768]{1,0:T(8,128)S(1)}, u32[]{:S(2)}, u32[]{:S(2)}) collective-permute-start(f32[512,768]{1,0:T(8,128)S(1)} %get-tuple-element.141.refs_0_), channel_id=1, source_target_pairs={{0,1},{1,0},{2,3},{3,2},{4,5},{5,4},{6,7},{7,6},{8,9},{9,8},{10,11... | collective-permute-start | bytes 4718600 | tf_op jit(solution)/shard_map/ppermute | solution.py:20
  132.8 4.1 %collective-permute-start.32 = (f32[176,768]{1,0:T(8,128)S(1)}, f32[176,768]{1,0:T(8,128)S(1)}, u32[]{:S(2)}, u32[]{:S(2)}) collective-permute-start(f32[176,768]{1,0:T(8,128)S(1)} %get-tuple-element.138.refs_2_.refs_0_), channel_id=1, source_target_pairs={{0,1},{1,0},{2,3},{3,2},{4,5},{5,4},{6,7},{7,6},{8,9},{9,8},{10,11... | collective-permute-start | bytes 1622024 | tf_op jit(solution)/shard_map/ppermute | solution.py:20
  132.9 4.0 %collective-permute-start.33 = (f32[176,768]{1,0:T(8,128)S(1)}, f32[176,768]{1,0:T(8,128)S(1)}, u32[]{:S(2)}, u32[]{:S(2)}) collective-permute-start(f32[176,768]{1,0:T(8,128)S(1)} %get-tuple-element.139.refs_1_), channel_id=1, source_target_pairs={{0,1},{1,0},{2,3},{3,2},{4,5},{5,4},{6,7},{7,6},{8,9},{9,8},{10,11... | collective-permute-start | bytes 1622024 | tf_op jit(solution)/shard_map/ppermute | solution.py:20
  (14 other events, 25.4 us)

commit v6 on v5

--- a/solution.py
+++ b/solution.py
@@ -713,9 +713,8 @@
     )(*(array for array, _, _ in parts))
 
 
-def small_kernel(*refs, where):
-    pieces, outs = refs[:-6], refs[-6:]
-    sums = [pieces[i][at : at + 8, :] for i, at in where]
+def add_small(places, outs):
+    sums = [array[at : at + 8, :] for array, at in places]
     while len(sums) > 1:
         sums = [a + b for a, b in zip(sums[::2], sums[1::2])]
     total = sums[0]
@@ -725,21 +724,10 @@
         out[:, 3 * cols :] = total[6 + i // 3 : 7 + i // 3, (i % 3) * cols : (i % 3 + 1) * cols]
 
 
-def small_sums(pieces, where):
-    width = pieces[0].shape[1] // 3 * 4
-    return pl.pallas_call(
-        functools.partial(small_kernel, where=where),
-        out_shape=(shaped((1, width)),) * 6,
-        in_specs=[vmem()] * len(pieces),
-        out_specs=(vmem(),) * 6,
-        compiler_params=params(8),
-        cost_estimate=cost(0.05),
-        name="small_sums",
-    )(*pieces)
-
-
-def place_kernel(sel, *refs, where, give):
-    target, sem = refs[-2 - bool(give)], refs[-1]
+def place_kernel(sel, *refs, where, give, count, small):
+    tails = 6 if small else 0
+    outs, scratch = refs[len(refs) - 2 - bool(give) - 2 * tails :], refs[len(refs) - 1 - tails :]
+    target, sem, sums = outs[0], scratch[0], scratch[1:]
     cols = refs[0].shape[1] // 3
     width = target.shape[1] // 3
     part = width // 8
@@ -757,30 +745,43 @@
             to = pl.multiple_of(col + k * width, cols)
             copy(piece.at[:, pl.ds(k * cols, cols)], target.at[pl.ds(to_row, rows), pl.ds(to, cols)])
         if at < give:
-            copy(piece, refs[-2].at[pl.ds(at * part, part)])
+            copy(piece, outs[1].at[pl.ds(at * part, part)])
+    if small:
+        add_small([(refs[count + i], at) for i, at in small], sums)
+        for i in range(tails):
+            copy(sums[i], outs[1 + i])
     for c in copies:
         c.wait()
 
 
-def place(sel, arrays, where, target, width, give, *waits):
+def place(sel, arrays, where, target, width, give, *waits, small=()):
     count = len(arrays)
     extra = [] if target is None else [target]
-    cols3 = 3 * width // 4
-    return pl.pallas_call(
-        functools.partial(place_kernel, where=where, give=give),
-        out_shape=(shaped((width, 3 * width)),)
-        + ((shaped((give * width // 8, cols3)),) if give else ()),
+    outs = [shaped((width, 3 * width))]
+    outs += [shaped((give * width // 8, 3 * width // 4))] if give else []
+    outs += [shaped((1, width))] * 6 if small else []
+    scratch = [pltpu.SemaphoreType.DMA((3 * len(where) + give + (6 if small else 0),))]
+    scratch += [pltpu.VMEM((1, width), F32)] * 6 if small else []
+    return pl.pallas_call(
+        functools.partial(
+            place_kernel,
+            where=where,
+            give=give,
+            count=count,
+            small=tuple((i, at) for i, (_, at) in enumerate(small)),
+        ),
+        out_shape=tuple(outs),
         in_specs=[smem()]
-        + [vmem()] * count
+        + [vmem()] * (count + len(small))
         + [hbm()] * len(extra)
         + [any_spec()] * len(waits),
-        out_specs=(hbm(), vmem()) if give else (hbm(),),
-        scratch_shapes=[pltpu.SemaphoreType.DMA((3 * len(where) + give,))],
-        input_output_aliases={1 + count: 0} if extra else {},
+        out_specs=(hbm(),) + ((vmem(),) if give else ()) + ((hbm(),) * 6 if small else ()),
+        scratch_shapes=scratch,
+        input_output_aliases={1 + count + len(small): 0} if extra else {},
         compiler_params=params(8),
         cost_estimate=cost(0.05),
         name="place",
-    )(sel, *arrays, *extra, *waits)
+    )(sel, *arrays, *(array for array, _ in small), *extra, *waits)
 
 
 def given(array, where):
@@ -916,7 +917,7 @@
         first_give, marked = swap(give, "c"), give
         own = [(0, 0, part, (2, 0), 0, 0, 0), (1, 0, part, (3, 1), 0, 1, 0)]
         proj_grad, give = place(sel, (z2, corner3), own, proj_grad, width, 2)
-        other += given(4, own)
+        last = given(3, own)
         px2, py2, corner12 = hold((px2, py2, corner12), give)
         own = [
             (0, 0, part, (2, 0), 0, 1, 0),
@@ -926,15 +927,14 @@
             (2, 0, part, (2, 1), 0, 1, 0),
             (2, part, rest, (1, 1), by_x + by_y, 1, 0),
         ]
-        arrays = (px2, py2, corner12, first_give, swap(give, "c"))
-        (proj_grad,) = place(
-            sel, arrays, own + other, proj_grad, width, 0, tick(marked, give, px2)
+        small = ((zs, part), (z2, part), (corner12, part + rest), (corner3, part))
+        arrays = (px2, py2, corner12, first_give)
+        proj_grad, *small = place(
+            sel, arrays, own + other, proj_grad, width, 0, tick(marked, give, px2), small=small
         )
         own = [(*place_of[:-1], 1) for place_of in own]
-        arrays = [swap(a, "c") for a in (px2, py2, corner12)]
-        (proj_grad,) = place(sel, arrays, own, proj_grad, width, 0)
-        where = [(0, part), (1, part), (2, part + rest), (3, part)]
-        small = small_sums((zs, z2, corner12, corner3), where)
+        arrays = [swap(a, "c") for a in (px2, py2, corner12, give)]
+        (proj_grad,) = place(sel, arrays, own + last, proj_grad, width, 0)
     else:
         s0, k3, k1, k0 = run_products(sel, normed, dproj, late)
         kept, kept_out, sent, sent_out, small = combine(sel, grad_mine, swap(grad_send, "c"))

time: 139 us -> 139 us (level)
    pallas_call x6 -> x5, Pallas kernels: 12.3 us -> 11.8 us  [place(): pl.pallas_call(functools.partial(place_kernel, where=where, give=give, co...]
  transfers between devices with their start and end apart: 37 -> 37, of which waited for: 16 -> 17; matrix products, arithmetic and copies ran while one was open for 0% -> 0% of each run, Pallas kernels for 23% -> 23%
where the time goes in v6:
time: 139 us; the launch traced here: 138 us
  waiting for transfers between devices  55.3 us (40%)
  starting transfers between devices  40.3 us (29%)
  Pallas kernels  37.8 us (27%)
  local copies, waits for them, and re-layouts  2.88 us (2%)
    ppermute x9, waiting for transfers between devices, xor_permute(): return lax.ppermute(block, axis, [(i, i ^ distance) for i in range(size)])  38.2 us
    ppermute x28, starting transfers between devices, swap(): return lax.ppermute(block, axis, SWAP)  24.3 us
    ppermute x28, waiting for transfers between devices, swap(): return lax.ppermute(block, axis, SWAP)  17.1 us
    ppermute x9, starting transfers between devices, xor_permute(): return lax.ppermute(block, axis, [(i, i ^ distance) for i in range(size)])  16 us
    pallas_call x5, Pallas kernels, place(): pl.pallas_call(functools.partial(place_kernel, where=where, give=give, co...  11.8 us
    pallas_call x1, Pallas kernels, run_forward(): pl.pallas_call(forward_kernel, out_shape=(shaped((length // 2, width), BF...  7.21 us
    pallas_call x1, Pallas kernels, run_backward(): pl.pallas_call(functools.partial(backward_kernel, rows=rows, count=len(to...  4.33 us
    pallas_call x1, Pallas kernels, run_input(): pl.pallas_call(functools.partial(input_kernel, count=len(toks)), out_shap...  2.86 us
  transfers between devices with their start and end apart: 37, of which 17 were waited for; matrix products, arithmetic and copies ran while one was open for 0% of the time, Pallas kernels for 23%

profile of v6, /device:TPU:0, one launch (start us, length us, event | category | flops | bytes accessed | tf_op | source)
XLA Modules:
  0.0 138.5 jit_solution(4417962639863926532)
XLA Ops:
  2.4 2.6 %collective-permute-start.1 = (f32[32,1024]{1,0:T(8,128)S(1)}, f32[32,1024]{1,0:T(8,128)S(1)}, u32[]{:S(2)}, u32[]{:S(2)}) collective-permute-start(f32[32,1024]{1,0:T(8,128)S(1)} %slice_bitcast_fusion.2), channel_id=1, source_target_pairs={{0,2},{2,0},{1,3},{3,1},{4,6},{6,4},{5,7},{7,5},{8,10},{10,8},{9,1... | collective-permute-start | bytes 393224 | tf_op jit(solution)/shard_map/ppermute | solution.py:20
  5.1 2.8 %copy-done = bf16[1024,3072]{1,0:T(8,128)(2,1)S(1)} copy-done((bf16[1024,3072]{1,0:T(8,128)(2,1)S(1)}, bf16[1024,3072]{1,0:T(8,128)(2,1)}, u32[]{:S(2)}) %copy-start) | copy-done | bytes 6291480
  8.8 2.2 %near_blocks.1 = (bf16[352,1024]{1,0:T(8,128)(2,1)S(1)}, f32[352,256]{1,0:T(8,128)S(1)}, f32[352,256]{1,0:T(8,128)S(1)}, f32[352,256]{1,0:T(8,128)S(1)}, f32[352,256]{1,0:T(8,128)S(1)}, /*index=5*/f32[704,256]{1,0:T(8,128)S(1)}) custom-call(s32[4]{0:T(128)S(1)} %pad_add_fusion.sel, s32[1,8]{1,0:T(1,128)S(1)} %copy-done.8, ...), custom_call_target="tpu_custom_call" | custom-call | flops 55000000 | bytes 180000 | tf_op jit(solution)/shard_map/near_blocks/pallas_call | solution.py:272
  12.3 1.9 %collective-permute-start.5 = (f32[80,1024]{1,0:T(8,128)S(1)}, f32[80,1024]{1,0:T(8,128)S(1)}, u32[]{:S(2)}, u32[]{:S(2)}) collective-permute-start(f32[80,1024]{1,0:T(8,128)S(1)} %slice_bitcast_fusion), channel_id=1, source_target_pairs={{0,2},{2,0},{1,3},{3,1},{4,6},{6,4},{5,7},{7,5},{8,10},{10,8},{9,1... | collective-permute-start | bytes 983048 | tf_op jit(solution)/shard_map/ppermute | solution.py:20
  15.3 1.8 %collective-permute-start.8 = (f32[352,256]{1,0:T(8,128)S(1)}, f32[352,256]{1,0:T(8,128)S(1)}, u32[]{:S(2)}, u32[]{:S(2)}) collective-permute-start(f32[352,256]{1,0:T(8,128)S(1)} %pack_cot.1), channel_id=1, source_target_pairs={{0,2},{2,0},{1,3},{3,1},{4,6},{6,4},{5,7},{7,5},{8,10},{10,8},{9,1... | collective-permute-start | bytes 1081352 | tf_op jit(solution)/shard_map/ppermute | solution.py:20
  18.3 4.5 %collective-permute-done.5.refs_0_ = f32[80,1024]{1,0:T(8,128)S(1)} collective-permute-done((f32[80,1024]{1,0:T(8,128)S(1)}, f32[80,1024]{1,0:T(8,128)S(1)}, u32[]{:S(2)}, u32[]{:S(2)}) %collective-permute-start.5) | collective-permute-done | bytes 327712 | tf_op jit(solution)/shard_map/ppermute | solution.py:20
  22.9 1.6 %collective-permute-done.6.tok1.refs_7_ = f32[80,1024]{1,0:T(8,128)S(1)} collective-permute-done((f32[80,1024]{1,0:T(8,128)S(1)}, f32[80,1024]{1,0:T(8,128)S(1)}, u32[]{:S(2)}, u32[]{:S(2)}) %collective-permute-start.6) | collective-permute-done | bytes 327712 | tf_op jit(solution)/shard_map/ppermute | solution.py:20
  24.5 7.2 %forward_scan.1 = (bf16[352,1024]{1,0:T(8,128)(2,1)S(1)}, f32[352,256]{1,0:T(8,128)S(1)}, f32[704,256]{1,0:T(8,128)S(1)}, f32[704,256]{1,0:T(8,128)S(1)}, f32[70...) custom-call(s32[4]{0:T(128)S(1)} %pad_add_fusion.sel, f32[80,1024]{1,0:T(8,128)S(1)} %hold.10.tok0.refs_6_, ...), custom_call_target="tpu_custom_call" | custom-call | flops 55000000 | bytes 180000 | tf_op jit(solution)/shard_map/forward_scan/pallas_call | solution.py:362
  31.7 4.3 %backward_scan.1 = (bf16[704,768]{1,0:T(8,128)(2,1)S(1)}, f32[704,256]{1,0:T(8,128)S(1)}, f32[704,256]{1,0:T(8,128)S(1)}, f32[8,256]{1,0:T(8,128)S(1)}, f32[128,768]{1,0:T(8,128)S(1)}, /*index=5*/f32[128,768]{1,0:T(8,128)S(1)}) custom-call(s32[4]{0:T(128)S(1)} %pad_add_fusion.sel, f32[176,1024]{1,0:T(8,128)S(1)} %get-tuple-element.80.tok0.refs_0_, ...), custom_call_target="tpu_custom_call" | custom-call | flops 55000000 | bytes 180000 | tf_op jit(solution)/shard_map/backward_scan/pallas_call | solution.py:479
  36.1 2.0 %collective-permute-start.10 = (f32[128,768]{1,0:T(8,128)S(1)}, f32[128,768]{1,0:T(8,128)S(1)}, u32[]{:S(2)}, u32[]{:S(2)}) collective-permute-start(f32[128,768]{1,0:T(8,128)S(1)} %get-tuple-element.109), channel_id=1, source_target_pairs={{0,4},{4,0},{1,5},{5,1},{2,6},{6,2},{3,7},{7,3},{8,12},{12,8},{9,1... | collective-permute-start | bytes 1179656 | tf_op jit(solution)/shard_map/ppermute | solution.py:20
  39.4 2.0 %collective-permute-start.11 = (f32[128,768]{1,0:T(8,128)S(1)}, f32[128,768]{1,0:T(8,128)S(1)}, u32[]{:S(2)}, u32[]{:S(2)}) collective-permute-start(f32[128,768]{1,0:T(8,128)S(1)} %get-tuple-element.114), channel_id=1, source_target_pairs={{0,8},{8,0},{16,24},{24,16},{1,9},{9,1},{17,25},{25,17},{2,10},{10... | collective-permute-start | bytes 1179656 | tf_op jit(solution)/shard_map/ppermute | solution.py:25
  43.0 2.9 %input_side.1 = (f32[360,1280]{1,0:T(8,128)S(1)}, f32[360,1280]{1,0:T(8,128)S(1)}) custom-call(s32[4]{0:T(128)S(1)} %pad_add_fusion.sel, f32[176,1024]{1,0:T(8,128)S(1)} %get-tuple-element.80.tok0.refs_0_, f32[176,1024]{1,0:T(8,128)S(1)} %collective-permute-done.tok1.refs_1_, f32[32,1024]{1,0:T(8,128)S(1)} %hold.8.refs_0_.refs_2_, ...), custom_call_target="tpu_custom_call" | custom-call | flops 55000000 | bytes 180000 | tf_op jit(solution)/shard_map/input_side/pallas_call | solution.py:570
  45.8 2.2 %collective-permute-done.10.b_ref = f32[128,768]{1,0:T(8,128)S(1)} collective-permute-done((f32[128,768]{1,0:T(8,128)S(1)}, f32[128,768]{1,0:T(8,128)S(1)}, u32[]{:S(2)}, u32[]{:S(2)}) %collective-permute-start.10) | collective-permute-done | bytes 393248 | tf_op jit(solution)/shard_map/ppermute | solution.py:20
  48.1 2.2 %collective-permute-start.15 = (f32[128,768]{1,0:T(8,128)S(1)}, f32[128,768]{1,0:T(8,128)S(1)}, u32[]{:S(2)}, u32[]{:S(2)}) collective-permute-start(f32[128,768]{1,0:T(8,128)S(1)} %add.10.refs_0_), channel_id=1, source_target_pairs={{0,8},{8,0},{16,24},{24,16},{1,9},{9,1},{17,25},{25,17},{2,10},{10... | collective-permute-start | bytes 1179656 | tf_op jit(solution)/shard_map/ppermute | solution.py:25
  50.7 1.9 %collective-permute-start.12 = (f32[128,768]{1,0:T(8,128)S(1)}, f32[128,768]{1,0:T(8,128)S(1)}, u32[]{:S(2)}, u32[]{:S(2)}) collective-permute-start(f32[128,768]{1,0:T(8,128)S(1)} %add.11), channel_id=1, source_target_pairs={{0,4},{4,0},{1,5},{5,1},{2,6},{6,2},{3,7},{7,3},{8,12},{12,8},{9,1... | collective-permute-start | bytes 1179656 | tf_op jit(solution)/shard_map/ppermute | solution.py:20
  52.6 3.8 %collective-permute-done.14.b_ref = f32[128,768]{1,0:T(8,128)S(1)} collective-permute-done((f32[128,768]{1,0:T(8,128)S(1)}, f32[128,768]{1,0:T(8,128)S(1)}, u32[]{:S(2)}, u32[]{:S(2)}) %collective-permute-start.14) | collective-permute-done | bytes 393248 | tf_op jit(solution)/shard_map/ppermute | solution.py:20
  56.5 3.7 %collective-permute-done.15.b_ref = f32[128,768]{1,0:T(8,128)S(1)} collective-permute-done((f32[128,768]{1,0:T(8,128)S(1)}, f32[128,768]{1,0:T(8,128)S(1)}, u32[]{:S(2)}, u32[]{:S(2)}) %collective-permute-start.15) | collective-permute-done | bytes 393248 | tf_op jit(solution)/shard_map/ppermute | solution.py:25
  60.3 4.1 %collective-permute-start.16 = (f32[128,768]{1,0:T(8,128)S(1)}, f32[128,768]{1,0:T(8,128)S(1)}, u32[]{:S(2)}, u32[]{:S(2)}) collective-permute-start(f32[128,768]{1,0:T(8,128)S(1)} %add.13), channel_id=1, source_target_pairs={{0,24},{8,16},{16,8},{24,0},{1,25},{9,17},{17,9},{25,1},{2,26},{10... | collective-permute-start | bytes 1179656 | tf_op jit(solution)/shard_map/ppermute | solution.py:25
  68.2 9.6 %collective-permute-done.16.a3_ref = f32[128,768]{1,0:T(8,128)S(1)} collective-permute-done((f32[128,768]{1,0:T(8,128)S(1)}, f32[128,768]{1,0:T(8,128)S(1)}, u32[]{:S(2)}, u32[]{:S(2)}) %collective-permute-start.16) | collective-permute-done | bytes 393248 | tf_op jit(solution)/shard_map/ppermute | solution.py:25
  81.0 2.5 %collective-permute-start.18 = (f32[136,768]{1,0:T(8,128)S(1)}, f32[136,768]{1,0:T(8,128)S(1)}, u32[]{:S(2)}, u32[]{:S(2)}) collective-permute-start(f32[136,768]{1,0:T(8,128)S(1)} %finish.1.both_ref.refs_0_), channel_id=1, source_target_pairs={{0,8},{8,0},{16,24},{24,16},{1,9},{9,1},{17,25},{25,17},{2,10},{10... | collective-permute-start | bytes 1253384 | tf_op jit(solution)/shard_map/ppermute | solution.py:25
  85.8 2.6 %collective-permute-done.19.refs_0_ = f32[136,768]{1,0:T(8,128)S(1)} collective-permute-done((f32[136,768]{1,0:T(8,128)S(1)}, f32[136,768]{1,0:T(8,128)S(1)}, u32[]{:S(2)}, u32[]{:S(2)}) %collective-permute-start.19) | collective-permute-done | bytes 417824 | tf_op jit(solution)/shard_map/ppermute | solution.py:20
  91.5 2.4 %collective-permute-done.17.refs_0_ = f32[136,768]{1,0:T(8,128)S(1)} collective-permute-done((f32[136,768]{1,0:T(8,128)S(1)}, f32[136,768]{1,0:T(8,128)S(1)}, u32[]{:S(2)}, u32[]{:S(2)}) %collective-permute-start.17) | collective-permute-done | bytes 417824 | tf_op jit(solution)/shard_map/ppermute | solution.py:25
  93.9 5.1 %collective-permute-done.18.refs_1_ = f32[136,768]{1,0:T(8,128)S(1)} collective-permute-done((f32[136,768]{1,0:T(8,128)S(1)}, f32[136,768]{1,0:T(8,128)S(1)}, u32[]{:S(2)}, u32[]{:S(2)}) %collective-permute-start.18) | collective-permute-done | bytes 417824 | tf_op jit(solution)/shard_map/ppermute | solution.py:25
  103.0 2.9 %collective-permute-start.27 = (f32[136,768]{1,0:T(8,128)S(1)}, f32[136,768]{1,0:T(8,128)S(1)}, u32[]{:S(2)}, u32[]{:S(2)}) collective-permute-start(f32[136,768]{1,0:T(8,128)S(1)} %get-tuple-element.130), channel_id=1, source_target_pairs={{0,24},{8,16},{16,8},{24,0},{1,25},{9,17},{17,9},{25,1},{2,26},{10... | collective-permute-start | bytes 1253384 | tf_op jit(solution)/shard_map/ppermute | solution.py:25
  105.9 2.5 %place.5 = (f32[1024,3072]{1,0:T(8,128)}, f32[768,768]{1,0:T(8,128)S(1)}) custom-call(s32[4]{0:T(128)S(1)} %pad_add_fusion.sel, f32[136,768]{1,0:T(8,128)S(1)} %finish.1.both_ref.refs_0_, f32[136,768]{1,0:T(8,128)S(1)} %hold.11.refs_1_.px0_ref, f32[136,768]{1,0:T(8,128)S(1)} %get-tuple-element.124.py0_ref.refs_2_, ...), custom_call_target="tpu_custom_call" | custom-call | flops 55000000 | bytes 180000 | tf_op jit(solution)/shard_map/place/pallas_call | solution.py:765
  109.8 4.4 %collective-permute-done.24.refs_0_ = f32[136,768]{1,0:T(8,128)S(1)} collective-permute-done((f32[136,768]{1,0:T(8,128)S(1)}, f32[136,768]{1,0:T(8,128)S(1)}, u32[]{:S(2)}, u32[]{:S(2)}) %collective-permute-start.24) | collective-permute-done | bytes 417824 | tf_op jit(solution)/shard_map/ppermute | solution.py:25
  114.2 8.5 %collective-permute-done.27.refs_3_ = f32[136,768]{1,0:T(8,128)S(1)} collective-permute-done((f32[136,768]{1,0:T(8,128)S(1)}, f32[136,768]{1,0:T(8,128)S(1)}, u32[]{:S(2)}, u32[]{:S(2)}) %collective-permute-start.27) | collective-permute-done | bytes 417824 | tf_op jit(solution)/shard_map/ppermute | solution.py:25
  123.2 1.6 %collective-permute-start.28 = (f32[176,768]{1,0:T(8,128)S(1)}, f32[176,768]{1,0:T(8,128)S(1)}, u32[]{:S(2)}, u32[]{:S(2)}) collective-permute-start(f32[176,768]{1,0:T(8,128)S(1)} %stack.23), channel_id=1, source_target_pairs={{0,2},{2,0},{1,3},{3,1},{4,6},{6,4},{5,7},{7,5},{8,10},{10,8},{9,1... | collective-permute-start | bytes 1622024 | tf_op jit(solution)/shard_map/ppermute | solution.py:20
  124.8 3.0 %place.6 = (f32[1024,3072]{1,0:T(8,128)}, f32[512,768]{1,0:T(8,128)S(1)}) custom-call(s32[4]{0:T(128)S(1)} %pad_add_fusion.sel, f32[256,768]{1,0:T(8,128)S(1)} %get-tuple-element.134.refs_1_.refs_0_, f32[256,768]{1,0:T(8,128)S(1)} %get-tuple-element.133.refs_1_, f32[768,768]{1,0:T(8,128)S(1)} %collective-permute-done.31.refs_2_, ...), custom_call_target="tpu_custom_call", output_to_operand_aliasing={{0}: (4, {})} | custom-call | flops 55000000 | bytes 180000 | tf_op jit(solution)/shard_map/place/pallas_call | solution.py:765
  130.0 2.8 %collective-permute-done.30.refs_2_ = f32[168,768]{1,0:T(8,128)S(1)} collective-permute-done((f32[168,768]{1,0:T(8,128)S(1)}, f32[168,768]{1,0:T(8,128)S(1)}, u32[]{:S(2)}, u32[]{:S(2)}) %collective-permute-start.30) | collective-permute-done | bytes 516128 | tf_op jit(solution)/shard_map/ppermute | solution.py:25
  133.5 2.5 %place.8 = (f32[1024,3072]{1,0:T(8,128)}, f32[1,1024]{1,0:T(1,128)}, f32[1,1024]{1,0:T(1,128)}, f32[1,1024]{1,0:T(1,128)}, f32[1,1024]{1,0:T(1,128)}, /*index=5*/f32[1,1024]{1,0:T(1,128)}, f32[1,1024]{1,0:T(1,128)}) custom-call(s32[4]{0:T(128)S(1)} %pad_add_fusion.sel, ...), custom_call_target="tpu_custom_call", output_to_operand_aliasing={{0}: (9, {})} | custom-call | flops 55000000 | bytes 180000 | tf_op jit(solution)/shard_map/place/pallas_call | solution.py:765
  136.3 2.1 %place.9 = f32[1024,3072]{1,0:T(8,128)} custom-call(s32[4]{0:T(128)S(1)} %pad_add_fusion.sel, f32[176,768]{1,0:T(8,128)S(1)} %collective-permute-done.32.refs_0_, f32[176,768]{1,0:T(8,128)S(1)} %collective-permute-done.33.refs_1_, f32[168,768]{1,0:T(8,128)S(1)} %collective-permute-done.34.refs_2_, ...), custom_call_target="tpu_custom_call", output_to_operand_aliasing={{}: (5, {})} | custom-call | flops 55000000 | bytes 180000 | tf_op jit(solution)/shard_map/place/pallas_call | solution.py:765
  (103 shorter events, 31.0 us)
Async XLA Ops:
  1.9 6.9 %collective-permute-start = (f32[176,1024]{1,0:T(8,128)S(1)}, f32[176,1024]{1,0:T(8,128)S(1)}, u32[]{:S(2)}, u32[]{:S(2)}) collective-permute-start(f32[176,1024]{1,0:T(8,128)S(1)} %get-tuple-element.80.tok0.refs_0_), channel_id=1, source_target_pairs={{0,1},{1,0},{2,3},{3,2},{4,5},{5,4},{6,7},{7,6},{8,9},{9,8},{10,11... | collective-permute-start | bytes 2162696 | tf_op jit(solution)/shard_map/ppermute | solution.py:20
  2.4 8.7 %collective-permute-start.1 = (f32[32,1024]{1,0:T(8,128)S(1)}, f32[32,1024]{1,0:T(8,128)S(1)}, u32[]{:S(2)}, u32[]{:S(2)}) collective-permute-start(f32[32,1024]{1,0:T(8,128)S(1)} %slice_bitcast_fusion.2), channel_id=1, source_target_pairs={{0,2},{2,0},{1,3},{3,1},{4,6},{6,4},{5,7},{7,5},{8,10},{10,8},{9,1... | collective-permute-start | bytes 393224 | tf_op jit(solution)/shard_map/ppermute | solution.py:20
  5.0 9.7 %collective-permute-start.3 = (f32[64,1024]{1,0:T(8,128)S(1)}, f32[64,1024]{1,0:T(8,128)S(1)}, u32[]{:S(2)}, u32[]{:S(2)}) collective-permute-start(f32[64,1024]{1,0:T(8,128)S(1)} %slice_bitcast_fusion.1), channel_id=1, source_target_pairs={{0,2},{2,0},{1,3},{3,1},{4,6},{6,4},{5,7},{7,5},{8,10},{10,8},{9,1... | collective-permute-start | bytes 786440 | tf_op jit(solution)/shard_map/ppermute | solution.py:20
  11.1 3.6 %collective-permute-start.2 = (f32[32,1024]{1,0:T(8,128)S(1)}, f32[32,1024]{1,0:T(8,128)S(1)}, u32[]{:S(2)}, u32[]{:S(2)}) collective-permute-start(f32[32,1024]{1,0:T(8,128)S(1)} %hold.8.refs_0_.refs_2_), channel_id=1, source_target_pairs={{0,1},{1,0},{2,3},{3,2},{4,5},{5,4},{6,7},{7,6},{8,9},{9,8},{10,11... | collective-permute-start | bytes 393224 | tf_op jit(solution)/shard_map/ppermute | solution.py:20
  12.3 10.5 %collective-permute-start.5 = (f32[80,1024]{1,0:T(8,128)S(1)}, f32[80,1024]{1,0:T(8,128)S(1)}, u32[]{:S(2)}, u32[]{:S(2)}) collective-permute-start(f32[80,1024]{1,0:T(8,128)S(1)} %slice_bitcast_fusion), channel_id=1, source_target_pairs={{0,2},{2,0},{1,3},{3,1},{4,6},{6,4},{5,7},{7,5},{8,10},{10,8},{9,1... | collective-permute-start | bytes 983048 | tf_op jit(solution)/shard_map/ppermute | solution.py:20
  15.3 16.5 %collective-permute-start.8 = (f32[352,256]{1,0:T(8,128)S(1)}, f32[352,256]{1,0:T(8,128)S(1)}, u32[]{:S(2)}, u32[]{:S(2)}) collective-permute-start(f32[352,256]{1,0:T(8,128)S(1)} %pack_cot.1), channel_id=1, source_target_pairs={{0,2},{2,0},{1,3},{3,1},{4,6},{6,4},{5,7},{7,5},{8,10},{10,8},{9,1... | collective-permute-start | bytes 1081352 | tf_op jit(solution)/shard_map/ppermute | solution.py:20
  36.1 12.0 %collective-permute-start.10 = (f32[128,768]{1,0:T(8,128)S(1)}, f32[128,768]{1,0:T(8,128)S(1)}, u32[]{:S(2)}, u32[]{:S(2)}) collective-permute-start(f32[128,768]{1,0:T(8,128)S(1)} %get-tuple-element.109), channel_id=1, source_target_pairs={{0,4},{4,0},{1,5},{5,1},{2,6},{6,2},{3,7},{7,3},{8,12},{12,8},{9,1... | collective-permute-start | bytes 1179656 | tf_op jit(solution)/shard_map/ppermute | solution.py:20
  39.2 17.2 %collective-permute-start.14 = (f32[128,768]{1,0:T(8,128)S(1)}, f32[128,768]{1,0:T(8,128)S(1)}, u32[]{:S(2)}, u32[]{:S(2)}) collective-permute-start(f32[128,768]{1,0:T(8,128)S(1)} %get-tuple-element.110.refs_0_), channel_id=1, source_target_pairs={{0,4},{4,0},{1,5},{5,1},{2,6},{6,2},{3,7},{7,3},{8,12},{12,8},{9,1... | collective-permute-start | bytes 1179656 | tf_op jit(solution)/shard_map/ppermute | solution.py:20
  39.4 11.3 %collective-permute-start.11 = (f32[128,768]{1,0:T(8,128)S(1)}, f32[128,768]{1,0:T(8,128)S(1)}, u32[]{:S(2)}, u32[]{:S(2)}) collective-permute-start(f32[128,768]{1,0:T(8,128)S(1)} %get-tuple-element.114), channel_id=1, source_target_pairs={{0,8},{8,0},{16,24},{24,16},{1,9},{9,1},{17,25},{25,17},{2,10},{10... | collective-permute-start | bytes 1179656 | tf_op jit(solution)/shard_map/ppermute | solution.py:25
  48.1 12.2 %collective-permute-start.15 = (f32[128,768]{1,0:T(8,128)S(1)}, f32[128,768]{1,0:T(8,128)S(1)}, u32[]{:S(2)}, u32[]{:S(2)}) collective-permute-start(f32[128,768]{1,0:T(8,128)S(1)} %add.10.refs_0_), channel_id=1, source_target_pairs={{0,8},{8,0},{16,24},{24,16},{1,9},{9,1},{17,25},{25,17},{2,10},{10... | collective-permute-start | bytes 1179656 | tf_op jit(solution)/shard_map/ppermute | solution.py:25
  50.2 14.2 %collective-permute-start.9 = (f32[360,1280]{1,0:T(8,128)S(1)}, f32[360,1280]{1,0:T(8,128)S(1)}, u32[]{:S(2)}, u32[]{:S(2)}) collective-permute-start(f32[360,1280]{1,0:T(8,128)S(1)} %get-tuple-element.107.refs_2_.refs_0_), channel_id=1, source_target_pairs={{0,1},{1,0},{2,3},{3,2},{4,5},{5,4},{6,7},{7,6},{8,9},{9,8},{10,11... | collective-permute-start | bytes 5529608 | tf_op jit(solution)/shard_map/ppermute | solution.py:20
  50.2 18.0 %collective-permute-start.13 = (f32[128,768]{1,0:T(8,128)S(1)}, f32[128,768]{1,0:T(8,128)S(1)}, u32[]{:S(2)}, u32[]{:S(2)}) collective-permute-start(f32[128,768]{1,0:T(8,128)S(1)} %get-tuple-element.115), channel_id=1, source_target_pairs={{0,8},{8,0},{16,24},{24,16},{1,9},{9,1},{17,25},{25,17},{2,10},{10... | collective-permute-start | bytes 1179656 | tf_op jit(solution)/shard_map/ppermute | solution.py:25
  50.7 17.5 %collective-permute-start.12 = (f32[128,768]{1,0:T(8,128)S(1)}, f32[128,768]{1,0:T(8,128)S(1)}, u32[]{:S(2)}, u32[]{:S(2)}) collective-permute-start(f32[128,768]{1,0:T(8,128)S(1)} %add.11), channel_id=1, source_target_pairs={{0,4},{4,0},{1,5},{5,1},{2,6},{6,2},{3,7},{7,3},{8,12},{12,8},{9,1... | collective-permute-start | bytes 1179656 | tf_op jit(solution)/shard_map/ppermute | solution.py:20
  60.3 17.5 %collective-permute-start.16 = (f32[128,768]{1,0:T(8,128)S(1)}, f32[128,768]{1,0:T(8,128)S(1)}, u32[]{:S(2)}, u32[]{:S(2)}) collective-permute-start(f32[128,768]{1,0:T(8,128)S(1)} %add.13), channel_id=1, source_target_pairs={{0,24},{8,16},{16,8},{24,0},{1,25},{9,17},{17,9},{25,1},{2,26},{10... | collective-permute-start | bytes 1179656 | tf_op jit(solution)/shard_map/ppermute | solution.py:25
  65.3 19.7 %collective-permute-start.20 = (f32[176,1024]{1,0:T(8,128)S(1)}, f32[176,1024]{1,0:T(8,128)S(1)}, u32[]{:S(2)}, u32[]{:S(2)}) collective-permute-start(f32[176,1024]{1,0:T(8,128)S(1)} %get-tuple-element.119), channel_id=1, source_target_pairs={{0,2},{2,0},{1,3},{3,1},{4,6},{6,4},{5,7},{7,5},{8,10},{10,8},{9,1... | collective-permute-start | bytes 2162696 | tf_op jit(solution)/shard_map/ppermute | solution.py:20
  77.9 10.5 %collective-permute-start.19 = (f32[136,768]{1,0:T(8,128)S(1)}, f32[136,768]{1,0:T(8,128)S(1)}, u32[]{:S(2)}, u32[]{:S(2)}) collective-permute-start(f32[136,768]{1,0:T(8,128)S(1)} %finish.1.both_ref.refs_0_), channel_id=1, source_target_pairs={{0,2},{2,0},{1,3},{3,1},{4,6},{6,4},{5,7},{7,5},{8,10},{10,8},{9,1... | collective-permute-start | bytes 1253384 | tf_op jit(solution)/shard_map/ppermute | solution.py:20
  79.5 14.4 %collective-permute-start.17 = (f32[136,768]{1,0:T(8,128)S(1)}, f32[136,768]{1,0:T(8,128)S(1)}, u32[]{:S(2)}, u32[]{:S(2)}) collective-permute-start(f32[136,768]{1,0:T(8,128)S(1)} %finish.1.both_ref.refs_0_), channel_id=1, source_target_pairs={{0,24},{8,16},{16,8},{24,0},{1,25},{9,17},{17,9},{25,1},{2,26},{10... | collective-permute-start | bytes 1253384 | tf_op jit(solution)/shard_map/ppermute | solution.py:25
  81.0 18.0 %collective-permute-start.18 = (f32[136,768]{1,0:T(8,128)S(1)}, f32[136,768]{1,0:T(8,128)S(1)}, u32[]{:S(2)}, u32[]{:S(2)}) collective-permute-start(f32[136,768]{1,0:T(8,128)S(1)} %finish.1.both_ref.refs_0_), channel_id=1, source_target_pairs={{0,8},{8,0},{16,24},{24,16},{1,9},{9,1},{17,25},{25,17},{2,10},{10... | collective-permute-start | bytes 1253384 | tf_op jit(solution)/shard_map/ppermute | solution.py:25
  83.5 15.5 %collective-permute-start.22 = (f32[136,768]{1,0:T(8,128)S(1)}, f32[136,768]{1,0:T(8,128)S(1)}, u32[]{:S(2)}, u32[]{:S(2)}) collective-permute-start(f32[136,768]{1,0:T(8,128)S(1)} %finish.1.both_ref.refs_0_), channel_id=1, source_target_pairs={{0,4},{4,0},{1,5},{5,1},{2,6},{6,2},{3,7},{7,3},{8,12},{12,8},{9,1... | collective-permute-start | bytes 1253384 | tf_op jit(solution)/shard_map/ppermute | solution.py:20
  88.4 12.0 %collective-permute-start.21 = (f32[136,768]{1,0:T(8,128)S(1)}, f32[136,768]{1,0:T(8,128)S(1)}, u32[]{:S(2)}, u32[]{:S(2)}) collective-permute-start(f32[136,768]{1,0:T(8,128)S(1)} %hold.11.refs_1_.px0_ref), channel_id=1, source_target_pairs={{0,4},{4,0},{1,5},{5,1},{2,6},{6,2},{3,7},{7,3},{8,12},{12,8},{9,1... | collective-permute-start | bytes 1253384 | tf_op jit(solution)/shard_map/ppermute | solution.py:20
  90.0 9.0 %collective-permute-start.23 = (f32[176,512]{1,0:T(8,128)S(1)}, f32[176,512]{1,0:T(8,128)S(1)}, u32[]{:S(2)}, u32[]{:S(2)}) collective-permute-start(f32[176,512]{1,0:T(8,128)S(1)} %hold.12), channel_id=1, source_target_pairs={{0,2},{2,0},{1,3},{3,1},{4,6},{6,4},{5,7},{7,5},{8,10},{10,8},{9,1... | collective-permute-start | bytes 1081352 | tf_op jit(solution)/shard_map/ppermute | solution.py:20
  100.6 22.1 %collective-permute-start.25 = (f32[256,768]{1,0:T(8,128)S(1)}, f32[256,768]{1,0:T(8,128)S(1)}, u32[]{:S(2)}, u32[]{:S(2)}) collective-permute-start(f32[256,768]{1,0:T(8,128)S(1)} %get-tuple-element.129.refs_4_), channel_id=1, source_target_pairs={{0,2},{2,0},{1,3},{3,1},{4,6},{6,4},{5,7},{7,5},{8,10},{10,8},{9,1... | collective-permute-start | bytes 2359304 | tf_op jit(solution)/shard_map/ppermute | solution.py:20
  100.9 21.8 %collective-permute-start.26 = (f32[256,768]{1,0:T(8,128)S(1)}, f32[256,768]{1,0:T(8,128)S(1)}, u32[]{:S(2)}, u32[]{:S(2)}) collective-permute-start(f32[256,768]{1,0:T(8,128)S(1)} %get-tuple-element.129.refs_4_), channel_id=1, source_target_pairs={{0,4},{4,0},{1,5},{5,1},{2,6},{6,2},{3,7},{7,3},{8,12},{12,8},{9,1... | collective-permute-start | bytes 2359304 | tf_op jit(solution)/shard_map/ppermute | solution.py:20
  102.3 11.8 %collective-permute-start.24 = (f32[136,768]{1,0:T(8,128)S(1)}, f32[136,768]{1,0:T(8,128)S(1)}, u32[]{:S(2)}, u32[]{:S(2)}) collective-permute-start(f32[136,768]{1,0:T(8,128)S(1)} %get-tuple-element.128.refs_4_), channel_id=1, source_target_pairs={{0,8},{8,0},{16,24},{24,16},{1,9},{9,1},{17,25},{25,17},{2,10},{10... | collective-permute-start | bytes 1253384 | tf_op jit(solution)/shard_map/ppermute | solution.py:25
  103.0 19.7 %collective-permute-start.27 = (f32[136,768]{1,0:T(8,128)S(1)}, f32[136,768]{1,0:T(8,128)S(1)}, u32[]{:S(2)}, u32[]{:S(2)}) collective-permute-start(f32[136,768]{1,0:T(8,128)S(1)} %get-tuple-element.130), channel_id=1, source_target_pairs={{0,24},{8,16},{16,8},{24,0},{1,25},{9,17},{17,9},{25,1},{2,26},{10... | collective-permute-start | bytes 1253384 | tf_op jit(solution)/shard_map/ppermute | solution.py:25
  108.4 16.4 %collective-permute-start.31 = (f32[768,768]{1,0:T(8,128)S(1)}, f32[768,768]{1,0:T(8,128)S(1)}, u32[]{:S(2)}, u32[]{:S(2)}) collective-permute-start(f32[768,768]{1,0:T(8,128)S(1)} %get-tuple-element.131.refs_4_.refs_0_), channel_id=1, source_target_pairs={{0,1},{1,0},{2,3},{3,2},{4,5},{5,4},{6,7},{7,6},{8,9},{9,8},{10,11... | collective-permute-start | bytes 7077896 | tf_op jit(solution)/shard_map/ppermute | solution.py:20
  122.7 10.1 %collective-permute-start.30 = (f32[168,768]{1,0:T(8,128)S(1)}, f32[168,768]{1,0:T(8,128)S(1)}, u32[]{:S(2)}, u32[]{:S(2)}) collective-permute-start(f32[168,768]{1,0:T(8,128)S(1)} %stack.25), channel_id=1, source_target_pairs={{0,8},{8,0},{16,24},{24,16},{1,9},{9,1},{17,25},{25,17},{2,10},{10... | collective-permute-start | bytes 1548296 | tf_op jit(solution)/shard_map/ppermute | solution.py:25
  122.9 10.0 %collective-permute-start.29 = (f32[176,768]{1,0:T(8,128)S(1)}, f32[176,768]{1,0:T(8,128)S(1)}, u32[]{:S(2)}, u32[]{:S(2)}) collective-permute-start(f32[176,768]{1,0:T(8,128)S(1)} %stack.24), channel_id=1, source_target_pairs={{0,4},{4,0},{1,5},{5,1},{2,6},{6,2},{3,7},{7,3},{8,12},{12,8},{9,1... | collective-permute-start | bytes 1622024 | tf_op jit(solution)/shard_map/ppermute | solution.py:20
  123.2 9.6 %collective-permute-start.28 = (f32[176,768]{1,0:T(8,128)S(1)}, f32[176,768]{1,0:T(8,128)S(1)}, u32[]{:S(2)}, u32[]{:S(2)}) collective-permute-start(f32[176,768]{1,0:T(8,128)S(1)} %stack.23), channel_id=1, source_target_pairs={{0,2},{2,0},{1,3},{3,1},{4,6},{6,4},{5,7},{7,5},{8,10},{10,8},{9,1... | collective-permute-start | bytes 1622024 | tf_op jit(solution)/shard_map/ppermute | solution.py:20
  127.8 5.7 %collective-permute-start.36 = (f32[512,768]{1,0:T(8,128)S(1)}, f32[512,768]{1,0:T(8,128)S(1)}, u32[]{:S(2)}, u32[]{:S(2)}) collective-permute-start(f32[512,768]{1,0:T(8,128)S(1)} %get-tuple-element.142.refs_0_), channel_id=1, source_target_pairs={{0,1},{1,0},{2,3},{3,2},{4,5},{5,4},{6,7},{7,6},{8,9},{9,8},{10,11... | collective-permute-start | bytes 4718600 | tf_op jit(solution)/shard_map/ppermute | solution.py:20
  129.5 6.9 %collective-permute-start.35 = (f32[256,768]{1,0:T(8,128)S(1)}, f32[256,768]{1,0:T(8,128)S(1)}, u32[]{:S(2)}, u32[]{:S(2)}) collective-permute-start(f32[256,768]{1,0:T(8,128)S(1)} %get-tuple-element.138.refs_3_.refs_1_), channel_id=1, source_target_pairs={{0,1},{1,0},{2,3},{3,2},{4,5},{5,4},{6,7},{7,6},{8,9},{9,8},{10,11... | collective-permute-start | bytes 2359304 | tf_op jit(solution)/shard_map/ppermute | solution.py:20
  132.8 3.5 %collective-permute-start.32 = (f32[176,768]{1,0:T(8,128)S(1)}, f32[176,768]{1,0:T(8,128)S(1)}, u32[]{:S(2)}, u32[]{:S(2)}) collective-permute-start(f32[176,768]{1,0:T(8,128)S(1)} %get-tuple-element.139.refs_2_.refs_0_), channel_id=1, source_target_pairs={{0,1},{1,0},{2,3},{3,2},{4,5},{5,4},{6,7},{7,6},{8,9},{9,8},{10,11... | collective-permute-start | bytes 1622024 | tf_op jit(solution)/shard_map/ppermute | solution.py:20
  (14 other events, 24.8 us)

commit v7 on v6

--- a/solution.py
+++ b/solution.py
@@ -875,7 +875,7 @@
         corner0 = swap(px0, "y")
         (sent_out,) = hold((sent_out,), px0)
         got_out = swap(sent_out, "x")
-        z3, z1, corner0, py0, got_out = hold((z3, z1, corner0, py0, got_out))
+        py0, corner0, got_out, z1, z3 = hold((py0, corner0, got_out, z1, z3))
         output = join_out(sel, kept_out, got_out)
         full = part + 8
         z13, zs, cs = second(both, px0, py0, corner0, z1, z3)
@@ -890,7 +890,7 @@
             (4, part, part, (3, 0), 0, 0, 0),
         ]
         proj_grad, give = place(sel, (both, px0, py0, corner0, z13), own, None, width, 6)
-        z2, px13, py13, corner3 = hold((z2, px13, py13, corner3), give)
+        px13, py13, z2, corner3 = hold((px13, py13, z2, corner3), give)
         by_x, by_y = 3 * part // 8, 3 * part // 8
         rest = part - by_x - by_y
         px2 = swap(stack((z2, 0, part), (py13, 0, by_x)), "x")

time: 139 us -> 137 us (0.986)
  waiting for transfers between devices: 55.3 us -> 53.6 us
    ppermute x9, waiting for transfers between devices: 38.2 us -> 36.2 us  [xor_permute(): return lax.ppermute(block, axis, [(i, i ^ distance) for i in range(size)])]
where the time goes in v7:
time: 137 us
  waiting for transfers between devices  53.6 us (39%)
  starting transfers between devices  40.1 us (29%)
  Pallas kernels  37.8 us (28%)
  local copies, waits for them, and re-layouts  2.88 us (2%)
    ppermute x9, waiting for transfers between devices, xor_permute(): return lax.ppermute(block, axis, [(i, i ^ distance) for i in range(size)])  36.2 us
    ppermute x28, starting transfers between devices, swap(): return lax.ppermute(block, axis, SWAP)  25 us
    ppermute x28, waiting for transfers between devices, swap(): return lax.ppermute(block, axis, SWAP)  17.4 us
    ppermute x9, starting transfers between devices, xor_permute(): return lax.ppermute(block, axis, [(i, i ^ distance) for i in range(size)])  15.1 us
    pallas_call x5, Pallas kernels, place(): pl.pallas_call(functools.partial(place_kernel, where=where, give=give, co...  11.8 us
    pallas_call x1, Pallas kernels, run_forward(): pl.pallas_call(forward_kernel, out_shape=(shaped((length // 2, width), BF...  7.21 us
    pallas_call x1, Pallas kernels, run_backward(): pl.pallas_call(functools.partial(backward_kernel, rows=rows, count=len(to...  4.33 us
    pallas_call x1, Pallas kernels, run_input(): pl.pallas_call(functools.partial(input_kernel, count=len(toks)), out_shap...  2.86 us
  transfers between devices with their start and end apart: 37, of which 17 were waited for; matrix products, arithmetic and copies ran while one was open for 0% of the time, Pallas kernels for 23%

profile of v7, /device:TPU:0, one launch (start us, length us, event | category | flops | bytes accessed | tf_op | source)
XLA Modules:
  0.0 136.7 jit_solution(13186608462459675785)
XLA Ops:
  2.4 2.6 %collective-permute-start.1 = (f32[32,1024]{1,0:T(8,128)S(1)}, f32[32,1024]{1,0:T(8,128)S(1)}, u32[]{:S(2)}, u32[]{:S(2)}) collective-permute-start(f32[32,1024]{1,0:T(8,128)S(1)} %slice_bitcast_fusion.2), channel_id=1, source_target_pairs={{0,2},{2,0},{1,3},{3,1},{4,6},{6,4},{5,7},{7,5},{8,10},{10,8},{9,1... | collective-permute-start | bytes 393224 | tf_op jit(solution)/shard_map/ppermute | solution.py:20
  5.1 2.8 %copy-done = bf16[1024,3072]{1,0:T(8,128)(2,1)S(1)} copy-done((bf16[1024,3072]{1,0:T(8,128)(2,1)S(1)}, bf16[1024,3072]{1,0:T(8,128)(2,1)}, u32[]{:S(2)}) %copy-start) | copy-done | bytes 6291480
  8.8 2.2 %near_blocks.1 = (bf16[352,1024]{1,0:T(8,128)(2,1)S(1)}, f32[352,256]{1,0:T(8,128)S(1)}, f32[352,256]{1,0:T(8,128)S(1)}, f32[352,256]{1,0:T(8,128)S(1)}, f32[352,256]{1,0:T(8,128)S(1)}, /*index=5*/f32[704,256]{1,0:T(8,128)S(1)}) custom-call(s32[4]{0:T(128)S(1)} %pad_add_fusion.sel, s32[1,8]{1,0:T(1,128)S(1)} %copy-done.8, ...), custom_call_target="tpu_custom_call" | custom-call | flops 55000000 | bytes 180000 | tf_op jit(solution)/shard_map/near_blocks/pallas_call | solution.py:272
  12.3 1.9 %collective-permute-start.5 = (f32[80,1024]{1,0:T(8,128)S(1)}, f32[80,1024]{1,0:T(8,128)S(1)}, u32[]{:S(2)}, u32[]{:S(2)}) collective-permute-start(f32[80,1024]{1,0:T(8,128)S(1)} %slice_bitcast_fusion), channel_id=1, source_target_pairs={{0,2},{2,0},{1,3},{3,1},{4,6},{6,4},{5,7},{7,5},{8,10},{10,8},{9,1... | collective-permute-start | bytes 983048 | tf_op jit(solution)/shard_map/ppermute | solution.py:20
  15.3 1.8 %collective-permute-start.8 = (f32[352,256]{1,0:T(8,128)S(1)}, f32[352,256]{1,0:T(8,128)S(1)}, u32[]{:S(2)}, u32[]{:S(2)}) collective-permute-start(f32[352,256]{1,0:T(8,128)S(1)} %pack_cot.1), channel_id=1, source_target_pairs={{0,2},{2,0},{1,3},{3,1},{4,6},{6,4},{5,7},{7,5},{8,10},{10,8},{9,1... | collective-permute-start | bytes 1081352 | tf_op jit(solution)/shard_map/ppermute | solution.py:20
  18.3 4.5 %collective-permute-done.5.refs_0_ = f32[80,1024]{1,0:T(8,128)S(1)} collective-permute-done((f32[80,1024]{1,0:T(8,128)S(1)}, f32[80,1024]{1,0:T(8,128)S(1)}, u32[]{:S(2)}, u32[]{:S(2)}) %collective-permute-start.5) | collective-permute-done | bytes 327712 | tf_op jit(solution)/shard_map/ppermute | solution.py:20
  22.9 1.6 %collective-permute-done.6.tok1.refs_7_ = f32[80,1024]{1,0:T(8,128)S(1)} collective-permute-done((f32[80,1024]{1,0:T(8,128)S(1)}, f32[80,1024]{1,0:T(8,128)S(1)}, u32[]{:S(2)}, u32[]{:S(2)}) %collective-permute-start.6) | collective-permute-done | bytes 327712 | tf_op jit(solution)/shard_map/ppermute | solution.py:20
  24.5 7.2 %forward_scan.1 = (bf16[352,1024]{1,0:T(8,128)(2,1)S(1)}, f32[352,256]{1,0:T(8,128)S(1)}, f32[704,256]{1,0:T(8,128)S(1)}, f32[704,256]{1,0:T(8,128)S(1)}, f32[70...) custom-call(s32[4]{0:T(128)S(1)} %pad_add_fusion.sel, f32[80,1024]{1,0:T(8,128)S(1)} %hold.10.tok0.refs_6_, ...), custom_call_target="tpu_custom_call" | custom-call | flops 55000000 | bytes 180000 | tf_op jit(solution)/shard_map/forward_scan/pallas_call | solution.py:362
  31.7 4.3 %backward_scan.1 = (bf16[704,768]{1,0:T(8,128)(2,1)S(1)}, f32[704,256]{1,0:T(8,128)S(1)}, f32[704,256]{1,0:T(8,128)S(1)}, f32[8,256]{1,0:T(8,128)S(1)}, f32[128,768]{1,0:T(8,128)S(1)}, /*index=5*/f32[128,768]{1,0:T(8,128)S(1)}) custom-call(s32[4]{0:T(128)S(1)} %pad_add_fusion.sel, f32[176,1024]{1,0:T(8,128)S(1)} %get-tuple-element.80.tok0.refs_0_, ...), custom_call_target="tpu_custom_call" | custom-call | flops 55000000 | bytes 180000 | tf_op jit(solution)/shard_map/backward_scan/pallas_call | solution.py:479
  36.1 2.0 %collective-permute-start.10 = (f32[128,768]{1,0:T(8,128)S(1)}, f32[128,768]{1,0:T(8,128)S(1)}, u32[]{:S(2)}, u32[]{:S(2)}) collective-permute-start(f32[128,768]{1,0:T(8,128)S(1)} %get-tuple-element.109), channel_id=1, source_target_pairs={{0,4},{4,0},{1,5},{5,1},{2,6},{6,2},{3,7},{7,3},{8,12},{12,8},{9,1... | collective-permute-start | bytes 1179656 | tf_op jit(solution)/shard_map/ppermute | solution.py:20
  39.4 2.0 %collective-permute-start.11 = (f32[128,768]{1,0:T(8,128)S(1)}, f32[128,768]{1,0:T(8,128)S(1)}, u32[]{:S(2)}, u32[]{:S(2)}) collective-permute-start(f32[128,768]{1,0:T(8,128)S(1)} %get-tuple-element.114), channel_id=1, source_target_pairs={{0,8},{8,0},{16,24},{24,16},{1,9},{9,1},{17,25},{25,17},{2,10},{10... | collective-permute-start | bytes 1179656 | tf_op jit(solution)/shard_map/ppermute | solution.py:25
  41.4 1.6 %products.3 = (f32[128,768]{1,0:T(8,128)S(1)}, f32[128,768]{1,0:T(8,128)S(1)}, f32[128,768]{1,0:T(8,128)S(1)}, f32[128,768]{1,0:T(8,128)S(1)}) custom-call(s32[4]{0:T(128)S(1)} %pad_add_fusion.sel, bf16[352,1024]{1,0:T(8,128)(2,1)S(1)} %get-tuple-element.100.refs_19_.near_ref, bf16[352,1024]{1,0:T(8,128)(2,1)S(1)} %get-tuple-element.101.refs_20_.far_ref, ...), custom_call_target="tpu_custom_call" | custom-call | flops 55000000 | bytes 180000 | tf_op jit(solution)/shard_map/products/pallas_call | solution.py:502
  43.0 2.9 %input_side.1 = (f32[360,1280]{1,0:T(8,128)S(1)}, f32[360,1280]{1,0:T(8,128)S(1)}) custom-call(s32[4]{0:T(128)S(1)} %pad_add_fusion.sel, f32[176,1024]{1,0:T(8,128)S(1)} %get-tuple-element.80.tok0.refs_0_, f32[176,1024]{1,0:T(8,128)S(1)} %collective-permute-done.tok1.refs_1_, f32[32,1024]{1,0:T(8,128)S(1)} %hold.8.refs_0_.refs_2_, ...), custom_call_target="tpu_custom_call" | custom-call | flops 55000000 | bytes 180000 | tf_op jit(solution)/shard_map/input_side/pallas_call | solution.py:570
  45.8 2.2 %collective-permute-done.10.b_ref = f32[128,768]{1,0:T(8,128)S(1)} collective-permute-done((f32[128,768]{1,0:T(8,128)S(1)}, f32[128,768]{1,0:T(8,128)S(1)}, u32[]{:S(2)}, u32[]{:S(2)}) %collective-permute-start.10) | collective-permute-done | bytes 393248 | tf_op jit(solution)/shard_map/ppermute | solution.py:20
  48.1 2.2 %collective-permute-start.15 = (f32[128,768]{1,0:T(8,128)S(1)}, f32[128,768]{1,0:T(8,128)S(1)}, u32[]{:S(2)}, u32[]{:S(2)}) collective-permute-start(f32[128,768]{1,0:T(8,128)S(1)} %add.10.refs_0_), channel_id=1, source_target_pairs={{0,8},{8,0},{16,24},{24,16},{1,9},{9,1},{17,25},{25,17},{2,10},{10... | collective-permute-start | bytes 1179656 | tf_op jit(solution)/shard_map/ppermute | solution.py:25
  50.7 1.9 %collective-permute-start.12 = (f32[128,768]{1,0:T(8,128)S(1)}, f32[128,768]{1,0:T(8,128)S(1)}, u32[]{:S(2)}, u32[]{:S(2)}) collective-permute-start(f32[128,768]{1,0:T(8,128)S(1)} %add.11), channel_id=1, source_target_pairs={{0,4},{4,0},{1,5},{5,1},{2,6},{6,2},{3,7},{7,3},{8,12},{12,8},{9,1... | collective-permute-start | bytes 1179656 | tf_op jit(solution)/shard_map/ppermute | solution.py:20
  52.6 3.8 %collective-permute-done.14.b_ref = f32[128,768]{1,0:T(8,128)S(1)} collective-permute-done((f32[128,768]{1,0:T(8,128)S(1)}, f32[128,768]{1,0:T(8,128)S(1)}, u32[]{:S(2)}, u32[]{:S(2)}) %collective-permute-start.14) | collective-permute-done | bytes 393248 | tf_op jit(solution)/shard_map/ppermute | solution.py:20
  56.5 3.7 %collective-permute-done.15.b_ref = f32[128,768]{1,0:T(8,128)S(1)} collective-permute-done((f32[128,768]{1,0:T(8,128)S(1)}, f32[128,768]{1,0:T(8,128)S(1)}, u32[]{:S(2)}, u32[]{:S(2)}) %collective-permute-start.15) | collective-permute-done | bytes 393248 | tf_op jit(solution)/shard_map/ppermute | solution.py:25
  60.3 4.1 %collective-permute-start.16 = (f32[128,768]{1,0:T(8,128)S(1)}, f32[128,768]{1,0:T(8,128)S(1)}, u32[]{:S(2)}, u32[]{:S(2)}) collective-permute-start(f32[128,768]{1,0:T(8,128)S(1)} %add.13), channel_id=1, source_target_pairs={{0,24},{8,16},{16,8},{24,0},{1,25},{9,17},{17,9},{25,1},{2,26},{10... | collective-permute-start | bytes 1179656 | tf_op jit(solution)/shard_map/ppermute | solution.py:25
  68.2 9.6 %collective-permute-done.16.a3_ref = f32[128,768]{1,0:T(8,128)S(1)} collective-permute-done((f32[128,768]{1,0:T(8,128)S(1)}, f32[128,768]{1,0:T(8,128)S(1)}, u32[]{:S(2)}, u32[]{:S(2)}) %collective-permute-start.16) | collective-permute-done | bytes 393248 | tf_op jit(solution)/shard_map/ppermute | solution.py:25
  81.8 2.5 %collective-permute-start.23 = (f32[136,768]{1,0:T(8,128)S(1)}, f32[136,768]{1,0:T(8,128)S(1)}, u32[]{:S(2)}, u32[]{:S(2)}) collective-permute-start(f32[136,768]{1,0:T(8,128)S(1)} %finish.1.both_ref.refs_0_), channel_id=1, source_target_pairs={{0,24},{8,16},{16,8},{24,0},{1,25},{9,17},{17,9},{25,1},{2,26},{10... | collective-permute-start | bytes 1253384 | tf_op jit(solution)/shard_map/ppermute | solution.py:25
  85.1 3.3 %collective-permute-done.18.refs_0_ = f32[136,768]{1,0:T(8,128)S(1)} collective-permute-done((f32[136,768]{1,0:T(8,128)S(1)}, f32[136,768]{1,0:T(8,128)S(1)}, u32[]{:S(2)}, u32[]{:S(2)}) %collective-permute-start.18) | collective-permute-done | bytes 417824 | tf_op jit(solution)/shard_map/ppermute | solution.py:20
  91.5 7.7 %collective-permute-done.22.refs_3_ = f32[136,768]{1,0:T(8,128)S(1)} collective-permute-done((f32[136,768]{1,0:T(8,128)S(1)}, f32[136,768]{1,0:T(8,128)S(1)}, u32[]{:S(2)}, u32[]{:S(2)}) %collective-permute-start.22) | collective-permute-done | bytes 417824 | tf_op jit(solution)/shard_map/ppermute | solution.py:25
  101.1 3.2 %collective-permute-start.26 = (f32[136,768]{1,0:T(8,128)S(1)}, f32[136,768]{1,0:T(8,128)S(1)}, u32[]{:S(2)}, u32[]{:S(2)}) collective-permute-start(f32[136,768]{1,0:T(8,128)S(1)} %get-tuple-element.129.refs_4_), channel_id=1, source_target_pairs={{0,8},{8,0},{16,24},{24,16},{1,9},{9,1},{17,25},{25,17},{2,10},{10... | collective-permute-start | bytes 1253384 | tf_op jit(solution)/shard_map/ppermute | solution.py:25
  104.5 2.5 %place.5 = (f32[1024,3072]{1,0:T(8,128)}, f32[768,768]{1,0:T(8,128)S(1)}) custom-call(s32[4]{0:T(128)S(1)} %pad_add_fusion.sel, f32[136,768]{1,0:T(8,128)S(1)} %finish.1.both_ref.refs_0_, f32[136,768]{1,0:T(8,128)S(1)} %hold.11.refs_1_.px0_ref, f32[136,768]{1,0:T(8,128)S(1)} %get-tuple-element.124.py0_ref.refs_2_, ...), custom_call_target="tpu_custom_call" | custom-call | flops 55000000 | bytes 180000 | tf_op jit(solution)/shard_map/place/pallas_call | solution.py:765
  108.4 8.3 %collective-permute-done.26.refs_2_ = f32[136,768]{1,0:T(8,128)S(1)} collective-permute-done((f32[136,768]{1,0:T(8,128)S(1)}, f32[136,768]{1,0:T(8,128)S(1)}, u32[]{:S(2)}, u32[]{:S(2)}) %collective-permute-start.26) | collective-permute-done | bytes 417824 | tf_op jit(solution)/shard_map/ppermute | solution.py:25
  116.7 4.1 %collective-permute-done.27.refs_3_ = f32[136,768]{1,0:T(8,128)S(1)} collective-permute-done((f32[136,768]{1,0:T(8,128)S(1)}, f32[136,768]{1,0:T(8,128)S(1)}, u32[]{:S(2)}, u32[]{:S(2)}) %collective-permute-start.27) | collective-permute-done | bytes 417824 | tf_op jit(solution)/shard_map/ppermute | solution.py:25
  121.6 2.0 %collective-permute-start.28 = (f32[176,768]{1,0:T(8,128)S(1)}, f32[176,768]{1,0:T(8,128)S(1)}, u32[]{:S(2)}, u32[]{:S(2)}) collective-permute-start(f32[176,768]{1,0:T(8,128)S(1)} %stack.23), channel_id=1, source_target_pairs={{0,2},{2,0},{1,3},{3,1},{4,6},{6,4},{5,7},{7,5},{8,10},{10,8},{9,1... | collective-permute-start | bytes 1622024 | tf_op jit(solution)/shard_map/ppermute | solution.py:20
  123.6 3.0 %place.6 = (f32[1024,3072]{1,0:T(8,128)}, f32[512,768]{1,0:T(8,128)S(1)}) custom-call(s32[4]{0:T(128)S(1)} %pad_add_fusion.sel, f32[256,768]{1,0:T(8,128)S(1)} %get-tuple-element.134.refs_1_.refs_0_, f32[256,768]{1,0:T(8,128)S(1)} %get-tuple-element.133.refs_1_, f32[768,768]{1,0:T(8,128)S(1)} %collective-permute-done.31.refs_2_, ...), custom_call_target="tpu_custom_call", output_to_operand_aliasing={{0}: (4, {})} | custom-call | flops 55000000 | bytes 180000 | tf_op jit(solution)/shard_map/place/pallas_call | solution.py:765
  126.7 1.6 %place.7 = (f32[1024,3072]{1,0:T(8,128)}, f32[256,768]{1,0:T(8,128)S(1)}) custom-call(s32[4]{0:T(128)S(1)} %pad_add_fusion.sel, f32[136,768]{1,0:T(8,128)S(1)} %get-tuple-element.132.refs_0_.refs_5_, f32[136,768]{1,0:T(8,128)S(1)} %get-tuple-element.135.refs_0_.refs_2_.refs_1_.refs_7_, ...), custom_call_target="tpu_custom_call", output_to_operand_aliasing={{0}: (3, {})} | custom-call | flops 55000000 | bytes 180000 | tf_op jit(solution)/shard_map/place/pallas_call | solution.py:765
  131.6 2.5 %place.8 = (f32[1024,3072]{1,0:T(8,128)}, f32[1,1024]{1,0:T(1,128)}, f32[1,1024]{1,0:T(1,128)}, f32[1,1024]{1,0:T(1,128)}, f32[1,1024]{1,0:T(1,128)}, /*index=5*/f32[1,1024]{1,0:T(1,128)}, f32[1,1024]{1,0:T(1,128)}) custom-call(s32[4]{0:T(128)S(1)} %pad_add_fusion.sel, ...), custom_call_target="tpu_custom_call", output_to_operand_aliasing={{0}: (9, {})} | custom-call | flops 55000000 | bytes 180000 | tf_op jit(solution)/shard_map/place/pallas_call | solution.py:765
  134.5 2.1 %place.9 = f32[1024,3072]{1,0:T(8,128)} custom-call(s32[4]{0:T(128)S(1)} %pad_add_fusion.sel, f32[176,768]{1,0:T(8,128)S(1)} %collective-permute-done.32.refs_0_, f32[176,768]{1,0:T(8,128)S(1)} %collective-permute-done.33.refs_1_, f32[168,768]{1,0:T(8,128)S(1)} %collective-permute-done.34.refs_2_, ...), custom_call_target="tpu_custom_call", output_to_operand_aliasing={{}: (5, {})} | custom-call | flops 55000000 | bytes 180000 | tf_op jit(solution)/shard_map/place/pallas_call | solution.py:765
  (103 shorter events, 27.7 us)
Async XLA Ops:
  1.9 6.9 %collective-permute-start = (f32[176,1024]{1,0:T(8,128)S(1)}, f32[176,1024]{1,0:T(8,128)S(1)}, u32[]{:S(2)}, u32[]{:S(2)}) collective-permute-start(f32[176,1024]{1,0:T(8,128)S(1)} %get-tuple-element.80.tok0.refs_0_), channel_id=1, source_target_pairs={{0,1},{1,0},{2,3},{3,2},{4,5},{5,4},{6,7},{7,6},{8,9},{9,8},{10,11... | collective-permute-start | bytes 2162696 | tf_op jit(solution)/shard_map/ppermute | solution.py:20
  2.4 8.7 %collective-permute-start.1 = (f32[32,1024]{1,0:T(8,128)S(1)}, f32[32,1024]{1,0:T(8,128)S(1)}, u32[]{:S(2)}, u32[]{:S(2)}) collective-permute-start(f32[32,1024]{1,0:T(8,128)S(1)} %slice_bitcast_fusion.2), channel_id=1, source_target_pairs={{0,2},{2,0},{1,3},{3,1},{4,6},{6,4},{5,7},{7,5},{8,10},{10,8},{9,1... | collective-permute-start | bytes 393224 | tf_op jit(solution)/shard_map/ppermute | solution.py:20
  5.0 9.7 %collective-permute-start.3 = (f32[64,1024]{1,0:T(8,128)S(1)}, f32[64,1024]{1,0:T(8,128)S(1)}, u32[]{:S(2)}, u32[]{:S(2)}) collective-permute-start(f32[64,1024]{1,0:T(8,128)S(1)} %slice_bitcast_fusion.1), channel_id=1, source_target_pairs={{0,2},{2,0},{1,3},{3,1},{4,6},{6,4},{5,7},{7,5},{8,10},{10,8},{9,1... | collective-permute-start | bytes 786440 | tf_op jit(solution)/shard_map/ppermute | solution.py:20
  11.1 3.6 %collective-permute-start.2 = (f32[32,1024]{1,0:T(8,128)S(1)}, f32[32,1024]{1,0:T(8,128)S(1)}, u32[]{:S(2)}, u32[]{:S(2)}) collective-permute-start(f32[32,1024]{1,0:T(8,128)S(1)} %hold.8.refs_0_.refs_2_), channel_id=1, source_target_pairs={{0,1},{1,0},{2,3},{3,2},{4,5},{5,4},{6,7},{7,6},{8,9},{9,8},{10,11... | collective-permute-start | bytes 393224 | tf_op jit(solution)/shard_map/ppermute | solution.py:20
  12.3 10.5 %collective-permute-start.5 = (f32[80,1024]{1,0:T(8,128)S(1)}, f32[80,1024]{1,0:T(8,128)S(1)}, u32[]{:S(2)}, u32[]{:S(2)}) collective-permute-start(f32[80,1024]{1,0:T(8,128)S(1)} %slice_bitcast_fusion), channel_id=1, source_target_pairs={{0,2},{2,0},{1,3},{3,1},{4,6},{6,4},{5,7},{7,5},{8,10},{10,8},{9,1... | collective-permute-start | bytes 983048 | tf_op jit(solution)/shard_map/ppermute | solution.py:20
  15.3 16.5 %collective-permute-start.8 = (f32[352,256]{1,0:T(8,128)S(1)}, f32[352,256]{1,0:T(8,128)S(1)}, u32[]{:S(2)}, u32[]{:S(2)}) collective-permute-start(f32[352,256]{1,0:T(8,128)S(1)} %pack_cot.1), channel_id=1, source_target_pairs={{0,2},{2,0},{1,3},{3,1},{4,6},{6,4},{5,7},{7,5},{8,10},{10,8},{9,1... | collective-permute-start | bytes 1081352 | tf_op jit(solution)/shard_map/ppermute | solution.py:20
  36.1 12.0 %collective-permute-start.10 = (f32[128,768]{1,0:T(8,128)S(1)}, f32[128,768]{1,0:T(8,128)S(1)}, u32[]{:S(2)}, u32[]{:S(2)}) collective-permute-start(f32[128,768]{1,0:T(8,128)S(1)} %get-tuple-element.109), channel_id=1, source_target_pairs={{0,4},{4,0},{1,5},{5,1},{2,6},{6,2},{3,7},{7,3},{8,12},{12,8},{9,1... | collective-permute-start | bytes 1179656 | tf_op jit(solution)/shard_map/ppermute | solution.py:20
  39.2 17.2 %collective-permute-start.14 = (f32[128,768]{1,0:T(8,128)S(1)}, f32[128,768]{1,0:T(8,128)S(1)}, u32[]{:S(2)}, u32[]{:S(2)}) collective-permute-start(f32[128,768]{1,0:T(8,128)S(1)} %get-tuple-element.110.refs_0_), channel_id=1, source_target_pairs={{0,4},{4,0},{1,5},{5,1},{2,6},{6,2},{3,7},{7,3},{8,12},{12,8},{9,1... | collective-permute-start | bytes 1179656 | tf_op jit(solution)/shard_map/ppermute | solution.py:20
  39.4 11.3 %collective-permute-start.11 = (f32[128,768]{1,0:T(8,128)S(1)}, f32[128,768]{1,0:T(8,128)S(1)}, u32[]{:S(2)}, u32[]{:S(2)}) collective-permute-start(f32[128,768]{1,0:T(8,128)S(1)} %get-tuple-element.114), channel_id=1, source_target_pairs={{0,8},{8,0},{16,24},{24,16},{1,9},{9,1},{17,25},{25,17},{2,10},{10... | collective-permute-start | bytes 1179656 | tf_op jit(solution)/shard_map/ppermute | solution.py:25
  48.1 12.2 %collective-permute-start.15 = (f32[128,768]{1,0:T(8,128)S(1)}, f32[128,768]{1,0:T(8,128)S(1)}, u32[]{:S(2)}, u32[]{:S(2)}) collective-permute-start(f32[128,768]{1,0:T(8,128)S(1)} %add.10.refs_0_), channel_id=1, source_target_pairs={{0,8},{8,0},{16,24},{24,16},{1,9},{9,1},{17,25},{25,17},{2,10},{10... | collective-permute-start | bytes 1179656 | tf_op jit(solution)/shard_map/ppermute | solution.py:25
  50.2 14.2 %collective-permute-start.9 = (f32[360,1280]{1,0:T(8,128)S(1)}, f32[360,1280]{1,0:T(8,128)S(1)}, u32[]{:S(2)}, u32[]{:S(2)}) collective-permute-start(f32[360,1280]{1,0:T(8,128)S(1)} %get-tuple-element.107.refs_2_.refs_0_), channel_id=1, source_target_pairs={{0,1},{1,0},{2,3},{3,2},{4,5},{5,4},{6,7},{7,6},{8,9},{9,8},{10,11... | collective-permute-start | bytes 5529608 | tf_op jit(solution)/shard_map/ppermute | solution.py:20
  50.2 18.0 %collective-permute-start.13 = (f32[128,768]{1,0:T(8,128)S(1)}, f32[128,768]{1,0:T(8,128)S(1)}, u32[]{:S(2)}, u32[]{:S(2)}) collective-permute-start(f32[128,768]{1,0:T(8,128)S(1)} %get-tuple-element.115), channel_id=1, source_target_pairs={{0,8},{8,0},{16,24},{24,16},{1,9},{9,1},{17,25},{25,17},{2,10},{10... | collective-permute-start | bytes 1179656 | tf_op jit(solution)/shard_map/ppermute | solution.py:25
  50.7 17.5 %collective-permute-start.12 = (f32[128,768]{1,0:T(8,128)S(1)}, f32[128,768]{1,0:T(8,128)S(1)}, u32[]{:S(2)}, u32[]{:S(2)}) collective-permute-start(f32[128,768]{1,0:T(8,128)S(1)} %add.11), channel_id=1, source_target_pairs={{0,4},{4,0},{1,5},{5,1},{2,6},{6,2},{3,7},{7,3},{8,12},{12,8},{9,1... | collective-permute-start | bytes 1179656 | tf_op jit(solution)/shard_map/ppermute | solution.py:20
  60.3 17.5 %collective-permute-start.16 = (f32[128,768]{1,0:T(8,128)S(1)}, f32[128,768]{1,0:T(8,128)S(1)}, u32[]{:S(2)}, u32[]{:S(2)}) collective-permute-start(f32[128,768]{1,0:T(8,128)S(1)} %add.13), channel_id=1, source_target_pairs={{0,24},{8,16},{16,8},{24,0},{1,25},{9,17},{17,9},{25,1},{2,26},{10... | collective-permute-start | bytes 1179656 | tf_op jit(solution)/shard_map/ppermute | solution.py:25
  65.3 19.0 %collective-permute-start.19 = (f32[176,1024]{1,0:T(8,128)S(1)}, f32[176,1024]{1,0:T(8,128)S(1)}, u32[]{:S(2)}, u32[]{:S(2)}) collective-permute-start(f32[176,1024]{1,0:T(8,128)S(1)} %get-tuple-element.119), channel_id=1, source_target_pairs={{0,2},{2,0},{1,3},{3,1},{4,6},{6,4},{5,7},{7,5},{8,10},{10,8},{9,1... | collective-permute-start | bytes 2162696 | tf_op jit(solution)/shard_map/ppermute | solution.py:20
  77.9 10.5 %collective-permute-start.18 = (f32[136,768]{1,0:T(8,128)S(1)}, f32[136,768]{1,0:T(8,128)S(1)}, u32[]{:S(2)}, u32[]{:S(2)}) collective-permute-start(f32[136,768]{1,0:T(8,128)S(1)} %finish.1.both_ref.refs_0_), channel_id=1, source_target_pairs={{0,2},{2,0},{1,3},{3,1},{4,6},{6,4},{5,7},{7,5},{8,10},{10,8},{9,1... | collective-permute-start | bytes 1253384 | tf_op jit(solution)/shard_map/ppermute | solution.py:20
  79.5 12.0 %collective-permute-start.17 = (f32[136,768]{1,0:T(8,128)S(1)}, f32[136,768]{1,0:T(8,128)S(1)}, u32[]{:S(2)}, u32[]{:S(2)}) collective-permute-start(f32[136,768]{1,0:T(8,128)S(1)} %finish.1.both_ref.refs_0_), channel_id=1, source_target_pairs={{0,4},{4,0},{1,5},{5,1},{2,6},{6,2},{3,7},{7,3},{8,12},{12,8},{9,1... | collective-permute-start | bytes 1253384 | tf_op jit(solution)/shard_map/ppermute | solution.py:20
  81.0 18.1 %collective-permute-start.22 = (f32[136,768]{1,0:T(8,128)S(1)}, f32[136,768]{1,0:T(8,128)S(1)}, u32[]{:S(2)}, u32[]{:S(2)}) collective-permute-start(f32[136,768]{1,0:T(8,128)S(1)} %finish.1.both_ref.refs_0_), channel_id=1, source_target_pairs={{0,8},{8,0},{16,24},{24,16},{1,9},{9,1},{17,25},{25,17},{2,10},{10... | collective-permute-start | bytes 1253384 | tf_op jit(solution)/shard_map/ppermute | solution.py:25
  81.8 17.4 %collective-permute-start.23 = (f32[136,768]{1,0:T(8,128)S(1)}, f32[136,768]{1,0:T(8,128)S(1)}, u32[]{:S(2)}, u32[]{:S(2)}) collective-permute-start(f32[136,768]{1,0:T(8,128)S(1)} %finish.1.both_ref.refs_0_), channel_id=1, source_target_pairs={{0,24},{8,16},{16,8},{24,0},{1,25},{9,17},{17,9},{25,1},{2,26},{10... | collective-permute-start | bytes 1253384 | tf_op jit(solution)/shard_map/ppermute | solution.py:25
  88.4 10.7 %collective-permute-start.20 = (f32[136,768]{1,0:T(8,128)S(1)}, f32[136,768]{1,0:T(8,128)S(1)}, u32[]{:S(2)}, u32[]{:S(2)}) collective-permute-start(f32[136,768]{1,0:T(8,128)S(1)} %hold.11.refs_1_.px0_ref), channel_id=1, source_target_pairs={{0,4},{4,0},{1,5},{5,1},{2,6},{6,2},{3,7},{7,3},{8,12},{12,8},{9,1... | collective-permute-start | bytes 1253384 | tf_op jit(solution)/shard_map/ppermute | solution.py:20
  90.0 9.2 %collective-permute-start.21 = (f32[176,512]{1,0:T(8,128)S(1)}, f32[176,512]{1,0:T(8,128)S(1)}, u32[]{:S(2)}, u32[]{:S(2)}) collective-permute-start(f32[176,512]{1,0:T(8,128)S(1)} %hold.12), channel_id=1, source_target_pairs={{0,2},{2,0},{1,3},{3,1},{4,6},{6,4},{5,7},{7,5},{8,10},{10,8},{9,1... | collective-permute-start | bytes 1081352 | tf_op jit(solution)/shard_map/ppermute | solution.py:20
  99.3 21.5 %collective-permute-start.24 = (f32[256,768]{1,0:T(8,128)S(1)}, f32[256,768]{1,0:T(8,128)S(1)}, u32[]{:S(2)}, u32[]{:S(2)}) collective-permute-start(f32[256,768]{1,0:T(8,128)S(1)} %get-tuple-element.128.refs_4_), channel_id=1, source_target_pairs={{0,2},{2,0},{1,3},{3,1},{4,6},{6,4},{5,7},{7,5},{8,10},{10,8},{9,1... | collective-permute-start | bytes 2359304 | tf_op jit(solution)/shard_map/ppermute | solution.py:20
  99.9 20.9 %collective-permute-start.25 = (f32[256,768]{1,0:T(8,128)S(1)}, f32[256,768]{1,0:T(8,128)S(1)}, u32[]{:S(2)}, u32[]{:S(2)}) collective-permute-start(f32[256,768]{1,0:T(8,128)S(1)} %get-tuple-element.128.refs_4_), channel_id=1, source_target_pairs={{0,4},{4,0},{1,5},{5,1},{2,6},{6,2},{3,7},{7,3},{8,12},{12,8},{9,1... | collective-permute-start | bytes 2359304 | tf_op jit(solution)/shard_map/ppermute | solution.py:20
  101.1 15.6 %collective-permute-start.26 = (f32[136,768]{1,0:T(8,128)S(1)}, f32[136,768]{1,0:T(8,128)S(1)}, u32[]{:S(2)}, u32[]{:S(2)}) collective-permute-start(f32[136,768]{1,0:T(8,128)S(1)} %get-tuple-element.129.refs_4_), channel_id=1, source_target_pairs={{0,8},{8,0},{16,24},{24,16},{1,9},{9,1},{17,25},{25,17},{2,10},{10... | collective-permute-start | bytes 1253384 | tf_op jit(solution)/shard_map/ppermute | solution.py:25
  104.4 16.4 %collective-permute-start.27 = (f32[136,768]{1,0:T(8,128)S(1)}, f32[136,768]{1,0:T(8,128)S(1)}, u32[]{:S(2)}, u32[]{:S(2)}) collective-permute-start(f32[136,768]{1,0:T(8,128)S(1)} %get-tuple-element.130), channel_id=1, source_target_pairs={{0,24},{8,16},{16,8},{24,0},{1,25},{9,17},{17,9},{25,1},{2,26},{10... | collective-permute-start | bytes 1253384 | tf_op jit(solution)/shard_map/ppermute | solution.py:25
  107.0 16.6 %collective-permute-start.31 = (f32[768,768]{1,0:T(8,128)S(1)}, f32[768,768]{1,0:T(8,128)S(1)}, u32[]{:S(2)}, u32[]{:S(2)}) collective-permute-start(f32[768,768]{1,0:T(8,128)S(1)} %get-tuple-element.131.refs_4_.refs_0_), channel_id=1, source_target_pairs={{0,1},{1,0},{2,3},{3,2},{4,5},{5,4},{6,7},{7,6},{8,9},{9,8},{10,11... | collective-permute-start | bytes 7077896 | tf_op jit(solution)/shard_map/ppermute | solution.py:20
  120.8 9.2 %collective-permute-start.30 = (f32[168,768]{1,0:T(8,128)S(1)}, f32[168,768]{1,0:T(8,128)S(1)}, u32[]{:S(2)}, u32[]{:S(2)}) collective-permute-start(f32[168,768]{1,0:T(8,128)S(1)} %stack.25), channel_id=1, source_target_pairs={{0,8},{8,0},{16,24},{24,16},{1,9},{9,1},{17,25},{25,17},{2,10},{10... | collective-permute-start | bytes 1548296 | tf_op jit(solution)/shard_map/ppermute | solution.py:25
  120.9 9.4 %collective-permute-start.29 = (f32[176,768]{1,0:T(8,128)S(1)}, f32[176,768]{1,0:T(8,128)S(1)}, u32[]{:S(2)}, u32[]{:S(2)}) collective-permute-start(f32[176,768]{1,0:T(8,128)S(1)} %stack.24), channel_id=1, source_target_pairs={{0,4},{4,0},{1,5},{5,1},{2,6},{6,2},{3,7},{7,3},{8,12},{12,8},{9,1... | collective-permute-start | bytes 1622024 | tf_op jit(solution)/shard_map/ppermute | solution.py:20
  121.6 9.4 %collective-permute-start.28 = (f32[176,768]{1,0:T(8,128)S(1)}, f32[176,768]{1,0:T(8,128)S(1)}, u32[]{:S(2)}, u32[]{:S(2)}) collective-permute-start(f32[176,768]{1,0:T(8,128)S(1)} %stack.23), channel_id=1, source_target_pairs={{0,2},{2,0},{1,3},{3,1},{4,6},{6,4},{5,7},{7,5},{8,10},{10,8},{9,1... | collective-permute-start | bytes 1622024 | tf_op jit(solution)/shard_map/ppermute | solution.py:20
  126.7 4.9 %collective-permute-start.36 = (f32[512,768]{1,0:T(8,128)S(1)}, f32[512,768]{1,0:T(8,128)S(1)}, u32[]{:S(2)}, u32[]{:S(2)}) collective-permute-start(f32[512,768]{1,0:T(8,128)S(1)} %get-tuple-element.142.refs_0_), channel_id=1, source_target_pairs={{0,1},{1,0},{2,3},{3,2},{4,5},{5,4},{6,7},{7,6},{8,9},{9,8},{10,11... | collective-permute-start | bytes 4718600 | tf_op jit(solution)/shard_map/ppermute | solution.py:20
  128.3 6.2 %collective-permute-start.35 = (f32[256,768]{1,0:T(8,128)S(1)}, f32[256,768]{1,0:T(8,128)S(1)}, u32[]{:S(2)}, u32[]{:S(2)}) collective-permute-start(f32[256,768]{1,0:T(8,128)S(1)} %get-tuple-element.138.refs_3_.refs_1_), channel_id=1, source_target_pairs={{0,1},{1,0},{2,3},{3,2},{4,5},{5,4},{6,7},{7,6},{8,9},{9,8},{10,11... | collective-permute-start | bytes 2359304 | tf_op jit(solution)/shard_map/ppermute | solution.py:20
  131.1 3.4 %collective-permute-start.32 = (f32[176,768]{1,0:T(8,128)S(1)}, f32[176,768]{1,0:T(8,128)S(1)}, u32[]{:S(2)}, u32[]{:S(2)}) collective-permute-start(f32[176,768]{1,0:T(8,128)S(1)} %get-tuple-element.139.refs_2_.refs_0_), channel_id=1, source_target_pairs={{0,1},{1,0},{2,3},{3,2},{4,5},{5,4},{6,7},{7,6},{8,9},{9,8},{10,11... | collective-permute-start | bytes 1622024 | tf_op jit(solution)/shard_map/ppermute | solution.py:20
  (14 other events, 24.8 us)

commit v8 on v7

--- a/solution.py
+++ b/solution.py
@@ -891,7 +891,7 @@
         ]
         proj_grad, give = place(sel, (both, px0, py0, corner0, z13), own, None, width, 6)
         px13, py13, z2, corner3 = hold((px13, py13, z2, corner3), give)
-        by_x, by_y = 3 * part // 8, 3 * part // 8
+        by_x, by_y = 5 * part // 16, 5 * part // 16
         rest = part - by_x - by_y
         px2 = swap(stack((z2, 0, part), (py13, 0, by_x)), "x")
         py2 = swap(stack((z2, 0, part), (px13, by_x, by_y)), "y")

time: 137 us -> 137 us (level)
  transfers between devices with their start and end apart: 37 -> 37, of which waited for: 17 -> 16; matrix products, arithmetic and copies ran while one was open for 0% -> 0% of each run, Pallas kernels for 23% -> 23%
where the time goes in v8:
time: 137 us; the launch traced here: 136 us
  waiting for transfers between devices  53.3 us (39%)
  starting transfers between devices  40.2 us (29%)
  Pallas kernels  37.8 us (28%)
  local copies, waits for them, and re-layouts  2.88 us (2%)
    ppermute x9, waiting for transfers between devices, xor_permute(): return lax.ppermute(block, axis, [(i, i ^ distance) for i in range(size)])  35.1 us
    ppermute x28, starting transfers between devices, swap(): return lax.ppermute(block, axis, SWAP)  25.1 us
    ppermute x28, waiting for transfers between devices, swap(): return lax.ppermute(block, axis, SWAP)  18.2 us
    ppermute x9, starting transfers between devices, xor_permute(): return lax.ppermute(block, axis, [(i, i ^ distance) for i in range(size)])  15.1 us
    pallas_call x5, Pallas kernels, place(): pl.pallas_call(functools.partial(place_kernel, where=where, give=give, co...  11.8 us
    pallas_call x1, Pallas kernels, run_forward(): pl.pallas_call(forward_kernel, out_shape=(shaped((length // 2, width), BF...  7.21 us
    pallas_call x1, Pallas kernels, run_backward(): pl.pallas_call(functools.partial(backward_kernel, rows=rows, count=len(to...  4.33 us
    pallas_call x1, Pallas kernels, run_input(): pl.pallas_call(functools.partial(input_kernel, count=len(toks)), out_shap...  2.86 us
  transfers between devices with their start and end apart: 37, of which 16 were waited for; matrix products, arithmetic and copies ran while one was open for 0% of the time, Pallas kernels for 23%

profile of v8, /device:TPU:0, one launch (start us, length us, event | category | flops | bytes accessed | tf_op | source)
XLA Modules:
  0.0 136.4 jit_solution(3575272911530108119)
XLA Ops:
  2.4 2.6 %collective-permute-start.1 = (f32[32,1024]{1,0:T(8,128)S(1)}, f32[32,1024]{1,0:T(8,128)S(1)}, u32[]{:S(2)}, u32[]{:S(2)}) collective-permute-start(f32[32,1024]{1,0:T(8,128)S(1)} %slice_bitcast_fusion.2), channel_id=1, source_target_pairs={{0,2},{2,0},{1,3},{3,1},{4,6},{6,4},{5,7},{7,5},{8,10},{10,8},{9,1... | collective-permute-start | bytes 393224 | tf_op jit(solution)/shard_map/ppermute | solution.py:20
  5.1 2.8 %copy-done = bf16[1024,3072]{1,0:T(8,128)(2,1)S(1)} copy-done((bf16[1024,3072]{1,0:T(8,128)(2,1)S(1)}, bf16[1024,3072]{1,0:T(8,128)(2,1)}, u32[]{:S(2)}) %copy-start) | copy-done | bytes 6291480
  8.8 2.2 %near_blocks.1 = (bf16[352,1024]{1,0:T(8,128)(2,1)S(1)}, f32[352,256]{1,0:T(8,128)S(1)}, f32[352,256]{1,0:T(8,128)S(1)}, f32[352,256]{1,0:T(8,128)S(1)}, f32[352,256]{1,0:T(8,128)S(1)}, /*index=5*/f32[704,256]{1,0:T(8,128)S(1)}) custom-call(s32[4]{0:T(128)S(1)} %pad_add_fusion.sel, s32[1,8]{1,0:T(1,128)S(1)} %copy-done.8, ...), custom_call_target="tpu_custom_call" | custom-call | flops 55000000 | bytes 180000 | tf_op jit(solution)/shard_map/near_blocks/pallas_call | solution.py:272
  12.3 1.9 %collective-permute-start.5 = (f32[80,1024]{1,0:T(8,128)S(1)}, f32[80,1024]{1,0:T(8,128)S(1)}, u32[]{:S(2)}, u32[]{:S(2)}) collective-permute-start(f32[80,1024]{1,0:T(8,128)S(1)} %slice_bitcast_fusion), channel_id=1, source_target_pairs={{0,2},{2,0},{1,3},{3,1},{4,6},{6,4},{5,7},{7,5},{8,10},{10,8},{9,1... | collective-permute-start | bytes 983048 | tf_op jit(solution)/shard_map/ppermute | solution.py:20
  15.3 1.8 %collective-permute-start.8 = (f32[352,256]{1,0:T(8,128)S(1)}, f32[352,256]{1,0:T(8,128)S(1)}, u32[]{:S(2)}, u32[]{:S(2)}) collective-permute-start(f32[352,256]{1,0:T(8,128)S(1)} %pack_cot.1), channel_id=1, source_target_pairs={{0,2},{2,0},{1,3},{3,1},{4,6},{6,4},{5,7},{7,5},{8,10},{10,8},{9,1... | collective-permute-start | bytes 1081352 | tf_op jit(solution)/shard_map/ppermute | solution.py:20
  18.3 4.5 %collective-permute-done.5.refs_0_ = f32[80,1024]{1,0:T(8,128)S(1)} collective-permute-done((f32[80,1024]{1,0:T(8,128)S(1)}, f32[80,1024]{1,0:T(8,128)S(1)}, u32[]{:S(2)}, u32[]{:S(2)}) %collective-permute-start.5) | collective-permute-done | bytes 327712 | tf_op jit(solution)/shard_map/ppermute | solution.py:20
  22.9 1.6 %collective-permute-done.6.tok1.refs_7_ = f32[80,1024]{1,0:T(8,128)S(1)} collective-permute-done((f32[80,1024]{1,0:T(8,128)S(1)}, f32[80,1024]{1,0:T(8,128)S(1)}, u32[]{:S(2)}, u32[]{:S(2)}) %collective-permute-start.6) | collective-permute-done | bytes 327712 | tf_op jit(solution)/shard_map/ppermute | solution.py:20
  24.5 7.2 %forward_scan.1 = (bf16[352,1024]{1,0:T(8,128)(2,1)S(1)}, f32[352,256]{1,0:T(8,128)S(1)}, f32[704,256]{1,0:T(8,128)S(1)}, f32[704,256]{1,0:T(8,128)S(1)}, f32[70...) custom-call(s32[4]{0:T(128)S(1)} %pad_add_fusion.sel, f32[80,1024]{1,0:T(8,128)S(1)} %hold.10.tok0.refs_6_, ...), custom_call_target="tpu_custom_call" | custom-call | flops 55000000 | bytes 180000 | tf_op jit(solution)/shard_map/forward_scan/pallas_call | solution.py:362
  31.7 4.3 %backward_scan.1 = (bf16[704,768]{1,0:T(8,128)(2,1)S(1)}, f32[704,256]{1,0:T(8,128)S(1)}, f32[704,256]{1,0:T(8,128)S(1)}, f32[8,256]{1,0:T(8,128)S(1)}, f32[128,768]{1,0:T(8,128)S(1)}, /*index=5*/f32[128,768]{1,0:T(8,128)S(1)}) custom-call(s32[4]{0:T(128)S(1)} %pad_add_fusion.sel, f32[176,1024]{1,0:T(8,128)S(1)} %get-tuple-element.80.tok0.refs_0_, ...), custom_call_target="tpu_custom_call" | custom-call | flops 55000000 | bytes 180000 | tf_op jit(solution)/shard_map/backward_scan/pallas_call | solution.py:479
  36.1 2.0 %collective-permute-start.10 = (f32[128,768]{1,0:T(8,128)S(1)}, f32[128,768]{1,0:T(8,128)S(1)}, u32[]{:S(2)}, u32[]{:S(2)}) collective-permute-start(f32[128,768]{1,0:T(8,128)S(1)} %get-tuple-element.109), channel_id=1, source_target_pairs={{0,4},{4,0},{1,5},{5,1},{2,6},{6,2},{3,7},{7,3},{8,12},{12,8},{9,1... | collective-permute-start | bytes 1179656 | tf_op jit(solution)/shard_map/ppermute | solution.py:20
  39.4 2.0 %collective-permute-start.11 = (f32[128,768]{1,0:T(8,128)S(1)}, f32[128,768]{1,0:T(8,128)S(1)}, u32[]{:S(2)}, u32[]{:S(2)}) collective-permute-start(f32[128,768]{1,0:T(8,128)S(1)} %get-tuple-element.114), channel_id=1, source_target_pairs={{0,8},{8,0},{16,24},{24,16},{1,9},{9,1},{17,25},{25,17},{2,10},{10... | collective-permute-start | bytes 1179656 | tf_op jit(solution)/shard_map/ppermute | solution.py:25
  41.4 1.6 %products.3 = (f32[128,768]{1,0:T(8,128)S(1)}, f32[128,768]{1,0:T(8,128)S(1)}, f32[128,768]{1,0:T(8,128)S(1)}, f32[128,768]{1,0:T(8,128)S(1)}) custom-call(s32[4]{0:T(128)S(1)} %pad_add_fusion.sel, bf16[352,1024]{1,0:T(8,128)(2,1)S(1)} %get-tuple-element.100.refs_19_.near_ref, bf16[352,1024]{1,0:T(8,128)(2,1)S(1)} %get-tuple-element.101.refs_20_.far_ref, ...), custom_call_target="tpu_custom_call" | custom-call | flops 55000000 | bytes 180000 | tf_op jit(solution)/shard_map/products/pallas_call | solution.py:502
  43.0 2.9 %input_side.1 = (f32[360,1280]{1,0:T(8,128)S(1)}, f32[360,1280]{1,0:T(8,128)S(1)}) custom-call(s32[4]{0:T(128)S(1)} %pad_add_fusion.sel, f32[176,1024]{1,0:T(8,128)S(1)} %get-tuple-element.80.tok0.refs_0_, f32[176,1024]{1,0:T(8,128)S(1)} %collective-permute-done.tok1.refs_1_, f32[32,1024]{1,0:T(8,128)S(1)} %hold.8.refs_0_.refs_2_, ...), custom_call_target="tpu_custom_call" | custom-call | flops 55000000 | bytes 180000 | tf_op jit(solution)/shard_map/input_side/pallas_call | solution.py:570
  45.8 2.2 %collective-permute-done.10.b_ref = f32[128,768]{1,0:T(8,128)S(1)} collective-permute-done((f32[128,768]{1,0:T(8,128)S(1)}, f32[128,768]{1,0:T(8,128)S(1)}, u32[]{:S(2)}, u32[]{:S(2)}) %collective-permute-start.10) | collective-permute-done | bytes 393248 | tf_op jit(solution)/shard_map/ppermute | solution.py:20
  48.1 2.2 %collective-permute-start.15 = (f32[128,768]{1,0:T(8,128)S(1)}, f32[128,768]{1,0:T(8,128)S(1)}, u32[]{:S(2)}, u32[]{:S(2)}) collective-permute-start(f32[128,768]{1,0:T(8,128)S(1)} %add.10.refs_0_), channel_id=1, source_target_pairs={{0,8},{8,0},{16,24},{24,16},{1,9},{9,1},{17,25},{25,17},{2,10},{10... | collective-permute-start | bytes 1179656 | tf_op jit(solution)/shard_map/ppermute | solution.py:25
  50.7 1.9 %collective-permute-start.12 = (f32[128,768]{1,0:T(8,128)S(1)}, f32[128,768]{1,0:T(8,128)S(1)}, u32[]{:S(2)}, u32[]{:S(2)}) collective-permute-start(f32[128,768]{1,0:T(8,128)S(1)} %add.11), channel_id=1, source_target_pairs={{0,4},{4,0},{1,5},{5,1},{2,6},{6,2},{3,7},{7,3},{8,12},{12,8},{9,1... | collective-permute-start | bytes 1179656 | tf_op jit(solution)/shard_map/ppermute | solution.py:20
  52.6 3.8 %collective-permute-done.14.b_ref = f32[128,768]{1,0:T(8,128)S(1)} collective-permute-done((f32[128,768]{1,0:T(8,128)S(1)}, f32[128,768]{1,0:T(8,128)S(1)}, u32[]{:S(2)}, u32[]{:S(2)}) %collective-permute-start.14) | collective-permute-done | bytes 393248 | tf_op jit(solution)/shard_map/ppermute | solution.py:20
  56.5 3.7 %collective-permute-done.15.b_ref = f32[128,768]{1,0:T(8,128)S(1)} collective-permute-done((f32[128,768]{1,0:T(8,128)S(1)}, f32[128,768]{1,0:T(8,128)S(1)}, u32[]{:S(2)}, u32[]{:S(2)}) %collective-permute-start.15) | collective-permute-done | bytes 393248 | tf_op jit(solution)/shard_map/ppermute | solution.py:25
  60.3 4.1 %collective-permute-start.16 = (f32[128,768]{1,0:T(8,128)S(1)}, f32[128,768]{1,0:T(8,128)S(1)}, u32[]{:S(2)}, u32[]{:S(2)}) collective-permute-start(f32[128,768]{1,0:T(8,128)S(1)} %add.13), channel_id=1, source_target_pairs={{0,24},{8,16},{16,8},{24,0},{1,25},{9,17},{17,9},{25,1},{2,26},{10... | collective-permute-start | bytes 1179656 | tf_op jit(solution)/shard_map/ppermute | solution.py:25
  68.2 9.6 %collective-permute-done.16.a3_ref = f32[128,768]{1,0:T(8,128)S(1)} collective-permute-done((f32[128,768]{1,0:T(8,128)S(1)}, f32[128,768]{1,0:T(8,128)S(1)}, u32[]{:S(2)}, u32[]{:S(2)}) %collective-permute-start.16) | collective-permute-done | bytes 393248 | tf_op jit(solution)/shard_map/ppermute | solution.py:25
  81.8 2.5 %collective-permute-start.23 = (f32[136,768]{1,0:T(8,128)S(1)}, f32[136,768]{1,0:T(8,128)S(1)}, u32[]{:S(2)}, u32[]{:S(2)}) collective-permute-start(f32[136,768]{1,0:T(8,128)S(1)} %finish.1.both_ref.refs_0_), channel_id=1, source_target_pairs={{0,24},{8,16},{16,8},{24,0},{1,25},{9,17},{17,9},{25,1},{2,26},{10... | collective-permute-start | bytes 1253384 | tf_op jit(solution)/shard_map/ppermute | solution.py:25
  85.1 3.3 %collective-permute-done.18.refs_0_ = f32[136,768]{1,0:T(8,128)S(1)} collective-permute-done((f32[136,768]{1,0:T(8,128)S(1)}, f32[136,768]{1,0:T(8,128)S(1)}, u32[]{:S(2)}, u32[]{:S(2)}) %collective-permute-start.18) | collective-permute-done | bytes 417824 | tf_op jit(solution)/shard_map/ppermute | solution.py:20
  91.5 7.7 %collective-permute-done.22.refs_3_ = f32[136,768]{1,0:T(8,128)S(1)} collective-permute-done((f32[136,768]{1,0:T(8,128)S(1)}, f32[136,768]{1,0:T(8,128)S(1)}, u32[]{:S(2)}, u32[]{:S(2)}) %collective-permute-start.22) | collective-permute-done | bytes 417824 | tf_op jit(solution)/shard_map/ppermute | solution.py:25
  101.1 3.2 %collective-permute-start.26 = (f32[136,768]{1,0:T(8,128)S(1)}, f32[136,768]{1,0:T(8,128)S(1)}, u32[]{:S(2)}, u32[]{:S(2)}) collective-permute-start(f32[136,768]{1,0:T(8,128)S(1)} %get-tuple-element.129.refs_4_), channel_id=1, source_target_pairs={{0,8},{8,0},{16,24},{24,16},{1,9},{9,1},{17,25},{25,17},{2,10},{10... | collective-permute-start | bytes 1253384 | tf_op jit(solution)/shard_map/ppermute | solution.py:25
  104.5 2.5 %place.5 = (f32[1024,3072]{1,0:T(8,128)}, f32[768,768]{1,0:T(8,128)S(1)}) custom-call(s32[4]{0:T(128)S(1)} %pad_add_fusion.sel, f32[136,768]{1,0:T(8,128)S(1)} %finish.1.both_ref.refs_0_, f32[136,768]{1,0:T(8,128)S(1)} %hold.11.refs_1_.px0_ref, f32[136,768]{1,0:T(8,128)S(1)} %get-tuple-element.124.py0_ref.refs_2_, ...), custom_call_target="tpu_custom_call" | custom-call | flops 55000000 | bytes 180000 | tf_op jit(solution)/shard_map/place/pallas_call | solution.py:765
  108.4 8.3 %collective-permute-done.26.refs_2_ = f32[136,768]{1,0:T(8,128)S(1)} collective-permute-done((f32[136,768]{1,0:T(8,128)S(1)}, f32[136,768]{1,0:T(8,128)S(1)}, u32[]{:S(2)}, u32[]{:S(2)}) %collective-permute-start.26) | collective-permute-done | bytes 417824 | tf_op jit(solution)/shard_map/ppermute | solution.py:25
  116.7 4.1 %collective-permute-done.27.refs_3_ = f32[136,768]{1,0:T(8,128)S(1)} collective-permute-done((f32[136,768]{1,0:T(8,128)S(1)}, f32[136,768]{1,0:T(8,128)S(1)}, u32[]{:S(2)}, u32[]{:S(2)}) %collective-permute-start.27) | collective-permute-done | bytes 417824 | tf_op jit(solution)/shard_map/ppermute | solution.py:25
  121.6 2.0 %collective-permute-start.28 = (f32[168,768]{1,0:T(8,128)S(1)}, f32[168,768]{1,0:T(8,128)S(1)}, u32[]{:S(2)}, u32[]{:S(2)}) collective-permute-start(f32[168,768]{1,0:T(8,128)S(1)} %stack.23), channel_id=1, source_target_pairs={{0,2},{2,0},{1,3},{3,1},{4,6},{6,4},{5,7},{7,5},{8,10},{10,8},{9,1... | collective-permute-start | bytes 1548296 | tf_op jit(solution)/shard_map/ppermute | solution.py:20
  123.6 3.0 %place.6 = (f32[1024,3072]{1,0:T(8,128)}, f32[512,768]{1,0:T(8,128)S(1)}) custom-call(s32[4]{0:T(128)S(1)} %pad_add_fusion.sel, f32[256,768]{1,0:T(8,128)S(1)} %get-tuple-element.134.refs_1_.refs_0_, f32[256,768]{1,0:T(8,128)S(1)} %get-tuple-element.133.refs_1_, f32[768,768]{1,0:T(8,128)S(1)} %collective-permute-done.31.refs_2_, ...), custom_call_target="tpu_custom_call", output_to_operand_aliasing={{0}: (4, {})} | custom-call | flops 55000000 | bytes 180000 | tf_op jit(solution)/shard_map/place/pallas_call | solution.py:765
  126.7 1.6 %place.7 = (f32[1024,3072]{1,0:T(8,128)}, f32[256,768]{1,0:T(8,128)S(1)}) custom-call(s32[4]{0:T(128)S(1)} %pad_add_fusion.sel, f32[136,768]{1,0:T(8,128)S(1)} %get-tuple-element.132.refs_0_.refs_5_, f32[136,768]{1,0:T(8,128)S(1)} %get-tuple-element.135.refs_0_.refs_2_.refs_1_.refs_7_, ...), custom_call_target="tpu_custom_call", output_to_operand_aliasing={{0}: (3, {})} | custom-call | flops 55000000 | bytes 180000 | tf_op jit(solution)/shard_map/place/pallas_call | solution.py:765
  131.4 2.5 %place.8 = (f32[1024,3072]{1,0:T(8,128)}, f32[1,1024]{1,0:T(1,128)}, f32[1,1024]{1,0:T(1,128)}, f32[1,1024]{1,0:T(1,128)}, f32[1,1024]{1,0:T(1,128)}, /*index=5*/f32[1,1024]{1,0:T(1,128)}, f32[1,1024]{1,0:T(1,128)}) custom-call(s32[4]{0:T(128)S(1)} %pad_add_fusion.sel, ...), custom_call_target="tpu_custom_call", output_to_operand_aliasing={{0}: (9, {})} | custom-call | flops 55000000 | bytes 180000 | tf_op jit(solution)/shard_map/place/pallas_call | solution.py:765
  134.2 2.1 %place.9 = f32[1024,3072]{1,0:T(8,128)} custom-call(s32[4]{0:T(128)S(1)} %pad_add_fusion.sel, f32[168,768]{1,0:T(8,128)S(1)} %collective-permute-done.32.refs_0_, f32[168,768]{1,0:T(8,128)S(1)} %collective-permute-done.33.refs_1_, f32[184,768]{1,0:T(8,128)S(1)} %collective-permute-done.34.refs_2_, ...), custom_call_target="tpu_custom_call", output_to_operand_aliasing={{}: (5, {})} | custom-call | flops 55000000 | bytes 180000 | tf_op jit(solution)/shard_map/place/pallas_call | solution.py:765
  (103 shorter events, 27.4 us)
Async XLA Ops:
  1.9 6.9 %collective-permute-start = (f32[176,1024]{1,0:T(8,128)S(1)}, f32[176,1024]{1,0:T(8,128)S(1)}, u32[]{:S(2)}, u32[]{:S(2)}) collective-permute-start(f32[176,1024]{1,0:T(8,128)S(1)} %get-tuple-element.80.tok0.refs_0_), channel_id=1, source_target_pairs={{0,1},{1,0},{2,3},{3,2},{4,5},{5,4},{6,7},{7,6},{8,9},{9,8},{10,11... | collective-permute-start | bytes 2162696 | tf_op jit(solution)/shard_map/ppermute | solution.py:20
  2.4 8.7 %collective-permute-start.1 = (f32[32,1024]{1,0:T(8,128)S(1)}, f32[32,1024]{1,0:T(8,128)S(1)}, u32[]{:S(2)}, u32[]{:S(2)}) collective-permute-start(f32[32,1024]{1,0:T(8,128)S(1)} %slice_bitcast_fusion.2), channel_id=1, source_target_pairs={{0,2},{2,0},{1,3},{3,1},{4,6},{6,4},{5,7},{7,5},{8,10},{10,8},{9,1... | collective-permute-start | bytes 393224 | tf_op jit(solution)/shard_map/ppermute | solution.py:20
  5.0 9.7 %collective-permute-start.3 = (f32[64,1024]{1,0:T(8,128)S(1)}, f32[64,1024]{1,0:T(8,128)S(1)}, u32[]{:S(2)}, u32[]{:S(2)}) collective-permute-start(f32[64,1024]{1,0:T(8,128)S(1)} %slice_bitcast_fusion.1), channel_id=1, source_target_pairs={{0,2},{2,0},{1,3},{3,1},{4,6},{6,4},{5,7},{7,5},{8,10},{10,8},{9,1... | collective-permute-start | bytes 786440 | tf_op jit(solution)/shard_map/ppermute | solution.py:20
  11.1 3.6 %collective-permute-start.2 = (f32[32,1024]{1,0:T(8,128)S(1)}, f32[32,1024]{1,0:T(8,128)S(1)}, u32[]{:S(2)}, u32[]{:S(2)}) collective-permute-start(f32[32,1024]{1,0:T(8,128)S(1)} %hold.8.refs_0_.refs_2_), channel_id=1, source_target_pairs={{0,1},{1,0},{2,3},{3,2},{4,5},{5,4},{6,7},{7,6},{8,9},{9,8},{10,11... | collective-permute-start | bytes 393224 | tf_op jit(solution)/shard_map/ppermute | solution.py:20
  12.3 10.5 %collective-permute-start.5 = (f32[80,1024]{1,0:T(8,128)S(1)}, f32[80,1024]{1,0:T(8,128)S(1)}, u32[]{:S(2)}, u32[]{:S(2)}) collective-permute-start(f32[80,1024]{1,0:T(8,128)S(1)} %slice_bitcast_fusion), channel_id=1, source_target_pairs={{0,2},{2,0},{1,3},{3,1},{4,6},{6,4},{5,7},{7,5},{8,10},{10,8},{9,1... | collective-permute-start | bytes 983048 | tf_op jit(solution)/shard_map/ppermute | solution.py:20
  15.3 16.5 %collective-permute-start.8 = (f32[352,256]{1,0:T(8,128)S(1)}, f32[352,256]{1,0:T(8,128)S(1)}, u32[]{:S(2)}, u32[]{:S(2)}) collective-permute-start(f32[352,256]{1,0:T(8,128)S(1)} %pack_cot.1), channel_id=1, source_target_pairs={{0,2},{2,0},{1,3},{3,1},{4,6},{6,4},{5,7},{7,5},{8,10},{10,8},{9,1... | collective-permute-start | bytes 1081352 | tf_op jit(solution)/shard_map/ppermute | solution.py:20
  36.1 12.0 %collective-permute-start.10 = (f32[128,768]{1,0:T(8,128)S(1)}, f32[128,768]{1,0:T(8,128)S(1)}, u32[]{:S(2)}, u32[]{:S(2)}) collective-permute-start(f32[128,768]{1,0:T(8,128)S(1)} %get-tuple-element.109), channel_id=1, source_target_pairs={{0,4},{4,0},{1,5},{5,1},{2,6},{6,2},{3,7},{7,3},{8,12},{12,8},{9,1... | collective-permute-start | bytes 1179656 | tf_op jit(solution)/shard_map/ppermute | solution.py:20
  39.2 17.2 %collective-permute-start.14 = (f32[128,768]{1,0:T(8,128)S(1)}, f32[128,768]{1,0:T(8,128)S(1)}, u32[]{:S(2)}, u32[]{:S(2)}) collective-permute-start(f32[128,768]{1,0:T(8,128)S(1)} %get-tuple-element.110.refs_0_), channel_id=1, source_target_pairs={{0,4},{4,0},{1,5},{5,1},{2,6},{6,2},{3,7},{7,3},{8,12},{12,8},{9,1... | collective-permute-start | bytes 1179656 | tf_op jit(solution)/shard_map/ppermute | solution.py:20
  39.4 11.3 %collective-permute-start.11 = (f32[128,768]{1,0:T(8,128)S(1)}, f32[128,768]{1,0:T(8,128)S(1)}, u32[]{:S(2)}, u32[]{:S(2)}) collective-permute-start(f32[128,768]{1,0:T(8,128)S(1)} %get-tuple-element.114), channel_id=1, source_target_pairs={{0,8},{8,0},{16,24},{24,16},{1,9},{9,1},{17,25},{25,17},{2,10},{10... | collective-permute-start | bytes 1179656 | tf_op jit(solution)/shard_map/ppermute | solution.py:25
  48.1 12.2 %collective-permute-start.15 = (f32[128,768]{1,0:T(8,128)S(1)}, f32[128,768]{1,0:T(8,128)S(1)}, u32[]{:S(2)}, u32[]{:S(2)}) collective-permute-start(f32[128,768]{1,0:T(8,128)S(1)} %add.10.refs_0_), channel_id=1, source_target_pairs={{0,8},{8,0},{16,24},{24,16},{1,9},{9,1},{17,25},{25,17},{2,10},{10... | collective-permute-start | bytes 1179656 | tf_op jit(solution)/shard_map/ppermute | solution.py:25
  50.2 14.2 %collective-permute-start.9 = (f32[360,1280]{1,0:T(8,128)S(1)}, f32[360,1280]{1,0:T(8,128)S(1)}, u32[]{:S(2)}, u32[]{:S(2)}) collective-permute-start(f32[360,1280]{1,0:T(8,128)S(1)} %get-tuple-element.107.refs_2_.refs_0_), channel_id=1, source_target_pairs={{0,1},{1,0},{2,3},{3,2},{4,5},{5,4},{6,7},{7,6},{8,9},{9,8},{10,11... | collective-permute-start | bytes 5529608 | tf_op jit(solution)/shard_map/ppermute | solution.py:20
  50.2 18.0 %collective-permute-start.13 = (f32[128,768]{1,0:T(8,128)S(1)}, f32[128,768]{1,0:T(8,128)S(1)}, u32[]{:S(2)}, u32[]{:S(2)}) collective-permute-start(f32[128,768]{1,0:T(8,128)S(1)} %get-tuple-element.115), channel_id=1, source_target_pairs={{0,8},{8,0},{16,24},{24,16},{1,9},{9,1},{17,25},{25,17},{2,10},{10... | collective-permute-start | bytes 1179656 | tf_op jit(solution)/shard_map/ppermute | solution.py:25
  50.7 17.5 %collective-permute-start.12 = (f32[128,768]{1,0:T(8,128)S(1)}, f32[128,768]{1,0:T(8,128)S(1)}, u32[]{:S(2)}, u32[]{:S(2)}) collective-permute-start(f32[128,768]{1,0:T(8,128)S(1)} %add.11), channel_id=1, source_target_pairs={{0,4},{4,0},{1,5},{5,1},{2,6},{6,2},{3,7},{7,3},{8,12},{12,8},{9,1... | collective-permute-start | bytes 1179656 | tf_op jit(solution)/shard_map/ppermute | solution.py:20
  60.3 17.5 %collective-permute-start.16 = (f32[128,768]{1,0:T(8,128)S(1)}, f32[128,768]{1,0:T(8,128)S(1)}, u32[]{:S(2)}, u32[]{:S(2)}) collective-permute-start(f32[128,768]{1,0:T(8,128)S(1)} %add.13), channel_id=1, source_target_pairs={{0,24},{8,16},{16,8},{24,0},{1,25},{9,17},{17,9},{25,1},{2,26},{10... | collective-permute-start | bytes 1179656 | tf_op jit(solution)/shard_map/ppermute | solution.py:25
  65.3 19.0 %collective-permute-start.19 = (f32[176,1024]{1,0:T(8,128)S(1)}, f32[176,1024]{1,0:T(8,128)S(1)}, u32[]{:S(2)}, u32[]{:S(2)}) collective-permute-start(f32[176,1024]{1,0:T(8,128)S(1)} %get-tuple-element.119), channel_id=1, source_target_pairs={{0,2},{2,0},{1,3},{3,1},{4,6},{6,4},{5,7},{7,5},{8,10},{10,8},{9,1... | collective-permute-start | bytes 2162696 | tf_op jit(solution)/shard_map/ppermute | solution.py:20
  77.9 10.5 %collective-permute-start.18 = (f32[136,768]{1,0:T(8,128)S(1)}, f32[136,768]{1,0:T(8,128)S(1)}, u32[]{:S(2)}, u32[]{:S(2)}) collective-permute-start(f32[136,768]{1,0:T(8,128)S(1)} %finish.1.both_ref.refs_0_), channel_id=1, source_target_pairs={{0,2},{2,0},{1,3},{3,1},{4,6},{6,4},{5,7},{7,5},{8,10},{10,8},{9,1... | collective-permute-start | bytes 1253384 | tf_op jit(solution)/shard_map/ppermute | solution.py:20
  79.5 12.0 %collective-permute-start.17 = (f32[136,768]{1,0:T(8,128)S(1)}, f32[136,768]{1,0:T(8,128)S(1)}, u32[]{:S(2)}, u32[]{:S(2)}) collective-permute-start(f32[136,768]{1,0:T(8,128)S(1)} %finish.1.both_ref.refs_0_), channel_id=1, source_target_pairs={{0,4},{4,0},{1,5},{5,1},{2,6},{6,2},{3,7},{7,3},{8,12},{12,8},{9,1... | collective-permute-start | bytes 1253384 | tf_op jit(solution)/shard_map/ppermute | solution.py:20
  81.0 18.1 %collective-permute-start.22 = (f32[136,768]{1,0:T(8,128)S(1)}, f32[136,768]{1,0:T(8,128)S(1)}, u32[]{:S(2)}, u32[]{:S(2)}) collective-permute-start(f32[136,768]{1,0:T(8,128)S(1)} %finish.1.both_ref.refs_0_), channel_id=1, source_target_pairs={{0,8},{8,0},{16,24},{24,16},{1,9},{9,1},{17,25},{25,17},{2,10},{10... | collective-permute-start | bytes 1253384 | tf_op jit(solution)/shard_map/ppermute | solution.py:25
  81.8 17.4 %collective-permute-start.23 = (f32[136,768]{1,0:T(8,128)S(1)}, f32[136,768]{1,0:T(8,128)S(1)}, u32[]{:S(2)}, u32[]{:S(2)}) collective-permute-start(f32[136,768]{1,0:T(8,128)S(1)} %finish.1.both_ref.refs_0_), channel_id=1, source_target_pairs={{0,24},{8,16},{16,8},{24,0},{1,25},{9,17},{17,9},{25,1},{2,26},{10... | collective-permute-start | bytes 1253384 | tf_op jit(solution)/shard_map/ppermute | solution.py:25
  88.4 10.7 %collective-permute-start.20 = (f32[136,768]{1,0:T(8,128)S(1)}, f32[136,768]{1,0:T(8,128)S(1)}, u32[]{:S(2)}, u32[]{:S(2)}) collective-permute-start(f32[136,768]{1,0:T(8,128)S(1)} %hold.11.refs_1_.px0_ref), channel_id=1, source_target_pairs={{0,4},{4,0},{1,5},{5,1},{2,6},{6,2},{3,7},{7,3},{8,12},{12,8},{9,1... | collective-permute-start | bytes 1253384 | tf_op jit(solution)/shard_map/ppermute | solution.py:20
  90.0 9.2 %collective-permute-start.21 = (f32[176,512]{1,0:T(8,128)S(1)}, f32[176,512]{1,0:T(8,128)S(1)}, u32[]{:S(2)}, u32[]{:S(2)}) collective-permute-start(f32[176,512]{1,0:T(8,128)S(1)} %hold.12), channel_id=1, source_target_pairs={{0,2},{2,0},{1,3},{3,1},{4,6},{6,4},{5,7},{7,5},{8,10},{10,8},{9,1... | collective-permute-start | bytes 1081352 | tf_op jit(solution)/shard_map/ppermute | solution.py:20
  99.3 21.5 %collective-permute-start.24 = (f32[256,768]{1,0:T(8,128)S(1)}, f32[256,768]{1,0:T(8,128)S(1)}, u32[]{:S(2)}, u32[]{:S(2)}) collective-permute-start(f32[256,768]{1,0:T(8,128)S(1)} %get-tuple-element.128.refs_4_), channel_id=1, source_target_pairs={{0,2},{2,0},{1,3},{3,1},{4,6},{6,4},{5,7},{7,5},{8,10},{10,8},{9,1... | collective-permute-start | bytes 2359304 | tf_op jit(solution)/shard_map/ppermute | solution.py:20
  99.9 20.9 %collective-permute-start.25 = (f32[256,768]{1,0:T(8,128)S(1)}, f32[256,768]{1,0:T(8,128)S(1)}, u32[]{:S(2)}, u32[]{:S(2)}) collective-permute-start(f32[256,768]{1,0:T(8,128)S(1)} %get-tuple-element.128.refs_4_), channel_id=1, source_target_pairs={{0,4},{4,0},{1,5},{5,1},{2,6},{6,2},{3,7},{7,3},{8,12},{12,8},{9,1... | collective-permute-start | bytes 2359304 | tf_op jit(solution)/shard_map/ppermute | solution.py:20
  101.1 15.6 %collective-permute-start.26 = (f32[136,768]{1,0:T(8,128)S(1)}, f32[136,768]{1,0:T(8,128)S(1)}, u32[]{:S(2)}, u32[]{:S(2)}) collective-permute-start(f32[136,768]{1,0:T(8,128)S(1)} %get-tuple-element.129.refs_4_), channel_id=1, source_target_pairs={{0,8},{8,0},{16,24},{24,16},{1,9},{9,1},{17,25},{25,17},{2,10},{10... | collective-permute-start | bytes 1253384 | tf_op jit(solution)/shard_map/ppermute | solution.py:25
  104.4 16.4 %collective-permute-start.27 = (f32[136,768]{1,0:T(8,128)S(1)}, f32[136,768]{1,0:T(8,128)S(1)}, u32[]{:S(2)}, u32[]{:S(2)}) collective-permute-start(f32[136,768]{1,0:T(8,128)S(1)} %get-tuple-element.130), channel_id=1, source_target_pairs={{0,24},{8,16},{16,8},{24,0},{1,25},{9,17},{17,9},{25,1},{2,26},{10... | collective-permute-start | bytes 1253384 | tf_op jit(solution)/shard_map/ppermute | solution.py:25
  107.0 16.6 %collective-permute-start.31 = (f32[768,768]{1,0:T(8,128)S(1)}, f32[768,768]{1,0:T(8,128)S(1)}, u32[]{:S(2)}, u32[]{:S(2)}) collective-permute-start(f32[768,768]{1,0:T(8,128)S(1)} %get-tuple-element.131.refs_4_.refs_0_), channel_id=1, source_target_pairs={{0,1},{1,0},{2,3},{3,2},{4,5},{5,4},{6,7},{7,6},{8,9},{9,8},{10,11... | collective-permute-start | bytes 7077896 | tf_op jit(solution)/shard_map/ppermute | solution.py:20
  120.8 10.0 %collective-permute-start.30 = (f32[184,768]{1,0:T(8,128)S(1)}, f32[184,768]{1,0:T(8,128)S(1)}, u32[]{:S(2)}, u32[]{:S(2)}) collective-permute-start(f32[184,768]{1,0:T(8,128)S(1)} %stack.25), channel_id=1, source_target_pairs={{0,8},{8,0},{16,24},{24,16},{1,9},{9,1},{17,25},{25,17},{2,10},{10... | collective-permute-start | bytes 1695752 | tf_op jit(solution)/shard_map/ppermute | solution.py:25
  120.9 9.2 %collective-permute-start.29 = (f32[168,768]{1,0:T(8,128)S(1)}, f32[168,768]{1,0:T(8,128)S(1)}, u32[]{:S(2)}, u32[]{:S(2)}) collective-permute-start(f32[168,768]{1,0:T(8,128)S(1)} %stack.24), channel_id=1, source_target_pairs={{0,4},{4,0},{1,5},{5,1},{2,6},{6,2},{3,7},{7,3},{8,12},{12,8},{9,1... | collective-permute-start | bytes 1548296 | tf_op jit(solution)/shard_map/ppermute | solution.py:20
  121.6 9.2 %collective-permute-start.28 = (f32[168,768]{1,0:T(8,128)S(1)}, f32[168,768]{1,0:T(8,128)S(1)}, u32[]{:S(2)}, u32[]{:S(2)}) collective-permute-start(f32[168,768]{1,0:T(8,128)S(1)} %stack.23), channel_id=1, source_target_pairs={{0,2},{2,0},{1,3},{3,1},{4,6},{6,4},{5,7},{7,5},{8,10},{10,8},{9,1... | collective-permute-start | bytes 1548296 | tf_op jit(solution)/shard_map/ppermute | solution.py:20
  126.7 4.7 %collective-permute-start.36 = (f32[512,768]{1,0:T(8,128)S(1)}, f32[512,768]{1,0:T(8,128)S(1)}, u32[]{:S(2)}, u32[]{:S(2)}) collective-permute-start(f32[512,768]{1,0:T(8,128)S(1)} %get-tuple-element.142.refs_0_), channel_id=1, source_target_pairs={{0,1},{1,0},{2,3},{3,2},{4,5},{5,4},{6,7},{7,6},{8,9},{9,8},{10,11... | collective-permute-start | bytes 4718600 | tf_op jit(solution)/shard_map/ppermute | solution.py:20
  128.3 5.9 %collective-permute-start.35 = (f32[256,768]{1,0:T(8,128)S(1)}, f32[256,768]{1,0:T(8,128)S(1)}, u32[]{:S(2)}, u32[]{:S(2)}) collective-permute-start(f32[256,768]{1,0:T(8,128)S(1)} %get-tuple-element.138.refs_3_.refs_1_), channel_id=1, source_target_pairs={{0,1},{1,0},{2,3},{3,2},{4,5},{5,4},{6,7},{7,6},{8,9},{9,8},{10,11... | collective-permute-start | bytes 2359304 | tf_op jit(solution)/shard_map/ppermute | solution.py:20
  130.8 3.4 %collective-permute-start.34 = (f32[184,768]{1,0:T(8,128)S(1)}, f32[184,768]{1,0:T(8,128)S(1)}, u32[]{:S(2)}, u32[]{:S(2)}) collective-permute-start(f32[184,768]{1,0:T(8,128)S(1)} %get-tuple-element.141.refs_2_.refs_6_), channel_id=1, source_target_pairs={{0,1},{1,0},{2,3},{3,2},{4,5},{5,4},{6,7},{7,6},{8,9},{9,8},{10,11... | collective-permute-start | bytes 1695752 | tf_op jit(solution)/shard_map/ppermute | solution.py:20
  (14 other events, 24.4 us)

commit v9 on v8

--- a/solution.py
+++ b/solution.py
@@ -873,7 +873,7 @@
         )
         (px0,) = hold((px0,), joined)
         corner0 = swap(px0, "y")
-        (sent_out,) = hold((sent_out,), px0)
+        (sent_out,) = hold((sent_out,), joined)
         got_out = swap(sent_out, "x")
         py0, corner0, got_out, z1, z3 = hold((py0, corner0, got_out, z1, z3))
         output = join_out(sel, kept_out, got_out)

time: 137 us -> 137 us (level)
  no operation moved by 1% of the time
where the time goes in v9:
time: 137 us; the launch traced here: 136 us
  waiting for transfers between devices  53.3 us (39%)
  starting transfers between devices  40.2 us (29%)
  Pallas kernels  37.8 us (28%)
  local copies, waits for them, and re-layouts  2.88 us (2%)
    ppermute x9, waiting for transfers between devices, xor_permute(): return lax.ppermute(block, axis, [(i, i ^ distance) for i in range(size)])  35.1 us
    ppermute x28, starting transfers between devices, swap(): return lax.ppermute(block, axis, SWAP)  25.1 us
    ppermute x28, waiting for transfers between devices, swap(): return lax.ppermute(block, axis, SWAP)  18.2 us
    ppermute x9, starting transfers between devices, xor_permute(): return lax.ppermute(block, axis, [(i, i ^ distance) for i in range(size)])  15.1 us
    pallas_call x5, Pallas kernels, place(): pl.pallas_call(functools.partial(place_kernel, where=where, give=give, co...  11.8 us
    pallas_call x1, Pallas kernels, run_forward(): pl.pallas_call(forward_kernel, out_shape=(shaped((length // 2, width), BF...  7.21 us
    pallas_call x1, Pallas kernels, run_backward(): pl.pallas_call(functools.partial(backward_kernel, rows=rows, count=len(to...  4.33 us
    pallas_call x1, Pallas kernels, run_input(): pl.pallas_call(functools.partial(input_kernel, count=len(toks)), out_shap...  2.86 us
  transfers between devices with their start and end apart: 37, of which 16 were waited for; matrix products, arithmetic and copies ran while one was open for 0% of the time, Pallas kernels for 23%

profile of v9, /device:TPU:0, one launch (start us, length us, event | category | flops | bytes accessed | tf_op | source)
XLA Modules:
  0.0 136.4 jit_solution(7828579909425114349)
XLA Ops:
  2.4 2.6 %collective-permute-start.1 = (f32[32,1024]{1,0:T(8,128)S(1)}, f32[32,1024]{1,0:T(8,128)S(1)}, u32[]{:S(2)}, u32[]{:S(2)}) collective-permute-start(f32[32,1024]{1,0:T(8,128)S(1)} %slice_bitcast_fusion.2), channel_id=1, source_target_pairs={{0,2},{2,0},{1,3},{3,1},{4,6},{6,4},{5,7},{7,5},{8,10},{10,8},{9,1... | collective-permute-start | bytes 393224 | tf_op jit(solution)/shard_map/ppermute | solution.py:20
  5.1 2.8 %copy-done = bf16[1024,3072]{1,0:T(8,128)(2,1)S(1)} copy-done((bf16[1024,3072]{1,0:T(8,128)(2,1)S(1)}, bf16[1024,3072]{1,0:T(8,128)(2,1)}, u32[]{:S(2)}) %copy-start) | copy-done | bytes 6291480
  8.8 2.2 %near_blocks.1 = (bf16[352,1024]{1,0:T(8,128)(2,1)S(1)}, f32[352,256]{1,0:T(8,128)S(1)}, f32[352,256]{1,0:T(8,128)S(1)}, f32[352,256]{1,0:T(8,128)S(1)}, f32[352,256]{1,0:T(8,128)S(1)}, /*index=5*/f32[704,256]{1,0:T(8,128)S(1)}) custom-call(s32[4]{0:T(128)S(1)} %pad_add_fusion.sel, s32[1,8]{1,0:T(1,128)S(1)} %copy-done.8, ...), custom_call_target="tpu_custom_call" | custom-call | flops 55000000 | bytes 180000 | tf_op jit(solution)/shard_map/near_blocks/pallas_call | solution.py:272
  12.3 1.9 %collective-permute-start.5 = (f32[80,1024]{1,0:T(8,128)S(1)}, f32[80,1024]{1,0:T(8,128)S(1)}, u32[]{:S(2)}, u32[]{:S(2)}) collective-permute-start(f32[80,1024]{1,0:T(8,128)S(1)} %slice_bitcast_fusion), channel_id=1, source_target_pairs={{0,2},{2,0},{1,3},{3,1},{4,6},{6,4},{5,7},{7,5},{8,10},{10,8},{9,1... | collective-permute-start | bytes 983048 | tf_op jit(solution)/shard_map/ppermute | solution.py:20
  15.3 1.8 %collective-permute-start.8 = (f32[352,256]{1,0:T(8,128)S(1)}, f32[352,256]{1,0:T(8,128)S(1)}, u32[]{:S(2)}, u32[]{:S(2)}) collective-permute-start(f32[352,256]{1,0:T(8,128)S(1)} %pack_cot.1), channel_id=1, source_target_pairs={{0,2},{2,0},{1,3},{3,1},{4,6},{6,4},{5,7},{7,5},{8,10},{10,8},{9,1... | collective-permute-start | bytes 1081352 | tf_op jit(solution)/shard_map/ppermute | solution.py:20
  18.3 4.5 %collective-permute-done.5.refs_0_ = f32[80,1024]{1,0:T(8,128)S(1)} collective-permute-done((f32[80,1024]{1,0:T(8,128)S(1)}, f32[80,1024]{1,0:T(8,128)S(1)}, u32[]{:S(2)}, u32[]{:S(2)}) %collective-permute-start.5) | collective-permute-done | bytes 327712 | tf_op jit(solution)/shard_map/ppermute | solution.py:20
  22.9 1.6 %collective-permute-done.6.tok1.refs_7_ = f32[80,1024]{1,0:T(8,128)S(1)} collective-permute-done((f32[80,1024]{1,0:T(8,128)S(1)}, f32[80,1024]{1,0:T(8,128)S(1)}, u32[]{:S(2)}, u32[]{:S(2)}) %collective-permute-start.6) | collective-permute-done | bytes 327712 | tf_op jit(solution)/shard_map/ppermute | solution.py:20
  24.5 7.2 %forward_scan.1 = (bf16[352,1024]{1,0:T(8,128)(2,1)S(1)}, f32[352,256]{1,0:T(8,128)S(1)}, f32[704,256]{1,0:T(8,128)S(1)}, f32[704,256]{1,0:T(8,128)S(1)}, f32[70...) custom-call(s32[4]{0:T(128)S(1)} %pad_add_fusion.sel, f32[80,1024]{1,0:T(8,128)S(1)} %hold.10.tok0.refs_6_, ...), custom_call_target="tpu_custom_call" | custom-call | flops 55000000 | bytes 180000 | tf_op jit(solution)/shard_map/forward_scan/pallas_call | solution.py:362
  31.7 4.3 %backward_scan.1 = (bf16[704,768]{1,0:T(8,128)(2,1)S(1)}, f32[704,256]{1,0:T(8,128)S(1)}, f32[704,256]{1,0:T(8,128)S(1)}, f32[8,256]{1,0:T(8,128)S(1)}, f32[128,768]{1,0:T(8,128)S(1)}, /*index=5*/f32[128,768]{1,0:T(8,128)S(1)}) custom-call(s32[4]{0:T(128)S(1)} %pad_add_fusion.sel, f32[176,1024]{1,0:T(8,128)S(1)} %get-tuple-element.80.tok0.refs_0_, ...), custom_call_target="tpu_custom_call" | custom-call | flops 55000000 | bytes 180000 | tf_op jit(solution)/shard_map/backward_scan/pallas_call | solution.py:479
  36.1 2.0 %collective-permute-start.10 = (f32[128,768]{1,0:T(8,128)S(1)}, f32[128,768]{1,0:T(8,128)S(1)}, u32[]{:S(2)}, u32[]{:S(2)}) collective-permute-start(f32[128,768]{1,0:T(8,128)S(1)} %get-tuple-element.109), channel_id=1, source_target_pairs={{0,4},{4,0},{1,5},{5,1},{2,6},{6,2},{3,7},{7,3},{8,12},{12,8},{9,1... | collective-permute-start | bytes 1179656 | tf_op jit(solution)/shard_map/ppermute | solution.py:20
  39.4 2.0 %collective-permute-start.11 = (f32[128,768]{1,0:T(8,128)S(1)}, f32[128,768]{1,0:T(8,128)S(1)}, u32[]{:S(2)}, u32[]{:S(2)}) collective-permute-start(f32[128,768]{1,0:T(8,128)S(1)} %get-tuple-element.114), channel_id=1, source_target_pairs={{0,8},{8,0},{16,24},{24,16},{1,9},{9,1},{17,25},{25,17},{2,10},{10... | collective-permute-start | bytes 1179656 | tf_op jit(solution)/shard_map/ppermute | solution.py:25
  41.4 1.6 %products.3 = (f32[128,768]{1,0:T(8,128)S(1)}, f32[128,768]{1,0:T(8,128)S(1)}, f32[128,768]{1,0:T(8,128)S(1)}, f32[128,768]{1,0:T(8,128)S(1)}) custom-call(s32[4]{0:T(128)S(1)} %pad_add_fusion.sel, bf16[352,1024]{1,0:T(8,128)(2,1)S(1)} %get-tuple-element.100.refs_19_.near_ref, bf16[352,1024]{1,0:T(8,128)(2,1)S(1)} %get-tuple-element.101.refs_20_.far_ref, ...), custom_call_target="tpu_custom_call" | custom-call | flops 55000000 | bytes 180000 | tf_op jit(solution)/shard_map/products/pallas_call | solution.py:502
  43.0 2.9 %input_side.1 = (f32[360,1280]{1,0:T(8,128)S(1)}, f32[360,1280]{1,0:T(8,128)S(1)}) custom-call(s32[4]{0:T(128)S(1)} %pad_add_fusion.sel, f32[176,1024]{1,0:T(8,128)S(1)} %get-tuple-element.80.tok0.refs_0_, f32[176,1024]{1,0:T(8,128)S(1)} %collective-permute-done.tok1.refs_1_, f32[32,1024]{1,0:T(8,128)S(1)} %hold.8.refs_0_.refs_2_, ...), custom_call_target="tpu_custom_call" | custom-call | flops 55000000 | bytes 180000 | tf_op jit(solution)/shard_map/input_side/pallas_call | solution.py:570
  45.8 2.2 %collective-permute-done.10.b_ref = f32[128,768]{1,0:T(8,128)S(1)} collective-permute-done((f32[128,768]{1,0:T(8,128)S(1)}, f32[128,768]{1,0:T(8,128)S(1)}, u32[]{:S(2)}, u32[]{:S(2)}) %collective-permute-start.10) | collective-permute-done | bytes 393248 | tf_op jit(solution)/shard_map/ppermute | solution.py:20
  48.1 2.2 %collective-permute-start.15 = (f32[128,768]{1,0:T(8,128)S(1)}, f32[128,768]{1,0:T(8,128)S(1)}, u32[]{:S(2)}, u32[]{:S(2)}) collective-permute-start(f32[128,768]{1,0:T(8,128)S(1)} %add.10.refs_0_), channel_id=1, source_target_pairs={{0,8},{8,0},{16,24},{24,16},{1,9},{9,1},{17,25},{25,17},{2,10},{10... | collective-permute-start | bytes 1179656 | tf_op jit(solution)/shard_map/ppermute | solution.py:25
  50.7 1.9 %collective-permute-start.12 = (f32[128,768]{1,0:T(8,128)S(1)}, f32[128,768]{1,0:T(8,128)S(1)}, u32[]{:S(2)}, u32[]{:S(2)}) collective-permute-start(f32[128,768]{1,0:T(8,128)S(1)} %add.11), channel_id=1, source_target_pairs={{0,4},{4,0},{1,5},{5,1},{2,6},{6,2},{3,7},{7,3},{8,12},{12,8},{9,1... | collective-permute-start | bytes 1179656 | tf_op jit(solution)/shard_map/ppermute | solution.py:20
  52.6 3.8 %collective-permute-done.14.b_ref = f32[128,768]{1,0:T(8,128)S(1)} collective-permute-done((f32[128,768]{1,0:T(8,128)S(1)}, f32[128,768]{1,0:T(8,128)S(1)}, u32[]{:S(2)}, u32[]{:S(2)}) %collective-permute-start.14) | collective-permute-done | bytes 393248 | tf_op jit(solution)/shard_map/ppermute | solution.py:20
  56.5 3.7 %collective-permute-done.15.b_ref = f32[128,768]{1,0:T(8,128)S(1)} collective-permute-done((f32[128,768]{1,0:T(8,128)S(1)}, f32[128,768]{1,0:T(8,128)S(1)}, u32[]{:S(2)}, u32[]{:S(2)}) %collective-permute-start.15) | collective-permute-done | bytes 393248 | tf_op jit(solution)/shard_map/ppermute | solution.py:25
  60.3 4.1 %collective-permute-start.16 = (f32[128,768]{1,0:T(8,128)S(1)}, f32[128,768]{1,0:T(8,128)S(1)}, u32[]{:S(2)}, u32[]{:S(2)}) collective-permute-start(f32[128,768]{1,0:T(8,128)S(1)} %add.13), channel_id=1, source_target_pairs={{0,24},{8,16},{16,8},{24,0},{1,25},{9,17},{17,9},{25,1},{2,26},{10... | collective-permute-start | bytes 1179656 | tf_op jit(solution)/shard_map/ppermute | solution.py:25
  68.2 9.6 %collective-permute-done.16.a3_ref = f32[128,768]{1,0:T(8,128)S(1)} collective-permute-done((f32[128,768]{1,0:T(8,128)S(1)}, f32[128,768]{1,0:T(8,128)S(1)}, u32[]{:S(2)}, u32[]{:S(2)}) %collective-permute-start.16) | collective-permute-done | bytes 393248 | tf_op jit(solution)/shard_map/ppermute | solution.py:25
  81.8 2.5 %collective-permute-start.23 = (f32[136,768]{1,0:T(8,128)S(1)}, f32[136,768]{1,0:T(8,128)S(1)}, u32[]{:S(2)}, u32[]{:S(2)}) collective-permute-start(f32[136,768]{1,0:T(8,128)S(1)} %finish.1.both_ref.refs_0_), channel_id=1, source_target_pairs={{0,24},{8,16},{16,8},{24,0},{1,25},{9,17},{17,9},{25,1},{2,26},{10... | collective-permute-start | bytes 1253384 | tf_op jit(solution)/shard_map/ppermute | solution.py:25
  85.1 3.3 %collective-permute-done.18.refs_0_ = f32[136,768]{1,0:T(8,128)S(1)} collective-permute-done((f32[136,768]{1,0:T(8,128)S(1)}, f32[136,768]{1,0:T(8,128)S(1)}, u32[]{:S(2)}, u32[]{:S(2)}) %collective-permute-start.18) | collective-permute-done | bytes 417824 | tf_op jit(solution)/shard_map/ppermute | solution.py:20
  91.5 7.7 %collective-permute-done.22.refs_3_ = f32[136,768]{1,0:T(8,128)S(1)} collective-permute-done((f32[136,768]{1,0:T(8,128)S(1)}, f32[136,768]{1,0:T(8,128)S(1)}, u32[]{:S(2)}, u32[]{:S(2)}) %collective-permute-start.22) | collective-permute-done | bytes 417824 | tf_op jit(solution)/shard_map/ppermute | solution.py:25
  101.1 3.2 %collective-permute-start.26 = (f32[136,768]{1,0:T(8,128)S(1)}, f32[136,768]{1,0:T(8,128)S(1)}, u32[]{:S(2)}, u32[]{:S(2)}) collective-permute-start(f32[136,768]{1,0:T(8,128)S(1)} %get-tuple-element.129.refs_4_), channel_id=1, source_target_pairs={{0,8},{8,0},{16,24},{24,16},{1,9},{9,1},{17,25},{25,17},{2,10},{10... | collective-permute-start | bytes 1253384 | tf_op jit(solution)/shard_map/ppermute | solution.py:25
  104.5 2.5 %place.5 = (f32[1024,3072]{1,0:T(8,128)}, f32[768,768]{1,0:T(8,128)S(1)}) custom-call(s32[4]{0:T(128)S(1)} %pad_add_fusion.sel, f32[136,768]{1,0:T(8,128)S(1)} %finish.1.both_ref.refs_0_, f32[136,768]{1,0:T(8,128)S(1)} %hold.11.px0_ref.refs_1_, f32[136,768]{1,0:T(8,128)S(1)} %get-tuple-element.124.py0_ref.refs_2_, ...), custom_call_target="tpu_custom_call" | custom-call | flops 55000000 | bytes 180000 | tf_op jit(solution)/shard_map/place/pallas_call | solution.py:765
  108.4 8.3 %collective-permute-done.26.refs_2_ = f32[136,768]{1,0:T(8,128)S(1)} collective-permute-done((f32[136,768]{1,0:T(8,128)S(1)}, f32[136,768]{1,0:T(8,128)S(1)}, u32[]{:S(2)}, u32[]{:S(2)}) %collective-permute-start.26) | collective-permute-done | bytes 417824 | tf_op jit(solution)/shard_map/ppermute | solution.py:25
  116.7 4.1 %collective-permute-done.27.refs_3_ = f32[136,768]{1,0:T(8,128)S(1)} collective-permute-done((f32[136,768]{1,0:T(8,128)S(1)}, f32[136,768]{1,0:T(8,128)S(1)}, u32[]{:S(2)}, u32[]{:S(2)}) %collective-permute-start.27) | collective-permute-done | bytes 417824 | tf_op jit(solution)/shard_map/ppermute | solution.py:25
  121.6 2.0 %collective-permute-start.28 = (f32[168,768]{1,0:T(8,128)S(1)}, f32[168,768]{1,0:T(8,128)S(1)}, u32[]{:S(2)}, u32[]{:S(2)}) collective-permute-start(f32[168,768]{1,0:T(8,128)S(1)} %stack.23), channel_id=1, source_target_pairs={{0,2},{2,0},{1,3},{3,1},{4,6},{6,4},{5,7},{7,5},{8,10},{10,8},{9,1... | collective-permute-start | bytes 1548296 | tf_op jit(solution)/shard_map/ppermute | solution.py:20
  123.6 3.0 %place.6 = (f32[1024,3072]{1,0:T(8,128)}, f32[512,768]{1,0:T(8,128)S(1)}) custom-call(s32[4]{0:T(128)S(1)} %pad_add_fusion.sel, f32[256,768]{1,0:T(8,128)S(1)} %get-tuple-element.134.refs_1_.refs_0_, f32[256,768]{1,0:T(8,128)S(1)} %get-tuple-element.133.refs_1_, f32[768,768]{1,0:T(8,128)S(1)} %collective-permute-done.31.refs_2_, ...), custom_call_target="tpu_custom_call", output_to_operand_aliasing={{0}: (4, {})} | custom-call | flops 55000000 | bytes 180000 | tf_op jit(solution)/shard_map/place/pallas_call | solution.py:765
  126.7 1.6 %place.7 = (f32[1024,3072]{1,0:T(8,128)}, f32[256,768]{1,0:T(8,128)S(1)}) custom-call(s32[4]{0:T(128)S(1)} %pad_add_fusion.sel, f32[136,768]{1,0:T(8,128)S(1)} %get-tuple-element.132.refs_0_.refs_5_, f32[136,768]{1,0:T(8,128)S(1)} %get-tuple-element.135.refs_0_.refs_2_.refs_1_.refs_7_, ...), custom_call_target="tpu_custom_call", output_to_operand_aliasing={{0}: (3, {})} | custom-call | flops 55000000 | bytes 180000 | tf_op jit(solution)/shard_map/place/pallas_call | solution.py:765
  131.4 2.5 %place.8 = (f32[1024,3072]{1,0:T(8,128)}, f32[1,1024]{1,0:T(1,128)}, f32[1,1024]{1,0:T(1,128)}, f32[1,1024]{1,0:T(1,128)}, f32[1,1024]{1,0:T(1,128)}, /*index=5*/f32[1,1024]{1,0:T(1,128)}, f32[1,1024]{1,0:T(1,128)}) custom-call(s32[4]{0:T(128)S(1)} %pad_add_fusion.sel, ...), custom_call_target="tpu_custom_call", output_to_operand_aliasing={{0}: (9, {})} | custom-call | flops 55000000 | bytes 180000 | tf_op jit(solution)/shard_map/place/pallas_call | solution.py:765
  134.2 2.1 %place.9 = f32[1024,3072]{1,0:T(8,128)} custom-call(s32[4]{0:T(128)S(1)} %pad_add_fusion.sel, f32[168,768]{1,0:T(8,128)S(1)} %collective-permute-done.32.refs_0_, f32[168,768]{1,0:T(8,128)S(1)} %collective-permute-done.33.refs_1_, f32[184,768]{1,0:T(8,128)S(1)} %collective-permute-done.34.refs_2_, ...), custom_call_target="tpu_custom_call", output_to_operand_aliasing={{}: (5, {})} | custom-call | flops 55000000 | bytes 180000 | tf_op jit(solution)/shard_map/place/pallas_call | solution.py:765
  (103 shorter events, 27.4 us)
Async XLA Ops:
  1.9 6.9 %collective-permute-start = (f32[176,1024]{1,0:T(8,128)S(1)}, f32[176,1024]{1,0:T(8,128)S(1)}, u32[]{:S(2)}, u32[]{:S(2)}) collective-permute-start(f32[176,1024]{1,0:T(8,128)S(1)} %get-tuple-element.80.tok0.refs_0_), channel_id=1, source_target_pairs={{0,1},{1,0},{2,3},{3,2},{4,5},{5,4},{6,7},{7,6},{8,9},{9,8},{10,11... | collective-permute-start | bytes 2162696 | tf_op jit(solution)/shard_map/ppermute | solution.py:20
  2.4 8.7 %collective-permute-start.1 = (f32[32,1024]{1,0:T(8,128)S(1)}, f32[32,1024]{1,0:T(8,128)S(1)}, u32[]{:S(2)}, u32[]{:S(2)}) collective-permute-start(f32[32,1024]{1,0:T(8,128)S(1)} %slice_bitcast_fusion.2), channel_id=1, source_target_pairs={{0,2},{2,0},{1,3},{3,1},{4,6},{6,4},{5,7},{7,5},{8,10},{10,8},{9,1... | collective-permute-start | bytes 393224 | tf_op jit(solution)/shard_map/ppermute | solution.py:20
  5.0 9.7 %collective-permute-start.3 = (f32[64,1024]{1,0:T(8,128)S(1)}, f32[64,1024]{1,0:T(8,128)S(1)}, u32[]{:S(2)}, u32[]{:S(2)}) collective-permute-start(f32[64,1024]{1,0:T(8,128)S(1)} %slice_bitcast_fusion.1), channel_id=1, source_target_pairs={{0,2},{2,0},{1,3},{3,1},{4,6},{6,4},{5,7},{7,5},{8,10},{10,8},{9,1... | collective-permute-start | bytes 786440 | tf_op jit(solution)/shard_map/ppermute | solution.py:20
  11.1 3.6 %collective-permute-start.2 = (f32[32,1024]{1,0:T(8,128)S(1)}, f32[32,1024]{1,0:T(8,128)S(1)}, u32[]{:S(2)}, u32[]{:S(2)}) collective-permute-start(f32[32,1024]{1,0:T(8,128)S(1)} %hold.8.refs_0_.refs_2_), channel_id=1, source_target_pairs={{0,1},{1,0},{2,3},{3,2},{4,5},{5,4},{6,7},{7,6},{8,9},{9,8},{10,11... | collective-permute-start | bytes 393224 | tf_op jit(solution)/shard_map/ppermute | solution.py:20
  12.3 10.5 %collective-permute-start.5 = (f32[80,1024]{1,0:T(8,128)S(1)}, f32[80,1024]{1,0:T(8,128)S(1)}, u32[]{:S(2)}, u32[]{:S(2)}) collective-permute-start(f32[80,1024]{1,0:T(8,128)S(1)} %slice_bitcast_fusion), channel_id=1, source_target_pairs={{0,2},{2,0},{1,3},{3,1},{4,6},{6,4},{5,7},{7,5},{8,10},{10,8},{9,1... | collective-permute-start | bytes 983048 | tf_op jit(solution)/shard_map/ppermute | solution.py:20
  15.3 16.5 %collective-permute-start.8 = (f32[352,256]{1,0:T(8,128)S(1)}, f32[352,256]{1,0:T(8,128)S(1)}, u32[]{:S(2)}, u32[]{:S(2)}) collective-permute-start(f32[352,256]{1,0:T(8,128)S(1)} %pack_cot.1), channel_id=1, source_target_pairs={{0,2},{2,0},{1,3},{3,1},{4,6},{6,4},{5,7},{7,5},{8,10},{10,8},{9,1... | collective-permute-start | bytes 1081352 | tf_op jit(solution)/shard_map/ppermute | solution.py:20
  36.1 12.0 %collective-permute-start.10 = (f32[128,768]{1,0:T(8,128)S(1)}, f32[128,768]{1,0:T(8,128)S(1)}, u32[]{:S(2)}, u32[]{:S(2)}) collective-permute-start(f32[128,768]{1,0:T(8,128)S(1)} %get-tuple-element.109), channel_id=1, source_target_pairs={{0,4},{4,0},{1,5},{5,1},{2,6},{6,2},{3,7},{7,3},{8,12},{12,8},{9,1... | collective-permute-start | bytes 1179656 | tf_op jit(solution)/shard_map/ppermute | solution.py:20
  39.2 17.2 %collective-permute-start.14 = (f32[128,768]{1,0:T(8,128)S(1)}, f32[128,768]{1,0:T(8,128)S(1)}, u32[]{:S(2)}, u32[]{:S(2)}) collective-permute-start(f32[128,768]{1,0:T(8,128)S(1)} %get-tuple-element.110.refs_0_), channel_id=1, source_target_pairs={{0,4},{4,0},{1,5},{5,1},{2,6},{6,2},{3,7},{7,3},{8,12},{12,8},{9,1... | collective-permute-start | bytes 1179656 | tf_op jit(solution)/shard_map/ppermute | solution.py:20
  39.4 11.3 %collective-permute-start.11 = (f32[128,768]{1,0:T(8,128)S(1)}, f32[128,768]{1,0:T(8,128)S(1)}, u32[]{:S(2)}, u32[]{:S(2)}) collective-permute-start(f32[128,768]{1,0:T(8,128)S(1)} %get-tuple-element.114), channel_id=1, source_target_pairs={{0,8},{8,0},{16,24},{24,16},{1,9},{9,1},{17,25},{25,17},{2,10},{10... | collective-permute-start | bytes 1179656 | tf_op jit(solution)/shard_map/ppermute | solution.py:25
  48.1 12.2 %collective-permute-start.15 = (f32[128,768]{1,0:T(8,128)S(1)}, f32[128,768]{1,0:T(8,128)S(1)}, u32[]{:S(2)}, u32[]{:S(2)}) collective-permute-start(f32[128,768]{1,0:T(8,128)S(1)} %add.10.refs_0_), channel_id=1, source_target_pairs={{0,8},{8,0},{16,24},{24,16},{1,9},{9,1},{17,25},{25,17},{2,10},{10... | collective-permute-start | bytes 1179656 | tf_op jit(solution)/shard_map/ppermute | solution.py:25
  50.2 14.2 %collective-permute-start.9 = (f32[360,1280]{1,0:T(8,128)S(1)}, f32[360,1280]{1,0:T(8,128)S(1)}, u32[]{:S(2)}, u32[]{:S(2)}) collective-permute-start(f32[360,1280]{1,0:T(8,128)S(1)} %get-tuple-element.107.refs_2_.refs_0_), channel_id=1, source_target_pairs={{0,1},{1,0},{2,3},{3,2},{4,5},{5,4},{6,7},{7,6},{8,9},{9,8},{10,11... | collective-permute-start | bytes 5529608 | tf_op jit(solution)/shard_map/ppermute | solution.py:20
  50.2 18.0 %collective-permute-start.13 = (f32[128,768]{1,0:T(8,128)S(1)}, f32[128,768]{1,0:T(8,128)S(1)}, u32[]{:S(2)}, u32[]{:S(2)}) collective-permute-start(f32[128,768]{1,0:T(8,128)S(1)} %get-tuple-element.115), channel_id=1, source_target_pairs={{0,8},{8,0},{16,24},{24,16},{1,9},{9,1},{17,25},{25,17},{2,10},{10... | collective-permute-start | bytes 1179656 | tf_op jit(solution)/shard_map/ppermute | solution.py:25
  50.7 17.5 %collective-permute-start.12 = (f32[128,768]{1,0:T(8,128)S(1)}, f32[128,768]{1,0:T(8,128)S(1)}, u32[]{:S(2)}, u32[]{:S(2)}) collective-permute-start(f32[128,768]{1,0:T(8,128)S(1)} %add.11), channel_id=1, source_target_pairs={{0,4},{4,0},{1,5},{5,1},{2,6},{6,2},{3,7},{7,3},{8,12},{12,8},{9,1... | collective-permute-start | bytes 1179656 | tf_op jit(solution)/shard_map/ppermute | solution.py:20
  60.3 17.5 %collective-permute-start.16 = (f32[128,768]{1,0:T(8,128)S(1)}, f32[128,768]{1,0:T(8,128)S(1)}, u32[]{:S(2)}, u32[]{:S(2)}) collective-permute-start(f32[128,768]{1,0:T(8,128)S(1)} %add.13), channel_id=1, source_target_pairs={{0,24},{8,16},{16,8},{24,0},{1,25},{9,17},{17,9},{25,1},{2,26},{10... | collective-permute-start | bytes 1179656 | tf_op jit(solution)/shard_map/ppermute | solution.py:25
  65.3 19.0 %collective-permute-start.19 = (f32[176,1024]{1,0:T(8,128)S(1)}, f32[176,1024]{1,0:T(8,128)S(1)}, u32[]{:S(2)}, u32[]{:S(2)}) collective-permute-start(f32[176,1024]{1,0:T(8,128)S(1)} %get-tuple-element.119), channel_id=1, source_target_pairs={{0,2},{2,0},{1,3},{3,1},{4,6},{6,4},{5,7},{7,5},{8,10},{10,8},{9,1... | collective-permute-start | bytes 2162696 | tf_op jit(solution)/shard_map/ppermute | solution.py:20
  77.9 10.5 %collective-permute-start.18 = (f32[136,768]{1,0:T(8,128)S(1)}, f32[136,768]{1,0:T(8,128)S(1)}, u32[]{:S(2)}, u32[]{:S(2)}) collective-permute-start(f32[136,768]{1,0:T(8,128)S(1)} %finish.1.both_ref.refs_0_), channel_id=1, source_target_pairs={{0,2},{2,0},{1,3},{3,1},{4,6},{6,4},{5,7},{7,5},{8,10},{10,8},{9,1... | collective-permute-start | bytes 1253384 | tf_op jit(solution)/shard_map/ppermute | solution.py:20
  79.5 12.0 %collective-permute-start.17 = (f32[136,768]{1,0:T(8,128)S(1)}, f32[136,768]{1,0:T(8,128)S(1)}, u32[]{:S(2)}, u32[]{:S(2)}) collective-permute-start(f32[136,768]{1,0:T(8,128)S(1)} %finish.1.both_ref.refs_0_), channel_id=1, source_target_pairs={{0,4},{4,0},{1,5},{5,1},{2,6},{6,2},{3,7},{7,3},{8,12},{12,8},{9,1... | collective-permute-start | bytes 1253384 | tf_op jit(solution)/shard_map/ppermute | solution.py:20
  81.0 18.1 %collective-permute-start.22 = (f32[136,768]{1,0:T(8,128)S(1)}, f32[136,768]{1,0:T(8,128)S(1)}, u32[]{:S(2)}, u32[]{:S(2)}) collective-permute-start(f32[136,768]{1,0:T(8,128)S(1)} %finish.1.both_ref.refs_0_), channel_id=1, source_target_pairs={{0,8},{8,0},{16,24},{24,16},{1,9},{9,1},{17,25},{25,17},{2,10},{10... | collective-permute-start | bytes 1253384 | tf_op jit(solution)/shard_map/ppermute | solution.py:25
  81.8 17.4 %collective-permute-start.23 = (f32[136,768]{1,0:T(8,128)S(1)}, f32[136,768]{1,0:T(8,128)S(1)}, u32[]{:S(2)}, u32[]{:S(2)}) collective-permute-start(f32[136,768]{1,0:T(8,128)S(1)} %finish.1.both_ref.refs_0_), channel_id=1, source_target_pairs={{0,24},{8,16},{16,8},{24,0},{1,25},{9,17},{17,9},{25,1},{2,26},{10... | collective-permute-start | bytes 1253384 | tf_op jit(solution)/shard_map/ppermute | solution.py:25
  88.4 10.7 %collective-permute-start.20 = (f32[136,768]{1,0:T(8,128)S(1)}, f32[136,768]{1,0:T(8,128)S(1)}, u32[]{:S(2)}, u32[]{:S(2)}) collective-permute-start(f32[136,768]{1,0:T(8,128)S(1)} %hold.11.px0_ref.refs_1_), channel_id=1, source_target_pairs={{0,4},{4,0},{1,5},{5,1},{2,6},{6,2},{3,7},{7,3},{8,12},{12,8},{9,1... | collective-permute-start | bytes 1253384 | tf_op jit(solution)/shard_map/ppermute | solution.py:20
  90.0 9.2 %collective-permute-start.21 = (f32[176,512]{1,0:T(8,128)S(1)}, f32[176,512]{1,0:T(8,128)S(1)}, u32[]{:S(2)}, u32[]{:S(2)}) collective-permute-start(f32[176,512]{1,0:T(8,128)S(1)} %hold.12), channel_id=1, source_target_pairs={{0,2},{2,0},{1,3},{3,1},{4,6},{6,4},{5,7},{7,5},{8,10},{10,8},{9,1... | collective-permute-start | bytes 1081352 | tf_op jit(solution)/shard_map/ppermute | solution.py:20
  99.3 21.5 %collective-permute-start.24 = (f32[256,768]{1,0:T(8,128)S(1)}, f32[256,768]{1,0:T(8,128)S(1)}, u32[]{:S(2)}, u32[]{:S(2)}) collective-permute-start(f32[256,768]{1,0:T(8,128)S(1)} %get-tuple-element.128.refs_4_), channel_id=1, source_target_pairs={{0,2},{2,0},{1,3},{3,1},{4,6},{6,4},{5,7},{7,5},{8,10},{10,8},{9,1... | collective-permute-start | bytes 2359304 | tf_op jit(solution)/shard_map/ppermute | solution.py:20
  99.9 20.9 %collective-permute-start.25 = (f32[256,768]{1,0:T(8,128)S(1)}, f32[256,768]{1,0:T(8,128)S(1)}, u32[]{:S(2)}, u32[]{:S(2)}) collective-permute-start(f32[256,768]{1,0:T(8,128)S(1)} %get-tuple-element.128.refs_4_), channel_id=1, source_target_pairs={{0,4},{4,0},{1,5},{5,1},{2,6},{6,2},{3,7},{7,3},{8,12},{12,8},{9,1... | collective-permute-start | bytes 2359304 | tf_op jit(solution)/shard_map/ppermute | solution.py:20
  101.1 15.6 %collective-permute-start.26 = (f32[136,768]{1,0:T(8,128)S(1)}, f32[136,768]{1,0:T(8,128)S(1)}, u32[]{:S(2)}, u32[]{:S(2)}) collective-permute-start(f32[136,768]{1,0:T(8,128)S(1)} %get-tuple-element.129.refs_4_), channel_id=1, source_target_pairs={{0,8},{8,0},{16,24},{24,16},{1,9},{9,1},{17,25},{25,17},{2,10},{10... | collective-permute-start | bytes 1253384 | tf_op jit(solution)/shard_map/ppermute | solution.py:25
  104.4 16.4 %collective-permute-start.27 = (f32[136,768]{1,0:T(8,128)S(1)}, f32[136,768]{1,0:T(8,128)S(1)}, u32[]{:S(2)}, u32[]{:S(2)}) collective-permute-start(f32[136,768]{1,0:T(8,128)S(1)} %get-tuple-element.130), channel_id=1, source_target_pairs={{0,24},{8,16},{16,8},{24,0},{1,25},{9,17},{17,9},{25,1},{2,26},{10... | collective-permute-start | bytes 1253384 | tf_op jit(solution)/shard_map/ppermute | solution.py:25
  107.0 16.6 %collective-permute-start.31 = (f32[768,768]{1,0:T(8,128)S(1)}, f32[768,768]{1,0:T(8,128)S(1)}, u32[]{:S(2)}, u32[]{:S(2)}) collective-permute-start(f32[768,768]{1,0:T(8,128)S(1)} %get-tuple-element.131.refs_4_.refs_0_), channel_id=1, source_target_pairs={{0,1},{1,0},{2,3},{3,2},{4,5},{5,4},{6,7},{7,6},{8,9},{9,8},{10,11... | collective-permute-start | bytes 7077896 | tf_op jit(solution)/shard_map/ppermute | solution.py:20
  120.8 10.0 %collective-permute-start.30 = (f32[184,768]{1,0:T(8,128)S(1)}, f32[184,768]{1,0:T(8,128)S(1)}, u32[]{:S(2)}, u32[]{:S(2)}) collective-permute-start(f32[184,768]{1,0:T(8,128)S(1)} %stack.25), channel_id=1, source_target_pairs={{0,8},{8,0},{16,24},{24,16},{1,9},{9,1},{17,25},{25,17},{2,10},{10... | collective-permute-start | bytes 1695752 | tf_op jit(solution)/shard_map/ppermute | solution.py:25
  120.9 9.2 %collective-permute-start.29 = (f32[168,768]{1,0:T(8,128)S(1)}, f32[168,768]{1,0:T(8,128)S(1)}, u32[]{:S(2)}, u32[]{:S(2)}) collective-permute-start(f32[168,768]{1,0:T(8,128)S(1)} %stack.24), channel_id=1, source_target_pairs={{0,4},{4,0},{1,5},{5,1},{2,6},{6,2},{3,7},{7,3},{8,12},{12,8},{9,1... | collective-permute-start | bytes 1548296 | tf_op jit(solution)/shard_map/ppermute | solution.py:20
  121.6 9.2 %collective-permute-start.28 = (f32[168,768]{1,0:T(8,128)S(1)}, f32[168,768]{1,0:T(8,128)S(1)}, u32[]{:S(2)}, u32[]{:S(2)}) collective-permute-start(f32[168,768]{1,0:T(8,128)S(1)} %stack.23), channel_id=1, source_target_pairs={{0,2},{2,0},{1,3},{3,1},{4,6},{6,4},{5,7},{7,5},{8,10},{10,8},{9,1... | collective-permute-start | bytes 1548296 | tf_op jit(solution)/shard_map/ppermute | solution.py:20
  126.7 4.7 %collective-permute-start.36 = (f32[512,768]{1,0:T(8,128)S(1)}, f32[512,768]{1,0:T(8,128)S(1)}, u32[]{:S(2)}, u32[]{:S(2)}) collective-permute-start(f32[512,768]{1,0:T(8,128)S(1)} %get-tuple-element.142.refs_0_), channel_id=1, source_target_pairs={{0,1},{1,0},{2,3},{3,2},{4,5},{5,4},{6,7},{7,6},{8,9},{9,8},{10,11... | collective-permute-start | bytes 4718600 | tf_op jit(solution)/shard_map/ppermute | solution.py:20
  128.3 5.9 %collective-permute-start.35 = (f32[256,768]{1,0:T(8,128)S(1)}, f32[256,768]{1,0:T(8,128)S(1)}, u32[]{:S(2)}, u32[]{:S(2)}) collective-permute-start(f32[256,768]{1,0:T(8,128)S(1)} %get-tuple-element.138.refs_3_.refs_1_), channel_id=1, source_target_pairs={{0,1},{1,0},{2,3},{3,2},{4,5},{5,4},{6,7},{7,6},{8,9},{9,8},{10,11... | collective-permute-start | bytes 2359304 | tf_op jit(solution)/shard_map/ppermute | solution.py:20
  130.8 3.4 %collective-permute-start.34 = (f32[184,768]{1,0:T(8,128)S(1)}, f32[184,768]{1,0:T(8,128)S(1)}, u32[]{:S(2)}, u32[]{:S(2)}) collective-permute-start(f32[184,768]{1,0:T(8,128)S(1)} %get-tuple-element.141.refs_2_.refs_6_), channel_id=1, source_target_pairs={{0,1},{1,0},{2,3},{3,2},{4,5},{5,4},{6,7},{7,6},{8,9},{9,8},{10,11... | collective-permute-start | bytes 1695752 | tf_op jit(solution)/shard_map/ppermute | solution.py:20
  (14 other events, 24.4 us)
